TPU v7x, 32 devices: a whole 2x2x4 slice. The times are simulated.
32 devices in a mesh: groups: 2 (over y), seq: 4 (over z), dp: 4 (over x, core).
Axes of the slice: x: 2, y: 2, z: 4, core: 2. Of those that a mesh axis runs over, the one named last changes fastest.
Arguments:
- tokens: bfloat16 [8, 1536, 1024], P(('groups', 'dp'), 'seq'), parts along dimension 0, may hold values from -36 to 36
- segment_ids: int32 [8, 1536], P(('groups', 'dp'), 'seq'), parts along dimension 0, may hold values from 0 to 3, never falling along the last dimension, each value on 1 to 768 neighbouring positions
- norm_gain: float32 [1024], replicated, may hold values from 0.25 to 1.75
- w_qkv: bfloat16 [1024, 1536], P('dp'), may hold values from -0.1875 to 0.1875
- head_gain: float32 [512], replicated, may hold values from 0.25 to 1.75
- w_out: bfloat16 [512, 1024], P('dp'), may hold values from -0.25 to 0.25
- cotangent: bfloat16 [8, 1536, 1024], P(('groups', 'dp'), 'seq'), parts along dimension 0, may hold values from -6 to 6
Outputs:
- output: bfloat16 [8, 1536, 1024], P(('groups', 'dp'), 'seq'), parts along dimension 0
- grad_input: bfloat16 [8, 1536, 1024], P(('groups', 'dp'), 'seq'), parts along dimension 0
- grad_out_weight: float32 [1024, 1024], P(('groups', 'dp')), parts along dimension 0
There are 2 independent parts, one for each index of `groups`. A program takes and returns all parts, laid end to end along the dimension named above; an argument that names none is the same for every part. Nothing has to cross between parts.
Inputs may be any that keep to these rules, and one draw needn't show every extreme that they name: `segment_ids`: within each micro-batch the segment numbers never fall along the samples, every number from 0 to 3 occurs, no segment has more than 768 samples, and one segment of each micro-batch has exactly 768.
All inputs are finite; a program needn't handle non-finite values.
Results may differ from a plain program's by a relative error of at most 0.0065.
Values may be sent and summed in bfloat16 or wider, within the bound.
No kernel may reach another device: no remote copies, remote signals or barrier semaphores. Data moves between devices by JAX's collectives and lax.ppermute only.
A program may use at most 128 MiB of HBM per device.

v0:
```python
import math

import jax
import jax.numpy as jnp
from jax import lax
from jax.sharding import PartitionSpec as P

D = 1024
HEADS = 4
HEAD_DIM = 128


epsilon = 1e-06


def prefix(array, axis, combine, identity, reverse):
    devices, position = (lax.axis_size(axis), lax.axis_index(axis))
    everything = jax.tree.map(lambda part: lax.all_gather(part, axis), array)
    start = jax.tree.map(
        lambda part, zero: jnp.broadcast_to(jnp.asarray(zero, part.dtype), part.shape),
        array,
        identity,
    )

    def turn(k, before):
        at = devices - 1 - k if reverse else k
        reached = at > position if reverse else at < position
        new = combine(before, jax.tree.map(lambda part: part[at], everything))
        return jax.tree.map(lambda a, b: jnp.where(reached, a, b), new, before)

    return lax.fori_loop(0, devices, turn, start)


def feature_map(raw_value):
    return jnp.where(raw_value > 0, raw_value + 1.0, jnp.exp(jnp.minimum(raw_value, 0.0)))


def feature_slope(raw_value):
    return jnp.where(raw_value > 0, 1.0, jnp.exp(jnp.minimum(raw_value, 0.0)))


def link_blocks(earlier, following):
    a_begin, a_end, a_state = earlier
    b_begin, b_end, b_state = following
    a_empty = a_begin < 0
    b_empty = b_begin < 0
    joined = (b_begin == b_end) & (a_end == b_begin)
    merged = b_state + jnp.where(joined[:, None, None, None], a_state, 0.0)
    merged = jnp.where(b_empty[:, None, None, None], a_state, merged)
    begin_id = jnp.where(a_empty, b_begin, a_begin)
    end_id = jnp.where(b_empty, a_end, b_end)
    return (begin_id, end_id, merged)


def contract_last(left, right):
    return lax.dot_general(
        left, right, (((1,), (1,)), ((), ())), preferred_element_type=jnp.float32
    )


def shards(tokens, segment_ids, norm_gain, w_qkv, head_gain, w_out, cotangent):
    highest = lax.Precision.HIGHEST
    micro_count, length = segment_ids.shape
    attn_width = HEADS * HEAD_DIM
    flat_in = tokens.reshape(-1, D).astype(jnp.float32)
    inv_rms = lax.rsqrt(jnp.mean(flat_in * flat_in, axis=1, keepdims=True) + epsilon)
    normed = (flat_in * inv_rms * norm_gain).astype(jnp.bfloat16)
    qkv_full = lax.all_gather(w_qkv, "dp", axis=0, tiled=True)
    out_full = lax.all_gather(w_out, "dp", axis=0, tiled=True)
    projected = jnp.dot(normed, qkv_full, preferred_element_type=jnp.float32).astype(jnp.bfloat16)
    shaped = projected.reshape(micro_count, length, 3, HEADS, HEAD_DIM)
    raw_q = shaped[:, :, 0]
    raw_k = shaped[:, :, 1]
    values = shaped[:, :, 2]
    feat_q = feature_map(raw_q.astype(jnp.float32)).astype(jnp.bfloat16)
    feat_k = feature_map(raw_k.astype(jnp.float32)).astype(jnp.bfloat16)
    same_seg = segment_ids[:, :, None] == segment_ids[:, None, :]
    causal_order = lax.broadcasted_iota(jnp.int32, (length, length), 0) >= lax.broadcasted_iota(
        jnp.int32, (length, length), 1
    )
    causal = (same_seg & causal_order[None]).astype(jnp.float32)
    scores = (
        jnp.einsum("mthd,mshd->mhts", feat_q, feat_k, preferred_element_type=jnp.float32)
        * causal[:, None]
    ).astype(jnp.bfloat16)
    intra_sum = jnp.einsum("mhts,mshe->mthe", scores, values, preferred_element_type=jnp.float32)
    seg_float = segment_ids.astype(jnp.float32)
    last_id = seg_float[:, -1]
    first_id = seg_float[:, 0]
    tail_mask = (seg_float == last_id[:, None]).astype(jnp.bfloat16)
    block_state = jnp.einsum(
        "mshd,mshe->mhde",
        feat_k * tail_mask[:, :, None, None],
        values,
        preferred_element_type=jnp.float32,
    )
    no_block = jnp.full((micro_count,), -1.0, jnp.float32)
    identity = (
        no_block,
        no_block,
        jnp.zeros((micro_count, HEADS, HEAD_DIM, HEAD_DIM), jnp.float32),
    )
    carry_begin, carry_id, carry_state = prefix(
        (first_id, last_id, block_state), "seq", link_blocks, identity, False
    )
    take_fwd = (seg_float == carry_id[:, None]).astype(jnp.float32)[:, :, None, None]
    q_wide = feat_q.astype(jnp.float32)
    carried = jnp.einsum("mthd,mhde->mthe", q_wide, carry_state, precision=highest) * take_fwd
    attention = intra_sum + carried
    norm_ratio = lax.rsqrt(jnp.mean(attention * attention, axis=-1, keepdims=True) + epsilon)
    head_scale = head_gain.reshape(HEADS, HEAD_DIM)
    mixed_out = (attention * norm_ratio * head_scale).astype(jnp.bfloat16).reshape(-1, attn_width)
    mapped = jnp.dot(mixed_out, out_full, preferred_element_type=jnp.float32)
    output = (flat_in + mapped).astype(jnp.bfloat16).reshape(tokens.shape)
    cot_flat = cotangent.reshape(-1, D)
    grad_scale = 1.0 / math.sqrt(micro_count * lax.axis_size("dp") * length * lax.axis_size("seq"))
    weight_term = lax.dot_general(
        mixed_out, cot_flat, (((0,), (0,)), ((), ())), preferred_element_type=jnp.float32
    )
    summed = lax.psum(weight_term, "seq")
    grad_out_weight = lax.psum_scatter(summed, "dp", scatter_dimension=0, tiled=True) * grad_scale
    d_mixed = contract_last(cot_flat, out_full)
    upstream = d_mixed.reshape(micro_count, length, HEADS, HEAD_DIM) * head_scale
    d_attn = (
        norm_ratio * upstream
        - norm_ratio**3 * attention * jnp.mean(attention * upstream, axis=-1, keepdims=True)
    ).astype(jnp.bfloat16)
    head_mask = (seg_float == first_id[:, None]).astype(jnp.bfloat16)
    block_grad = jnp.einsum(
        "mthd,mthe->mhde",
        feat_q * head_mask[:, :, None, None],
        d_attn,
        preferred_element_type=jnp.float32,
    )
    back_begin, back_id, back_state = prefix(
        (last_id, first_id, block_grad), "seq", link_blocks, identity, True
    )
    take_back = (seg_float == back_id[:, None]).astype(jnp.float32)[:, :, None, None]
    d_scores = (
        jnp.einsum("mthe,mshe->mhts", d_attn, values, preferred_element_type=jnp.float32)
        * causal[:, None]
    ).astype(jnp.bfloat16)
    d_wide = d_attn.astype(jnp.float32)
    d_feat_q = (
        jnp.einsum("mhts,mshd->mthd", d_scores, feat_k, preferred_element_type=jnp.float32)
        + jnp.einsum("mthe,mhde->mthd", d_wide, carry_state, precision=highest) * take_fwd
    )
    d_feat_k = (
        jnp.einsum("mhts,mthd->mshd", d_scores, feat_q, preferred_element_type=jnp.float32)
        + jnp.einsum("mshe,mhde->mshd", values.astype(jnp.float32), back_state, precision=highest)
        * take_back
    )
    d_values = (
        jnp.einsum("mhts,mthe->mshe", scores, d_attn, preferred_element_type=jnp.float32)
        + jnp.einsum("mshd,mhde->mshe", feat_k.astype(jnp.float32), back_state, precision=highest)
        * take_back
    )
    d_query = (d_feat_q * feature_slope(raw_q.astype(jnp.float32))).astype(jnp.bfloat16)
    d_key = (d_feat_k * feature_slope(raw_k.astype(jnp.float32))).astype(jnp.bfloat16)
    d_value = d_values.astype(jnp.bfloat16)
    d_proj = jnp.stack([d_query, d_key, d_value], axis=2).reshape(-1, 3 * attn_width)
    d_normed = contract_last(d_proj, qkv_full)
    norm_grad = d_normed * norm_gain
    grad_flat = (
        cot_flat.astype(jnp.float32)
        + inv_rms * norm_grad
        - inv_rms**3 * flat_in * jnp.mean(flat_in * norm_grad, axis=1, keepdims=True)
    )
    grad_input = grad_flat.astype(jnp.bfloat16).reshape(tokens.shape)
    return (output, grad_input, grad_out_weight)


def solution(mesh):
    in_specs = (
        P(("groups", "dp"), "seq", None),
        P(("groups", "dp"), "seq"),
        P(),
        P("dp", None),
        P(),
        P("dp", None),
        P(("groups", "dp"), "seq", None),
    )
    out_specs = (
        P(("groups", "dp"), "seq", None),
        P(("groups", "dp"), "seq", None),
        P(("groups", "dp"), None),
    )
    return jax.shard_map(shards, mesh=mesh, in_specs=in_specs, out_specs=out_specs, check_vma=False)
```

profile of v0, /device:TPU:0, one launch (start us, length us, event | category | flops | bytes accessed | tf_op | source)
XLA Modules:
  0.0 223.9 jit_solution(10019679156791507659)
XLA Ops:
  10.1 1.9 fusion.65
  12.2 28.6 %all-gather.7.cloned.1.call-done = bf16[1024,1536]{1,0:T(8,128)(2,1)} async-done(((bf16[256,1536]{1,0:T(8,128)(2,1)}), bf16[1024,1536]{1,0:T(8,128)(2,1)}) %all-gather.7.cloned.1.call-update) | async-done | bytes 3145744 | tf_op jit(solution)/shard_map/all_gather | solution.py:68
  40.8 4.4 %convolution_convert_fusion = bf16[384,1536]{1,0:T(8,128)(2,1)} fusion(bf16[1024,1536]{1,0:T(8,128)(2,1)} %all-gather.7.cloned.1.call-done, bf16[1,384,1024]{2,1,0:T(8,128)(2,1)S(1)} %copy-done.1, f32[1024]{0:T(1024)S(1)} %copy-done.17, f32[384]{0:T(512)S(1)} %get-tuple-element.428), kind=kOutput, calls=%fused_computation.13 | convolution fusion | flops 1210122240 | bytes 5117440 | tf_op jit(solution)/shard_map/dot_general | solution.py:70
  45.2 1.7 copy.56
  48.7 1.3 bitcast_dynamic-update-slice_fusion
  51.3 11.7 %all-reduce.2 = (f32[4]{0:T(128)S(1)}, f32[4]{0:T(128)S(1)}) all-reduce(f32[4]{0:T(128)S(1)} %bitcast_dynamic-update-slice_fusion.1, f32[4]{0:T(128)S(1)} %bitcast_dynamic-update-slice_fusion), channel_id=1, replica_groups=mesh['groups'=2,'seq'=4,'dp'=4] {'seq'}, use_global_device_ids=true, to_apply=%add | all-reduce | flops 8 | bytes 64
  63.2 2.1 convolution_multiply_fusion.1
  67.5 21.8 %all-gather.11.cloned.1.call-done = f32[16,128,128]{2,1,0:T(8,128)} async-done(((f32[4,128,128]{2,1,0:T(8,128)}), f32[16,128,128]{2,1,0:T(8,128)}) %all-gather.11.cloned.1.call-update) | async-done | bytes 1048592 | tf_op jit(solution)/shard_map/all_gather | solution.py:18
  89.3 19.5 %while.34 = (s32[]{:T(128)}, f32[1]{0:T(128)}, f32[1,4,128,128]{3,2,1,0:T(8,128)S(1)}, s32[]{:T(128)}, f32[4,1]{0,1:T(1,128)S(1)}, /*index=5*/f32[4,1]{0,1:T(1,1...) while((s32[]{:T(128)}, f32[1]{0:T(128)}, ...), condition=%wide.region_2.3_spmd.clone, body=%wide.region_1.2_spmd.clone.sunk | while | flops 327690 | bytes 786643 | solution.py:31
  108.8 1.7 fusion.40
  111.6 2.1 fusion.53
  113.7 2.1 fusion.43
  116.1 2.8 %convolution_bitcast_fusion = f32[1,4,128,384]{3,2,1,0:T(8,128)} fusion(bf16[384,4,128]{0,2,1:T(8,128)(2,1)} %copy-done.5, bf16[4,384,384]{2,1,0:T(8,128)(2,1)} %copy-done.7), kind=kOutput, calls=%fused_computation.25 | convolution fusion | flops 150994944 | bytes 2359296 | tf_op jit(solution)/shard_map/mhts,mthe->mshe/dot_general | solution.py:154
  120.0 1.4 fusion.26
  121.4 1.4 convolution_bitcast_fusion.1
  122.8 1.5 fusion.8
  124.3 17.0 %all-gather.13.cloned.1.call-done = f32[16,128,128]{2,1,0:T(8,128)} async-done(((f32[4,128,128]{2,1,0:T(8,128)}), f32[16,128,128]{2,1,0:T(8,128)}) %all-gather.13.cloned.1.call-update) | async-done | bytes 1048592 | tf_op jit(solution)/shard_map/all_gather | solution.py:18
  141.2 19.8 %while.35 = (s32[]{:T(128)}, f32[1]{0:T(128)}, f32[1,4,128,128]{3,2,1,0:T(8,128)S(1)}, s32[]{:T(128)}, f32[4,1]{0,1:T(1,128)S(1)}, /*index=5*/f32[4,1]{0,1:T(1,1...) while((s32[]{:T(128)}, f32[1]{0:T(128)}, ...), condition=%wide.region_6.7_spmd.clone, body=%wide.region_5.6_spmd.clone.sunk | while | flops 327694 | bytes 786705 | solution.py:31
  161.1 1.8 fusion.25
  165.0 1.5 fusion.7
  166.5 8.1 %reduce-scatter.2.cloned.1.call-done = f32[128,1024]{1,0:T(8,128)} async-done(((f32[512,1024]{1,0:T(8,128)}), f32[128,1024]{1,0:T(8,128)}) %reduce-scatter.2.cloned.1.call-update) | async-done | bytes 524304 | tf_op jit(solution)/shard_map/reduce_scatter | solution.py:121
  174.6 1.3 fusion.38
  175.9 39.2 %all-reduce.5.cloned.1.call-done = f32[128,1024]{1,0:T(8,128)} async-done(((f32[128,1024]{1,0:T(8,128)}), f32[128,1024]{1,0:T(8,128)}) %all-reduce.5.cloned.1.call-update) | async-done | bytes 524304 | tf_op jit(solution)/shard_map/psum | solution.py:120
  215.2 1.9 broadcast_multiply_fusion
  (92 shorter events, 26.6 us)
Async XLA Ops:
  7.2 4.8 %copy-start.1 = (bf16[1,384,1024]{2,1,0:T(8,128)(2,1)S(1)}, bf16[1,384,1024]{2,1,0:T(8,128)(2,1)}, u32[]{:S(2)}) copy-start(bf16[1,384,1024]{2,1,0:T(8,128)(2,1)} %param.11) | copy-start | bytes 2359300
  7.2 33.7 %copy-start.17 = (f32[1024]{0:T(1024)S(1)}, f32[1024]{0:T(1024)}, u32[]{:S(2)}) copy-start(f32[1024]{0:T(1024)} %param.13) | copy-start | bytes 12292
  7.2 33.7 %all-gather.7.cloned.1.call-start = ((), (), s32[]{:S(2)}) async-start(), calls=%async_computation.1 | async-start | bytes 3932160 | tf_op jit(solution)/shard_map/all_gather | solution.py:68
  7.9 55.2 %all-gather.9.cloned.1.call-start = ((), (), s32[]{:S(2)}) async-start(), calls=%async_computation.2 | async-start | bytes 1310720 | tf_op jit(solution)/shard_map/all_gather | solution.py:69
  8.7 80.6 %all-gather.11.cloned.1.call-start = ((), (), s32[]{:S(2)}) async-start(), calls=%async_computation.3 | async-start | bytes 1310720 | tf_op jit(solution)/shard_map/all_gather | solution.py:18
  46.9 1.1 copy-start.2
  46.9 1.2 copy-start.18
  46.9 16.2 %copy-start = (bf16[1,384,1024]{2,1,0:T(8,128)(2,1)S(1)}, bf16[1,384,1024]{2,1,0:T(8,128)(2,1)}, u32[]{:S(2)}) copy-start(bf16[1,384,1024]{2,1,0:T(8,128)(2,1)} %param.17) | copy-start | bytes 2359300
  46.9 16.2 %copy-start.15 = (f32[512]{0:T(512)S(1)}, f32[512]{0:T(512)}, u32[]{:S(2)}) copy-start(f32[512]{0:T(512)} %param.15) | copy-start | bytes 6148
  48.0 93.2 %all-gather.13.cloned.1.call-start = ((), (), s32[]{:S(2)}) async-start(), calls=%async_computation.4 | async-start | bytes 1310720 | tf_op jit(solution)/shard_map/all_gather | solution.py:18
  63.1 2.2 copy-start.11
  63.2 2.2 copy-start.3
  66.0 1.0 copy-start.7
  89.3 19.5 %copy-start.14 = (s32[1,384]{1,0:T(1,128)S(1)}, s32[1,384]{1,0:T(1,128)}, u32[]{:S(2)}) copy-start(s32[1,384]{1,0:T(1,128)} %param.12) | copy-start | bytes 4612
  110.8 2.9 %copy-start.9 = (bf16[1,384,4,128]{1,3,2,0:T(8,128)(2,1)}, bf16[1,384,4,128]{1,3,2,0:T(8,128)(2,1)S(1)}, u32[]{:S(2)}) copy-start(bf16[1,384,4,128]{1,3,2,0:T(8,128)(2,1)S(1)} %get-tuple-element.424) | copy-start | bytes 1179652
  113.7 60.9 %reduce-scatter.2.cloned.1.call-start = ((), (), s32[]{:S(2)}) async-start(), calls=%async_computation.5 | async-start | bytes 2621440 | tf_op jit(solution)/shard_map/reduce_scatter | solution.py:121
  115.8 99.4 %all-reduce.5.cloned.1.call-start = ((), (), s32[]{:S(2)}) async-start(), calls=%async_computation.6 | async-start | bytes 1048576 | tf_op jit(solution)/shard_map/psum | solution.py:120
  116.1 2.9 %copy-start.4 = (bf16[384,1536]{0,1:T(8,128)(2,1)S(1)}, bf16[384,1536]{0,1:T(8,128)(2,1)}, u32[]{:S(2)}) copy-start(bf16[384,1536]{0,1:T(8,128)(2,1)} %copy-done.2) | copy-start | bytes 3538948
  116.1 2.9 %copy-start.6 = (bf16[384,4,128]{0,2,1:T(8,128)(2,1)S(1)}, bf16[384,4,128]{0,2,1:T(8,128)(2,1)}, u32[]{:S(2)}) copy-start(bf16[384,4,128]{0,2,1:T(8,128)(2,1)} %copy-done.5) | copy-start | bytes 1179652
  116.1 2.9 %copy-start.12 = (f32[384,384]{1,0:T(8,128)S(1)}, f32[384,384]{1,0:T(8,128)}, u32[]{:S(2)}) copy-start(f32[384,384]{1,0:T(8,128)} %copy-done.11) | copy-start | bytes 1769476
  121.4 1.4 copy-start.8
  121.4 1.4 copy-start.10
  161.0 1.9 copy-start.19
  162.9 2.0 copy-start.16
  (2 other events, 1.8 us)
Sparse Core Ops, SparseCore 0:
  9.6 31.2 all-gather.6
  42.4 16.7 all-gather.8
  61.3 27.9 all-gather.10
  113.8 27.4 all-gather.12
  143.6 30.9 reduce-scatter.1
  176.9 38.2 all-reduce.4
where the time goes:
time: 225 us; the launch traced here: 224 us
  waiting for transfers between devices  116 us (52%)
  matrix products  26.8 us (12%)
  loops' own time  25.5 us (11%)
  other arithmetic  15.4 us (7%)
  between operations  14.5 us (6%)
  local copies, waits for them, and re-layouts  13.5 us (6%)
  blocking collectives  11.7 us (5%)
    psum x1, waiting for transfers between devices, shards(): summed = lax.psum(weight_term, 'seq')  39.2 us
    all_gather x2, waiting for transfers between devices, prefix(): everything = jax.tree.map(lambda part: lax.all_gather(part, axis), array)  38.7 us
    all_gather x1, waiting for transfers between devices, shards(): qkv_full = lax.all_gather(w_qkv, 'dp', axis=0, tiled=True)  28.6 us
    another operation x2, loops' own time, prefix(): return lax.fori_loop(0, devices, turn, start)  25.5 us
    unnamed x1, blocking collectives  11.7 us
    select_n x8, other arithmetic, turn(): return jax.tree.map(lambda a, b: jnp.where(reached, a, b), new, before)  8.69 us
    reduce_scatter x1, waiting for transfers between devices, shards(): lax.psum_scatter(summed, 'dp', scatter_dimension=0, tiled=True) * grad_scale  8.07 us
    unnamed x45, local copies, waits for them, and re-layouts  6.17 us
  transfers between devices with their start and end apart: 6, of which 5 were waited for; matrix products, arithmetic and copies ran while one was open for 18% of the time, Pallas kernels for 0%

commit v1 on v0

v1 whole, which is shorter than its diff:
```python
import math

import jax
import jax.numpy as jnp
from jax import lax
from jax.experimental import pallas as pl
from jax.experimental.pallas import tpu as pltpu
from jax.sharding import PartitionSpec as P

D = 1024
HEADS = 4
HEAD_DIM = 128
ID_ROWS = 16
STATE_ROWS = HEADS * HEAD_DIM

epsilon = 1e-06

f32 = jnp.float32
bf16 = jnp.bfloat16


def dot_nn(a, b):
    return lax.dot_general(a, b, (((1,), (0,)), ((), ())), preferred_element_type=f32)


def dot_nt(a, b):
    return lax.dot_general(a, b, (((1,), (1,)), ((), ())), preferred_element_type=f32)


def dot_tn(a, b):
    return lax.dot_general(a, b, (((0,), (0,)), ((), ())), preferred_element_type=f32)


def feature_map(u):
    return jnp.where(u > 0, u + 1.0, jnp.exp(jnp.minimum(u, 0.0)))


def head(h):
    return slice(h * HEAD_DIM, (h + 1) * HEAD_DIM)


VMEM = pl.BlockSpec(memory_space=pltpu.VMEM)
SMEM = pl.BlockSpec(memory_space=pltpu.SMEM)


def call(body, outs, *args, scalars=0, scratch=()):
    return pl.pallas_call(
        body,
        scratch_shapes=[pltpu.VMEM(shape, dtype) for shape, dtype in scratch],
        out_shape=[jax.ShapeDtypeStruct(shape, dtype) for shape, dtype in outs],
        in_specs=[SMEM] * scalars + [VMEM] * (len(args) - scalars),
        out_specs=[VMEM] * len(outs),
        compiler_params=pltpu.CompilerParams(vmem_limit_bytes=40 * 1024 * 1024),
    )(*args)


def columns(index, width):
    return pl.ds(pl.multiple_of(index * width, width), width)


def prep_body(me, tokens, seg, gain, normed, inv_rms, mask, seg_col):
    x = tokens[...].astype(f32)
    inv = lax.rsqrt(jnp.mean(x * x, axis=1, keepdims=True) + epsilon)
    inv_rms[...] = inv
    for j in range(4):
        at = columns(me[0] ^ j, 256)
        normed[j] = (tokens[:, at].astype(f32) * inv * gain[:, at]).astype(bf16)
    length = seg.shape[1]
    across = jnp.broadcast_to(seg[...].astype(f32), (length, length))
    down = across.T
    order = lax.broadcasted_iota(jnp.int32, (length, length), 0) >= lax.broadcasted_iota(
        jnp.int32, (length, length), 1
    )
    mask[...] = jnp.where((across == down) & order, 1.0, 0.0)
    seg_col[...] = down[:, :HEAD_DIM]


def kv_body(normed, w0, w1, w2, w3, seg_col, feat_k, values, state):
    raw = dot_nn(normed[0], w0[...])
    raw += dot_nn(normed[1], w1[...])
    raw += dot_nn(normed[2], w2[...])
    raw += dot_nn(normed[3], w3[...])
    raw = raw.astype(bf16)
    length = normed.shape[1]
    last = seg_col[length - 1 : length, :]
    tail = seg_col[...] == last
    for h in range(HEADS):
        k = feature_map(raw[:, head(h)].astype(f32))
        v = raw[:, head(HEADS + h)]
        feat_k[h] = k.astype(bf16)
        values[h] = v
        state[head(h), :] = dot_tn(jnp.where(tail, k, 0.0).astype(bf16), v).astype(bf16)
    state[STATE_ROWS:, :] = jnp.broadcast_to(last, (ID_ROWS, HEAD_DIM)).astype(bf16)


def q_body(normed, w0, w1, w2, w3, feat_k, values, mask, feat_q, scores, intra):
    raw = dot_nn(normed[0], w0[...])
    raw += dot_nn(normed[1], w1[...])
    raw += dot_nn(normed[2], w2[...])
    raw += dot_nn(normed[3], w3[...])
    raw = raw.astype(bf16)
    for h in range(HEADS):
        q = feature_map(raw[:, head(h)].astype(f32)).astype(bf16)
        feat_q[h] = q
        s = (dot_nt(q, feat_k[h]) * mask[...]).astype(bf16)
        scores[h] = s
        intra[h] = dot_nn(s, values[h])


def mixed_grad_body(me, cot, o0, o1, o2, o3, gain, upstream):
    for j, o in enumerate((o0, o1, o2, o3)):
        h = me[0] ^ j
        upstream[h] = dot_nt(cot[...], o[...]) * gain[:, columns(h, HEAD_DIM)]


def joined(near, far, h):
    same = near[STATE_ROWS : STATE_ROWS + 1, :] == far[STATE_ROWS : STATE_ROWS + 1, :]
    total = near[head(h), :].astype(f32) + jnp.where(same, far[head(h), :].astype(f32), 0.0)
    return total.astype(bf16)


def attn_body(near, far, seg_col, feat_q, intra, upstream, gain, mixed, d_attn, state):
    first = seg_col[0:1, :]
    begin = seg_col[...] == first
    take = seg_col[...] == near[STATE_ROWS : STATE_ROWS + 1, :].astype(f32)
    for h in range(HEADS):
        q = feat_q[h]
        attention = intra[h] + jnp.where(take, dot_nn(q, joined(near, far, h)), 0.0)
        ratio = lax.rsqrt(jnp.mean(attention * attention, axis=1, keepdims=True) + epsilon)
        mixed[h] = (attention * ratio * gain[:, head(h)]).astype(bf16)
        up = upstream[h]
        inner = jnp.mean(attention * up, axis=1, keepdims=True)
        da = (ratio * up - ratio**3 * attention * inner).astype(bf16)
        d_attn[h] = da
        state[head(h), :] = dot_tn(jnp.where(begin, q.astype(f32), 0.0).astype(bf16), da).astype(bf16)
    state[STATE_ROWS:, :] = jnp.broadcast_to(first, (ID_ROWS, HEAD_DIM)).astype(bf16)


def weight_body(me, mixed, cot, keep, send):
    for j in range(4):
        part = dot_tn(mixed[me[0] ^ j], cot[...])
        if j % 2 == 0:
            keep[j // 2] = part
        else:
            send[j // 2] = part.astype(bf16)


def back_body(
    me, near, far, seg_col, mask, mixed, d_attn, values, feat_k, feat_q, scores,
    o0, o1, o2, o3, w0, w1, w2, w3, tokens, output, dk_intra, dv_intra, d_normed,
):
    take = seg_col[...] == near[STATE_ROWS : STATE_ROWS + 1, :].astype(f32)
    d_query = []
    for h in range(HEADS):
        da = d_attn[h]
        q = feat_q[h]
        ds = (dot_nt(da, values[h]) * mask[...]).astype(bf16)
        dq = dot_nn(ds, feat_k[h]) + jnp.where(take, dot_nt(da, joined(near, far, h)), 0.0)
        d_query.append((dq * jnp.minimum(q.astype(f32), 1.0)).astype(bf16))
        dk_intra[h] = dot_tn(ds, q)
        dv_intra[h] = dot_tn(scores[h], da)
    d_query = jnp.concatenate(d_query, axis=1)
    total = tokens[...].astype(f32)
    for j, (o, w) in enumerate(((o0, w0), (o1, w1), (o2, w2), (o3, w3))):
        total += dot_nn(mixed[me[0] ^ j], o[...])
        d_normed[j] = dot_nt(d_query, w[...])
    output[...] = total.astype(bf16)


def final_body(
    me, near, far, seg_col, feat_k, values, dk_intra, dv_intra, d_normed,
    w0, w1, w2, w3, tokens, cot, inv_rms, gain, grad, work,
):
    take = seg_col[...] == near[STATE_ROWS : STATE_ROWS + 1, :].astype(f32)
    d_key, d_value = [], []
    for h in range(HEADS):
        back = joined(near, far, h)
        k, v = feat_k[h], values[h]
        dk = dk_intra[h] + jnp.where(take, dot_nt(v, back), 0.0)
        dv = dv_intra[h] + jnp.where(take, dot_nn(k, back), 0.0)
        d_key.append((dk * jnp.minimum(k.astype(f32), 1.0)).astype(bf16))
        d_value.append(dv.astype(bf16))
    d_proj = jnp.concatenate(d_key + d_value, axis=1)
    inner = None
    for j, w in enumerate((w0, w1, w2, w3)):
        at = columns(me[0] ^ j, 256)
        norm_grad = (d_normed[j] + dot_nt(d_proj, w[...])) * gain[:, at]
        work[j] = norm_grad
        part = jnp.sum(tokens[:, at].astype(f32) * norm_grad, axis=1, keepdims=True)
        inner = part if inner is None else inner + part
    inv = inv_rms[...]
    scale = inv**3 * (inner * (1.0 / D))
    for j in range(4):
        at = columns(me[0] ^ j, 256)
        value = cot[:, at].astype(f32) + inv * work[j] - tokens[:, at].astype(f32) * scale
        grad[:, at] = value.astype(bf16)


def flip(array, axis, bit):
    n = lax.axis_size(axis)
    return lax.ppermute(array, axis, [(i, i ^ bit) for i in range(n)])


def shift(array, axis, step):
    n = lax.axis_size(axis)
    return lax.ppermute(array, axis, [(i, i + step) for i in range(n) if 0 <= i + step < n])


def carry(message, first, last, step):
    n = lax.axis_size("seq")
    if n <= 4:
        near = shift(message, "seq", step)
        return near, shift(near, "seq", step)
    position = lax.axis_index("seq")
    begin, end = (first, last) if step > 0 else (last, first)
    total = message[:STATE_ROWS].astype(f32)
    reach = 1
    while reach < n:
        before = shift(total, "seq", step * reach)
        ids = shift(jnp.stack([begin, end]), "seq", step * reach)
        there = position - step * reach
        there = (there >= 0) & (there < n)
        total = total + jnp.where(there & (begin == end) & (ids[1] == begin), before, 0.0)
        begin = jnp.where(there, ids[0], begin)
        reach *= 2
    rows = jnp.concatenate([total.astype(bf16), message[STATE_ROWS:]], axis=0)
    near = shift(rows, "seq", step)
    return near, jnp.zeros_like(near)


def gather(shard):
    other = flip(shard, "dp", 2)
    return [shard, flip(shard, "dp", 1), other, flip(other, "dp", 1)]


def reduce_weight(keep, send, scale):
    n = lax.axis_size("seq")
    odd = lax.axis_index("seq") % 2
    total = keep + flip(send, "dp", 1).astype(f32)
    rows = total.shape[1]
    half, quarter = rows // 2, rows // 4

    def part(array, start):
        return lax.dynamic_slice_in_dim(array, start, quarter, axis=-2)

    a_in = flip(total[1, :half].astype(bf16), "dp", 2)
    b_in = flip(part(total, half + (1 - odd) * quarter).astype(bf16), "seq", 1)
    a = total[0, :half] + a_in.astype(f32)
    b = part(total, half + odd * quarter) + b_in.astype(f32)
    b_next = flip(b[1].astype(bf16), "dp", 2)
    a_next = flip(part(a, (1 - odd) * quarter).astype(bf16), "seq", 1)
    mine = jnp.stack([part(a, odd * quarter) + a_next.astype(f32), b[0] + b_next.astype(f32)])
    reach = 2
    while reach < n:
        mine = mine + flip(mine.astype(bf16), "seq", reach).astype(f32)
        reach *= 2
    theirs = flip(mine.astype(bf16), "seq", 1).astype(f32)
    low = jnp.where(odd == 0, mine, theirs)
    high = jnp.where(odd == 0, theirs, mine)
    return jnp.stack([low, high], axis=1).reshape(rows, -1) * scale


def shards(tokens, segment_ids, norm_gain, w_qkv, head_gain, w_out, cotangent):
    length = segment_ids.shape[1]
    width = HEADS * HEAD_DIM
    me = lax.axis_index("dp").astype(jnp.int32).reshape(1)
    flat = tokens.reshape(length, D)
    cot = cotangent.reshape(length, D)
    gain = norm_gain.reshape(1, D)
    gain_h = head_gain.reshape(1, width)
    first = segment_ids[0, 0].astype(f32)
    last = segment_ids[0, -1].astype(f32)
    wide = (HEADS, length, HEAD_DIM)
    square = (HEADS, length, length)

    kv = gather(w_qkv[:, width:])
    wq = gather(w_qkv[:, :width])
    wo = gather(w_out)

    normed, inv_rms, mask, seg_col = call(
        prep_body,
        [((4, length, D // 4), bf16), ((length, 1), f32), ((length, length), f32), ((length, HEAD_DIM), f32)],
        me, flat, segment_ids, gain, scalars=1,
    )
    message = ((STATE_ROWS + ID_ROWS, HEAD_DIM), bf16)
    feat_k, values, state = call(
        kv_body, [(wide, bf16), (wide, bf16), message], normed, *kv, seg_col
    )
    near, far = carry(state, first, last, 1)
    feat_q, scores, intra = call(
        q_body, [(wide, bf16), (square, bf16), (wide, f32)], normed, *wq, feat_k, values, mask
    )
    (upstream,) = call(mixed_grad_body, [(wide, f32)], me, cot, *wo, gain_h, scalars=1)
    mixed, d_attn, back = call(
        attn_body,
        [(wide, bf16), (wide, bf16), message],
        near, far, seg_col, feat_q, intra, upstream, gain_h,
    )
    keep, send = call(
        weight_body,
        [((2, HEAD_DIM, D), f32), ((2, HEAD_DIM, D), bf16)],
        me, mixed, cot, scalars=1,
    )
    back_near, back_far = carry(back, first, last, -1)
    scale = 1.0 / math.sqrt(length * lax.axis_size("dp") * lax.axis_size("seq"))
    grad_out_weight = reduce_weight(keep, send, scale)
    output, dk_intra, dv_intra, d_normed = call(
        back_body,
        [((length, D), bf16), (wide, f32), (wide, f32), ((4, length, D // 4), f32)],
        me, near, far, seg_col, mask, mixed, d_attn, values, feat_k, feat_q, scores, *wo, *wq, flat, scalars=1,
    )
    (grad,) = call(
        final_body,
        [((length, D), bf16)],
        me, back_near, back_far, seg_col, feat_k, values, dk_intra, dv_intra, d_normed, *kv, flat, cot, inv_rms, gain,
        scalars=1, scratch=[((4, length, D // 4), f32)],
    )
    return (output.reshape(tokens.shape), grad.reshape(tokens.shape), grad_out_weight)


def solution(mesh):
    in_specs = (
        P(("groups", "dp"), "seq", None),
        P(("groups", "dp"), "seq"),
        P(),
        P("dp", None),
        P(),
        P("dp", None),
        P(("groups", "dp"), "seq", None),
    )
    out_specs = (
        P(("groups", "dp"), "seq", None),
        P(("groups", "dp"), "seq", None),
        P(("groups", "dp"), None),
    )
    return jax.shard_map(shards, mesh=mesh, in_specs=in_specs, out_specs=out_specs, check_vma=False)
```

time: 225 us -> 96.2 us (0.43)
  waiting for transfers between devices: 116 us -> 27.8 us
  matrix products: 26.8 us -> 0 us
  loops' own time: 25.5 us -> 0 us
  starting transfers between devices: 0.42 us -> 24.3 us
  Pallas kernels: 0 us -> 19.4 us
  between operations: 14.5 us -> 1.12 us
  other arithmetic: 15.4 us -> 3.33 us
  blocking collectives: 11.7 us -> 0 us
  local copies, waits for them, and re-layouts: 13.5 us -> 19.4 us
    all_gather x4 -> x0, waiting for transfers between devices: 67.3 us -> none  [the longest x2 38.7 us: prefix(): everything = jax.tree.map(lambda part: lax.all_gather(part, axis), array)]
    psum x1 -> x0, waiting for transfers between devices: 39.2 us -> none  [shards(): summed = lax.psum(weight_term, 'seq')]
    ppermute x0 -> x20, waiting for transfers between devices: none -> 27.8 us  [the longest x16 27.7 us: flip(): return lax.ppermute(array, axis, [(i, i ^ bit) for i in range(n)])]
    dot_general x17 -> x0, matrix products: 26.8 us -> none  [the longest x1 4.36 us: shards(): jnp.dot(normed, qkv_full, preferred_element_type=jnp.float32)]
    another operation x2 -> x0, loops' own time: 25.5 us -> none  [prefix(): return lax.fori_loop(0, devices, turn, start)]
    ppermute x0 -> x20, starting transfers between devices: none -> 24.3 us  [the longest x16 13.6 us: flip(): return lax.ppermute(array, axis, [(i, i ^ bit) for i in range(n)])]
    pallas_call x0 -> x8, Pallas kernels: none -> 19.4 us  [call(): pl.pallas_call(body, scratch_shapes=[pltpu.VMEM(shape, dtype) for shape,...]
    unnamed x1 -> x0, blocking collectives: 11.7 us -> none
  transfers between devices with their start and end apart: 6 -> 20, of which waited for: 5 -> 7; matrix products, arithmetic and copies ran while one was open for 18% -> 4% of each run, Pallas kernels for 0% -> 18%
where the time goes in v1:
time: 96.2 us; the launch traced here: 95.4 us
  waiting for transfers between devices  27.8 us (29%)
  starting transfers between devices  24.3 us (25%)
  local copies, waits for them, and re-layouts  19.4 us (20%)
  Pallas kernels  19.4 us (20%)
  other arithmetic  3.33 us (3%)
  between operations  1.12 us (1%)
    ppermute x16, waiting for transfers between devices, flip(): return lax.ppermute(array, axis, [(i, i ^ bit) for i in range(n)])  27.7 us
    pallas_call x8, Pallas kernels, call(): pl.pallas_call(body, scratch_shapes=[pltpu.VMEM(shape, dtype) for shape,...  19.4 us
    unnamed x80, local copies, waits for them, and re-layouts  16.4 us
    ppermute x16, starting transfers between devices, flip(): return lax.ppermute(array, axis, [(i, i ^ bit) for i in range(n)])  13.6 us
    ppermute x4, starting transfers between devices, shift(): lax.ppermute(array, axis, [(i, i + step) for i in range(n) if 0 <= i + st...  10.7 us
  transfers between devices with their start and end apart: 20, of which 7 were waited for; matrix products, arithmetic and copies ran while one was open for 4% of the time, Pallas kernels for 18%

profile of v1, /device:TPU:0, one launch (start us, length us, event | category | flops | bytes accessed | tf_op | source)
XLA Modules:
  0.0 95.4 jit_solution(9831658726686342650)
XLA Ops:
  1.8 3.0 %collective-permute-start.1 = (bf16[256,1024]{1,0:T(8,128)(2,1)S(1)}, bf16[256,1024]{1,0:T(8,128)(2,1)S(1)}, u32[]{:S(2)}, u32[]{:S(2)}) collective-permute-start(bf16[256,1024]{1,0:T(8,128)(2,1)S(1)} %slice.20.w0), channel_id=1, source_target_pairs={{0,2},{1,3},{2,0},{3,1},{4,6},{5,7},{6,4},{7,5},{8,10},{9,11},{10,... | collective-permute-start | bytes 1572872 | tf_op jit(solution)/shard_map/ppermute | solution.py:201
  4.8 11.9 %collective-permute-done.1.w2 = bf16[256,1024]{1,0:T(8,128)(2,1)S(1)} collective-permute-done((bf16[256,1024]{1,0:T(8,128)(2,1)S(1)}, bf16[256,1024]{1,0:T(8,128)(2,1)S(1)}, u32[]{:S(2)}, u32[]{:S(2)}) %collective-permute-start.1) | collective-permute-done | bytes 524320 | tf_op jit(solution)/shard_map/ppermute | solution.py:201
  16.7 1.7 %collective-permute-start.9 = (bf16[128,1024]{1,0:T(8,128)(2,1)}, bf16[128,1024]{1,0:T(8,128)(2,1)}, u32[]{:S(2)}, u32[]{:S(2)}) collective-permute-start(bf16[128,1024]{1,0:T(8,128)(2,1)} %o0.3), channel_id=1, source_target_pairs={{0,2},{1,3},{2,0},{3,1},{4,6},{5,7},{6,4},{7,5},{8,10},{9,11},{10,... | collective-permute-start | bytes 786440 | tf_op jit(solution)/shard_map/ppermute | solution.py:201
  22.2 2.5 %shard_map.95 = (bf16[4,384,128]{2,1,0:T(8,128)(2,1)S(1)}, bf16[4,384,128]{2,1,0:T(8,128)(2,1)S(1)}, bf16[528,128]{1,0:T(8,128)(2,1)S(1)}) custom-call(bf16[4,384,256]{2,1,0:T(8,128)(2,1)S(1)} %get-tuple-element.22.normed, bf16[256,1024]{1,0:T(8,128)(2,1)S(1)} %slice.20.w0, bf16[256,1024]{1,0:T(8,128)(2,1)} %collective-permute-done.w1, ...), custom_call_target="tpu_custom_call" | custom-call | tf_op jit(solution)/shard_map/pallas_call | solution.py:47
  24.8 3.7 %collective-permute-start.3 = (bf16[528,128]{1,0:T(8,128)(2,1)S(1)}, bf16[528,128]{1,0:T(8,128)(2,1)S(1)}, u32[]{:S(2)}, u32[]{:S(2)}) collective-permute-start(bf16[528,128]{1,0:T(8,128)(2,1)S(1)} %get-tuple-element.24), channel_id=1, source_target_pairs={{0,4},{4,8},{8,12},{1,5},{5,9},{9,13},{2,6},{6,10},{10,14},{3,7},{... | collective-permute-start | bytes 405512 | tf_op jit(solution)/shard_map/ppermute | solution.py:206
  29.2 2.2 %collective-permute-done.6.w2 = bf16[256,512]{1,0:T(8,128)(2,1)} collective-permute-done((bf16[256,512]{1,0:T(8,128)(2,1)S(1)}, bf16[256,512]{1,0:T(8,128)(2,1)}, u32[]{:S(2)}, u32[]{:S(2)}) %collective-permute-start.6) | collective-permute-done | bytes 262176 | tf_op jit(solution)/shard_map/ppermute | solution.py:201
  31.4 4.4 %collective-permute-start.4 = (bf16[528,128]{1,0:T(8,128)(2,1)S(1)}, bf16[528,128]{1,0:T(8,128)(2,1)S(1)}, u32[]{:S(2)}, u32[]{:S(2)}) collective-permute-start(bf16[528,128]{1,0:T(8,128)(2,1)S(1)} %collective-permute-done.3.near), channel_id=1, source_target_pairs={{0,4},{4,8},{8,12},{1,5},{5,9},{9,13},{2,6},{6,10},{10,14},{3,7},{... | collective-permute-start | bytes 405512 | tf_op jit(solution)/shard_map/ppermute | solution.py:206
  35.9 2.1 %shard_map.97.upstream = f32[4,384,128]{2,1,0:T(8,128)S(1)} custom-call(s32[1]{0:T(128)} %bitcast.me, bf16[384,1024]{1,0:T(8,128)(2,1)S(1)} %bitcast.30, bf16[128,1024]{1,0:T(8,128)(2,1)S(1)} %copy-done.13, bf16[128,1024]{1,0:T(8,128)(2,1)S(1)} %collective-permute-done.8.o1, bf16[128,1024]{1,0:T(8,128)(2,1)} %collective-permute-done.9.o2, ...), custom_call_target="tpu_custom_call" | custom-call | tf_op jit(solution)/shard_map/pallas_call | solution.py:47
  38.0 2.7 %shard_map.96 = (bf16[4,384,128]{2,1,0:T(8,128)(2,1)S(1)}, bf16[4,384,384]{2,1,0:T(8,128)(2,1)S(1)}, f32[4,384,128]{2,1,0:T(8,128)S(1)}) custom-call(bf16[4,384,256]{2,1,0:T(8,128)(2,1)S(1)} %get-tuple-element.22.normed, bf16[256,512]{1,0:T(8,128)(2,1)S(1)} %slice.21.w0, bf16[256,512]{1,0:T(8,128)(2,1)S(1)} %collective-permute-done.5.w1, ...), custom_call_target="tpu_custom_call" | custom-call | tf_op jit(solution)/shard_map/pallas_call | solution.py:47
  43.4 1.5 %shard_map.101 = (f32[2,128,1024]{2,1,0:T(8,128)S(1)}, bf16[2,128,1024]{2,1,0:T(8,128)(2,1)}) custom-call(s32[1]{0:T(128)} %bitcast.me, bf16[4,384,128]{2,1,0:T(8,128)(2,1)S(1)} %get-tuple-element.30.mixed, bf16[384,1024]{1,0:T(8,128)(2,1)S(1)} %bitcast.31), custom_call_target="tpu_custom_call" | custom-call | tf_op jit(solution)/shard_map/pallas_call | solution.py:47
  46.7 1.3 %collective-permute-start.11 = (bf16[528,128]{1,0:T(8,128)(2,1)}, bf16[528,128]{1,0:T(8,128)(2,1)}, u32[]{:S(2)}, u32[]{:S(2)}) collective-permute-start(bf16[528,128]{1,0:T(8,128)(2,1)} %copy-done.33), channel_id=1, source_target_pairs={{4,0},{8,4},{12,8},{5,1},{9,5},{13,9},{6,2},{10,6},{14,10},{7,3},{... | collective-permute-start | bytes 405512 | tf_op jit(solution)/shard_map/ppermute | solution.py:206
  49.0 1.5 %convert_add_fusion = f32[2,128,1024]{2,1,0:T(8,128)S(1)} fusion(f32[2,128,1024]{2,1,0:T(8,128)} %copy-done.23, bf16[2,128,1024]{2,1,0:T(8,128)(2,1)} %collective-permute-done.13), kind=kLoop, calls=%fused_computation | loop fusion | flops 524288 | bytes 2621440 | tf_op jit(solution)/shard_map/add | solution.py:239
  50.5 1.8 %collective-permute-start.16 = (bf16[2,32,1024]{2,1,0:T(8,128)(2,1)S(1)}, bf16[2,32,1024]{2,1,0:T(8,128)(2,1)S(1)}, u32[]{:S(2)}, u32[]{:S(2)}) collective-permute-start(bf16[2,32,1024]{2,1,0:T(8,128)(2,1)S(1)} %dynamic-slice_convert_fusion), channel_id=1, source_target_pairs={{0,4},{4,0},{8,12},{12,8},{1,5},{5,1},{9,13},{13,9},{2,6},{6,2},{1... | collective-permute-start | bytes 393224 | tf_op jit(solution)/shard_map/ppermute | solution.py:201
  52.3 1.6 %collective-permute-start.14 = (bf16[64,1024]{1,0:T(8,128)(2,1)S(1)}, bf16[64,1024]{1,0:T(8,128)(2,1)S(1)}, u32[]{:S(2)}, u32[]{:S(2)}) collective-permute-start(bf16[64,1024]{1,0:T(8,128)(2,1)S(1)} %fusion.4), channel_id=1, source_target_pairs={{0,2},{1,3},{2,0},{3,1},{4,6},{5,7},{6,4},{7,5},{8,10},{9,11},{10,... | collective-permute-start | bytes 393224 | tf_op jit(solution)/shard_map/ppermute | solution.py:201
  53.8 3.8 %collective-permute-done.16 = bf16[2,32,1024]{2,1,0:T(8,128)(2,1)S(1)} collective-permute-done((bf16[2,32,1024]{2,1,0:T(8,128)(2,1)S(1)}, bf16[2,32,1024]{2,1,0:T(8,128)(2,1)S(1)}, u32[]{:S(2)}, u32[]{:S(2)}) %collective-permute-start.16) | collective-permute-done | bytes 131104 | tf_op jit(solution)/shard_map/ppermute | solution.py:201
  57.7 1.6 %collective-permute-start.17 = (bf16[32,1024]{1,0:T(8,128)(2,1)S(1)}, bf16[32,1024]{1,0:T(8,128)(2,1)S(1)}, u32[]{:S(2)}, u32[]{:S(2)}) collective-permute-start(bf16[32,1024]{1,0:T(8,128)(2,1)S(1)} %fusion.7), channel_id=1, source_target_pairs={{0,2},{1,3},{2,0},{3,1},{4,6},{5,7},{6,4},{7,5},{8,10},{9,11},{10,... | collective-permute-start | bytes 196616 | tf_op jit(solution)/shard_map/ppermute | solution.py:201
  59.6 2.4 %collective-permute-done.17 = bf16[32,1024]{1,0:T(8,128)(2,1)S(1)} collective-permute-done((bf16[32,1024]{1,0:T(8,128)(2,1)S(1)}, bf16[32,1024]{1,0:T(8,128)(2,1)S(1)}, u32[]{:S(2)}, u32[]{:S(2)}) %collective-permute-start.17) | collective-permute-done | bytes 65568 | tf_op jit(solution)/shard_map/ppermute | solution.py:201
  62.0 1.6 %collective-permute-done.15 = bf16[32,1024]{1,0:T(8,128)(2,1)S(1)} collective-permute-done((bf16[32,1024]{1,0:T(8,128)(2,1)S(1)}, bf16[32,1024]{1,0:T(8,128)(2,1)S(1)}, u32[]{:S(2)}, u32[]{:S(2)}) %collective-permute-start.15) | collective-permute-done | bytes 65568 | tf_op jit(solution)/shard_map/ppermute | solution.py:201
  63.7 2.7 %collective-permute-start.18 = (bf16[2,32,1024]{2,1,0:T(8,128)(2,1)S(1)}, bf16[2,32,1024]{2,1,0:T(8,128)(2,1)S(1)}, u32[]{:S(2)}, u32[]{:S(2)}) collective-permute-start(bf16[2,32,1024]{2,1,0:T(8,128)(2,1)S(1)} %fusion.3), channel_id=1, source_target_pairs={{0,8},{4,12},{8,0},{12,4},{1,9},{5,13},{9,1},{13,5},{2,10},{6,14},... | collective-permute-start | bytes 393224 | tf_op jit(solution)/shard_map/ppermute | solution.py:201
  66.3 1.3 %collective-permute-start.12 = (bf16[528,128]{1,0:T(8,128)(2,1)}, bf16[528,128]{1,0:T(8,128)(2,1)}, u32[]{:S(2)}, u32[]{:S(2)}) collective-permute-start(bf16[528,128]{1,0:T(8,128)(2,1)} %collective-permute-done.11.near), channel_id=1, source_target_pairs={{4,0},{8,4},{12,8},{5,1},{9,5},{13,9},{6,2},{10,6},{14,10},{7,3},{... | collective-permute-start | bytes 405512 | tf_op jit(solution)/shard_map/ppermute | solution.py:206
  67.6 4.9 %collective-permute-done.18 = bf16[2,32,1024]{2,1,0:T(8,128)(2,1)S(1)} collective-permute-done((bf16[2,32,1024]{2,1,0:T(8,128)(2,1)S(1)}, bf16[2,32,1024]{2,1,0:T(8,128)(2,1)S(1)}, u32[]{:S(2)}, u32[]{:S(2)}) %collective-permute-start.18) | collective-permute-done | bytes 131104 | tf_op jit(solution)/shard_map/ppermute | solution.py:201
  76.3 1.3 %copy-done.12 = bf16[4,384,384]{2,1,0:T(8,128)(2,1)S(1)} copy-done((bf16[4,384,384]{2,1,0:T(8,128)(2,1)S(1)}, bf16[4,384,384]{2,1,0:T(8,128)(2,1)}, u32[]{:S(2)}) %copy-start.12) | copy-done | bytes 1179672
  84.2 5.0 %shard_map.99 = (bf16[384,1024]{1,0:T(8,128)(2,1)}, f32[4,384,128]{2,1,0:T(8,128)S(1)}, f32[4,384,128]{2,1,0:T(8,128)S(1)}, f32[4,384,256]{2,1,0:T(8,128)S(1)}) custom-call(s32[1]{0:T(128)} %bitcast.me, bf16[528,128]{1,0:T(8,128)(2,1)S(1)} %collective-permute-done.3.near, bf16[528,128]{1,0:T(8,128)(2,1)S(1)} %copy-done.25, ...), custom_call_target="tpu_custom_call" | custom-call | tf_op jit(solution)/shard_map/pallas_call | solution.py:47
  89.2 4.2 %shard_map.100 = bf16[384,1024]{1,0:T(8,128)(2,1)} custom-call(s32[1]{0:T(128)} %bitcast.me, bf16[528,128]{1,0:T(8,128)(2,1)} %collective-permute-done.11.near, bf16[528,128]{1,0:T(8,128)(2,1)} %collective-permute-done.12.far, f32[384,128]{1,0:T(8,128)S(1)} %get-tuple-element.23.seg_col, bf16[4,384,128]{2,1,0:T(8,128)(2,1)S(1)} %get-tuple-element.26.feat_k, ...), custom_call_target="tpu_custom_call" | custom-call | tf_op jit(solution)/shard_map/pallas_call | solution.py:47
  (120 shorter events, 23.7 us)
Async XLA Ops:
  0.6 19.2 %copy-start.1 = (bf16[1,384,1024]{2,1,0:T(8,128)(2,1)S(1)}, bf16[1,384,1024]{2,1,0:T(8,128)(2,1)}, u32[]{:S(2)}) copy-start(bf16[1,384,1024]{2,1,0:T(8,128)(2,1)} %param.7) | copy-start | bytes 2359300
  0.6 19.2 %copy-start.32 = (s32[1,384]{1,0:T(1,128)S(1)}, s32[1,384]{1,0:T(1,128)}, u32[]{:S(2)}) copy-start(s32[1,384]{1,0:T(1,128)} %seg.1) | copy-start | bytes 4612
  0.7 19.2 %copy-start.30 = (f32[1024]{0:T(1024)S(1)}, f32[1024]{0:T(1024)}, u32[]{:S(2)}) copy-start(f32[1024]{0:T(1024)} %param.9) | copy-start | bytes 12292
  1.8 14.9 %collective-permute-start.1 = (bf16[256,1024]{1,0:T(8,128)(2,1)S(1)}, bf16[256,1024]{1,0:T(8,128)(2,1)S(1)}, u32[]{:S(2)}, u32[]{:S(2)}) collective-permute-start(bf16[256,1024]{1,0:T(8,128)(2,1)S(1)} %slice.20.w0), channel_id=1, source_target_pairs={{0,2},{1,3},{2,0},{3,1},{4,6},{5,7},{6,4},{7,5},{8,10},{9,11},{10,... | collective-permute-start | bytes 1572872 | tf_op jit(solution)/shard_map/ppermute | solution.py:201
  4.8 16.1 %collective-permute-start = (bf16[256,1024]{1,0:T(8,128)(2,1)S(1)}, bf16[256,1024]{1,0:T(8,128)(2,1)}, u32[]{:S(2)}, u32[]{:S(2)}) collective-permute-start(bf16[256,1024]{1,0:T(8,128)(2,1)S(1)} %slice.20.w0), channel_id=1, source_target_pairs={{0,1},{1,0},{2,3},{3,2},{4,5},{5,4},{6,7},{7,6},{8,9},{9,8},{10,11... | collective-permute-start | bytes 1572872 | tf_op jit(solution)/shard_map/ppermute | solution.py:201
  16.7 4.2 %collective-permute-start.2 = (bf16[256,1024]{1,0:T(8,128)(2,1)S(1)}, bf16[256,1024]{1,0:T(8,128)(2,1)}, u32[]{:S(2)}, u32[]{:S(2)}) collective-permute-start(bf16[256,1024]{1,0:T(8,128)(2,1)S(1)} %collective-permute-done.1.w2), channel_id=1, source_target_pairs={{0,1},{1,0},{2,3},{3,2},{4,5},{5,4},{6,7},{7,6},{8,9},{9,8},{10,11... | collective-permute-start | bytes 1572872 | tf_op jit(solution)/shard_map/ppermute | solution.py:201
  16.7 11.9 %collective-permute-start.9 = (bf16[128,1024]{1,0:T(8,128)(2,1)}, bf16[128,1024]{1,0:T(8,128)(2,1)}, u32[]{:S(2)}, u32[]{:S(2)}) collective-permute-start(bf16[128,1024]{1,0:T(8,128)(2,1)} %o0.3), channel_id=1, source_target_pairs={{0,2},{1,3},{2,0},{3,1},{4,6},{5,7},{6,4},{7,5},{8,10},{9,11},{10,... | collective-permute-start | bytes 786440 | tf_op jit(solution)/shard_map/ppermute | solution.py:201
  19.5 11.9 %collective-permute-start.6 = (bf16[256,512]{1,0:T(8,128)(2,1)S(1)}, bf16[256,512]{1,0:T(8,128)(2,1)}, u32[]{:S(2)}, u32[]{:S(2)}) collective-permute-start(bf16[256,512]{1,0:T(8,128)(2,1)S(1)} %slice.21.w0), channel_id=1, source_target_pairs={{0,2},{1,3},{2,0},{3,1},{4,6},{5,7},{6,4},{7,5},{8,10},{9,11},{10,... | collective-permute-start | bytes 786440 | tf_op jit(solution)/shard_map/ppermute | solution.py:201
  20.9 17.1 %copy-start.2 = (f32[384,384]{1,0:T(8,128)}, f32[384,384]{1,0:T(8,128)S(1)}, u32[]{:S(2)}) copy-start(f32[384,384]{1,0:T(8,128)S(1)} %get-tuple-element.25.mask) | copy-start | bytes 1769476
  24.8 6.7 %collective-permute-start.3 = (bf16[528,128]{1,0:T(8,128)(2,1)S(1)}, bf16[528,128]{1,0:T(8,128)(2,1)S(1)}, u32[]{:S(2)}, u32[]{:S(2)}) collective-permute-start(bf16[528,128]{1,0:T(8,128)(2,1)S(1)} %get-tuple-element.24), channel_id=1, source_target_pairs={{0,4},{4,8},{8,12},{1,5},{5,9},{9,13},{2,6},{6,10},{10,14},{3,7},{... | collective-permute-start | bytes 405512 | tf_op jit(solution)/shard_map/ppermute | solution.py:206
  28.5 7.3 %collective-permute-start.8 = (bf16[128,1024]{1,0:T(8,128)(2,1)S(1)}, bf16[128,1024]{1,0:T(8,128)(2,1)S(1)}, u32[]{:S(2)}, u32[]{:S(2)}) collective-permute-start(bf16[128,1024]{1,0:T(8,128)(2,1)S(1)} %copy-done.13), channel_id=1, source_target_pairs={{0,1},{1,0},{2,3},{3,2},{4,5},{5,4},{6,7},{7,6},{8,9},{9,8},{10,11... | collective-permute-start | bytes 786440 | tf_op jit(solution)/shard_map/ppermute | solution.py:201
  28.6 7.2 %collective-permute-start.10 = (bf16[128,1024]{1,0:T(8,128)(2,1)}, bf16[128,1024]{1,0:T(8,128)(2,1)S(1)}, u32[]{:S(2)}, u32[]{:S(2)}) collective-permute-start(bf16[128,1024]{1,0:T(8,128)(2,1)} %collective-permute-done.9.o2), channel_id=1, source_target_pairs={{0,1},{1,0},{2,3},{3,2},{4,5},{5,4},{6,7},{7,6},{8,9},{9,8},{10,11... | collective-permute-start | bytes 786440 | tf_op jit(solution)/shard_map/ppermute | solution.py:201
  29.1 8.9 %collective-permute-start.5 = (bf16[256,512]{1,0:T(8,128)(2,1)S(1)}, bf16[256,512]{1,0:T(8,128)(2,1)S(1)}, u32[]{:S(2)}, u32[]{:S(2)}) collective-permute-start(bf16[256,512]{1,0:T(8,128)(2,1)S(1)} %slice.21.w0), channel_id=1, source_target_pairs={{0,1},{1,0},{2,3},{3,2},{4,5},{5,4},{6,7},{7,6},{8,9},{9,8},{10,11... | collective-permute-start | bytes 786440 | tf_op jit(solution)/shard_map/ppermute | solution.py:201
  31.4 6.6 %collective-permute-start.7 = (bf16[256,512]{1,0:T(8,128)(2,1)}, bf16[256,512]{1,0:T(8,128)(2,1)S(1)}, u32[]{:S(2)}, u32[]{:S(2)}) collective-permute-start(bf16[256,512]{1,0:T(8,128)(2,1)} %collective-permute-done.6.w2), channel_id=1, source_target_pairs={{0,1},{1,0},{2,3},{3,2},{4,5},{5,4},{6,7},{7,6},{8,9},{9,8},{10,11... | collective-permute-start | bytes 786440 | tf_op jit(solution)/shard_map/ppermute | solution.py:201
  31.4 10.4 %collective-permute-start.4 = (bf16[528,128]{1,0:T(8,128)(2,1)S(1)}, bf16[528,128]{1,0:T(8,128)(2,1)S(1)}, u32[]{:S(2)}, u32[]{:S(2)}) collective-permute-start(bf16[528,128]{1,0:T(8,128)(2,1)S(1)} %collective-permute-done.3.near), channel_id=1, source_target_pairs={{0,4},{4,8},{8,12},{1,5},{5,9},{9,13},{2,6},{6,10},{10,14},{3,7},{... | collective-permute-start | bytes 405512 | tf_op jit(solution)/shard_map/ppermute | solution.py:206
  46.7 2.3 %collective-permute-start.13 = (bf16[2,128,1024]{2,1,0:T(8,128)(2,1)}, bf16[2,128,1024]{2,1,0:T(8,128)(2,1)}, u32[]{:S(2)}, u32[]{:S(2)}) collective-permute-start(bf16[2,128,1024]{2,1,0:T(8,128)(2,1)} %get-tuple-element.40), channel_id=1, source_target_pairs={{0,1},{1,0},{2,3},{3,2},{4,5},{5,4},{6,7},{7,6},{8,9},{9,8},{10,11... | collective-permute-start | bytes 1572872 | tf_op jit(solution)/shard_map/ppermute | solution.py:201
  46.7 19.6 %collective-permute-start.11 = (bf16[528,128]{1,0:T(8,128)(2,1)}, bf16[528,128]{1,0:T(8,128)(2,1)}, u32[]{:S(2)}, u32[]{:S(2)}) collective-permute-start(bf16[528,128]{1,0:T(8,128)(2,1)} %copy-done.33), channel_id=1, source_target_pairs={{4,0},{8,4},{12,8},{5,1},{9,5},{13,9},{6,2},{10,6},{14,10},{7,3},{... | collective-permute-start | bytes 405512 | tf_op jit(solution)/shard_map/ppermute | solution.py:206
  50.5 7.1 %collective-permute-start.16 = (bf16[2,32,1024]{2,1,0:T(8,128)(2,1)S(1)}, bf16[2,32,1024]{2,1,0:T(8,128)(2,1)S(1)}, u32[]{:S(2)}, u32[]{:S(2)}) collective-permute-start(bf16[2,32,1024]{2,1,0:T(8,128)(2,1)S(1)} %dynamic-slice_convert_fusion), channel_id=1, source_target_pairs={{0,4},{4,0},{8,12},{12,8},{1,5},{5,1},{9,13},{13,9},{2,6},{6,2},{1... | collective-permute-start | bytes 393224 | tf_op jit(solution)/shard_map/ppermute | solution.py:201
  52.3 7.0 %collective-permute-start.14 = (bf16[64,1024]{1,0:T(8,128)(2,1)S(1)}, bf16[64,1024]{1,0:T(8,128)(2,1)S(1)}, u32[]{:S(2)}, u32[]{:S(2)}) collective-permute-start(bf16[64,1024]{1,0:T(8,128)(2,1)S(1)} %fusion.4), channel_id=1, source_target_pairs={{0,2},{1,3},{2,0},{3,1},{4,6},{5,7},{6,4},{7,5},{8,10},{9,11},{10,... | collective-permute-start | bytes 393224 | tf_op jit(solution)/shard_map/ppermute | solution.py:201
  57.7 4.3 %collective-permute-start.17 = (bf16[32,1024]{1,0:T(8,128)(2,1)S(1)}, bf16[32,1024]{1,0:T(8,128)(2,1)S(1)}, u32[]{:S(2)}, u32[]{:S(2)}) collective-permute-start(bf16[32,1024]{1,0:T(8,128)(2,1)S(1)} %fusion.7), channel_id=1, source_target_pairs={{0,2},{1,3},{2,0},{3,1},{4,6},{5,7},{6,4},{7,5},{8,10},{9,11},{10,... | collective-permute-start | bytes 196616 | tf_op jit(solution)/shard_map/ppermute | solution.py:201
  59.3 4.3 %collective-permute-start.15 = (bf16[32,1024]{1,0:T(8,128)(2,1)S(1)}, bf16[32,1024]{1,0:T(8,128)(2,1)S(1)}, u32[]{:S(2)}, u32[]{:S(2)}) collective-permute-start(bf16[32,1024]{1,0:T(8,128)(2,1)S(1)} %dynamic-slice_convert_fusion.1), channel_id=1, source_target_pairs={{0,4},{4,0},{8,12},{12,8},{1,5},{5,1},{9,13},{13,9},{2,6},{6,2},{1... | collective-permute-start | bytes 196616 | tf_op jit(solution)/shard_map/ppermute | solution.py:201
  63.7 8.8 %collective-permute-start.18 = (bf16[2,32,1024]{2,1,0:T(8,128)(2,1)S(1)}, bf16[2,32,1024]{2,1,0:T(8,128)(2,1)S(1)}, u32[]{:S(2)}, u32[]{:S(2)}) collective-permute-start(bf16[2,32,1024]{2,1,0:T(8,128)(2,1)S(1)} %fusion.3), channel_id=1, source_target_pairs={{0,8},{4,12},{8,0},{12,4},{1,9},{5,13},{9,1},{13,5},{2,10},{6,14},... | collective-permute-start | bytes 393224 | tf_op jit(solution)/shard_map/ppermute | solution.py:201
  66.3 22.9 %collective-permute-start.12 = (bf16[528,128]{1,0:T(8,128)(2,1)}, bf16[528,128]{1,0:T(8,128)(2,1)}, u32[]{:S(2)}, u32[]{:S(2)}) collective-permute-start(bf16[528,128]{1,0:T(8,128)(2,1)} %collective-permute-done.11.near), channel_id=1, source_target_pairs={{4,0},{8,4},{12,8},{5,1},{9,5},{13,9},{6,2},{10,6},{14,10},{7,3},{... | collective-permute-start | bytes 405512 | tf_op jit(solution)/shard_map/ppermute | solution.py:206
  73.2 20.3 %collective-permute-start.19 = (bf16[2,32,1024]{2,1,0:T(8,128)(2,1)}, bf16[2,32,1024]{2,1,0:T(8,128)(2,1)}, u32[]{:S(2)}, u32[]{:S(2)}) collective-permute-start(bf16[2,32,1024]{2,1,0:T(8,128)(2,1)} %fusion.8), channel_id=1, source_target_pairs={{0,4},{4,0},{8,12},{12,8},{1,5},{5,1},{9,13},{13,9},{2,6},{6,2},{1... | collective-permute-start | bytes 393224 | tf_op jit(solution)/shard_map/ppermute | solution.py:201
  (36 other events, 126.5 us)

commit v2 on v1

v2 whole, which is shorter than its diff:
```python
import math

import jax
import jax.numpy as jnp
from jax import lax
from jax.experimental import pallas as pl
from jax.experimental.pallas import tpu as pltpu
from jax.sharding import PartitionSpec as P

D = 1024
HEADS = 4
HEAD_DIM = 128
ID_ROWS = 16

epsilon = 1e-06

f32 = jnp.float32
bf16 = jnp.bfloat16


def dot_nn(a, b):
    return lax.dot_general(a, b, (((1,), (0,)), ((), ())), preferred_element_type=f32)


def dot_nt(a, b):
    return lax.dot_general(a, b, (((1,), (1,)), ((), ())), preferred_element_type=f32)


def dot_tn(a, b):
    return lax.dot_general(a, b, (((0,), (0,)), ((), ())), preferred_element_type=f32)


def feature_map(u):
    return jnp.where(u > 0, u + 1.0, jnp.exp(jnp.minimum(u, 0.0)))


def head(h):
    return slice(h * HEAD_DIM, (h + 1) * HEAD_DIM)


VMEM = pl.BlockSpec(memory_space=pltpu.VMEM)
SMEM = pl.BlockSpec(memory_space=pltpu.SMEM)


def call(body, outs, *args, scalars=0, scratch=()):
    return pl.pallas_call(
        body,
        scratch_shapes=[pltpu.VMEM(shape, dtype) for shape, dtype in scratch],
        out_shape=[jax.ShapeDtypeStruct(shape, dtype) for shape, dtype in outs],
        in_specs=[SMEM] * scalars + [VMEM] * (len(args) - scalars),
        out_specs=[VMEM] * len(outs),
        compiler_params=pltpu.CompilerParams(vmem_limit_bytes=16 * 1024 * 1024),
    )(*args)


def columns(index, width):
    return pl.ds(pl.multiple_of(index * width, width), width)


def prep_body(me, tokens, partner, seg, seg_partner, gain, normed, inv_rms, mask, seg_col):
    length = seg.shape[1]
    order = lax.broadcasted_iota(jnp.int32, (length, length), 0) >= lax.broadcasted_iota(
        jnp.int32, (length, length), 1
    )
    for i, (part, ids) in enumerate(((tokens, seg), (partner, seg_partner))):
        x = part[...].astype(f32)
        inv = lax.rsqrt(jnp.mean(x * x, axis=1, keepdims=True) + epsilon)
        if i == 0:
            inv_rms[...] = inv
        for j in range(4):
            at = columns(me[0] ^ j, 256)
            normed[j, i * length : (i + 1) * length] = (part[:, at].astype(f32) * inv * gain[:, at]).astype(bf16)
        across = jnp.broadcast_to(ids[...], (length, length))
        down = across.T
        mask[i] = jnp.where((across == down) & order, 1.0, 0.0)
        seg_col[i] = down[:, :HEAD_DIM]


def kv_near_body(normed, w0, w1, raw):
    raw[...] = dot_nn(normed[0], w0[...]) + dot_nn(normed[1], w1[...])


def kv_body(near, normed, w2, w3, seg_col, feat_k, values, state):
    raw = near[...] + dot_nn(normed[2], w2[...]) + dot_nn(normed[3], w3[...])
    raw = raw.astype(bf16)
    length = seg_col.shape[1]
    for i in range(2):
        last = seg_col[i, length - 1 : length, :]
        tail = seg_col[i] == last
        rows = slice(i * length, (i + 1) * length)
        for g in range(2):
            k = feature_map(raw[rows, head(g)].astype(f32))
            v = raw[rows, head(2 + g)]
            feat_k[i, g] = k.astype(bf16)
            values[i, g] = v
            state[i, head(g), :] = dot_tn(jnp.where(tail, k, 0.0).astype(bf16), v).astype(bf16)
        state[i, 2 * HEAD_DIM :, :] = jnp.broadcast_to(last, (ID_ROWS, HEAD_DIM)).astype(bf16)


def q_body(normed, w0, w1, w2, w3, feat_k, values, mask, feat_q, scores, intra):
    raw = dot_nn(normed[0], w0[...])
    raw += dot_nn(normed[1], w1[...])
    raw += dot_nn(normed[2], w2[...])
    raw += dot_nn(normed[3], w3[...])
    raw = raw.astype(bf16)
    length = mask.shape[1]
    for i in range(2):
        for g in range(2):
            q = feature_map(raw[i * length : (i + 1) * length, head(g)].astype(f32)).astype(bf16)
            feat_q[i, g] = q
            s = (dot_nt(q, feat_k[i, g]) * mask[i]).astype(bf16)
            scores[i, g] = s
            intra[i, g] = dot_nn(s, values[i, g])


def mixed_grad_body(me, cot, cot_partner, own, other, gain, upstream):
    for j, o in enumerate((own, other)):
        full = me[0] ^ (2 * j)
        for i, part in enumerate((cot, cot_partner)):
            upstream[i, full // 2] = dot_nt(part[...], o[...]) * gain[:, columns(full, HEAD_DIM)]


def id_of(message, i):
    return message[i, 2 * HEAD_DIM : 2 * HEAD_DIM + 1, :]


def joined(near, far, i, g):
    same = id_of(near, i) == id_of(far, i)
    total = near[i, head(g), :].astype(f32) + jnp.where(same, far[i, head(g), :].astype(f32), 0.0)
    return total.astype(bf16)


def attn_body(me, near, far, seg_col, feat_q, intra, upstream, gain, mixed, d_attn, state):
    for i in range(2):
        first = seg_col[i, 0:1, :]
        begin = seg_col[i] == first
        take = seg_col[i] == id_of(near, i).astype(f32)
        for g in range(2):
            q = feat_q[i, g]
            attention = intra[i, g] + jnp.where(take, dot_nn(q, joined(near, far, i, g)), 0.0)
            ratio = lax.rsqrt(jnp.mean(attention * attention, axis=1, keepdims=True) + epsilon)
            mixed[i, g] = (attention * ratio * gain[:, columns(2 * g + me[0] % 2, HEAD_DIM)]).astype(bf16)
            up = upstream[i, g]
            inner = jnp.mean(attention * up, axis=1, keepdims=True)
            da = (ratio * up - ratio**3 * attention * inner).astype(bf16)
            d_attn[i, g] = da
            state[i, head(g), :] = dot_tn(jnp.where(begin, q.astype(f32), 0.0).astype(bf16), da).astype(bf16)
        state[i, 2 * HEAD_DIM :, :] = jnp.broadcast_to(first, (ID_ROWS, HEAD_DIM)).astype(bf16)


def weight_body(me, odd, mixed, cot, cot_partner, a_keep, a_send, b_keep, b_send):
    half = HEAD_DIM // 2
    quarter = half // 2
    for j in range(2):
        g = (me[0] ^ (2 * j)) // 2
        part = dot_tn(mixed[0, g], cot[...]) + dot_tn(mixed[1, g], cot_partner[...])
        if j == 0:
            a_keep[...] = part[:half]
        else:
            a_send[...] = part[:half].astype(bf16)
        low, high = part[half : half + quarter], part[half + quarter :]
        second = odd[0] == 1
        b_keep[j] = jnp.where(second, high, low)
        b_send[j] = jnp.where(second, low, high).astype(bf16)


def back_body(
    me, near, far, seg_col, mask, mixed, d_attn, values, feat_k, feat_q, scores,
    own, other, w0, w1, w2, w3, tokens, out_own, out_partner, dk_intra, dv_intra, d_normed,
):
    length = mask.shape[1]
    for i in range(2):
        take = seg_col[i] == id_of(near, i).astype(f32)
        d_query = []
        for g in range(2):
            da = d_attn[i, g]
            q = feat_q[i, g]
            ds = (dot_nt(da, values[i, g]) * mask[i]).astype(bf16)
            dq = dot_nn(ds, feat_k[i, g]) + jnp.where(take, dot_nt(da, joined(near, far, i, g)), 0.0)
            d_query.append((dq * jnp.minimum(q.astype(f32), 1.0)).astype(bf16))
            dk_intra[i, g] = dot_tn(ds, q)
            dv_intra[i, g] = dot_tn(scores[i, g], da)
        d_query = jnp.concatenate(d_query, axis=1)
        for j, w in enumerate((w0, w1, w2, w3)):
            d_normed[j, i * length : (i + 1) * length] = dot_nt(d_query, w[...])
        total = dot_nn(mixed[i, me[0] // 2], own[...]) + dot_nn(mixed[i, 1 - me[0] // 2], other[...])
        if i == 0:
            out_own[...] = tokens[...].astype(f32) + total
        else:
            out_partner[...] = total.astype(bf16)


def key_value_body(
    near, far, seg_col, feat_k, values, dk_intra, dv_intra, d_normed, w0, w1, w2, w3, own, partner,
):
    length = seg_col.shape[1]
    for i in (1, 0):
        take = seg_col[i] == id_of(near, i).astype(f32)
        d_key, d_value = [], []
        for g in range(2):
            back = joined(near, far, i, g)
            k, v = feat_k[i, g], values[i, g]
            dk = dk_intra[i, g] + jnp.where(take, dot_nt(v, back), 0.0)
            dv = dv_intra[i, g] + jnp.where(take, dot_nn(k, back), 0.0)
            d_key.append((dk * jnp.minimum(k.astype(f32), 1.0)).astype(bf16))
            d_value.append(dv.astype(bf16))
        d_proj = jnp.concatenate(d_key + d_value, axis=1)
        for j, w in enumerate((w0, w1, w2, w3)):
            value = d_normed[j, i * length : (i + 1) * length] + dot_nt(d_proj, w[...])
            if i == 1:
                partner[j ^ 1] = value.astype(bf16)
            else:
                own[j] = value


def final_body(me, own, partner, tokens, cot, inv_rms, gain, grad, work):
    inner = None
    for j in range(4):
        at = columns(me[0] ^ j, 256)
        norm_grad = (own[j] + partner[j].astype(f32)) * gain[:, at]
        work[j] = norm_grad
        part = jnp.sum(tokens[:, at].astype(f32) * norm_grad, axis=1, keepdims=True)
        inner = part if inner is None else inner + part
    inv = inv_rms[...]
    scale = inv**3 * (inner * (1.0 / D))
    for j in range(4):
        at = columns(me[0] ^ j, 256)
        value = cot[:, at].astype(f32) + inv * work[j] - tokens[:, at].astype(f32) * scale
        grad[:, at] = value.astype(bf16)


def flip(array, axis, bit):
    n = lax.axis_size(axis)
    return lax.ppermute(array, axis, [(i, i ^ bit) for i in range(n)])


def shift(array, axis, step):
    n = lax.axis_size(axis)
    return lax.ppermute(array, axis, [(i, i + step) for i in range(n) if 0 <= i + step < n])


def carry(message, ends, step):
    n = lax.axis_size("seq")
    if n <= 4:
        near = shift(message, "seq", step)
        return near, shift(near, "seq", step)
    position = lax.axis_index("seq")
    begin, end = (ends[0], ends[1]) if step > 0 else (ends[1], ends[0])
    total = message[:, : 2 * HEAD_DIM].astype(f32)
    reach = 1
    while reach < n:
        before = shift(total, "seq", step * reach)
        ids = shift(jnp.stack([begin, end]), "seq", step * reach)
        there = position - step * reach
        there = (there >= 0) & (there < n)
        goes_on = there & (begin == end) & (ids[1] == begin)
        total = total + jnp.where(goes_on[:, None, None], before, 0.0)
        begin = jnp.where(there, ids[0], begin)
        reach *= 2
    rows = jnp.concatenate([total.astype(bf16), message[:, 2 * HEAD_DIM :]], axis=1)
    near = shift(rows, "seq", step)
    return near, jnp.zeros_like(near)


def reduce_weight(a_keep, a_send, b_keep, b_send, scale):
    n = lax.axis_size("seq")
    odd = lax.axis_index("seq") % 2
    rows = 2 * a_keep.shape[0]
    quarter = rows // 4
    a_in = flip(a_send, "dp", 2)
    b_in = flip(b_send, "seq", 1)
    a = a_keep + a_in.astype(f32)
    b = b_keep + b_in.astype(f32)
    low, high = a[:quarter], a[quarter:]
    a_next = flip(jnp.where(odd == 1, low, high).astype(bf16), "seq", 1)
    b_next = flip(b[1].astype(bf16), "dp", 2)
    mine = jnp.concatenate([jnp.where(odd == 1, high, low) + a_next.astype(f32), b[0] + b_next.astype(f32)])
    reach = 2
    while reach < n:
        mine = mine + flip(mine.astype(bf16), "seq", reach).astype(f32)
        reach *= 2
    theirs = flip(mine.astype(bf16), "seq", 1).astype(f32)
    low = jnp.where(odd == 0, mine, theirs)
    high = jnp.where(odd == 0, theirs, mine)
    return jnp.concatenate([low[:quarter], high[:quarter], low[quarter:], high[quarter:]]) * scale


def shards(tokens, segment_ids, norm_gain, w_qkv, head_gain, w_out, cotangent):
    length = segment_ids.shape[1]
    width = HEADS * HEAD_DIM
    dp = lax.axis_index("dp").astype(jnp.int32)
    me = dp.reshape(1)
    odd = (lax.axis_index("seq").astype(jnp.int32) % 2).reshape(1)
    flat = tokens.reshape(length, D)
    cot = cotangent.reshape(length, D)
    gain = norm_gain.reshape(1, D)
    gain_h = head_gain.reshape(1, width)
    seg = segment_ids.astype(f32)
    wide = (2, 2, length, HEAD_DIM)

    blocks = w_qkv.reshape(-1, 3, 2, 2, HEAD_DIM)

    def half(which):
        part = lax.dynamic_index_in_dim(blocks, which, axis=3, keepdims=False)
        rows = part.shape[0]
        return part[:, 0].reshape(rows, 2 * HEAD_DIM), part[:, 1:].reshape(rows, 4 * HEAD_DIM)

    q_mine, kv_mine = half(dp % 2)
    q_other, kv_other = half(1 - dp % 2)
    kv = [kv_mine, flip(kv_other, "dp", 1), flip(kv_mine, "dp", 2), flip(kv_other, "dp", 3)]
    partner = flip(flat, "dp", 1)
    seg_partner = flip(seg, "dp", 1)

    normed, inv_rms, mask, seg_col = call(
        prep_body,
        [
            ((4, 2 * length, D // 4), bf16),
            ((length, 1), f32),
            ((2, length, length), f32),
            ((2, length, HEAD_DIM), f32),
        ],
        me, flat, partner, seg, seg_partner, gain, scalars=1,
    )
    message = ((2, 2 * HEAD_DIM + ID_ROWS, HEAD_DIM), bf16)
    (raw_near,) = call(kv_near_body, [((2 * length, 4 * HEAD_DIM), f32)], normed, kv[0], kv[1])
    feat_k, values, state = call(
        kv_body, [(wide, bf16), (wide, bf16), message], raw_near, normed, kv[2], kv[3], seg_col
    )
    ends = jnp.stack([seg_col[:, 0, 0], seg_col[:, -1, 0]])
    near, far = carry(state, ends, 1)

    q_far, q_other, out_own, cot, state = lax.optimization_barrier((q_mine, q_other, w_out, cot, state))
    cot_partner = flip(cot, "dp", 1)
    wq = [q_mine, flip(q_other, "dp", 1), flip(q_far, "dp", 2), flip(q_other, "dp", 3)]
    out_other = flip(out_own, "dp", 2)
    feat_q, scores, intra = call(
        q_body,
        [(wide, bf16), ((2, 2, length, length), bf16), (wide, f32)],
        normed, *wq, feat_k, values, mask,
    )
    (upstream,) = call(
        mixed_grad_body, [(wide, f32)], me, cot, cot_partner, w_out, out_other, gain_h, scalars=1
    )
    mixed, d_attn, back = call(
        attn_body,
        [(wide, bf16), (wide, bf16), message],
        me, near, far, seg_col, feat_q, intra, upstream, gain_h, scalars=1,
    )
    rows = HEAD_DIM // 2
    parts = call(
        weight_body,
        [((rows, D), f32), ((rows, D), bf16), ((2, rows // 2, D), f32), ((2, rows // 2, D), bf16)],
        me, odd, mixed, cot, cot_partner, scalars=2,
    )
    back_near, back_far = carry(back, ends, -1)
    scale = 1.0 / math.sqrt(length * lax.axis_size("dp") * lax.axis_size("seq"))
    grad_out_weight = reduce_weight(*parts, scale)
    sums = (4, 2 * length, D // 4)
    out_sum, out_partner, dk_intra, dv_intra, d_normed = call(
        back_body,
        [((length, D), f32), ((length, D), bf16), (wide, f32), (wide, f32), (sums, f32)],
        me, near, far, seg_col, mask, mixed, d_attn, values, feat_k, feat_q, scores, w_out, out_other, *wq, flat,
        scalars=1,
    )
    output = (out_sum + flip(out_partner, "dp", 1).astype(f32)).astype(bf16)
    own, theirs = call(
        key_value_body,
        [((4, length, D // 4), f32), ((4, length, D // 4), bf16)],
        back_near, back_far, seg_col, feat_k, values, dk_intra, dv_intra, d_normed, *kv,
    )
    (grad,) = call(
        final_body,
        [((length, D), bf16)],
        me, own, flip(theirs, "dp", 1), flat, cot, inv_rms, gain,
        scalars=1, scratch=[((4, length, D // 4), f32)],
    )
    return (output.reshape(tokens.shape), grad.reshape(tokens.shape), grad_out_weight)


def solution(mesh):
    in_specs = (
        P(("groups", "dp"), "seq", None),
        P(("groups", "dp"), "seq"),
        P(),
        P("dp", None),
        P(),
        P("dp", None),
        P(("groups", "dp"), "seq", None),
    )
    out_specs = (
        P(("groups", "dp"), "seq", None),
        P(("groups", "dp"), "seq", None),
        P(("groups", "dp"), None),
    )
    return jax.shard_map(shards, mesh=mesh, in_specs=in_specs, out_specs=out_specs, check_vma=False)
```

time: 96.2 us -> 116 us (1.21)
  local copies, waits for them, and re-layouts: 19.4 us -> 36 us
  waiting for transfers between devices: 27.8 us -> 21.1 us
  other arithmetic: 3.33 us -> 6.99 us
  starting transfers between devices: 24.3 us -> 27.9 us
  Pallas kernels: 19.4 us -> 21.4 us
    unnamed x80 -> x115, local copies, waits for them, and re-layouts: 16.4 us -> 33.6 us
    ppermute x16 -> x18, waiting for transfers between devices: 27.7 us -> 16.2 us  [flip(): return lax.ppermute(array, axis, [(i, i ^ bit) for i in range(n)])]
    ppermute x4, waiting for transfers between devices: 0.04 us -> 4.84 us  [shift(): lax.ppermute(array, axis, [(i, i + step) for i in range(n) if 0 <= i + st...]
    reshape x0 -> x1, other arithmetic: none -> 2.34 us  [shards(): output.reshape(tokens.shape)]
    ppermute x16 -> x18, starting transfers between devices: 13.6 us -> 15.6 us  [flip(): return lax.ppermute(array, axis, [(i, i ^ bit) for i in range(n)])]
    pallas_call x8 -> x10, Pallas kernels: 19.4 us -> 21.4 us  [call(): pl.pallas_call(body, scratch_shapes=[pltpu.VMEM(shape, dtype) for shape,...]
    ppermute x4, starting transfers between devices: 10.7 us -> 12.3 us  [shift(): lax.ppermute(array, axis, [(i, i + step) for i in range(n) if 0 <= i + st...]
    slice x2 -> x9, local copies, waits for them, and re-layouts: 2.11 us -> 0.91 us  [the longest x4 0.58 us: half(): part[:, 1:].reshape(rows, 4 * HEAD_DIM)]
  transfers between devices with their start and end apart: 20 -> 22, of which waited for: 7 -> 9; matrix products, arithmetic and copies ran while one was open for 4% -> 11% of each run, Pallas kernels for 18% -> 12%
where the time goes in v2:
time: 116 us; the launch traced here: 114 us
  local copies, waits for them, and re-layouts  36 us (31%)
  starting transfers between devices  27.9 us (24%)
  Pallas kernels  21.4 us (18%)
  waiting for transfers between devices  21.1 us (18%)
  other arithmetic  6.99 us (6%)
    unnamed x115, local copies, waits for them, and re-layouts  33.6 us
    pallas_call x10, Pallas kernels, call(): pl.pallas_call(body, scratch_shapes=[pltpu.VMEM(shape, dtype) for shape,...  21.4 us
    ppermute x18, waiting for transfers between devices, flip(): return lax.ppermute(array, axis, [(i, i ^ bit) for i in range(n)])  16.2 us
    ppermute x18, starting transfers between devices, flip(): return lax.ppermute(array, axis, [(i, i ^ bit) for i in range(n)])  15.6 us
    ppermute x4, starting transfers between devices, shift(): lax.ppermute(array, axis, [(i, i + step) for i in range(n) if 0 <= i + st...  12.3 us
    ppermute x4, waiting for transfers between devices, shift(): lax.ppermute(array, axis, [(i, i + step) for i in range(n) if 0 <= i + st...  4.84 us
    reshape x1, other arithmetic, shards(): output.reshape(tokens.shape)  2.34 us
  transfers between devices with their start and end apart: 22, of which 9 were waited for; matrix products, arithmetic and copies ran while one was open for 11% of the time, Pallas kernels for 12%

profile of v2, /device:TPU:0, one launch (start us, length us, event | category | flops | bytes accessed | tf_op | source)
XLA Modules:
  0.0 114.5 jit_solution(2151416521091015123)
XLA Ops:
  4.7 3.0 %collective-permute-start.3 = (bf16[256,512]{1,0:T(8,128)(2,1)S(1)}, bf16[256,512]{1,0:T(8,128)(2,1)S(1)}, u32[]{:S(2)}, u32[]{:S(2)}) collective-permute-start(bf16[256,512]{1,0:T(8,128)(2,1)S(1)} %reshape.44.w0), channel_id=1, source_target_pairs={{0,2},{1,3},{2,0},{3,1},{4,6},{5,7},{6,4},{7,5},{8,10},{9,11},{10,... | collective-permute-start | bytes 786440 | tf_op jit(solution)/shard_map/ppermute | solution.py:234
  14.8 4.4 %collective-permute-done.4.w3 = bf16[256,512]{1,0:T(8,128)(2,1)S(1)} collective-permute-done((bf16[256,512]{1,0:T(8,128)(2,1)}, bf16[256,512]{1,0:T(8,128)(2,1)S(1)}, u32[]{:S(2)}, u32[]{:S(2)}) %collective-permute-start.4) | collective-permute-done | bytes 262176 | tf_op jit(solution)/shard_map/ppermute | solution.py:234
  22.1 4.4 %collective-permute-start.5 = (bf16[2,272,128]{2,1,0:T(8,128)(2,1)S(1)}, bf16[2,272,128]{2,1,0:T(8,128)(2,1)}, u32[]{:S(2)}, u32[]{:S(2)}) collective-permute-start(bf16[2,272,128]{2,1,0:T(8,128)(2,1)S(1)} %get-tuple-element.33), channel_id=1, source_target_pairs={{0,4},{4,8},{8,12},{1,5},{5,9},{9,13},{2,6},{6,10},{10,14},{3,7},{... | collective-permute-start | bytes 417800 | tf_op jit(solution)/shard_map/ppermute | solution.py:239
  26.5 1.5 %collective-permute-start.11 = (bf16[128,1024]{1,0:T(8,128)(2,1)}, bf16[128,1024]{1,0:T(8,128)(2,1)}, u32[]{:S(2)}, u32[]{:S(2)}) collective-permute-start(bf16[128,1024]{1,0:T(8,128)(2,1)} %own.3), channel_id=1, source_target_pairs={{0,2},{1,3},{2,0},{3,1},{4,6},{5,7},{6,4},{7,5},{8,10},{9,11},{10,... | collective-permute-start | bytes 786440 | tf_op jit(solution)/shard_map/ppermute | solution.py:234
  28.9 5.2 %collective-permute-start.6 = (bf16[2,272,128]{2,1,0:T(8,128)(2,1)}, bf16[2,272,128]{2,1,0:T(8,128)(2,1)}, u32[]{:S(2)}, u32[]{:S(2)}) collective-permute-start(bf16[2,272,128]{2,1,0:T(8,128)(2,1)} %collective-permute-done.5.near), channel_id=1, source_target_pairs={{0,4},{4,8},{8,12},{1,5},{5,9},{9,13},{2,6},{6,10},{10,14},{3,7},{... | collective-permute-start | bytes 417800 | tf_op jit(solution)/shard_map/ppermute | solution.py:239
  34.1 1.5 %collective-permute-start.8 = (bf16[256,256]{1,0:T(8,128)(2,1)}, bf16[256,256]{1,0:T(8,128)(2,1)}, u32[]{:S(2)}, u32[]{:S(2)}) collective-permute-start(bf16[256,256]{1,0:T(8,128)(2,1)} %bitcast.29.w0), channel_id=1, source_target_pairs={{0,2},{1,3},{2,0},{3,1},{4,6},{5,7},{6,4},{7,5},{8,10},{9,11},{10,... | collective-permute-start | bytes 393224 | tf_op jit(solution)/shard_map/ppermute | solution.py:234
  36.2 3.1 %collective-permute-done.8.w2 = bf16[256,256]{1,0:T(8,128)(2,1)} collective-permute-done((bf16[256,256]{1,0:T(8,128)(2,1)}, bf16[256,256]{1,0:T(8,128)(2,1)}, u32[]{:S(2)}, u32[]{:S(2)}) %collective-permute-start.8) | collective-permute-done | bytes 131104 | tf_op jit(solution)/shard_map/ppermute | solution.py:234
  39.4 2.8 %collective-permute-done.9.w3 = bf16[256,256]{1,0:T(8,128)(2,1)} collective-permute-done((bf16[256,256]{1,0:T(8,128)(2,1)}, bf16[256,256]{1,0:T(8,128)(2,1)}, u32[]{:S(2)}, u32[]{:S(2)}) %collective-permute-start.9) | collective-permute-done | bytes 131104 | tf_op jit(solution)/shard_map/ppermute | solution.py:234
  46.3 3.1 %shard_map.97 = (bf16[2,2,384,128]{3,2,1,0:T(8,128)(2,1)S(1)}, bf16[2,2,384,384]{3,2,1,0:T(8,128)(2,1)S(1)}, f32[2,2,384,128]{3,2,1,0:T(8,128)S(1)}) custom-call(bf16[4,768,256]{2,1,0:T(8,128)(2,1)S(1)} %get-tuple-element.31.normed, bf16[256,256]{1,0:T(8,128)(2,1)} %bitcast.29.w0, bf16[256,256]{1,0:T(8,128)(2,1)S(1)} %copy-done.37, ...), custom_call_target="tpu_custom_call" | custom-call | tf_op jit(solution)/shard_map/pallas_call | solution.py:46
  50.4 2.4 %shard_map.98.upstream = f32[2,2,384,128]{3,2,1,0:T(8,128)S(1)} custom-call(s32[1]{0:T(128)} %bitcast.me, bf16[384,1024]{1,0:T(8,128)(2,1)S(1)} %bitcast.31, bf16[384,1024]{1,0:T(8,128)(2,1)} %collective-permute-done.10.cot_partner, bf16[128,1024]{1,0:T(8,128)(2,1)} %own.3, bf16[128,1024]{1,0:T(8,128)(2,1)} %collective-permute-done.11.other, ...), custom_call_target="tpu_custom_call" | custom-call | tf_op jit(solution)/shard_map/pallas_call | solution.py:46
  52.8 1.9 %shard_map.99 = (bf16[2,2,384,128]{3,2,1,0:T(8,128)(2,1)S(1)}, bf16[2,2,384,128]{3,2,1,0:T(8,128)(2,1)S(1)}, bf16[2,272,128]{2,1,0:T(8,128)(2,1)S(1)}) custom-call(s32[1]{0:T(128)} %bitcast.me, bf16[2,272,128]{2,1,0:T(8,128)(2,1)} %collective-permute-done.5.near, bf16[2,272,128]{2,1,0:T(8,128)(2,1)} %collective-permute-done.6.far, ...), custom_call_target="tpu_custom_call" | custom-call | tf_op jit(solution)/shard_map/pallas_call | solution.py:46
  56.1 2.5 %shard_map.103 = (f32[64,1024]{1,0:T(8,128)S(1)}, bf16[64,1024]{1,0:T(8,128)(2,1)}, f32[2,32,1024]{2,1,0:T(8,128)S(1)}, bf16[2,32,1024]{2,1,0:T(8,128)(2,1)S(1)}) custom-call(s32[1]{0:T(128)} %bitcast.me, s32[1]{0:T(128)} %bitcast.10.odd, bf16[2,2,384,128]{3,2,1,0:T(8,128)(2,1)S(1)} %get-tuple-element.43.mixed, bf16[384,1024]{1,0:T(8,128)(2,1)S(1)} %bitcast.32, ...), custom_call_target="tpu_custom_call" | custom-call | tf_op jit(solution)/shard_map/pallas_call | solution.py:46
  63.9 2.5 %collective-permute-done.16 = bf16[64,1024]{1,0:T(8,128)(2,1)} collective-permute-done((bf16[64,1024]{1,0:T(8,128)(2,1)}, bf16[64,1024]{1,0:T(8,128)(2,1)}, u32[]{:S(2)}, u32[]{:S(2)}) %collective-permute-start.16) | collective-permute-done | bytes 131104 | tf_op jit(solution)/shard_map/ppermute | solution.py:234
  69.5 1.5 %collective-permute-start.19 = (bf16[32,1024]{1,0:T(8,128)(2,1)S(1)}, bf16[32,1024]{1,0:T(8,128)(2,1)S(1)}, u32[]{:S(2)}, u32[]{:S(2)}) collective-permute-start(bf16[32,1024]{1,0:T(8,128)(2,1)S(1)} %fusion.3), channel_id=1, source_target_pairs={{0,2},{1,3},{2,0},{3,1},{4,6},{5,7},{6,4},{7,5},{8,10},{9,11},{10,... | collective-permute-start | bytes 196616 | tf_op jit(solution)/shard_map/ppermute | solution.py:234
  71.9 1.9 %collective-permute-done.19 = bf16[32,1024]{1,0:T(8,128)(2,1)S(1)} collective-permute-done((bf16[32,1024]{1,0:T(8,128)(2,1)S(1)}, bf16[32,1024]{1,0:T(8,128)(2,1)S(1)}, u32[]{:S(2)}, u32[]{:S(2)}) %collective-permute-start.19) | collective-permute-done | bytes 65568 | tf_op jit(solution)/shard_map/ppermute | solution.py:234
  73.9 1.5 %collective-permute-start.20 = (bf16[64,1024]{1,0:T(8,128)(2,1)S(1)}, bf16[64,1024]{1,0:T(8,128)(2,1)S(1)}, u32[]{:S(2)}, u32[]{:S(2)}) collective-permute-start(bf16[64,1024]{1,0:T(8,128)(2,1)S(1)} %fusion.1), channel_id=1, source_target_pairs={{0,8},{4,12},{8,0},{12,4},{1,9},{5,13},{9,1},{13,5},{2,10},{6,14},... | collective-permute-start | bytes 393224 | tf_op jit(solution)/shard_map/ppermute | solution.py:234
  78.6 5.2 %shard_map.100 = (f32[384,1024]{1,0:T(8,128)S(1)}, bf16[384,1024]{1,0:T(8,128)(2,1)}, f32[2,2,384,128]{3,2,1,0:T(8,128)S(1)}, f32[2,2,384,128]{3,2,1,0:T(8,128)S(1)}, f32[4,768,256]{2,1,0:T(8,128)S(1)}) custom-call(s32[1]{0:T(128)} %bitcast.me, bf16[2,272,128]{2,1,0:T(8,128)(2,1)} %collective-permute-done.5.near, ...), custom_call_target="tpu_custom_call" | custom-call | tf_op jit(solution)/shard_map/pallas_call | solution.py:46
  83.8 1.6 %copy-done.12 = f32[4,768,256]{2,1,0:T(8,128)} copy-done((f32[4,768,256]{2,1,0:T(8,128)}, f32[4,768,256]{2,1,0:T(8,128)S(1)}, u32[]{:S(2)}) %copy-start.12) | copy-done | bytes 3145752
  90.4 2.6 %collective-permute-start.21 = (bf16[64,1024]{1,0:T(8,128)(2,1)}, bf16[64,1024]{1,0:T(8,128)(2,1)}, u32[]{:S(2)}, u32[]{:S(2)}) collective-permute-start(bf16[64,1024]{1,0:T(8,128)(2,1)} %fusion.4), channel_id=1, source_target_pairs={{0,4},{4,0},{8,12},{12,8},{1,5},{5,1},{9,13},{13,9},{2,6},{6,2},{1... | collective-permute-start | bytes 393224 | tf_op jit(solution)/shard_map/ppermute | solution.py:234
  93.0 3.9 %collective-permute-done.14.far = bf16[2,272,128]{2,1,0:T(8,128)(2,1)S(1)} collective-permute-done((bf16[2,272,128]{2,1,0:T(8,128)(2,1)}, bf16[2,272,128]{2,1,0:T(8,128)(2,1)S(1)}, u32[]{:S(2)}, u32[]{:S(2)}) %collective-permute-start.14) | collective-permute-done | bytes 139296 | tf_op jit(solution)/shard_map/ppermute | solution.py:239
  97.9 1.9 %copy-done.13 = f32[4,768,256]{2,1,0:T(8,128)S(1)} copy-done((f32[4,768,256]{2,1,0:T(8,128)S(1)}, f32[4,768,256]{2,1,0:T(8,128)}, u32[]{:S(2)}) %copy-start.13) | copy-done | bytes 3145752
  105.9 2.3 %shard_map.101 = (f32[4,384,256]{2,1,0:T(8,128)S(1)}, bf16[4,384,256]{2,1,0:T(8,128)(2,1)S(1)}) custom-call(bf16[2,272,128]{2,1,0:T(8,128)(2,1)} %collective-permute-done.13.near, bf16[2,272,128]{2,1,0:T(8,128)(2,1)S(1)} %collective-permute-done.14.far, f32[2,384,128]{2,1,0:T(8,128)S(1)} %get-tuple-element.32.seg_col, ...), custom_call_target="tpu_custom_call" | custom-call | tf_op jit(solution)/shard_map/pallas_call | solution.py:46
  110.3 2.3 %fusion = bf16[1,384,1024]{2,1,0:T(8,128)(2,1)} fusion(f32[384,1024]{1,0:T(8,128)S(1)} %copy-done.17, bf16[384,1024]{1,0:T(8,128)(2,1)} %collective-permute-done.12), kind=kLoop, calls=%fused_computation.1 | loop fusion | flops 1179648 | bytes 3145728 | tf_op jit(solution)/shard_map/reshape | solution.py:377
  112.7 1.8 %shard_map.102 = bf16[384,1024]{1,0:T(8,128)(2,1)} custom-call(s32[1]{0:T(128)} %bitcast.me, f32[4,384,256]{2,1,0:T(8,128)S(1)} %get-tuple-element.52.own, bf16[4,384,256]{2,1,0:T(8,128)(2,1)S(1)} %collective-permute-done.15.partner, bf16[384,1024]{1,0:T(8,128)(2,1)S(1)} %bitcast.37, bf16[384,1024]{1,0:T(8,128)(2,1)S(1)} %bitcast.33, ...), custom_call_target="tpu_custom_call" | custom-call | tf_op jit(solution)/shard_map/pallas_call | solution.py:46
  (171 shorter events, 48.5 us)
Async XLA Ops:
  0.6 9.0 %collective-permute-start = (bf16[384,1024]{1,0:T(8,128)(2,1)}, bf16[384,1024]{1,0:T(8,128)(2,1)S(1)}, u32[]{:S(2)}, u32[]{:S(2)}) collective-permute-start(bf16[384,1024]{1,0:T(8,128)(2,1)} %bitcast.34), channel_id=1, source_target_pairs={{0,1},{1,0},{2,3},{3,2},{4,5},{5,4},{6,7},{7,6},{8,9},{9,8},{10,11... | collective-permute-start | bytes 2359304 | tf_op jit(solution)/shard_map/ppermute | solution.py:234
  4.0 9.5 %collective-permute-start.2 = (bf16[256,512]{1,0:T(8,128)(2,1)}, bf16[256,512]{1,0:T(8,128)(2,1)S(1)}, u32[]{:S(2)}, u32[]{:S(2)}) collective-permute-start(bf16[256,512]{1,0:T(8,128)(2,1)} %reshape.45), channel_id=1, source_target_pairs={{0,1},{1,0},{2,3},{3,2},{4,5},{5,4},{6,7},{7,6},{8,9},{9,8},{10,11... | collective-permute-start | bytes 786440 | tf_op jit(solution)/shard_map/ppermute | solution.py:234
  4.7 10.1 %collective-permute-start.3 = (bf16[256,512]{1,0:T(8,128)(2,1)S(1)}, bf16[256,512]{1,0:T(8,128)(2,1)S(1)}, u32[]{:S(2)}, u32[]{:S(2)}) collective-permute-start(bf16[256,512]{1,0:T(8,128)(2,1)S(1)} %reshape.44.w0), channel_id=1, source_target_pairs={{0,2},{1,3},{2,0},{3,1},{4,6},{5,7},{6,4},{7,5},{8,10},{9,11},{10,... | collective-permute-start | bytes 786440 | tf_op jit(solution)/shard_map/ppermute | solution.py:234
  7.7 11.5 %collective-permute-start.4 = (bf16[256,512]{1,0:T(8,128)(2,1)}, bf16[256,512]{1,0:T(8,128)(2,1)S(1)}, u32[]{:S(2)}, u32[]{:S(2)}) collective-permute-start(bf16[256,512]{1,0:T(8,128)(2,1)} %reshape.45), channel_id=1, source_target_pairs={{0,3},{1,2},{2,1},{3,0},{4,7},{5,6},{6,5},{7,4},{8,11},{9,10},{10,... | collective-permute-start | bytes 786440 | tf_op jit(solution)/shard_map/ppermute | solution.py:234
  7.7 1.9 %collective-permute-start.1 = (f32[1,384]{1,0:T(1,128)S(1)}, f32[1,384]{1,0:T(1,128)S(1)}, u32[]{:S(2)}, u32[]{:S(2)}) collective-permute-start(f32[1,384]{1,0:T(1,128)S(1)} %convert_element_type.40.seg), channel_id=1, source_target_pairs={{0,1},{1,0},{2,3},{3,2},{4,5},{5,4},{6,7},{7,6},{8,9},{9,8},{10,11... | collective-permute-start | bytes 4616 | tf_op jit(solution)/shard_map/ppermute | solution.py:234
  21.7 28.8 %collective-permute-start.10 = (bf16[384,1024]{1,0:T(8,128)(2,1)S(1)}, bf16[384,1024]{1,0:T(8,128)(2,1)}, u32[]{:S(2)}, u32[]{:S(2)}) collective-permute-start(bf16[384,1024]{1,0:T(8,128)(2,1)S(1)} %bitcast.30), channel_id=1, source_target_pairs={{0,1},{1,0},{2,3},{3,2},{4,5},{5,4},{6,7},{7,6},{8,9},{9,8},{10,11... | collective-permute-start | bytes 2359304 | tf_op jit(solution)/shard_map/ppermute | solution.py:234
  22.1 6.8 %collective-permute-start.5 = (bf16[2,272,128]{2,1,0:T(8,128)(2,1)S(1)}, bf16[2,272,128]{2,1,0:T(8,128)(2,1)}, u32[]{:S(2)}, u32[]{:S(2)}) collective-permute-start(bf16[2,272,128]{2,1,0:T(8,128)(2,1)S(1)} %get-tuple-element.33), channel_id=1, source_target_pairs={{0,4},{4,8},{8,12},{1,5},{5,9},{9,13},{2,6},{6,10},{10,14},{3,7},{... | collective-permute-start | bytes 417800 | tf_op jit(solution)/shard_map/ppermute | solution.py:239
  26.5 9.1 %collective-permute-start.7 = (bf16[256,256]{1,0:T(8,128)(2,1)}, bf16[256,256]{1,0:T(8,128)(2,1)S(1)}, u32[]{:S(2)}, u32[]{:S(2)}) collective-permute-start(bf16[256,256]{1,0:T(8,128)(2,1)} %bitcast.28), channel_id=1, source_target_pairs={{0,1},{1,0},{2,3},{3,2},{4,5},{5,4},{6,7},{7,6},{8,9},{9,8},{10,11... | collective-permute-start | bytes 393224 | tf_op jit(solution)/shard_map/ppermute | solution.py:234
  26.5 23.9 %collective-permute-start.11 = (bf16[128,1024]{1,0:T(8,128)(2,1)}, bf16[128,1024]{1,0:T(8,128)(2,1)}, u32[]{:S(2)}, u32[]{:S(2)}) collective-permute-start(bf16[128,1024]{1,0:T(8,128)(2,1)} %own.3), channel_id=1, source_target_pairs={{0,2},{1,3},{2,0},{3,1},{4,6},{5,7},{6,4},{7,5},{8,10},{9,11},{10,... | collective-permute-start | bytes 786440 | tf_op jit(solution)/shard_map/ppermute | solution.py:234
  28.9 23.9 %collective-permute-start.6 = (bf16[2,272,128]{2,1,0:T(8,128)(2,1)}, bf16[2,272,128]{2,1,0:T(8,128)(2,1)}, u32[]{:S(2)}, u32[]{:S(2)}) collective-permute-start(bf16[2,272,128]{2,1,0:T(8,128)(2,1)} %collective-permute-done.5.near), channel_id=1, source_target_pairs={{0,4},{4,8},{8,12},{1,5},{5,9},{9,13},{2,6},{6,10},{10,14},{3,7},{... | collective-permute-start | bytes 417800 | tf_op jit(solution)/shard_map/ppermute | solution.py:239
  34.1 5.3 %collective-permute-start.8 = (bf16[256,256]{1,0:T(8,128)(2,1)}, bf16[256,256]{1,0:T(8,128)(2,1)}, u32[]{:S(2)}, u32[]{:S(2)}) collective-permute-start(bf16[256,256]{1,0:T(8,128)(2,1)} %bitcast.29.w0), channel_id=1, source_target_pairs={{0,2},{1,3},{2,0},{3,1},{4,6},{5,7},{6,4},{7,5},{8,10},{9,11},{10,... | collective-permute-start | bytes 393224 | tf_op jit(solution)/shard_map/ppermute | solution.py:234
  36.2 5.9 %collective-permute-start.9 = (bf16[256,256]{1,0:T(8,128)(2,1)}, bf16[256,256]{1,0:T(8,128)(2,1)}, u32[]{:S(2)}, u32[]{:S(2)}) collective-permute-start(bf16[256,256]{1,0:T(8,128)(2,1)} %bitcast.28), channel_id=1, source_target_pairs={{0,3},{1,2},{2,1},{3,0},{4,7},{5,6},{6,5},{7,4},{8,11},{9,10},{10,... | collective-permute-start | bytes 393224 | tf_op jit(solution)/shard_map/ppermute | solution.py:234
  60.8 5.6 %collective-permute-start.16 = (bf16[64,1024]{1,0:T(8,128)(2,1)}, bf16[64,1024]{1,0:T(8,128)(2,1)}, u32[]{:S(2)}, u32[]{:S(2)}) collective-permute-start(bf16[64,1024]{1,0:T(8,128)(2,1)} %get-tuple-element.56), channel_id=1, source_target_pairs={{0,2},{1,3},{2,0},{3,1},{4,6},{5,7},{6,4},{7,5},{8,10},{9,11},{10,... | collective-permute-start | bytes 393224 | tf_op jit(solution)/shard_map/ppermute | solution.py:234
  61.5 7.0 %collective-permute-start.18 = (bf16[2,32,1024]{2,1,0:T(8,128)(2,1)}, bf16[2,32,1024]{2,1,0:T(8,128)(2,1)S(1)}, u32[]{:S(2)}, u32[]{:S(2)}) collective-permute-start(bf16[2,32,1024]{2,1,0:T(8,128)(2,1)} %copy-done.48), channel_id=1, source_target_pairs={{0,4},{4,0},{8,12},{12,8},{1,5},{5,1},{9,13},{13,9},{2,6},{6,2},{1... | collective-permute-start | bytes 393224 | tf_op jit(solution)/shard_map/ppermute | solution.py:234
  62.4 25.9 %collective-permute-start.13 = (bf16[2,272,128]{2,1,0:T(8,128)(2,1)}, bf16[2,272,128]{2,1,0:T(8,128)(2,1)}, u32[]{:S(2)}, u32[]{:S(2)}) collective-permute-start(bf16[2,272,128]{2,1,0:T(8,128)(2,1)} %copy-done.47), channel_id=1, source_target_pairs={{4,0},{8,4},{12,8},{5,1},{9,5},{13,9},{6,2},{10,6},{14,10},{7,3},{... | collective-permute-start | bytes 417800 | tf_op jit(solution)/shard_map/ppermute | solution.py:239
  67.4 4.4 %collective-permute-start.17 = (bf16[32,1024]{1,0:T(8,128)(2,1)S(1)}, bf16[32,1024]{1,0:T(8,128)(2,1)S(1)}, u32[]{:S(2)}, u32[]{:S(2)}) collective-permute-start(bf16[32,1024]{1,0:T(8,128)(2,1)S(1)} %select_convert_fusion), channel_id=1, source_target_pairs={{0,4},{4,0},{8,12},{12,8},{1,5},{5,1},{9,13},{13,9},{2,6},{6,2},{1... | collective-permute-start | bytes 196616 | tf_op jit(solution)/shard_map/ppermute | solution.py:234
  69.5 4.3 %collective-permute-start.19 = (bf16[32,1024]{1,0:T(8,128)(2,1)S(1)}, bf16[32,1024]{1,0:T(8,128)(2,1)S(1)}, u32[]{:S(2)}, u32[]{:S(2)}) collective-permute-start(bf16[32,1024]{1,0:T(8,128)(2,1)S(1)} %fusion.3), channel_id=1, source_target_pairs={{0,2},{1,3},{2,0},{3,1},{4,6},{5,7},{6,4},{7,5},{8,10},{9,11},{10,... | collective-permute-start | bytes 196616 | tf_op jit(solution)/shard_map/ppermute | solution.py:234
  71.9 17.8 %copy-start.49 = (f32[32,1024]{1,0:T(8,128)}, f32[32,1024]{1,0:T(8,128)S(1)}, u32[]{:S(2)}) copy-start(f32[32,1024]{1,0:T(8,128)S(1)} %convert_add_fusion.3) | copy-start | bytes 393220
  73.8 15.9 %copy-start.51 = (f32[32,1024]{1,0:T(8,128)}, f32[32,1024]{1,0:T(8,128)S(1)}, u32[]{:S(2)}) copy-start(f32[32,1024]{1,0:T(8,128)S(1)} %fusion.2) | copy-start | bytes 393220
  73.9 15.8 %collective-permute-start.20 = (bf16[64,1024]{1,0:T(8,128)(2,1)S(1)}, bf16[64,1024]{1,0:T(8,128)(2,1)S(1)}, u32[]{:S(2)}, u32[]{:S(2)}) collective-permute-start(bf16[64,1024]{1,0:T(8,128)(2,1)S(1)} %fusion.1), channel_id=1, source_target_pairs={{0,8},{4,12},{8,0},{12,4},{1,9},{5,13},{9,1},{13,5},{2,10},{6,14},... | collective-permute-start | bytes 393224 | tf_op jit(solution)/shard_map/ppermute | solution.py:234
  88.4 22.0 %collective-permute-start.12 = (bf16[384,1024]{1,0:T(8,128)(2,1)}, bf16[384,1024]{1,0:T(8,128)(2,1)}, u32[]{:S(2)}, u32[]{:S(2)}) collective-permute-start(bf16[384,1024]{1,0:T(8,128)(2,1)} %get-tuple-element.47), channel_id=1, source_target_pairs={{0,1},{1,0},{2,3},{3,2},{4,5},{5,4},{6,7},{7,6},{8,9},{9,8},{10,11... | collective-permute-start | bytes 2359304 | tf_op jit(solution)/shard_map/ppermute | solution.py:234
  88.4 8.6 %collective-permute-start.14 = (bf16[2,272,128]{2,1,0:T(8,128)(2,1)}, bf16[2,272,128]{2,1,0:T(8,128)(2,1)S(1)}, u32[]{:S(2)}, u32[]{:S(2)}) collective-permute-start(bf16[2,272,128]{2,1,0:T(8,128)(2,1)} %collective-permute-done.13.near), channel_id=1, source_target_pairs={{4,0},{8,4},{12,8},{5,1},{9,5},{13,9},{6,2},{10,6},{14,10},{7,3},{... | collective-permute-start | bytes 417800 | tf_op jit(solution)/shard_map/ppermute | solution.py:239
  90.4 17.9 %collective-permute-start.21 = (bf16[64,1024]{1,0:T(8,128)(2,1)}, bf16[64,1024]{1,0:T(8,128)(2,1)}, u32[]{:S(2)}, u32[]{:S(2)}) collective-permute-start(bf16[64,1024]{1,0:T(8,128)(2,1)} %fusion.4), channel_id=1, source_target_pairs={{0,4},{4,0},{8,12},{12,8},{1,5},{5,1},{9,13},{13,9},{2,6},{6,2},{1... | collective-permute-start | bytes 393224 | tf_op jit(solution)/shard_map/ppermute | solution.py:234
  108.3 4.4 %collective-permute-start.15 = (bf16[4,384,256]{2,1,0:T(8,128)(2,1)S(1)}, bf16[4,384,256]{2,1,0:T(8,128)(2,1)S(1)}, u32[]{:S(2)}, u32[]{:S(2)}) collective-permute-start(bf16[4,384,256]{2,1,0:T(8,128)(2,1)S(1)} %get-tuple-element.53), channel_id=1, source_target_pairs={{0,1},{1,0},{2,3},{3,2},{4,5},{5,4},{6,7},{7,6},{8,9},{9,8},{10,11... | collective-permute-start | bytes 2359304 | tf_op jit(solution)/shard_map/ppermute | solution.py:234
  (54 other events, 160.7 us)

commit v3 on v2

v3 whole, which is shorter than its diff:
```python
import functools
import math

import jax
import jax.numpy as jnp
from jax import lax
from jax.experimental import pallas as pl
from jax.experimental.pallas import tpu as pltpu
from jax.sharding import PartitionSpec as P

D = 1024
HEADS = 4
HEAD_DIM = 128
ID_ROWS = 16

epsilon = 1e-06

f32 = jnp.float32
bf16 = jnp.bfloat16


def dot_nn(a, b):
    return lax.dot_general(a, b, (((1,), (0,)), ((), ())), preferred_element_type=f32)


def dot_nt(a, b):
    return lax.dot_general(a, b, (((1,), (1,)), ((), ())), preferred_element_type=f32)


def dot_tn(a, b):
    return lax.dot_general(a, b, (((0,), (0,)), ((), ())), preferred_element_type=f32)


def feature_map(u):
    return jnp.where(u > 0, u + 1.0, jnp.exp(jnp.minimum(u, 0.0)))


def head(h):
    return slice(h * HEAD_DIM, (h + 1) * HEAD_DIM)


VMEM = pl.BlockSpec(memory_space=pltpu.VMEM)
SMEM = pl.BlockSpec(memory_space=pltpu.SMEM)
FAR = pl.BlockSpec(memory_space=pltpu.HBM)
FREE = pl.BlockSpec()


class Far:
    def __init__(self, array):
        self.array = array


class Fetched:
    def __init__(self, ref, copy):
        self.ref, self.copy = ref, copy

    def wait(self):
        if self.copy is not None:
            self.copy.wait()
            self.copy = None

    def __getitem__(self, index):
        self.wait()
        return self.ref[index]


def call(body, outs, scalars, *args, scratch=(), us=2.0):
    far = [isinstance(arg, Far) for arg in args]
    arrays = [arg.array if isinstance(arg, Far) else arg for arg in args]
    fetched = [arg for arg, is_far in zip(arrays, far) if is_far]

    def kernel(*refs):
        operands = refs[1 : 1 + len(arrays)]
        results = refs[1 + len(arrays) : 1 + len(arrays) + len(outs)]
        rest = refs[1 + len(arrays) + len(outs) :]
        given, at = [], 0
        for ref, is_far in zip(operands, far):
            if is_far:
                copy = pltpu.make_async_copy(ref, rest[at], rest[len(fetched)].at[at])
                copy.start()
                given.append(Fetched(rest[at], copy))
                at += 1
            else:
                given.append(ref)
        body(refs[0], *given, *results, *rest[len(fetched) + bool(fetched) :])
        for operand in given:
            if isinstance(operand, Fetched):
                operand.wait()

    buffers = [pltpu.VMEM(arg.shape, arg.dtype) for arg in fetched]
    if fetched:
        buffers.append(pltpu.SemaphoreType.DMA((len(fetched),)))
    return pl.pallas_call(
        kernel,
        out_shape=[jax.ShapeDtypeStruct(out[0], out[1]) for out in outs],
        in_specs=[SMEM] + [FAR if is_far else VMEM for is_far in far],
        out_specs=[out[2] if len(out) > 2 else VMEM for out in outs],
        scratch_shapes=buffers + [pltpu.VMEM(shape, dtype) for shape, dtype in scratch],
        compiler_params=pltpu.CompilerParams(vmem_limit_bytes=32 * 1024 * 1024),
        cost_estimate=pl.CostEstimate(flops=int(us * 1e9), transcendentals=0, bytes_accessed=int(us * 3e6)),
    )(scalars, *arrays)


def columns(index, width):
    return pl.ds(pl.multiple_of(index * width, width), width)


def causal(seg_col, seg_row, i):
    length = seg_row.shape[1]
    order = lax.broadcasted_iota(jnp.int32, (length, length), 0) >= lax.broadcasted_iota(
        jnp.int32, (length, length), 1
    )
    down = jnp.concatenate([seg_col[i]] * (length // HEAD_DIM), axis=1)
    return (down == seg_row[...]) & order


ME, ODD, NEAR, FURTHER, BACK_NEAR, BACK_FURTHER = range(6)


def split_body(info, w, kv_mine, kv_other, q_mine, q_other, sem):
    c = info[ME] % 2
    copies = []
    for kind, mine, other, first in ((4, kv_mine, kv_other, 0), (8, kv_mine, kv_other, 2), (0, q_mine, q_other, 0)):
        for target, which in ((mine, c), (other, 1 - c)):
            for g in range(2):
                copy = pltpu.make_async_copy(
                    w.at[:, columns(kind + 2 * g + which, HEAD_DIM)], target.at[:, head(first + g)], sem.at[len(copies)]
                )
                copy.start()
                copies.append(copy)
    for copy in copies:
        copy.wait()


def prep_body(info, tokens, partner, seg, seg_partner, gain, w0, w1, normed, inv_rms, seg_col, raw):
    length = seg.shape[1]
    for i, (part, ids) in enumerate(((tokens, seg), (partner, seg_partner))):
        x = part[...].astype(f32)
        inv = lax.rsqrt(jnp.mean(x * x, axis=1, keepdims=True) + epsilon)
        if i == 0:
            inv_rms[...] = inv
        for j in range(4):
            at = columns(info[ME] ^ j, 256)
            normed[j, i * length : (i + 1) * length] = (part[:, at].astype(f32) * inv * gain[:, at]).astype(bf16)
        seg_col[i] = jnp.broadcast_to(ids[...], (HEAD_DIM, length)).T
    raw[...] = dot_nn(normed[0], w0[...]) + dot_nn(normed[1], w1[...])


def kv_body(info, near, normed, w2, w3, seg_col, feat_k, values, state):
    raw = near[...] + dot_nn(normed[2], w2[...]) + dot_nn(normed[3], w3[...])
    raw = raw.astype(bf16)
    length = seg_col.shape[1]
    for i in range(2):
        last = seg_col[i, length - 1 : length, :]
        tail = seg_col[i] == last
        rows = slice(i * length, (i + 1) * length)
        for g in range(2):
            k = feature_map(raw[rows, head(g)].astype(f32))
            v = raw[rows, head(2 + g)]
            feat_k[i, g] = k.astype(bf16)
            values[i, g] = v
            state[i, head(g), :] = dot_tn(jnp.where(tail, k, 0.0).astype(bf16), v).astype(bf16)
        state[i, 2 * HEAD_DIM :, :] = jnp.broadcast_to(last, (ID_ROWS, HEAD_DIM)).astype(bf16)


def query_body(
    info, normed, w0, w1, w2, w3, feat_k, values, seg_col, seg, seg_partner, cot, cot_partner, own, other, gain,
    feat_q, intra, upstream,
):
    raw = dot_nn(normed[0], w0[...])
    raw += dot_nn(normed[1], w1[...])
    raw += dot_nn(normed[2], w2[...])
    raw += dot_nn(normed[3], w3[...])
    raw = raw.astype(bf16)
    length = seg.shape[1]
    for i, ids in enumerate((seg, seg_partner)):
        mask = causal(seg_col, ids, i)
        for g in range(2):
            q = feature_map(raw[i * length : (i + 1) * length, head(g)].astype(f32)).astype(bf16)
            feat_q[i, g] = q
            s = jnp.where(mask, dot_nt(q, feat_k[i, g]), 0.0).astype(bf16)
            intra[i, g] = dot_nn(s, values[i, g])
    for j, o in enumerate((own, other)):
        full = info[ME] ^ (2 * j)
        for i, part in enumerate((cot, cot_partner)):
            upstream[i, full // 2] = dot_nt(part[...], o[...]) * gain[:, columns(full, HEAD_DIM)]


def received(info, which, pair, middle, further, i):
    use_pair, use_further = info[which] == 1, info[which + 1] == 1
    near = jnp.where(use_pair, pair[i].astype(f32), middle[i].astype(f32))
    ids = near[2 * HEAD_DIM : 2 * HEAD_DIM + 1, :]
    far = further[i].astype(f32)
    same = (far[2 * HEAD_DIM : 2 * HEAD_DIM + 1, :] == ids) & use_further
    total = near[: 2 * HEAD_DIM] + jnp.where(same, far[: 2 * HEAD_DIM], 0.0)
    return ids, total.astype(bf16)


def attn_body(
    info, pair, middle, further, seg_col, feat_q, intra, upstream, gain, cot, cot_partner,
    mixed, d_attn, state, before, rest, a_send, b_send,
):
    for i in range(2):
        first = seg_col[i, 0:1, :]
        begin = seg_col[i] == first
        ids, total = received(info, NEAR, pair, middle, further, i)
        before[i] = total
        take = seg_col[i] == ids
        for g in range(2):
            q = feat_q[i, g]
            attention = intra[i, g] + jnp.where(take, dot_nn(q, total[head(g)]), 0.0)
            ratio = lax.rsqrt(jnp.mean(attention * attention, axis=1, keepdims=True) + epsilon)
            mixed[i, g] = (attention * ratio * gain[:, columns(2 * g + info[ME] % 2, HEAD_DIM)]).astype(bf16)
            up = upstream[i, g]
            inner = jnp.mean(attention * up, axis=1, keepdims=True)
            da = (ratio * up - ratio**3 * attention * inner).astype(bf16)
            d_attn[i, g] = da
            state[i, head(g), :] = dot_tn(jnp.where(begin, q.astype(f32), 0.0).astype(bf16), da).astype(bf16)
        state[i, 2 * HEAD_DIM :, :] = jnp.broadcast_to(first, (ID_ROWS, HEAD_DIM)).astype(bf16)
    half = HEAD_DIM // 2
    quarter = half // 2
    second = info[ODD] == 1
    for j in range(2):
        g = (info[ME] ^ (2 * j)) // 2
        part = dot_tn(mixed[0, g], cot[...]) + dot_tn(mixed[1, g], cot_partner[...])
        if j == 0:
            rest[:half] = part[:half]
        else:
            a_send[...] = part[:half].astype(bf16)
        low, high = part[half : half + quarter], part[half + quarter :]
        rest[half + j * quarter : half + (j + 1) * quarter] = jnp.where(second, high, low)
        b_send[j] = jnp.where(second, low, high).astype(bf16)


def weight_one_body(info, rest, a_in, b_in, kept, a_send, b_send):
    second = info[ODD] == 1
    quarter = b_in.shape[1]
    low = rest[:quarter] + a_in[:quarter].astype(f32)
    high = rest[quarter : 2 * quarter] + a_in[quarter:].astype(f32)
    kept[:quarter] = jnp.where(second, high, low)
    a_send[...] = jnp.where(second, low, high).astype(bf16)
    kept[quarter:] = rest[2 * quarter : 3 * quarter] + b_in[0].astype(f32)
    b_send[...] = (rest[3 * quarter :] + b_in[1].astype(f32)).astype(bf16)


def weight_two_body(info, kept, a_in, b_in, total, send):
    quarter = a_in.shape[0]
    total[:quarter] = kept[:quarter] + a_in[...].astype(f32)
    total[quarter:] = kept[quarter:] + b_in[...].astype(f32)
    send[...] = total[...].astype(bf16)


def weight_three_body(info, kept, arrived, total, send):
    total[...] = kept[...] + arrived[...].astype(f32)
    send[...] = total[...].astype(bf16)


def weight_last_body(scale, info, kept, arrived, grad):
    quarter = kept.shape[0] // 2
    second = info[ODD] == 1
    mine, theirs = kept[...] * scale, arrived[...].astype(f32) * scale
    low = jnp.where(second, theirs, mine)
    high = jnp.where(second, mine, theirs)
    for n, part in enumerate((low[:quarter], high[:quarter], low[quarter:], high[quarter:])):
        grad[n * quarter : (n + 1) * quarter] = part


def back_body(
    info, pair, before, middle, seg_col, seg, seg_partner, d_attn, values, feat_k, feat_q, mixed, own, other,
    d_query, dk_intra, dv_intra, out_partner,
):
    x = info[ME] // 2
    out_partner[...] = (dot_nn(mixed[1, x], own[...]) + dot_nn(mixed[1, 1 - x], other[...])).astype(bf16)
    for i, row in enumerate((seg, seg_partner)):
        mask = causal(seg_col, row, i)
        use_pair = info[NEAR] == 1
        last = 2 * HEAD_DIM
        ids = jnp.where(use_pair, pair[i, last : last + 1].astype(f32), middle[i, last : last + 1].astype(f32))
        take = seg_col[i] == ids
        for g in range(2):
            da, q, k = d_attn[i, g], feat_q[i, g], feat_k[i, g]
            s = jnp.where(mask, dot_nt(q, k), 0.0).astype(bf16)
            ds = jnp.where(mask, dot_nt(da, values[i, g]), 0.0).astype(bf16)
            dq = dot_nn(ds, k) + jnp.where(take, dot_nt(da, before[i, head(g)]), 0.0)
            d_query[i, :, head(g)] = (dq * jnp.minimum(q.astype(f32), 1.0)).astype(bf16)
            dk_intra[i, g] = dot_tn(ds, q)
            dv_intra[i, g] = dot_tn(s, da)


def output_body(info, tokens, partner, mixed, own, other, output):
    x = info[ME] // 2
    total = dot_nn(mixed[0, x], own[...]) + dot_nn(mixed[0, 1 - x], other[...])
    output[...] = (tokens[...].astype(f32) + (total + partner[...].astype(f32))).astype(bf16)


def project_back_body(
    info, pair, middle, further, seg_col, feat_k, values, dk_intra, dv_intra, d_query,
    q0, q1, q2, q3, w0, w1, w2, w3, own, partner,
):
    for i in (1, 0):
        ids, total = received(info, BACK_NEAR, pair, middle, further, i)
        take = seg_col[i] == ids
        d_key, d_value = [], []
        for g in range(2):
            back = total[head(g)]
            k, v = feat_k[i, g], values[i, g]
            dk = dk_intra[i, g] + jnp.where(take, dot_nt(v, back), 0.0)
            dv = dv_intra[i, g] + jnp.where(take, dot_nn(k, back), 0.0)
            d_key.append((dk * jnp.minimum(k.astype(f32), 1.0)).astype(bf16))
            d_value.append(dv.astype(bf16))
        d_proj = jnp.concatenate(d_key + d_value, axis=1)
        for j, (q, w) in enumerate(((q0, w0), (q1, w1), (q2, w2), (q3, w3))):
            value = dot_nt(d_query[i], q[...]) + dot_nt(d_proj, w[...])
            if i == 1:
                partner[j ^ 1] = value.astype(bf16)
            else:
                own[j] = value


def final_body(info, own, partner, tokens, cot, inv_rms, gain, grad, work):
    inner = None
    for j in range(4):
        at = columns(info[ME] ^ j, 256)
        norm_grad = (own[j] + partner[j].astype(f32)) * gain[:, at]
        work[j] = norm_grad
        part = jnp.sum(tokens[:, at].astype(f32) * norm_grad, axis=1, keepdims=True)
        inner = part if inner is None else inner + part
    inv = inv_rms[...]
    scale = inv**3 * (inner * (1.0 / D))
    for j in range(4):
        at = columns(info[ME] ^ j, 256)
        value = cot[:, at].astype(f32) + inv * work[j] - tokens[:, at].astype(f32) * scale
        grad[:, at] = value.astype(bf16)


def flip(array, axis, bit):
    n = lax.axis_size(axis)
    return lax.ppermute(array, axis, [(i, i ^ bit) for i in range(n)])


def shift(array, axis, step):
    n = lax.axis_size(axis)
    return lax.ppermute(array, axis, [(i, i + step) for i in range(n) if 0 <= i + step < n])


def carry(message, ends, step):
    n = lax.axis_size("seq")
    if n == 4:
        middle = lax.ppermute(message, "seq", [(1, 2), (2, 1)])
        return flip(message, "seq", 1), middle, flip(message, "seq", 2)
    position = lax.axis_index("seq")
    begin, end = (ends[0], ends[1]) if step > 0 else (ends[1], ends[0])
    total = message[:, : 2 * HEAD_DIM].astype(f32)
    reach = 1
    while reach < n:
        before = shift(total, "seq", step * reach)
        ids = shift(jnp.stack([begin, end]), "seq", step * reach)
        there = position - step * reach
        there = (there >= 0) & (there < n)
        goes_on = there & (begin == end) & (ids[1] == begin)
        total = total + jnp.where(goes_on[:, None, None], before, 0.0)
        begin = jnp.where(there, ids[0], begin)
        reach *= 2
    rows = jnp.concatenate([total.astype(bf16), message[:, 2 * HEAD_DIM :]], axis=1)
    near = shift(rows, "seq", step)
    return near, near, near


def reduce_weight(info, rest, a_send, b_send, scale):
    n = lax.axis_size("seq")
    half, width = a_send.shape
    quarter = half // 2
    kept, a_send, b_send = call(
        weight_one_body,
        [((half, width), f32), ((quarter, width), bf16), ((quarter, width), bf16)],
        info, rest, flip(a_send, "dp", 2), flip(b_send, "seq", 1),
    )
    outs = [((half, width), f32), ((half, width), bf16)]
    kept, send = call(weight_two_body, outs, info, kept, flip(a_send, "seq", 1), flip(b_send, "dp", 2))
    reach = 2
    while reach < n:
        kept, send = call(weight_three_body, outs, info, kept, flip(send, "seq", reach))
        reach *= 2
    (grad,) = call(
        functools.partial(weight_last_body, scale),
        [((2 * half, width), f32, FREE)],
        info, kept, flip(send, "seq", 1),
    )
    return grad


def shards(tokens, segment_ids, norm_gain, w_qkv, head_gain, w_out, cotangent):
    length = segment_ids.shape[1]
    width = HEADS * HEAD_DIM
    dp = lax.axis_index("dp").astype(jnp.int32)
    at = lax.axis_index("seq").astype(jnp.int32)
    n = lax.axis_size("seq")
    if n == 4:
        facts = [dp, at % 2, at % 2, at // 2, 1 - at % 2, 1 - at // 2]
    else:
        facts = [dp, at % 2, 0 * at, 0 * at, 0 * at, 0 * at]
    info = jnp.stack(facts)
    flat = tokens.reshape(length, D)
    cot = cotangent.reshape(length, D)
    gain = norm_gain.reshape(1, D)
    gain_h = head_gain.reshape(1, width)
    seg = segment_ids.astype(f32)
    wide = (2, 2, length, HEAD_DIM)
    shard_rows = w_qkv.shape[0]

    kv_mine, kv_other, q_mine, q_other = pl.pallas_call(
        split_body,
        out_shape=[jax.ShapeDtypeStruct((shard_rows, m * HEAD_DIM), bf16) for m in (4, 4, 2, 2)],
        in_specs=[SMEM, FAR],
        out_specs=[VMEM] * 4,
        scratch_shapes=[pltpu.SemaphoreType.DMA((12,))],
    )(info, w_qkv)
    kv = [kv_mine, flip(kv_other, "dp", 1), flip(kv_mine, "dp", 2), flip(kv_other, "dp", 3)]
    partner = flip(flat, "dp", 1)
    seg_partner = flip(seg, "dp", 1)

    normed, inv_rms, seg_col, raw_near = call(
        prep_body,
        [
            ((4, 2 * length, D // 4), bf16),
            ((length, 1), f32),
            ((2, length, HEAD_DIM), f32),
            ((2 * length, 4 * HEAD_DIM), f32),
        ],
        info, Far(flat), Far(partner), seg, seg_partner, gain, kv[0], kv[1], us=20.0,
    )
    kv[2], q_mine, q_other, out_own, cot = lax.optimization_barrier((kv[2], q_mine, q_other, w_out, cot))
    cot_partner = flip(cot, "dp", 1)
    wq = [q_mine, flip(q_other, "dp", 1), flip(q_mine, "dp", 2), flip(q_other, "dp", 3)]
    out_other = flip(out_own, "dp", 2)

    message = ((2, 2 * HEAD_DIM + ID_ROWS, HEAD_DIM), bf16)
    feat_k, values, state = call(
        kv_body, [(wide, bf16), (wide, bf16), message], info, raw_near, normed, kv[2], kv[3], seg_col
    )
    ends = jnp.stack([seg_col[:, 0, 0], seg_col[:, -1, 0]])
    near = carry(state, ends, 1)
    feat_q, intra, upstream = call(
        query_body,
        [(wide, bf16), (wide, f32), (wide, f32)],
        info, Far(normed), *map(Far, wq), feat_k, values, seg_col, seg, seg_partner,
        Far(cot), Far(cot_partner), Far(w_out), Far(out_other), gain_h,
    )
    rows = HEAD_DIM // 2
    mixed, d_attn, back, before, rest, a_send, b_send = call(
        attn_body,
        [
            (wide, bf16),
            (wide, bf16),
            message,
            ((2, 2 * HEAD_DIM, HEAD_DIM), bf16),
            ((2 * rows, D), f32),
            ((rows, D), bf16),
            ((2, rows // 2, D), bf16),
        ],
        info, *near, seg_col, feat_q, intra, upstream, gain_h, Far(cot), Far(cot_partner),
    )
    back_near = carry(back, ends, -1)
    scale = 1.0 / math.sqrt(length * lax.axis_size("dp") * n)
    grad_out_weight = reduce_weight(info, rest, a_send, b_send, scale)
    d_query, dk_intra, dv_intra, out_partner = call(
        back_body,
        [((2, length, 2 * HEAD_DIM), bf16), (wide, f32), (wide, f32), ((length, D), bf16)],
        info, near[0], before, near[1], seg_col, seg, seg_partner, d_attn, values, feat_k, feat_q, mixed,
        Far(w_out), Far(out_other),
    )
    (output,) = call(
        output_body,
        [((length, D), bf16, FREE)],
        info, Far(flat), Far(flip(out_partner, "dp", 1)), mixed, Far(w_out), Far(out_other),
    )
    own, theirs = call(
        project_back_body,
        [((4, length, D // 4), f32), ((4, length, D // 4), bf16)],
        info, *back_near, seg_col, feat_k, values, dk_intra, dv_intra, d_query, *map(Far, wq), *map(Far, kv),
    )
    (grad,) = call(
        final_body,
        [((length, D), bf16, FREE)],
        info, own, flip(theirs, "dp", 1), Far(flat), Far(cot), inv_rms, gain,
        scratch=[((4, length, D // 4), f32)],
    )
    return (output.reshape(tokens.shape), grad.reshape(tokens.shape), grad_out_weight)


def solution(mesh):
    in_specs = (
        P(("groups", "dp"), "seq", None),
        P(("groups", "dp"), "seq"),
        P(),
        P("dp", None),
        P(),
        P("dp", None),
        P(("groups", "dp"), "seq", None),
    )
    out_specs = (
        P(("groups", "dp"), "seq", None),
        P(("groups", "dp"), "seq", None),
        P(("groups", "dp"), None),
    )
    return jax.shard_map(shards, mesh=mesh, in_specs=in_specs, out_specs=out_specs, check_vma=False)
```

time: 116 us -> 83.1 us (0.72); the launches traced: 114 us -> 82.7 us
  local copies, waits for them, and re-layouts: 36 us -> 4.11 us
  Pallas kernels: 21.4 us -> 29.7 us
  other arithmetic: 6.99 us -> 0.68 us
  starting transfers between devices: 27.9 us -> 26 us
    unnamed x115 -> x22, local copies, waits for them, and re-layouts: 33.6 us -> 3.45 us
    ppermute x4 -> x2, starting transfers between devices: 12.3 us -> 1.5 us  [carry(): middle = lax.ppermute(message, 'seq', [(1, 2), (2, 1)])]
    ppermute x18 -> x22, starting transfers between devices: 15.6 us -> 24.5 us  [flip(): return lax.ppermute(array, axis, [(i, i ^ bit) for i in range(n)])]
    pallas_call x10 -> x13, Pallas kernels: 21.4 us -> 29.7 us  [the longest x12 26.9 us: call(): pl.pallas_call(kernel, out_shape=[jax.ShapeDtypeStruct(out[0], out[1]) fo...]
    ppermute x18 -> x22, waiting for transfers between devices: 16.2 us -> 21.2 us  [flip(): return lax.ppermute(array, axis, [(i, i ^ bit) for i in range(n)])]
    ppermute x4 -> x2, waiting for transfers between devices: 4.84 us -> 0.01 us  [carry(): middle = lax.ppermute(message, 'seq', [(1, 2), (2, 1)])]
    reshape x1 -> x0, other arithmetic: 2.34 us -> none  [shards(): output.reshape(tokens.shape)]
    add x4 -> x0, other arithmetic: 2.03 us -> none  [the longest x1 1.01 us: reduce_weight(): a = a_keep + a_in.astype(f32)]
  transfers between devices with their start and end apart: 22 -> 24, of which waited for: 9 -> 7; matrix products, arithmetic and copies ran while one was open for 11% -> 2% of each run, Pallas kernels for 12% -> 30%
where the time goes in v3:
time: 83.1 us; the launch traced here: 82.7 us
  Pallas kernels  29.7 us (36%)
  starting transfers between devices  26 us (31%)
  waiting for transfers between devices  21.2 us (26%)
  local copies, waits for them, and re-layouts  4.11 us (5%)
  between operations  1.03 us (1%)
    pallas_call x12, Pallas kernels, call(): pl.pallas_call(kernel, out_shape=[jax.ShapeDtypeStruct(out[0], out[1]) fo...  26.9 us
    ppermute x22, starting transfers between devices, flip(): return lax.ppermute(array, axis, [(i, i ^ bit) for i in range(n)])  24.5 us
    ppermute x22, waiting for transfers between devices, flip(): return lax.ppermute(array, axis, [(i, i ^ bit) for i in range(n)])  21.2 us
    unnamed x22, local copies, waits for them, and re-layouts  3.45 us
    pallas_call x1, Pallas kernels, shards(): pl.pallas_call(split_body, out_shape=[jax.ShapeDtypeStruct((shard_rows, m...  2.82 us
  transfers between devices with their start and end apart: 24, of which 7 were waited for; matrix products, arithmetic and copies ran while one was open for 2% of the time, Pallas kernels for 30%

profile of v3, /device:TPU:0, one launch (start us, length us, event | category | flops | bytes accessed | tf_op | source)
XLA Modules:
  0.0 82.7 jit_solution(8261501836069296032)
XLA Ops:
  1.8 2.8 %shard_map.94 = (bf16[256,512]{1,0:T(8,128)(2,1)}, bf16[256,512]{1,0:T(8,128)(2,1)}, bf16[256,256]{1,0:T(8,128)(2,1)}, bf16[256,256]{1,0:T(8,128)(2,1)}) custom-call(s32[6]{0:T(128)} %stack.24.info.refs_0_, bf16[256,1536]{1,0:T(8,128)(2,1)} %w.1), custom_call_target="tpu_custom_call" | custom-call | tf_op jit(solution)/shard_map/pallas_call | solution.py:411
  4.6 2.6 %collective-permute-start.3 = (bf16[256,512]{1,0:T(8,128)(2,1)}, bf16[256,512]{1,0:T(8,128)(2,1)S(1)}, u32[]{:S(2)}, u32[]{:S(2)}) collective-permute-start(bf16[256,512]{1,0:T(8,128)(2,1)} %get-tuple-element.42.refs_6_.refs_14_), channel_id=1, source_target_pairs={{0,2},{1,3},{2,0},{3,1},{4,6},{5,7},{6,4},{7,5},{8,10},{9,11},{10,... | collective-permute-start | bytes 786440 | tf_op jit(solution)/shard_map/ppermute | solution.py:338
  8.6 6.0 %collective-permute-done.3.refs_3_.refs_16_ = bf16[256,512]{1,0:T(8,128)(2,1)S(1)} collective-permute-done((bf16[256,512]{1,0:T(8,128)(2,1)}, bf16[256,512]{1,0:T(8,128)(2,1)S(1)}, u32[]{:S(2)}, u32[]{:S(2)}) %collective-permute-start.3) | collective-permute-done | bytes 262176 | tf_op jit(solution)/shard_map/ppermute | solution.py:338
  14.6 2.1 %collective-permute-start.10 = (bf16[256,256]{1,0:T(8,128)(2,1)}, bf16[256,256]{1,0:T(8,128)(2,1)S(1)}, u32[]{:S(2)}, u32[]{:S(2)}) collective-permute-start(bf16[256,256]{1,0:T(8,128)(2,1)} %get-tuple-element.52), channel_id=1, source_target_pairs={{0,3},{1,2},{2,1},{3,0},{4,7},{5,6},{6,5},{7,4},{8,11},{9,10},{10,... | collective-permute-start | bytes 393224 | tf_op jit(solution)/shard_map/ppermute | solution.py:338
  20.6 1.7 %shard_map.95 = (bf16[4,768,256]{2,1,0:T(8,128)(2,1)S(1)}, f32[384,1]{1,0:T(8,128)S(1)}, f32[2,384,128]{2,1,0:T(8,128)S(1)}, f32[768,512]{1,0:T(8,128)S(1)}) custom-call(s32[6]{0:T(128)S(1)} %copy-done, bf16[384,1024]{1,0:T(8,128)(2,1)S(1)} %bitcast.12, bf16[384,1024]{1,0:T(8,128)(2,1)S(1)} %collective-permute-done.refs_2_, ...), custom_call_target="tpu_custom_call" | custom-call | flops 20000000000 | bytes 60000000 | tf_op jit(solution)/shard_map/pallas_call | solution.py:93
  22.3 1.7 %collective-permute-start.9 = (bf16[256,256]{1,0:T(8,128)(2,1)S(1)}, bf16[256,256]{1,0:T(8,128)(2,1)S(1)}, u32[]{:S(2)}, u32[]{:S(2)}) collective-permute-start(bf16[256,256]{1,0:T(8,128)(2,1)S(1)} %copy-done.7), channel_id=1, source_target_pairs={{0,2},{1,3},{2,0},{3,1},{4,6},{5,7},{6,4},{7,5},{8,10},{9,11},{10,... | collective-permute-start | bytes 393224 | tf_op jit(solution)/shard_map/ppermute | solution.py:338
  24.0 1.5 %shard_map.96 = (bf16[2,2,384,128]{3,2,1,0:T(8,128)(2,1)S(1)}, bf16[2,2,384,128]{3,2,1,0:T(8,128)(2,1)S(1)}, bf16[2,272,128]{2,1,0:T(8,128)(2,1)S(1)}) custom-call(s32[6]{0:T(128)S(1)} %copy-done, f32[768,512]{1,0:T(8,128)S(1)} %get-tuple-element.44.refs_1_, bf16[4,768,256]{2,1,0:T(8,128)(2,1)S(1)} %get-tuple-element.45.refs_2_.refs_1_, ...), custom_call_target="tpu_custom_call" | custom-call | flops 2000000000 | bytes 6000000 | tf_op jit(solution)/shard_map/pallas_call | solution.py:93
  25.5 1.6 %collective-permute-start.5 = (bf16[2,272,128]{2,1,0:T(8,128)(2,1)S(1)}, bf16[2,272,128]{2,1,0:T(8,128)(2,1)S(1)}, u32[]{:S(2)}, u32[]{:S(2)}) collective-permute-start(bf16[2,272,128]{2,1,0:T(8,128)(2,1)S(1)} %get-tuple-element.50), channel_id=1, source_target_pairs={{0,4},{4,0},{8,12},{12,8},{1,5},{5,1},{9,13},{13,9},{2,6},{6,2},{1... | collective-permute-start | bytes 417800 | tf_op jit(solution)/shard_map/ppermute | solution.py:338
  27.2 4.0 %collective-permute-done.9.refs_4_.refs_12_ = bf16[256,256]{1,0:T(8,128)(2,1)S(1)} collective-permute-done((bf16[256,256]{1,0:T(8,128)(2,1)S(1)}, bf16[256,256]{1,0:T(8,128)(2,1)S(1)}, u32[]{:S(2)}, u32[]{:S(2)}) %collective-permute-start.9) | collective-permute-done | bytes 131104 | tf_op jit(solution)/shard_map/ppermute | solution.py:338
  31.9 4.6 %collective-permute-start.7 = (bf16[2,272,128]{2,1,0:T(8,128)(2,1)S(1)}, bf16[2,272,128]{2,1,0:T(8,128)(2,1)S(1)}, u32[]{:S(2)}, u32[]{:S(2)}) collective-permute-start(bf16[2,272,128]{2,1,0:T(8,128)(2,1)S(1)} %get-tuple-element.50), channel_id=1, source_target_pairs={{0,8},{4,12},{8,0},{12,4},{1,9},{5,13},{9,1},{13,5},{2,10},{6,14},... | collective-permute-start | bytes 417800 | tf_op jit(solution)/shard_map/ppermute | solution.py:338
  36.5 5.5 %shard_map.97 = (bf16[2,2,384,128]{3,2,1,0:T(8,128)(2,1)S(1)}, f32[2,2,384,128]{3,2,1,0:T(8,128)S(1)}, f32[2,2,384,128]{3,2,1,0:T(8,128)S(1)}) custom-call(s32[6]{0:T(128)S(1)} %copy-done, bf16[4,768,256]{2,1,0:T(8,128)(2,1)S(1)} %get-tuple-element.45.refs_2_.refs_1_, bf16[256,256]{1,0:T(8,128)(2,1)S(1)} %copy-done.7, ...), custom_call_target="tpu_custom_call" | custom-call | flops 2000000000 | bytes 6000000 | tf_op jit(solution)/shard_map/pallas_call | solution.py:93
  42.1 3.5 %collective-permute-done.7.refs_3_ = bf16[2,272,128]{2,1,0:T(8,128)(2,1)S(1)} collective-permute-done((bf16[2,272,128]{2,1,0:T(8,128)(2,1)S(1)}, bf16[2,272,128]{2,1,0:T(8,128)(2,1)S(1)}, u32[]{:S(2)}, u32[]{:S(2)}) %collective-permute-start.7) | collective-permute-done | bytes 139296 | tf_op jit(solution)/shard_map/ppermute | solution.py:338
  45.6 2.4 %shard_map.98 = (bf16[2,2,384,128]{3,2,1,0:T(8,128)(2,1)S(1)}, bf16[2,2,384,128]{3,2,1,0:T(8,128)(2,1)S(1)}, bf16[2,272,128]{2,1,0:T(8,128)(2,1)S(1)}, bf16[2,25...) custom-call(s32[6]{0:T(128)S(1)} %copy-done, ...), custom_call_target="tpu_custom_call" | custom-call | flops 2000000000 | bytes 6000000 | tf_op jit(solution)/shard_map/pallas_call | solution.py:93
  48.1 1.6 %collective-permute-start.18 = (bf16[64,1024]{1,0:T(8,128)(2,1)S(1)}, bf16[64,1024]{1,0:T(8,128)(2,1)S(1)}, u32[]{:S(2)}, u32[]{:S(2)}) collective-permute-start(bf16[64,1024]{1,0:T(8,128)(2,1)S(1)} %get-tuple-element.72), channel_id=1, source_target_pairs={{0,2},{1,3},{2,0},{3,1},{4,6},{5,7},{6,4},{7,5},{8,10},{9,11},{10,... | collective-permute-start | bytes 393224 | tf_op jit(solution)/shard_map/ppermute | solution.py:338
  49.6 2.0 %collective-permute-start.14 = (bf16[2,272,128]{2,1,0:T(8,128)(2,1)S(1)}, bf16[2,272,128]{2,1,0:T(8,128)(2,1)S(1)}, u32[]{:S(2)}, u32[]{:S(2)}) collective-permute-start(bf16[2,272,128]{2,1,0:T(8,128)(2,1)S(1)} %get-tuple-element.64), channel_id=1, source_target_pairs={{0,4},{4,0},{8,12},{12,8},{1,5},{5,1},{9,13},{13,9},{2,6},{6,2},{1... | collective-permute-start | bytes 417800 | tf_op jit(solution)/shard_map/ppermute | solution.py:338
  52.5 2.8 %collective-permute-start.16 = (bf16[2,272,128]{2,1,0:T(8,128)(2,1)S(1)}, bf16[2,272,128]{2,1,0:T(8,128)(2,1)S(1)}, u32[]{:S(2)}, u32[]{:S(2)}) collective-permute-start(bf16[2,272,128]{2,1,0:T(8,128)(2,1)S(1)} %get-tuple-element.64), channel_id=1, source_target_pairs={{0,8},{4,12},{8,0},{12,4},{1,9},{5,13},{9,1},{13,5},{2,10},{6,14},... | collective-permute-start | bytes 417800 | tf_op jit(solution)/shard_map/ppermute | solution.py:338
  56.8 3.1 %shard_map.99 = (bf16[2,384,256]{2,1,0:T(8,128)(2,1)S(1)}, f32[2,2,384,128]{3,2,1,0:T(8,128)S(1)}, f32[2,2,384,128]{3,2,1,0:T(8,128)S(1)}, bf16[384,1024]{1,0:T(8,128)(2,1)S(1)}) custom-call(s32[6]{0:T(128)S(1)} %copy-done, bf16[2,272,128]{2,1,0:T(8,128)(2,1)S(1)} %collective-permute-done.5.refs_1_, bf16[2,256,128]{2,1,0:T(8,128)(2,1)S(1)} %get-tuple-element.60.refs_2_, ...), custom_call_target="tpu_custom_call" | custom-call | flops 2000000000 | bytes 6000000 | tf_op jit(solution)/shard_map/pallas_call | solution.py:93
  61.1 2.8 %collective-permute-start.22 = (bf16[64,1024]{1,0:T(8,128)(2,1)S(1)}, bf16[64,1024]{1,0:T(8,128)(2,1)S(1)}, u32[]{:S(2)}, u32[]{:S(2)}) collective-permute-start(bf16[64,1024]{1,0:T(8,128)(2,1)S(1)} %get-tuple-element.78), channel_id=1, source_target_pairs={{0,8},{4,12},{8,0},{12,4},{1,9},{5,13},{9,1},{13,5},{2,10},{6,14},... | collective-permute-start | bytes 393224 | tf_op jit(solution)/shard_map/ppermute | solution.py:338
  64.0 4.4 %shard_map.101 = (f32[4,384,256]{2,1,0:T(8,128)S(1)}, bf16[4,384,256]{2,1,0:T(8,128)(2,1)S(1)}) custom-call(s32[6]{0:T(128)S(1)} %copy-done, bf16[2,272,128]{2,1,0:T(8,128)(2,1)S(1)} %collective-permute-done.14.refs_1_, bf16[2,272,128]{2,1,0:T(8,128)(2,1)S(1)} %collective-permute-done.15.refs_2_, bf16[2,272,128]{2,1,0:T(8,128)(2,1)S(1)} %collective-permute-done.16.refs_3_, ...), custom_call_target="tpu_custom_call" | custom-call | flops 2000000000 | bytes 6000000 | tf_op jit(solution)/shard_map/pallas_call | solution.py:93
  68.5 2.0 %collective-permute-done.22.refs_2_ = bf16[64,1024]{1,0:T(8,128)(2,1)S(1)} collective-permute-done((bf16[64,1024]{1,0:T(8,128)(2,1)S(1)}, bf16[64,1024]{1,0:T(8,128)(2,1)S(1)}, u32[]{:S(2)}, u32[]{:S(2)}) %collective-permute-start.22) | collective-permute-done | bytes 131104 | tf_op jit(solution)/shard_map/ppermute | solution.py:338
  71.2 5.0 %collective-permute-done.23.refs_2_ = bf16[64,1024]{1,0:T(8,128)(2,1)S(1)} collective-permute-done((bf16[64,1024]{1,0:T(8,128)(2,1)S(1)}, bf16[64,1024]{1,0:T(8,128)(2,1)S(1)}, u32[]{:S(2)}, u32[]{:S(2)}) %collective-permute-start.23) | collective-permute-done | bytes 131104 | tf_op jit(solution)/shard_map/ppermute | solution.py:338
  76.1 1.4 %shard_map.106 = f32[128,1024]{1,0:T(8,128)} custom-call(s32[6]{0:T(128)S(1)} %copy-done, f32[64,1024]{1,0:T(8,128)S(1)} %get-tuple-element.79.refs_1_, bf16[64,1024]{1,0:T(8,128)(2,1)S(1)} %collective-permute-done.23.refs_2_), custom_call_target="tpu_custom_call" | custom-call | flops 2000000000 | bytes 6000000 | tf_op jit(solution)/shard_map/pallas_call | solution.py:93
  77.6 2.5 %shard_map.100 = bf16[384,1024]{1,0:T(8,128)(2,1)} custom-call(s32[6]{0:T(128)S(1)} %copy-done, bf16[384,1024]{1,0:T(8,128)(2,1)S(1)} %bitcast.13, bf16[384,1024]{1,0:T(8,128)(2,1)S(1)} %collective-permute-done.13.refs_2_, bf16[2,2,384,128]{3,2,1,0:T(8,128)(2,1)S(1)} %get-tuple-element.62.refs_11_.refs_3_, bf16[128,1024]{1,0:T(8,128)(2,1)S(1)} %copy-done.4, ...), custom_call_target="tpu_custom_call" | custom-call | flops 2000000000 | bytes 6000000 | tf_op jit(solution)/shard_map/pallas_call | solution.py:93
  80.1 2.5 %shard_map.102 = bf16[384,1024]{1,0:T(8,128)(2,1)} custom-call(s32[6]{0:T(128)S(1)} %copy-done, f32[4,384,256]{2,1,0:T(8,128)S(1)} %get-tuple-element.68.refs_1_, bf16[4,384,256]{2,1,0:T(8,128)(2,1)S(1)} %collective-permute-done.17.refs_2_, bf16[384,1024]{1,0:T(8,128)(2,1)S(1)} %bitcast.14, bf16[384,1024]{1,0:T(8,128)(2,1)S(1)} %bitcast.18, ...), custom_call_target="tpu_custom_call" | custom-call | flops 2000000000 | bytes 6000000 | tf_op jit(solution)/shard_map/pallas_call | solution.py:93
  (61 shorter events, 11.4 us)
Async XLA Ops:
  0.6 16.0 %collective-permute-start = (bf16[384,1024]{1,0:T(8,128)(2,1)}, bf16[384,1024]{1,0:T(8,128)(2,1)S(1)}, u32[]{:S(2)}, u32[]{:S(2)}) collective-permute-start(bf16[384,1024]{1,0:T(8,128)(2,1)} %bitcast.11), channel_id=1, source_target_pairs={{0,1},{1,0},{2,3},{3,2},{4,5},{5,4},{6,7},{7,6},{8,9},{9,8},{10,11... | collective-permute-start | bytes 2359304 | tf_op jit(solution)/shard_map/ppermute | solution.py:338
  4.6 10.0 %collective-permute-start.3 = (bf16[256,512]{1,0:T(8,128)(2,1)}, bf16[256,512]{1,0:T(8,128)(2,1)S(1)}, u32[]{:S(2)}, u32[]{:S(2)}) collective-permute-start(bf16[256,512]{1,0:T(8,128)(2,1)} %get-tuple-element.42.refs_6_.refs_14_), channel_id=1, source_target_pairs={{0,2},{1,3},{2,0},{3,1},{4,6},{5,7},{6,4},{7,5},{8,10},{9,11},{10,... | collective-permute-start | bytes 786440 | tf_op jit(solution)/shard_map/ppermute | solution.py:338
  7.2 9.4 %collective-permute-start.2 = (bf16[256,512]{1,0:T(8,128)(2,1)}, bf16[256,512]{1,0:T(8,128)(2,1)S(1)}, u32[]{:S(2)}, u32[]{:S(2)}) collective-permute-start(bf16[256,512]{1,0:T(8,128)(2,1)} %get-tuple-element.43), channel_id=1, source_target_pairs={{0,1},{1,0},{2,3},{3,2},{4,5},{5,4},{6,7},{7,6},{8,9},{9,8},{10,11... | collective-permute-start | bytes 786440 | tf_op jit(solution)/shard_map/ppermute | solution.py:338
  8.1 6.5 %collective-permute-start.1 = (f32[1,384]{1,0:T(1,128)S(1)}, f32[1,384]{1,0:T(1,128)S(1)}, u32[]{:S(2)}, u32[]{:S(2)}) collective-permute-start(f32[1,384]{1,0:T(1,128)S(1)} %convert_element_type.3.refs_3_.refs_9_.refs_5_), channel_id=1, source_target_pairs={{0,1},{1,0},{2,3},{3,2},{4,5},{5,4},{6,7},{7,6},{8,9},{9,8},{10,11... | collective-permute-start | bytes 4616 | tf_op jit(solution)/shard_map/ppermute | solution.py:338
  8.4 13.9 %collective-permute-start.4 = (bf16[256,512]{1,0:T(8,128)(2,1)}, bf16[256,512]{1,0:T(8,128)(2,1)S(1)}, u32[]{:S(2)}, u32[]{:S(2)}) collective-permute-start(bf16[256,512]{1,0:T(8,128)(2,1)} %get-tuple-element.43), channel_id=1, source_target_pairs={{0,3},{1,2},{2,1},{3,0},{4,7},{5,6},{6,5},{7,4},{8,11},{9,10},{10,... | collective-permute-start | bytes 786440 | tf_op jit(solution)/shard_map/ppermute | solution.py:338
  14.6 10.9 %collective-permute-start.8 = (bf16[256,256]{1,0:T(8,128)(2,1)}, bf16[256,256]{1,0:T(8,128)(2,1)S(1)}, u32[]{:S(2)}, u32[]{:S(2)}) collective-permute-start(bf16[256,256]{1,0:T(8,128)(2,1)} %get-tuple-element.52), channel_id=1, source_target_pairs={{0,1},{1,0},{2,3},{3,2},{4,5},{5,4},{6,7},{7,6},{8,9},{9,8},{10,11... | collective-permute-start | bytes 393224 | tf_op jit(solution)/shard_map/ppermute | solution.py:338
  14.6 17.3 %collective-permute-start.10 = (bf16[256,256]{1,0:T(8,128)(2,1)}, bf16[256,256]{1,0:T(8,128)(2,1)S(1)}, u32[]{:S(2)}, u32[]{:S(2)}) collective-permute-start(bf16[256,256]{1,0:T(8,128)(2,1)} %get-tuple-element.52), channel_id=1, source_target_pairs={{0,3},{1,2},{2,1},{3,0},{4,7},{5,6},{6,5},{7,4},{8,11},{9,10},{10,... | collective-permute-start | bytes 393224 | tf_op jit(solution)/shard_map/ppermute | solution.py:338
  16.7 19.8 %collective-permute-start.11 = (bf16[384,1024]{1,0:T(8,128)(2,1)}, bf16[384,1024]{1,0:T(8,128)(2,1)S(1)}, u32[]{:S(2)}, u32[]{:S(2)}) collective-permute-start(bf16[384,1024]{1,0:T(8,128)(2,1)} %bitcast.15), channel_id=1, source_target_pairs={{0,1},{1,0},{2,3},{3,2},{4,5},{5,4},{6,7},{7,6},{8,9},{9,8},{10,11... | collective-permute-start | bytes 2359304 | tf_op jit(solution)/shard_map/ppermute | solution.py:338
  16.7 19.8 %collective-permute-start.12 = (bf16[128,1024]{1,0:T(8,128)(2,1)}, bf16[128,1024]{1,0:T(8,128)(2,1)S(1)}, u32[]{:S(2)}, u32[]{:S(2)}) collective-permute-start(bf16[128,1024]{1,0:T(8,128)(2,1)} %refs_4_.1), channel_id=1, source_target_pairs={{0,2},{1,3},{2,0},{3,1},{4,6},{5,7},{6,4},{7,5},{8,10},{9,11},{10,... | collective-permute-start | bytes 786440 | tf_op jit(solution)/shard_map/ppermute | solution.py:338
  22.3 8.9 %collective-permute-start.9 = (bf16[256,256]{1,0:T(8,128)(2,1)S(1)}, bf16[256,256]{1,0:T(8,128)(2,1)S(1)}, u32[]{:S(2)}, u32[]{:S(2)}) collective-permute-start(bf16[256,256]{1,0:T(8,128)(2,1)S(1)} %copy-done.7), channel_id=1, source_target_pairs={{0,2},{1,3},{2,0},{3,1},{4,6},{5,7},{6,4},{7,5},{8,10},{9,11},{10,... | collective-permute-start | bytes 393224 | tf_op jit(solution)/shard_map/ppermute | solution.py:338
  25.5 16.5 %collective-permute-start.5 = (bf16[2,272,128]{2,1,0:T(8,128)(2,1)S(1)}, bf16[2,272,128]{2,1,0:T(8,128)(2,1)S(1)}, u32[]{:S(2)}, u32[]{:S(2)}) collective-permute-start(bf16[2,272,128]{2,1,0:T(8,128)(2,1)S(1)} %get-tuple-element.50), channel_id=1, source_target_pairs={{0,4},{4,0},{8,12},{12,8},{1,5},{5,1},{9,13},{13,9},{2,6},{6,2},{1... | collective-permute-start | bytes 417800 | tf_op jit(solution)/shard_map/ppermute | solution.py:338
  31.2 10.9 %collective-permute-start.6 = (bf16[2,272,128]{2,1,0:T(8,128)(2,1)S(1)}, bf16[2,272,128]{2,1,0:T(8,128)(2,1)S(1)}, u32[]{:S(2)}, u32[]{:S(2)}) collective-permute-start(bf16[2,272,128]{2,1,0:T(8,128)(2,1)S(1)} %get-tuple-element.50), channel_id=1, source_target_pairs={{4,8},{8,4},{5,9},{9,5},{6,10},{10,6},{7,11},{11,7},{20,24},{24,20... | collective-permute-start | bytes 417800 | tf_op jit(solution)/shard_map/ppermute | solution.py:349
  31.9 13.7 %collective-permute-start.7 = (bf16[2,272,128]{2,1,0:T(8,128)(2,1)S(1)}, bf16[2,272,128]{2,1,0:T(8,128)(2,1)S(1)}, u32[]{:S(2)}, u32[]{:S(2)}) collective-permute-start(bf16[2,272,128]{2,1,0:T(8,128)(2,1)S(1)} %get-tuple-element.50), channel_id=1, source_target_pairs={{0,8},{4,12},{8,0},{12,4},{1,9},{5,13},{9,1},{13,5},{2,10},{6,14},... | collective-permute-start | bytes 417800 | tf_op jit(solution)/shard_map/ppermute | solution.py:338
  48.1 7.2 %collective-permute-start.18 = (bf16[64,1024]{1,0:T(8,128)(2,1)S(1)}, bf16[64,1024]{1,0:T(8,128)(2,1)S(1)}, u32[]{:S(2)}, u32[]{:S(2)}) collective-permute-start(bf16[64,1024]{1,0:T(8,128)(2,1)S(1)} %get-tuple-element.72), channel_id=1, source_target_pairs={{0,2},{1,3},{2,0},{3,1},{4,6},{5,7},{6,4},{7,5},{8,10},{9,11},{10,... | collective-permute-start | bytes 393224 | tf_op jit(solution)/shard_map/ppermute | solution.py:338
  49.6 5.7 %collective-permute-start.19 = (bf16[2,32,1024]{2,1,0:T(8,128)(2,1)S(1)}, bf16[2,32,1024]{2,1,0:T(8,128)(2,1)S(1)}, u32[]{:S(2)}, u32[]{:S(2)}) collective-permute-start(bf16[2,32,1024]{2,1,0:T(8,128)(2,1)S(1)} %get-tuple-element.73), channel_id=1, source_target_pairs={{0,4},{4,0},{8,12},{12,8},{1,5},{5,1},{9,13},{13,9},{2,6},{6,2},{1... | collective-permute-start | bytes 393224 | tf_op jit(solution)/shard_map/ppermute | solution.py:338
  49.6 14.3 %collective-permute-start.14 = (bf16[2,272,128]{2,1,0:T(8,128)(2,1)S(1)}, bf16[2,272,128]{2,1,0:T(8,128)(2,1)S(1)}, u32[]{:S(2)}, u32[]{:S(2)}) collective-permute-start(bf16[2,272,128]{2,1,0:T(8,128)(2,1)S(1)} %get-tuple-element.64), channel_id=1, source_target_pairs={{0,4},{4,0},{8,12},{12,8},{1,5},{5,1},{9,13},{13,9},{2,6},{6,2},{1... | collective-permute-start | bytes 417800 | tf_op jit(solution)/shard_map/ppermute | solution.py:338
  51.7 12.3 %collective-permute-start.15 = (bf16[2,272,128]{2,1,0:T(8,128)(2,1)S(1)}, bf16[2,272,128]{2,1,0:T(8,128)(2,1)S(1)}, u32[]{:S(2)}, u32[]{:S(2)}) collective-permute-start(bf16[2,272,128]{2,1,0:T(8,128)(2,1)S(1)} %get-tuple-element.64), channel_id=1, source_target_pairs={{4,8},{8,4},{5,9},{9,5},{6,10},{10,6},{7,11},{11,7},{20,24},{24,20... | collective-permute-start | bytes 417800 | tf_op jit(solution)/shard_map/ppermute | solution.py:349
  52.5 11.4 %collective-permute-start.16 = (bf16[2,272,128]{2,1,0:T(8,128)(2,1)S(1)}, bf16[2,272,128]{2,1,0:T(8,128)(2,1)S(1)}, u32[]{:S(2)}, u32[]{:S(2)}) collective-permute-start(bf16[2,272,128]{2,1,0:T(8,128)(2,1)S(1)} %get-tuple-element.64), channel_id=1, source_target_pairs={{0,8},{4,12},{8,0},{12,4},{1,9},{5,13},{9,1},{13,5},{2,10},{6,14},... | collective-permute-start | bytes 417800 | tf_op jit(solution)/shard_map/ppermute | solution.py:338
  55.9 4.3 %collective-permute-start.20 = (bf16[32,1024]{1,0:T(8,128)(2,1)S(1)}, bf16[32,1024]{1,0:T(8,128)(2,1)S(1)}, u32[]{:S(2)}, u32[]{:S(2)}) collective-permute-start(bf16[32,1024]{1,0:T(8,128)(2,1)S(1)} %get-tuple-element.75), channel_id=1, source_target_pairs={{0,4},{4,0},{8,12},{12,8},{1,5},{5,1},{9,13},{13,9},{2,6},{6,2},{1... | collective-permute-start | bytes 196616 | tf_op jit(solution)/shard_map/ppermute | solution.py:338
  56.3 4.3 %collective-permute-start.21 = (bf16[32,1024]{1,0:T(8,128)(2,1)S(1)}, bf16[32,1024]{1,0:T(8,128)(2,1)S(1)}, u32[]{:S(2)}, u32[]{:S(2)}) collective-permute-start(bf16[32,1024]{1,0:T(8,128)(2,1)S(1)} %get-tuple-element.76), channel_id=1, source_target_pairs={{0,2},{1,3},{2,0},{3,1},{4,6},{5,7},{6,4},{7,5},{8,10},{9,11},{10,... | collective-permute-start | bytes 196616 | tf_op jit(solution)/shard_map/ppermute | solution.py:338
  60.2 17.3 %collective-permute-start.13 = (bf16[384,1024]{1,0:T(8,128)(2,1)S(1)}, bf16[384,1024]{1,0:T(8,128)(2,1)S(1)}, u32[]{:S(2)}, u32[]{:S(2)}) collective-permute-start(bf16[384,1024]{1,0:T(8,128)(2,1)S(1)} %get-tuple-element.63), channel_id=1, source_target_pairs={{0,1},{1,0},{2,3},{3,2},{4,5},{5,4},{6,7},{7,6},{8,9},{9,8},{10,11... | collective-permute-start | bytes 2359304 | tf_op jit(solution)/shard_map/ppermute | solution.py:338
  61.1 9.4 %collective-permute-start.22 = (bf16[64,1024]{1,0:T(8,128)(2,1)S(1)}, bf16[64,1024]{1,0:T(8,128)(2,1)S(1)}, u32[]{:S(2)}, u32[]{:S(2)}) collective-permute-start(bf16[64,1024]{1,0:T(8,128)(2,1)S(1)} %get-tuple-element.78), channel_id=1, source_target_pairs={{0,8},{4,12},{8,0},{12,4},{1,9},{5,13},{9,1},{13,5},{2,10},{6,14},... | collective-permute-start | bytes 393224 | tf_op jit(solution)/shard_map/ppermute | solution.py:338
  68.4 11.6 %collective-permute-start.17 = (bf16[4,384,256]{2,1,0:T(8,128)(2,1)S(1)}, bf16[4,384,256]{2,1,0:T(8,128)(2,1)S(1)}, u32[]{:S(2)}, u32[]{:S(2)}) collective-permute-start(bf16[4,384,256]{2,1,0:T(8,128)(2,1)S(1)} %get-tuple-element.69), channel_id=1, source_target_pairs={{0,1},{1,0},{2,3},{3,2},{4,5},{5,4},{6,7},{7,6},{8,9},{9,8},{10,11... | collective-permute-start | bytes 2359304 | tf_op jit(solution)/shard_map/ppermute | solution.py:338
  71.1 5.0 %collective-permute-start.23 = (bf16[64,1024]{1,0:T(8,128)(2,1)S(1)}, bf16[64,1024]{1,0:T(8,128)(2,1)S(1)}, u32[]{:S(2)}, u32[]{:S(2)}) collective-permute-start(bf16[64,1024]{1,0:T(8,128)(2,1)S(1)} %get-tuple-element.80), channel_id=1, source_target_pairs={{0,4},{4,0},{8,12},{12,8},{1,5},{5,1},{9,13},{13,9},{2,6},{6,2},{1... | collective-permute-start | bytes 393224 | tf_op jit(solution)/shard_map/ppermute | solution.py:338
  (11 other events, 50.0 us)

commit v4 on v3

v4 whole, which is shorter than its diff:
```python
import functools
import math

import jax
import jax.numpy as jnp
from jax import lax
from jax.experimental import pallas as pl
from jax.experimental.pallas import tpu as pltpu
from jax.sharding import PartitionSpec as P

D = 1024
HEADS = 4
HEAD_DIM = 128
ID_ROWS = 16

epsilon = 1e-06
W1, W2, W3 = 8.0, 8.0, 8.0

f32 = jnp.float32
bf16 = jnp.bfloat16


def dot_nn(a, b):
    return lax.dot_general(a, b, (((1,), (0,)), ((), ())), preferred_element_type=f32)


def dot_nt(a, b):
    return lax.dot_general(a, b, (((1,), (1,)), ((), ())), preferred_element_type=f32)


def dot_tn(a, b):
    return lax.dot_general(a, b, (((0,), (0,)), ((), ())), preferred_element_type=f32)


def feature_map(u):
    return jnp.where(u > 0, u + 1.0, jnp.exp(jnp.minimum(u, 0.0)))


def head(h):
    return slice(h * HEAD_DIM, (h + 1) * HEAD_DIM)


VMEM = pl.BlockSpec(memory_space=pltpu.VMEM)
ANY = pl.BlockSpec(memory_space=pl.ANY)


def call(body, outs, *args, scratch=(), us=2.0):
    return pl.pallas_call(
        body,
        out_shape=[jax.ShapeDtypeStruct(shape, dtype) for shape, dtype in outs],
        in_specs=[VMEM] * len(args),
        out_specs=[VMEM] * len(outs),
        scratch_shapes=[pltpu.VMEM(shape, dtype) for shape, dtype in scratch],
        compiler_params=pltpu.CompilerParams(vmem_limit_bytes=16 * 1024 * 1024),
        cost_estimate=pl.CostEstimate(flops=int(us * 1e9), transcendentals=0, bytes_accessed=int(us * 3e6)),
    )(*args)


def columns(index, width):
    return pl.ds(pl.multiple_of(index * width, width), width)


def causal(seg_col, seg_row, i):
    length = seg_row.shape[2]
    order = lax.broadcasted_iota(jnp.int32, (length, length), 0) >= lax.broadcasted_iota(
        jnp.int32, (length, length), 1
    )
    down = jnp.concatenate([seg_col[i]] * (length // HEAD_DIM), axis=1)
    return (down == seg_row[i]) & order


def split_body(w, kv_mine, kv_other, sem):
    c = lax.axis_index("dp") % 2
    copies = []
    for target, which in ((kv_mine, c), (kv_other, 1 - c)):
        for n in range(4):
            at = columns(4 + 4 * (n // 2) + 2 * (n % 2) + which, HEAD_DIM)
            copies.append(pltpu.make_async_copy(w.at[:, at], target.at[:, head(n)], sem.at[len(copies)]))
    for copy in copies:
        copy.start()
    for copy in copies:
        copy.wait()


def pack_body(w, w_out, seg, kv_other, pair, far, q_other, sem):
    c = lax.axis_index("dp") % 2
    rows, half = w_out.shape[0], w_out.shape[1] // 2
    full = w.shape[0]
    copies = [
        (w_out.at[:, :half], far.at[:rows, 2 * HEAD_DIM :]),
        (w_out.at[:, half:], far.at[rows:, 2 * HEAD_DIM :]),
    ]
    for g in range(2):
        mine, other = columns(2 * g + c, HEAD_DIM), columns(2 * g + 1 - c, HEAD_DIM)
        copies.append((w.at[:, mine], far.at[:, head(g)]))
        copies.append((w.at[:, other], q_other.at[:, head(g)]))
        copies.append((w.at[:, other], pair.at[:full, head(4 + g)]))
    copies = [pltpu.make_async_copy(source, target, sem.at[n]) for n, (source, target) in enumerate(copies)]
    for copy in copies:
        copy.start()
    pair[:full, KV_COLUMNS] = kv_other[...]
    pair[full:, : seg.shape[1]] = jnp.broadcast_to(seg[...].astype(f32), (ID_ROWS, seg.shape[1])).astype(bf16)
    for copy in copies:
        copy.wait()


def split(w):
    out = jax.ShapeDtypeStruct((w.shape[0], 4 * HEAD_DIM), bf16)
    return pl.pallas_call(
        split_body,
        out_shape=[out, out],
        in_specs=[ANY],
        out_specs=[VMEM, VMEM],
        scratch_shapes=[pltpu.SemaphoreType.DMA((8,))],
        cost_estimate=pl.CostEstimate(flops=10**9, transcendentals=0, bytes_accessed=10**6),
    )(w)


def pack(w, w_out, seg, kv_other):
    rows = w.shape[0]
    return pl.pallas_call(
        pack_body,
        out_shape=[
            jax.ShapeDtypeStruct((rows + ID_ROWS, 6 * HEAD_DIM), bf16),
            jax.ShapeDtypeStruct((rows, 6 * HEAD_DIM), bf16),
            jax.ShapeDtypeStruct((rows, 2 * HEAD_DIM), bf16),
        ],
        in_specs=[ANY, ANY, VMEM, VMEM],
        out_specs=[VMEM] * 3,
        scratch_shapes=[pltpu.SemaphoreType.DMA((8,))],
        cost_estimate=pl.CostEstimate(flops=10**9, transcendentals=0, bytes_accessed=10**6),
    )(w, w_out, seg, kv_other)


KV_COLUMNS = slice(0, 4 * HEAD_DIM)
PAIR_Q_COLUMNS = slice(4 * HEAD_DIM, 6 * HEAD_DIM)
FAR_Q_COLUMNS = slice(0, 2 * HEAD_DIM)


def out_rows(far):
    rows = far.shape[0] // 2
    return jnp.concatenate([far[:rows, 2 * HEAD_DIM :], far[rows:, 2 * HEAD_DIM :]], axis=1)


def pair_ids(pair, length):
    return pair[pair.shape[0] - ID_ROWS : pair.shape[0] - ID_ROWS + 1, :length].astype(f32)


def sources(step):
    at, n = lax.axis_index("seq"), lax.axis_size("seq")
    if n != 4:
        return at < 0, at < 0
    return (at % 2 == 1, at >= 2) if step > 0 else (at % 2 == 0, at < 2)


def prep_body(tokens, partner, seg, gain, w0, pair, normed, inv_rms, seg_col, seg_row, raw):
    length = seg.shape[1]
    for i, (part, ids) in enumerate(((tokens, seg[...].astype(f32)), (partner, pair_ids(pair, length)))):
        x = part[...].astype(f32)
        inv = lax.rsqrt(jnp.mean(x * x, axis=1, keepdims=True) + epsilon)
        if i == 0:
            inv_rms[...] = inv
        for j in range(4):
            at = columns(lax.axis_index("dp") ^ j, 256)
            normed[j, i * length : (i + 1) * length] = (part[:, at].astype(f32) * inv * gain[:, at]).astype(bf16)
        seg_row[i] = ids
        seg_col[i] = jnp.broadcast_to(ids, (HEAD_DIM, length)).T
    rows = w0.shape[0]
    raw[...] = dot_nn(normed[0], w0[...]) + dot_nn(normed[1], pair[:rows, KV_COLUMNS])


def kv_body(near, normed, w2, w3, seg_col, feat_k, values, state):
    raw = near[...] + dot_nn(normed[2], w2[...]) + dot_nn(normed[3], w3[...])
    raw = raw.astype(bf16)
    length = seg_col.shape[1]
    for i in range(2):
        last = seg_col[i, length - 1 : length, :]
        tail = seg_col[i] == last
        rows = slice(i * length, (i + 1) * length)
        for g in range(2):
            k = feature_map(raw[rows, head(g)].astype(f32))
            v = raw[rows, head(2 + g)]
            feat_k[i, g] = k.astype(bf16)
            values[i, g] = v
            state[i, head(g), :] = dot_tn(jnp.where(tail, k, 0.0).astype(bf16), v).astype(bf16)
        state[i, 2 * HEAD_DIM :, :] = jnp.broadcast_to(last, (ID_ROWS, HEAD_DIM)).astype(bf16)


def query_body(
    normed, own, pair, other, w3, feat_k, values, seg_col, seg_row, cot, cot_partner, gain,
    feat_q, intra, upstream,
):
    rows, length = own.shape[0], seg_row.shape[2]
    raw = dot_nn(normed[0], own[:, FAR_Q_COLUMNS])
    raw += dot_nn(normed[1], pair[:rows, PAIR_Q_COLUMNS])
    raw += dot_nn(normed[2], other[:, FAR_Q_COLUMNS])
    raw += dot_nn(normed[3], w3[...])
    raw = raw.astype(bf16)
    for i in range(2):
        mask = causal(seg_col, seg_row, i)
        for g in range(2):
            q = feature_map(raw[i * length : (i + 1) * length, head(g)].astype(f32)).astype(bf16)
            feat_q[i, g] = q
            s = jnp.where(mask, dot_nt(q, feat_k[i, g]), 0.0).astype(bf16)
            intra[i, g] = dot_nn(s, values[i, g])
    for j, o in enumerate((out_rows(own), out_rows(other))):
        full = lax.axis_index("dp") ^ (2 * j)
        for i, part in enumerate((cot, cot_partner)):
            upstream[i, full // 2] = dot_nt(part[...], o) * gain[:, columns(full, HEAD_DIM)]


def received(step, pair, middle, further, i):
    use_pair, use_further = sources(step)
    near = jnp.where(use_pair, pair[i].astype(f32), middle[i].astype(f32))
    ids = near[2 * HEAD_DIM : 2 * HEAD_DIM + 1, :]
    far = further[i].astype(f32)
    same = (far[2 * HEAD_DIM : 2 * HEAD_DIM + 1, :] == ids) & use_further
    total = near[: 2 * HEAD_DIM] + jnp.where(same, far[: 2 * HEAD_DIM], 0.0)
    return ids, total.astype(bf16)


def attn_body(
    pair, middle, further, seg_col, feat_q, intra, upstream, gain, cot, cot_partner,
    mixed, d_attn, state, before, rest, a_send, b_send,
):
    for i in range(2):
        first = seg_col[i, 0:1, :]
        begin = seg_col[i] == first
        ids, total = received(1, pair, middle, further, i)
        before[i] = total
        take = seg_col[i] == ids
        for g in range(2):
            q = feat_q[i, g]
            attention = intra[i, g] + jnp.where(take, dot_nn(q, total[head(g)]), 0.0)
            ratio = lax.rsqrt(jnp.mean(attention * attention, axis=1, keepdims=True) + epsilon)
            mixed[i, g] = (attention * ratio * gain[:, columns(2 * g + lax.axis_index("dp") % 2, HEAD_DIM)]).astype(bf16)
            up = upstream[i, g]
            inner = jnp.mean(attention * up, axis=1, keepdims=True)
            da = (ratio * up - ratio**3 * attention * inner).astype(bf16)
            d_attn[i, g] = da
            state[i, head(g), :] = dot_tn(jnp.where(begin, q.astype(f32), 0.0).astype(bf16), da).astype(bf16)
        state[i, 2 * HEAD_DIM :, :] = jnp.broadcast_to(first, (ID_ROWS, HEAD_DIM)).astype(bf16)
    half = HEAD_DIM // 2
    quarter = half // 2
    second = lax.axis_index("seq") % 2 == 1
    for j in range(2):
        g = (lax.axis_index("dp") ^ (2 * j)) // 2
        part = dot_tn(mixed[0, g], cot[...]) + dot_tn(mixed[1, g], cot_partner[...])
        if j == 0:
            rest[:half] = part[:half]
        else:
            a_send[...] = part[:half].astype(bf16)
        low, high = part[half : half + quarter], part[half + quarter :]
        rest[half + j * quarter : half + (j + 1) * quarter] = jnp.where(second, high, low)
        b_send[j] = jnp.where(second, low, high).astype(bf16)


def weight_one_body(rest, a_in, b_in, kept, a_send, b_send):
    second = lax.axis_index("seq") % 2 == 1
    quarter = b_in.shape[1]
    low = rest[:quarter] + a_in[:quarter].astype(f32)
    high = rest[quarter : 2 * quarter] + a_in[quarter:].astype(f32)
    kept[:quarter] = jnp.where(second, high, low)
    a_send[...] = jnp.where(second, low, high).astype(bf16)
    kept[quarter:] = rest[2 * quarter : 3 * quarter] + b_in[0].astype(f32)
    b_send[...] = (rest[3 * quarter :] + b_in[1].astype(f32)).astype(bf16)


def weight_two_body(kept, a_in, b_in, total, send):
    quarter = a_in.shape[0]
    total[:quarter] = kept[:quarter] + a_in[...].astype(f32)
    total[quarter:] = kept[quarter:] + b_in[...].astype(f32)
    send[...] = total[...].astype(bf16)


def weight_three_body(kept, arrived, total, send):
    total[...] = kept[...] + arrived[...].astype(f32)
    send[...] = total[...].astype(bf16)


def weight_last_body(scale, kept, arrived, grad):
    quarter = kept.shape[0] // 2
    second = lax.axis_index("seq") % 2 == 1
    mine, theirs = kept[...] * scale, arrived[...].astype(f32) * scale
    low = jnp.where(second, theirs, mine)
    high = jnp.where(second, mine, theirs)
    for n, part in enumerate((low[:quarter], high[:quarter], low[quarter:], high[quarter:])):
        grad[n * quarter : (n + 1) * quarter] = part


def back_body(
    pair, before, middle, seg_col, seg_row, d_attn, values, feat_k, feat_q, mixed, own, other,
    d_query, dk_intra, dv_intra, out_partner,
):
    x = lax.axis_index("dp") // 2
    out_partner[...] = (dot_nn(mixed[1, x], out_rows(own)) + dot_nn(mixed[1, 1 - x], out_rows(other))).astype(bf16)
    for i in range(2):
        mask = causal(seg_col, seg_row, i)
        use_pair, _ = sources(1)
        last = 2 * HEAD_DIM
        ids = jnp.where(use_pair, pair[i, last : last + 1].astype(f32), middle[i, last : last + 1].astype(f32))
        take = seg_col[i] == ids
        for g in range(2):
            da, q, k = d_attn[i, g], feat_q[i, g], feat_k[i, g]
            s = jnp.where(mask, dot_nt(q, k), 0.0).astype(bf16)
            ds = jnp.where(mask, dot_nt(da, values[i, g]), 0.0).astype(bf16)
            dq = dot_nn(ds, k) + jnp.where(take, dot_nt(da, before[i, head(g)]), 0.0)
            d_query[i, :, head(g)] = (dq * jnp.minimum(q.astype(f32), 1.0)).astype(bf16)
            dk_intra[i, g] = dot_tn(ds, q)
            dv_intra[i, g] = dot_tn(s, da)


def output_body(tokens, partner, mixed, own, other, output):
    x = lax.axis_index("dp") // 2
    total = dot_nn(mixed[0, x], out_rows(own)) + dot_nn(mixed[0, 1 - x], out_rows(other))
    output[...] = (tokens[...].astype(f32) + (total + partner[...].astype(f32))).astype(bf16)


def project_back_body(
    pair, middle, further, seg_col, feat_k, values, dk_intra, dv_intra, d_query,
    own_far, pair_in, other_far, q3, w0, w2, w3, own, partner,
):
    rows = w0.shape[0]
    weights = (
        (own_far[:, FAR_Q_COLUMNS], w0[...]),
        (pair_in[:rows, PAIR_Q_COLUMNS], pair_in[:rows, KV_COLUMNS]),
        (other_far[:, FAR_Q_COLUMNS], w2[...]),
        (q3[...], w3[...]),
    )
    for i in (1, 0):
        ids, total = received(-1, pair, middle, further, i)
        take = seg_col[i] == ids
        d_key, d_value = [], []
        for g in range(2):
            back = total[head(g)]
            k, v = feat_k[i, g], values[i, g]
            dk = dk_intra[i, g] + jnp.where(take, dot_nt(v, back), 0.0)
            dv = dv_intra[i, g] + jnp.where(take, dot_nn(k, back), 0.0)
            d_key.append((dk * jnp.minimum(k.astype(f32), 1.0)).astype(bf16))
            d_value.append(dv.astype(bf16))
        d_proj = jnp.concatenate(d_key + d_value, axis=1)
        for j, (q, w) in enumerate(weights):
            value = dot_nt(d_query[i], q) + dot_nt(d_proj, w)
            if i == 1:
                partner[j ^ 1] = value.astype(bf16)
            else:
                own[j] = value


def final_body(own, partner, tokens, cot, inv_rms, gain, grad, work):
    inner = None
    for j in range(4):
        at = columns(lax.axis_index("dp") ^ j, 256)
        norm_grad = (own[j] + partner[j].astype(f32)) * gain[:, at]
        work[j] = norm_grad
        part = jnp.sum(tokens[:, at].astype(f32) * norm_grad, axis=1, keepdims=True)
        inner = part if inner is None else inner + part
    inv = inv_rms[...]
    scale = inv**3 * (inner * (1.0 / D))
    for j in range(4):
        at = columns(lax.axis_index("dp") ^ j, 256)
        value = cot[:, at].astype(f32) + inv * work[j] - tokens[:, at].astype(f32) * scale
        grad[:, at] = value.astype(bf16)


def flip(array, axis, bit):
    n = lax.axis_size(axis)
    return lax.ppermute(array, axis, [(i, i ^ bit) for i in range(n)])


def shift(array, axis, step):
    n = lax.axis_size(axis)
    return lax.ppermute(array, axis, [(i, i + step) for i in range(n) if 0 <= i + step < n])


def carry(message, ends, step):
    n = lax.axis_size("seq")
    if n == 4:
        middle = lax.ppermute(message, "seq", [(1, 2), (2, 1)])
        return flip(message, "seq", 1), middle, flip(message, "seq", 2)
    position = lax.axis_index("seq")
    begin, end = (ends[0], ends[1]) if step > 0 else (ends[1], ends[0])
    total = message[:, : 2 * HEAD_DIM].astype(f32)
    reach = 1
    while reach < n:
        before = shift(total, "seq", step * reach)
        ids = shift(jnp.stack([begin, end]), "seq", step * reach)
        there = position - step * reach
        there = (there >= 0) & (there < n)
        goes_on = there & (begin == end) & (ids[1] == begin)
        total = total + jnp.where(goes_on[:, None, None], before, 0.0)
        begin = jnp.where(there, ids[0], begin)
        reach *= 2
    rows = jnp.concatenate([total.astype(bf16), message[:, 2 * HEAD_DIM :]], axis=1)
    near = shift(rows, "seq", step)
    return near, near, near


def reduce_weight(rest, a_send, b_send):
    n = lax.axis_size("seq")
    half, width = a_send.shape
    quarter = half // 2
    kept, a_send, b_send = call(
        weight_one_body,
        [((half, width), f32), ((quarter, width), bf16), ((quarter, width), bf16)],
        rest, flip(a_send, "dp", 2), flip(b_send, "seq", 1), us=W1,
    )
    outs = [((half, width), f32), ((half, width), bf16)]
    kept, send = call(weight_two_body, outs, kept, flip(a_send, "seq", 1), flip(b_send, "dp", 2), us=W2)
    reach = 2
    while reach < n:
        kept, send = call(weight_three_body, outs, kept, flip(send, "seq", reach), us=W3)
        reach *= 2
    return kept, flip(send, "seq", 1)


def shards(tokens, segment_ids, norm_gain, w_qkv, head_gain, w_out, cotangent):
    length = segment_ids.shape[1]
    width = HEADS * HEAD_DIM
    n = lax.axis_size("seq")
    flat = tokens.reshape(length, D)
    cot = cotangent.reshape(length, D)
    gain = norm_gain.reshape(1, D)
    gain_h = head_gain.reshape(1, width)
    wide = (2, 2, length, HEAD_DIM)

    kv_mine, kv_other = split(w_qkv)
    kv_x, kv_diagonal = flip(kv_mine, "dp", 2), flip(kv_other, "dp", 3)
    partner = flip(flat, "dp", 1)
    partner, w_late, out_late = lax.optimization_barrier((partner, w_qkv, w_out))
    for_pair, far_own, q_other = pack(w_late, out_late, segment_ids, kv_other)
    pair = flip(for_pair, "dp", 1)

    normed, inv_rms, seg_col, seg_row, raw_near = call(
        prep_body,
        [
            ((4, 2 * length, D // 4), bf16),
            ((length, 1), f32),
            ((2, length, HEAD_DIM), f32),
            ((2, 1, length), f32),
            ((2 * length, 4 * HEAD_DIM), f32),
        ],
        flat, partner, segment_ids, gain, kv_mine, pair, us=20.0,
    )
    kv_x, far_own, q_other = lax.optimization_barrier((kv_x, far_own, q_other))
    kv_diagonal, cot_partner = lax.optimization_barrier((kv_diagonal, flip(cot, "dp", 1)))
    far_x, q_diagonal = flip(far_own, "dp", 2), flip(q_other, "dp", 3)

    message = ((2, 2 * HEAD_DIM + ID_ROWS, HEAD_DIM), bf16)
    feat_k, values, state = call(
        kv_body, [(wide, bf16), (wide, bf16), message], raw_near, normed, kv_x, kv_diagonal, seg_col
    )
    ends = jnp.stack([seg_col[:, 0, 0], seg_col[:, -1, 0]])
    near = carry(state, ends, 1)
    feat_q, intra, upstream = call(
        query_body,
        [(wide, bf16), (wide, f32), (wide, f32)],
        normed, far_own, pair, far_x, q_diagonal, feat_k, values, seg_col, seg_row, cot, cot_partner, gain_h, us=0.1,
    )
    rows = HEAD_DIM // 2
    mixed, d_attn, back, before, rest, a_send, b_send = call(
        attn_body,
        [
            (wide, bf16),
            (wide, bf16),
            message,
            ((2, 2 * HEAD_DIM, HEAD_DIM), bf16),
            ((2 * rows, D), f32),
            ((rows, D), bf16),
            ((2, rows // 2, D), bf16),
        ],
        *near, seg_col, feat_q, intra, upstream, gain_h, cot, cot_partner,
    )
    back_near = carry(back, ends, -1)
    scale = 1.0 / math.sqrt(length * lax.axis_size("dp") * n)
    kept, arrived = reduce_weight(rest, a_send, b_send)
    d_query, dk_intra, dv_intra, out_partner = call(
        back_body,
        [((2, length, 2 * HEAD_DIM), bf16), (wide, f32), (wide, f32), ((length, D), bf16)],
        near[0], before, near[1], seg_col, seg_row, d_attn, values, feat_k, feat_q, mixed, far_own, far_x,
    )
    (output,) = call(
        output_body,
        [((length, D), bf16)],
        flat, flip(out_partner, "dp", 1), mixed, far_own, far_x,
    )
    own, theirs = call(
        project_back_body,
        [((4, length, D // 4), f32), ((4, length, D // 4), bf16)],
        *back_near, seg_col, feat_k, values, dk_intra, dv_intra, d_query,
        far_own, pair, far_x, q_diagonal, kv_mine, kv_x, kv_diagonal,
    )
    (grad,) = call(
        final_body,
        [((length, D), bf16)],
        own, flip(theirs, "dp", 1), flat, cot, inv_rms, gain,
        scratch=[((4, length, D // 4), f32)],
    )
    output, grad, kept = lax.optimization_barrier((output, grad, kept))
    (grad_out_weight,) = call(
        functools.partial(weight_last_body, scale), [((HEAD_DIM, D), f32)], kept, arrived
    )
    return (output.reshape(tokens.shape), grad.reshape(tokens.shape), grad_out_weight)


def solution(mesh):
    in_specs = (
        P(("groups", "dp"), "seq", None),
        P(("groups", "dp"), "seq"),
        P(),
        P("dp", None),
        P(),
        P("dp", None),
        P(("groups", "dp"), "seq", None),
    )
    out_specs = (
        P(("groups", "dp"), "seq", None),
        P(("groups", "dp"), "seq", None),
        P(("groups", "dp"), None),
    )
    return jax.shard_map(shards, mesh=mesh, in_specs=in_specs, out_specs=out_specs, check_vma=False)
```

time: 83.1 us -> 69.2 us (0.83)
  Pallas kernels: 29.7 us -> 20.1 us
  local copies, waits for them, and re-layouts: 4.11 us -> 0.04 us
    pallas_call x13 -> x14, Pallas kernels: 29.7 us -> 20.1 us  [the longest x12 15 us: call(): pl.pallas_call(body, out_shape=[jax.ShapeDtypeStruct(shape, dtype) for sh...]
    unnamed x22 -> x16, local copies, waits for them, and re-layouts: 3.45 us -> 0.04 us
    ppermute x22 -> x19, starting transfers between devices: 24.5 us -> 25.2 us  [flip(): return lax.ppermute(array, axis, [(i, i ^ bit) for i in range(n)])]
    ppermute x22 -> x19, waiting for transfers between devices: 21.2 us -> 21.3 us  [flip(): return lax.ppermute(array, axis, [(i, i ^ bit) for i in range(n)])]
  transfers between devices with their start and end apart: 24 -> 21, of which waited for: 7 -> 8; matrix products, arithmetic and copies ran while one was open for 2% -> 0% of each run, Pallas kernels for 30% -> 26%
where the time goes in v4:
time: 69.2 us; the launch traced here: 68.9 us
  starting transfers between devices  26.7 us (39%)
  waiting for transfers between devices  21.3 us (31%)
  Pallas kernels  20.1 us (29%)
  between operations  0.8 us (1%)
    ppermute x19, starting transfers between devices, flip(): return lax.ppermute(array, axis, [(i, i ^ bit) for i in range(n)])  25.2 us
    ppermute x19, waiting for transfers between devices, flip(): return lax.ppermute(array, axis, [(i, i ^ bit) for i in range(n)])  21.3 us
    pallas_call x12, Pallas kernels, call(): pl.pallas_call(body, out_shape=[jax.ShapeDtypeStruct(shape, dtype) for sh...  15 us
    pallas_call x1, Pallas kernels, pack(): pl.pallas_call(pack_body, out_shape=[jax.ShapeDtypeStruct((rows + ID_ROWS...  3.19 us
    pallas_call x1, Pallas kernels, split(): pl.pallas_call(split_body, out_shape=[out, out], in_specs=[ANY], out_spec...  1.92 us
    ppermute x2, starting transfers between devices, carry(): middle = lax.ppermute(message, 'seq', [(1, 2), (2, 1)])  1.5 us
  transfers between devices with their start and end apart: 21, of which 8 were waited for; matrix products, arithmetic and copies ran while one was open for 0% of the time, Pallas kernels for 26%

profile of v4, /device:TPU:0, one launch (start us, length us, event | category | flops | bytes accessed | tf_op | source)
XLA Modules:
  0.0 68.9 jit_solution(5506596680946999755)
XLA Ops:
  1.2 1.9 %shard_map.94 = (bf16[256,512]{1,0:T(8,128)(2,1)}, bf16[256,512]{1,0:T(8,128)(2,1)}) custom-call(bf16[256,1536]{1,0:T(8,128)(2,1)} %w.2), custom_call_target="tpu_custom_call" | custom-call | flops 1000000000 | bytes 1000000 | tf_op jit(solution)/shard_map/pallas_call | solution.py:109
  3.3 3.2 %shard_map.95 = (bf16[272,768]{1,0:T(8,128)(2,1)}, bf16[256,768]{1,0:T(8,128)(2,1)}, bf16[256,256]{1,0:T(8,128)(2,1)}) custom-call(bf16[256,1536]{1,0:T(8,128)(2,1)} %w.2, bf16[128,1024]{1,0:T(8,128)(2,1)} %w_out, s32[1,384]{1,0:T(1,128)} %seg.3, bf16[256,512]{1,0:T(8,128)(2,1)} %get-tuple-element.54.kv_other), custom_call_target="tpu_custom_call" | custom-call | flops 1000000000 | bytes 1000000 | tf_op jit(solution)/shard_map/pallas_call | solution.py:121
  6.9 2.6 %collective-permute-start.2 = (bf16[256,512]{1,0:T(8,128)(2,1)S(1)}, bf16[256,512]{1,0:T(8,128)(2,1)S(1)}, u32[]{:S(2)}, u32[]{:S(2)}) collective-permute-start(bf16[256,512]{1,0:T(8,128)(2,1)S(1)} %copy-done.4), channel_id=1, source_target_pairs={{0,2},{1,3},{2,0},{3,1},{4,6},{5,7},{6,4},{7,5},{8,10},{9,11},{10,... | collective-permute-start | bytes 786440 | tf_op jit(solution)/shard_map/ppermute | solution.py:368
  9.6 7.1 %collective-permute-done.2.w2 = bf16[256,512]{1,0:T(8,128)(2,1)S(1)} collective-permute-done((bf16[256,512]{1,0:T(8,128)(2,1)S(1)}, bf16[256,512]{1,0:T(8,128)(2,1)S(1)}, u32[]{:S(2)}, u32[]{:S(2)}) %collective-permute-start.2) | collective-permute-done | bytes 262176 | tf_op jit(solution)/shard_map/ppermute | solution.py:368
  17.3 1.4 %collective-permute-start.8 = (bf16[256,768]{1,0:T(8,128)(2,1)}, bf16[256,768]{1,0:T(8,128)(2,1)S(1)}, u32[]{:S(2)}, u32[]{:S(2)}) collective-permute-start(bf16[256,768]{1,0:T(8,128)(2,1)} %get-tuple-element.64.own.own_far), channel_id=1, source_target_pairs={{0,2},{1,3},{2,0},{3,1},{4,6},{5,7},{6,4},{7,5},{8,10},{9,11},{10,... | collective-permute-start | bytes 1179656 | tf_op jit(solution)/shard_map/ppermute | solution.py:368
  18.7 3.1 %collective-permute-done.3.w3 = bf16[256,512]{1,0:T(8,128)(2,1)S(1)} collective-permute-done((bf16[256,512]{1,0:T(8,128)(2,1)S(1)}, bf16[256,512]{1,0:T(8,128)(2,1)S(1)}, u32[]{:S(2)}, u32[]{:S(2)}) %collective-permute-start.3) | collective-permute-done | bytes 262176 | tf_op jit(solution)/shard_map/ppermute | solution.py:368
  21.9 1.0 %shard_map.96 = (bf16[4,768,256]{2,1,0:T(8,128)(2,1)S(1)}, f32[384,1]{1,0:T(8,128)S(1)}, f32[2,384,128]{2,1,0:T(8,128)S(1)}, f32[2,1,384]{2,1,0:T(1,128)S(1)}, f32[768,512]{1,0:T(8,128)S(1)}) custom-call(bf16[384,1024]{1,0:T(8,128)(2,1)S(1)} %bitcast.13, bf16[384,1024]{1,0:T(8,128)(2,1)S(1)} %collective-permute-done.partner, s32[1,384]{1,0:T(1,128)S(1)} %copy-done.6, ...), custom_call_target="tpu_custom_call" | custom-call | flops 20000000000 | bytes 60000000 | tf_op jit(solution)/shard_map/pallas_call | solution.py:48
  23.8 2.7 %collective-permute-start.7 = (bf16[2,272,128]{2,1,0:T(8,128)(2,1)S(1)}, bf16[2,272,128]{2,1,0:T(8,128)(2,1)S(1)}, u32[]{:S(2)}, u32[]{:S(2)}) collective-permute-start(bf16[2,272,128]{2,1,0:T(8,128)(2,1)S(1)} %get-tuple-element.63), channel_id=1, source_target_pairs={{0,8},{4,12},{8,0},{12,4},{1,9},{5,13},{9,1},{13,5},{2,10},{6,14},... | collective-permute-start | bytes 417800 | tf_op jit(solution)/shard_map/ppermute | solution.py:368
  27.1 2.9 %collective-permute-start.5 = (bf16[2,272,128]{2,1,0:T(8,128)(2,1)S(1)}, bf16[2,272,128]{2,1,0:T(8,128)(2,1)S(1)}, u32[]{:S(2)}, u32[]{:S(2)}) collective-permute-start(bf16[2,272,128]{2,1,0:T(8,128)(2,1)S(1)} %get-tuple-element.63), channel_id=1, source_target_pairs={{0,4},{4,0},{8,12},{12,8},{1,5},{5,1},{9,13},{13,9},{2,6},{6,2},{1... | collective-permute-start | bytes 417800 | tf_op jit(solution)/shard_map/ppermute | solution.py:368
  30.0 3.2 %collective-permute-done.8.other.other_far = bf16[256,768]{1,0:T(8,128)(2,1)S(1)} collective-permute-done((bf16[256,768]{1,0:T(8,128)(2,1)}, bf16[256,768]{1,0:T(8,128)(2,1)S(1)}, u32[]{:S(2)}, u32[]{:S(2)}) %collective-permute-start.8) | collective-permute-done | bytes 393248 | tf_op jit(solution)/shard_map/ppermute | solution.py:368
  33.3 2.9 %shard_map.98 = (bf16[2,2,384,128]{3,2,1,0:T(8,128)(2,1)S(1)}, f32[2,2,384,128]{3,2,1,0:T(8,128)S(1)}, f32[2,2,384,128]{3,2,1,0:T(8,128)S(1)}) custom-call(bf16[4,768,256]{2,1,0:T(8,128)(2,1)S(1)} %get-tuple-element.57.normed, bf16[256,768]{1,0:T(8,128)(2,1)S(1)} %copy-done.1, bf16[272,768]{1,0:T(8,128)(2,1)S(1)} %collective-permute-done.1.pair.pair_in, ...), custom_call_target="tpu_custom_call" | custom-call | flops 100000000 | bytes 300000 | tf_op jit(solution)/shard_map/pallas_call | solution.py:48
  36.3 1.6 %shard_map.99 = (bf16[2,2,384,128]{3,2,1,0:T(8,128)(2,1)S(1)}, bf16[2,2,384,128]{3,2,1,0:T(8,128)(2,1)S(1)}, bf16[2,272,128]{2,1,0:T(8,128)(2,1)S(1)}, bf16[2,25...) custom-call(bf16[2,272,128]{2,1,0:T(8,128)(2,1)S(1)} %collective-per, ...), custom_call_target="tpu_custom_call" | custom-call | flops 2000000000 | bytes 6000000 | tf_op jit(solution)/shard_map/pallas_call | solution.py:48
  37.9 1.7 %collective-permute-start.15 = (bf16[64,1024]{1,0:T(8,128)(2,1)S(1)}, bf16[64,1024]{1,0:T(8,128)(2,1)S(1)}, u32[]{:S(2)}, u32[]{:S(2)}) collective-permute-start(bf16[64,1024]{1,0:T(8,128)(2,1)S(1)} %get-tuple-element.85), channel_id=1, source_target_pairs={{0,2},{1,3},{2,0},{3,1},{4,6},{5,7},{6,4},{7,5},{8,10},{9,11},{10,... | collective-permute-start | bytes 393224 | tf_op jit(solution)/shard_map/ppermute | solution.py:368
  39.6 1.6 %collective-permute-start.16 = (bf16[2,32,1024]{2,1,0:T(8,128)(2,1)S(1)}, bf16[2,32,1024]{2,1,0:T(8,128)(2,1)S(1)}, u32[]{:S(2)}, u32[]{:S(2)}) collective-permute-start(bf16[2,32,1024]{2,1,0:T(8,128)(2,1)S(1)} %get-tuple-element.86), channel_id=1, source_target_pairs={{0,4},{4,0},{8,12},{12,8},{1,5},{5,1},{9,13},{13,9},{2,6},{6,2},{1... | collective-permute-start | bytes 393224 | tf_op jit(solution)/shard_map/ppermute | solution.py:368
  41.2 2.8 %collective-permute-start.13 = (bf16[2,272,128]{2,1,0:T(8,128)(2,1)S(1)}, bf16[2,272,128]{2,1,0:T(8,128)(2,1)S(1)}, u32[]{:S(2)}, u32[]{:S(2)}) collective-permute-start(bf16[2,272,128]{2,1,0:T(8,128)(2,1)S(1)} %get-tuple-element.77), channel_id=1, source_target_pairs={{0,8},{4,12},{8,0},{12,4},{1,9},{5,13},{9,1},{13,5},{2,10},{6,14},... | collective-permute-start | bytes 417800 | tf_op jit(solution)/shard_map/ppermute | solution.py:368
  44.8 2.4 %collective-permute-start.11 = (bf16[2,272,128]{2,1,0:T(8,128)(2,1)S(1)}, bf16[2,272,128]{2,1,0:T(8,128)(2,1)S(1)}, u32[]{:S(2)}, u32[]{:S(2)}) collective-permute-start(bf16[2,272,128]{2,1,0:T(8,128)(2,1)S(1)} %get-tuple-element.77), channel_id=1, source_target_pairs={{0,4},{4,0},{8,12},{12,8},{1,5},{5,1},{9,13},{13,9},{2,6},{6,2},{1... | collective-permute-start | bytes 417800 | tf_op jit(solution)/shard_map/ppermute | solution.py:368
  48.2 2.5 %shard_map.100 = (bf16[2,384,256]{2,1,0:T(8,128)(2,1)S(1)}, f32[2,2,384,128]{3,2,1,0:T(8,128)S(1)}, f32[2,2,384,128]{3,2,1,0:T(8,128)S(1)}, bf16[384,1024]{1,0:T(8,128)(2,1)S(1)}) custom-call(bf16[2,272,128]{2,1,0:T(8,128)(2,1)S(1)} %collective-permute-done.5.pair, bf16[2,256,128]{2,1,0:T(8,128)(2,1)S(1)} %get-tuple-element.73.before, ...), custom_call_target="tpu_custom_call" | custom-call | flops 2000000000 | bytes 6000000 | tf_op jit(solution)/shard_map/pallas_call | solution.py:48
  50.6 1.5 %collective-permute-done.17.a_in = bf16[32,1024]{1,0:T(8,128)(2,1)S(1)} collective-permute-done((bf16[32,1024]{1,0:T(8,128)(2,1)S(1)}, bf16[32,1024]{1,0:T(8,128)(2,1)S(1)}, u32[]{:S(2)}, u32[]{:S(2)}) %collective-permute-start.17) | collective-permute-done | bytes 65568 | tf_op jit(solution)/shard_map/ppermute | solution.py:368
  52.2 3.5 %collective-permute-start.19 = (bf16[64,1024]{1,0:T(8,128)(2,1)S(1)}, bf16[64,1024]{1,0:T(8,128)(2,1)S(1)}, u32[]{:S(2)}, u32[]{:S(2)}) collective-permute-start(bf16[64,1024]{1,0:T(8,128)(2,1)S(1)} %get-tuple-element.91), channel_id=1, source_target_pairs={{0,8},{4,12},{8,0},{12,4},{1,9},{5,13},{9,1},{13,5},{2,10},{6,14},... | collective-permute-start | bytes 393224 | tf_op jit(solution)/shard_map/ppermute | solution.py:368
  55.7 1.8 %shard_map.102 = (f32[4,384,256]{2,1,0:T(8,128)S(1)}, bf16[4,384,256]{2,1,0:T(8,128)(2,1)S(1)}) custom-call(bf16[2,272,128]{2,1,0:T(8,128)(2,1)S(1)} %collective-permute-done.11.pair, bf16[2,272,128]{2,1,0:T(8,128)(2,1)S(1)} %collective-permute-done.12.middle, bf16[2,272,128]{2,1,0:T(8,128)(2,1)S(1)} %collective-permute-done.13.further, ...), custom_call_target="tpu_custom_call" | custom-call | flops 2000000000 | bytes 6000000 | tf_op jit(solution)/shard_map/pallas_call | solution.py:48
  57.8 4.8 %collective-permute-done.19.arrived = bf16[64,1024]{1,0:T(8,128)(2,1)S(1)} collective-permute-done((bf16[64,1024]{1,0:T(8,128)(2,1)S(1)}, bf16[64,1024]{1,0:T(8,128)(2,1)S(1)}, u32[]{:S(2)}, u32[]{:S(2)}) %collective-permute-start.19) | collective-permute-done | bytes 131104 | tf_op jit(solution)/shard_map/ppermute | solution.py:368
  63.5 1.5 %shard_map.101 = bf16[384,1024]{1,0:T(8,128)(2,1)} custom-call(bf16[384,1024]{1,0:T(8,128)(2,1)S(1)} %bitcast.14, bf16[384,1024]{1,0:T(8,128)(2,1)S(1)} %collective-permute-done.10.partner, bf16[2,2,384,128]{3,2,1,0:T(8,128)(2,1)S(1)} %get-tuple-element.75.mixed, bf16[256,768]{1,0:T(8,128)(2,1)S(1)} %copy-done.1, ...), custom_call_target="tpu_custom_call" | custom-call | flops 2000000000 | bytes 6000000 | tf_op jit(solution)/shard_map/pallas_call | solution.py:48
  65.0 1.8 %shard_map.103 = bf16[384,1024]{1,0:T(8,128)(2,1)} custom-call(f32[4,384,256]{2,1,0:T(8,128)S(1)} %get-tuple-element.81.own, bf16[4,384,256]{2,1,0:T(8,128)(2,1)S(1)} %collective-permute-done.14.partner, bf16[384,1024]{1,0:T(8,128)(2,1)S(1)} %bitcast.15, bf16[384,1024]{1,0:T(8,128)(2,1)S(1)} %bitcast.9, f32[384,1]{1,0:T(8,128)S(1)} %get-tuple-element.83.inv_rms, ...), custom_call_target="tpu_custom_call" | custom-call | flops 2000000000 | bytes 6000000 | tf_op jit(solution)/shard_map/pallas_call | solution.py:48
  66.8 1.3 %collective-permute-done.20.arrived = bf16[64,1024]{1,0:T(8,128)(2,1)S(1)} collective-permute-done((bf16[64,1024]{1,0:T(8,128)(2,1)S(1)}, bf16[64,1024]{1,0:T(8,128)(2,1)S(1)}, u32[]{:S(2)}, u32[]{:S(2)}) %collective-permute-start.20) | collective-permute-done | bytes 131104 | tf_op jit(solution)/shard_map/ppermute | solution.py:368
  (48 shorter events, 7.5 us)
Async XLA Ops:
  0.6 2.6 %collective-permute-start = (bf16[384,1024]{1,0:T(8,128)(2,1)}, bf16[384,1024]{1,0:T(8,128)(2,1)S(1)}, u32[]{:S(2)}, u32[]{:S(2)}) collective-permute-start(bf16[384,1024]{1,0:T(8,128)(2,1)} %bitcast.12), channel_id=1, source_target_pairs={{0,1},{1,0},{2,3},{3,2},{4,5},{5,4},{6,7},{7,6},{8,9},{9,8},{10,11... | collective-permute-start | bytes 2359304 | tf_op jit(solution)/shard_map/ppermute | solution.py:368
  1.1 20.7 %collective-permute-start.4 = (bf16[384,1024]{1,0:T(8,128)(2,1)}, bf16[384,1024]{1,0:T(8,128)(2,1)S(1)}, u32[]{:S(2)}, u32[]{:S(2)}) collective-permute-start(bf16[384,1024]{1,0:T(8,128)(2,1)} %bitcast.6), channel_id=1, source_target_pairs={{0,1},{1,0},{2,3},{3,2},{4,5},{5,4},{6,7},{7,6},{8,9},{9,8},{10,11... | collective-permute-start | bytes 2359304 | tf_op jit(solution)/shard_map/ppermute | solution.py:368
  3.3 18.6 %copy-start.3 = (bf16[1,384,1024]{2,1,0:T(8,128)(2,1)S(1)}, bf16[1,384,1024]{2,1,0:T(8,128)(2,1)}, u32[]{:S(2)}) copy-start(bf16[1,384,1024]{2,1,0:T(8,128)(2,1)} %param.7) | copy-start | bytes 2359300
  3.3 18.6 %copy-start.5 = (f32[1024]{0:T(1024)S(1)}, f32[1024]{0:T(1024)}, u32[]{:S(2)}) copy-start(f32[1024]{0:T(1024)} %param.9) | copy-start | bytes 12292
  3.3 18.6 %copy-start.6 = (s32[1,384]{1,0:T(1,128)S(1)}, s32[1,384]{1,0:T(1,128)}, u32[]{:S(2)}) copy-start(s32[1,384]{1,0:T(1,128)} %seg.3) | copy-start | bytes 4612
  6.5 15.3 %collective-permute-start.1 = (bf16[272,768]{1,0:T(8,128)(2,1)}, bf16[272,768]{1,0:T(8,128)(2,1)S(1)}, u32[]{:S(2)}, u32[]{:S(2)}) collective-permute-start(bf16[272,768]{1,0:T(8,128)(2,1)} %get-tuple-element.55), channel_id=1, source_target_pairs={{0,1},{1,0},{2,3},{3,2},{4,5},{5,4},{6,7},{7,6},{8,9},{9,8},{10,11... | collective-permute-start | bytes 1253384 | tf_op jit(solution)/shard_map/ppermute | solution.py:368
  6.9 9.8 %collective-permute-start.2 = (bf16[256,512]{1,0:T(8,128)(2,1)S(1)}, bf16[256,512]{1,0:T(8,128)(2,1)S(1)}, u32[]{:S(2)}, u32[]{:S(2)}) collective-permute-start(bf16[256,512]{1,0:T(8,128)(2,1)S(1)} %copy-done.4), channel_id=1, source_target_pairs={{0,2},{1,3},{2,0},{3,1},{4,6},{5,7},{6,4},{7,5},{8,10},{9,11},{10,... | collective-permute-start | bytes 786440 | tf_op jit(solution)/shard_map/ppermute | solution.py:368
  9.6 12.3 %collective-permute-start.3 = (bf16[256,512]{1,0:T(8,128)(2,1)S(1)}, bf16[256,512]{1,0:T(8,128)(2,1)S(1)}, u32[]{:S(2)}, u32[]{:S(2)}) collective-permute-start(bf16[256,512]{1,0:T(8,128)(2,1)S(1)} %copy-done.7), channel_id=1, source_target_pairs={{0,3},{1,2},{2,1},{3,0},{4,7},{5,6},{6,5},{7,4},{8,11},{9,10},{10,... | collective-permute-start | bytes 786440 | tf_op jit(solution)/shard_map/ppermute | solution.py:368
  16.7 13.3 %collective-permute-start.9 = (bf16[256,256]{1,0:T(8,128)(2,1)}, bf16[256,256]{1,0:T(8,128)(2,1)S(1)}, u32[]{:S(2)}, u32[]{:S(2)}) collective-permute-start(bf16[256,256]{1,0:T(8,128)(2,1)} %get-tuple-element.65), channel_id=1, source_target_pairs={{0,3},{1,2},{2,1},{3,0},{4,7},{5,6},{6,5},{7,4},{8,11},{9,10},{10,... | collective-permute-start | bytes 393224 | tf_op jit(solution)/shard_map/ppermute | solution.py:368
  17.3 15.9 %collective-permute-start.8 = (bf16[256,768]{1,0:T(8,128)(2,1)}, bf16[256,768]{1,0:T(8,128)(2,1)S(1)}, u32[]{:S(2)}, u32[]{:S(2)}) collective-permute-start(bf16[256,768]{1,0:T(8,128)(2,1)} %get-tuple-element.64.own.own_far), channel_id=1, source_target_pairs={{0,2},{1,3},{2,0},{3,1},{4,6},{5,7},{6,4},{7,5},{8,10},{9,11},{10,... | collective-permute-start | bytes 1179656 | tf_op jit(solution)/shard_map/ppermute | solution.py:368
  23.8 12.3 %collective-permute-start.7 = (bf16[2,272,128]{2,1,0:T(8,128)(2,1)S(1)}, bf16[2,272,128]{2,1,0:T(8,128)(2,1)S(1)}, u32[]{:S(2)}, u32[]{:S(2)}) collective-permute-start(bf16[2,272,128]{2,1,0:T(8,128)(2,1)S(1)} %get-tuple-element.63), channel_id=1, source_target_pairs={{0,8},{4,12},{8,0},{12,4},{1,9},{5,13},{9,1},{13,5},{2,10},{6,14},... | collective-permute-start | bytes 417800 | tf_op jit(solution)/shard_map/ppermute | solution.py:368
  26.4 9.7 %collective-permute-start.6 = (bf16[2,272,128]{2,1,0:T(8,128)(2,1)S(1)}, bf16[2,272,128]{2,1,0:T(8,128)(2,1)S(1)}, u32[]{:S(2)}, u32[]{:S(2)}) collective-permute-start(bf16[2,272,128]{2,1,0:T(8,128)(2,1)S(1)} %get-tuple-element.63), channel_id=1, source_target_pairs={{4,8},{8,4},{5,9},{9,5},{6,10},{10,6},{7,11},{11,7},{20,24},{24,20... | collective-permute-start | bytes 417800 | tf_op jit(solution)/shard_map/ppermute | solution.py:379
  27.1 9.2 %collective-permute-start.5 = (bf16[2,272,128]{2,1,0:T(8,128)(2,1)S(1)}, bf16[2,272,128]{2,1,0:T(8,128)(2,1)S(1)}, u32[]{:S(2)}, u32[]{:S(2)}) collective-permute-start(bf16[2,272,128]{2,1,0:T(8,128)(2,1)S(1)} %get-tuple-element.63), channel_id=1, source_target_pairs={{0,4},{4,0},{8,12},{12,8},{1,5},{5,1},{9,13},{13,9},{2,6},{6,2},{1... | collective-permute-start | bytes 417800 | tf_op jit(solution)/shard_map/ppermute | solution.py:368
  37.9 9.3 %collective-permute-start.15 = (bf16[64,1024]{1,0:T(8,128)(2,1)S(1)}, bf16[64,1024]{1,0:T(8,128)(2,1)S(1)}, u32[]{:S(2)}, u32[]{:S(2)}) collective-permute-start(bf16[64,1024]{1,0:T(8,128)(2,1)S(1)} %get-tuple-element.85), channel_id=1, source_target_pairs={{0,2},{1,3},{2,0},{3,1},{4,6},{5,7},{6,4},{7,5},{8,10},{9,11},{10,... | collective-permute-start | bytes 393224 | tf_op jit(solution)/shard_map/ppermute | solution.py:368
  39.6 7.6 %collective-permute-start.16 = (bf16[2,32,1024]{2,1,0:T(8,128)(2,1)S(1)}, bf16[2,32,1024]{2,1,0:T(8,128)(2,1)S(1)}, u32[]{:S(2)}, u32[]{:S(2)}) collective-permute-start(bf16[2,32,1024]{2,1,0:T(8,128)(2,1)S(1)} %get-tuple-element.86), channel_id=1, source_target_pairs={{0,4},{4,0},{8,12},{12,8},{1,5},{5,1},{9,13},{13,9},{2,6},{6,2},{1... | collective-permute-start | bytes 393224 | tf_op jit(solution)/shard_map/ppermute | solution.py:368
  41.2 14.5 %collective-permute-start.13 = (bf16[2,272,128]{2,1,0:T(8,128)(2,1)S(1)}, bf16[2,272,128]{2,1,0:T(8,128)(2,1)S(1)}, u32[]{:S(2)}, u32[]{:S(2)}) collective-permute-start(bf16[2,272,128]{2,1,0:T(8,128)(2,1)S(1)} %get-tuple-element.77), channel_id=1, source_target_pairs={{0,8},{4,12},{8,0},{12,4},{1,9},{5,13},{9,1},{13,5},{2,10},{6,14},... | collective-permute-start | bytes 417800 | tf_op jit(solution)/shard_map/ppermute | solution.py:368
  43.9 11.7 %collective-permute-start.12 = (bf16[2,272,128]{2,1,0:T(8,128)(2,1)S(1)}, bf16[2,272,128]{2,1,0:T(8,128)(2,1)S(1)}, u32[]{:S(2)}, u32[]{:S(2)}) collective-permute-start(bf16[2,272,128]{2,1,0:T(8,128)(2,1)S(1)} %get-tuple-element.77), channel_id=1, source_target_pairs={{4,8},{8,4},{5,9},{9,5},{6,10},{10,6},{7,11},{11,7},{20,24},{24,20... | collective-permute-start | bytes 417800 | tf_op jit(solution)/shard_map/ppermute | solution.py:379
  44.8 10.9 %collective-permute-start.11 = (bf16[2,272,128]{2,1,0:T(8,128)(2,1)S(1)}, bf16[2,272,128]{2,1,0:T(8,128)(2,1)S(1)}, u32[]{:S(2)}, u32[]{:S(2)}) collective-permute-start(bf16[2,272,128]{2,1,0:T(8,128)(2,1)S(1)} %get-tuple-element.77), channel_id=1, source_target_pairs={{0,4},{4,0},{8,12},{12,8},{1,5},{5,1},{9,13},{13,9},{2,6},{6,2},{1... | collective-permute-start | bytes 417800 | tf_op jit(solution)/shard_map/ppermute | solution.py:368
  47.2 4.9 %collective-permute-start.17 = (bf16[32,1024]{1,0:T(8,128)(2,1)S(1)}, bf16[32,1024]{1,0:T(8,128)(2,1)S(1)}, u32[]{:S(2)}, u32[]{:S(2)}) collective-permute-start(bf16[32,1024]{1,0:T(8,128)(2,1)S(1)} %get-tuple-element.88), channel_id=1, source_target_pairs={{0,4},{4,0},{8,12},{12,8},{1,5},{5,1},{9,13},{13,9},{2,6},{6,2},{1... | collective-permute-start | bytes 196616 | tf_op jit(solution)/shard_map/ppermute | solution.py:368
  47.3 4.8 %collective-permute-start.18 = (bf16[32,1024]{1,0:T(8,128)(2,1)S(1)}, bf16[32,1024]{1,0:T(8,128)(2,1)S(1)}, u32[]{:S(2)}, u32[]{:S(2)}) collective-permute-start(bf16[32,1024]{1,0:T(8,128)(2,1)S(1)} %get-tuple-element.89), channel_id=1, source_target_pairs={{0,2},{1,3},{2,0},{3,1},{4,6},{5,7},{6,4},{7,5},{8,10},{9,11},{10,... | collective-permute-start | bytes 196616 | tf_op jit(solution)/shard_map/ppermute | solution.py:368
  52.1 11.4 %collective-permute-start.10 = (bf16[384,1024]{1,0:T(8,128)(2,1)S(1)}, bf16[384,1024]{1,0:T(8,128)(2,1)S(1)}, u32[]{:S(2)}, u32[]{:S(2)}) collective-permute-start(bf16[384,1024]{1,0:T(8,128)(2,1)S(1)} %get-tuple-element.76), channel_id=1, source_target_pairs={{0,1},{1,0},{2,3},{3,2},{4,5},{5,4},{6,7},{7,6},{8,9},{9,8},{10,11... | collective-permute-start | bytes 2359304 | tf_op jit(solution)/shard_map/ppermute | solution.py:368
  52.2 10.5 %collective-permute-start.19 = (bf16[64,1024]{1,0:T(8,128)(2,1)S(1)}, bf16[64,1024]{1,0:T(8,128)(2,1)S(1)}, u32[]{:S(2)}, u32[]{:S(2)}) collective-permute-start(bf16[64,1024]{1,0:T(8,128)(2,1)S(1)} %get-tuple-element.91), channel_id=1, source_target_pairs={{0,8},{4,12},{8,0},{12,4},{1,9},{5,13},{9,1},{13,5},{2,10},{6,14},... | collective-permute-start | bytes 393224 | tf_op jit(solution)/shard_map/ppermute | solution.py:368
  57.5 7.5 %collective-permute-start.14 = (bf16[4,384,256]{2,1,0:T(8,128)(2,1)S(1)}, bf16[4,384,256]{2,1,0:T(8,128)(2,1)S(1)}, u32[]{:S(2)}, u32[]{:S(2)}) collective-permute-start(bf16[4,384,256]{2,1,0:T(8,128)(2,1)S(1)} %get-tuple-element.82), channel_id=1, source_target_pairs={{0,1},{1,0},{2,3},{3,2},{4,5},{5,4},{6,7},{7,6},{8,9},{9,8},{10,11... | collective-permute-start | bytes 2359304 | tf_op jit(solution)/shard_map/ppermute | solution.py:368
  62.7 5.4 %collective-permute-start.20 = (bf16[64,1024]{1,0:T(8,128)(2,1)S(1)}, bf16[64,1024]{1,0:T(8,128)(2,1)S(1)}, u32[]{:S(2)}, u32[]{:S(2)}) collective-permute-start(bf16[64,1024]{1,0:T(8,128)(2,1)S(1)} %get-tuple-element.96), channel_id=1, source_target_pairs={{0,4},{4,0},{8,12},{12,8},{1,5},{5,1},{9,13},{13,9},{2,6},{6,2},{1... | collective-permute-start | bytes 393224 | tf_op jit(solution)/shard_map/ppermute | solution.py:368
  (5 other events, 41.2 us)

commit v5 on v4

--- a/solution.py
+++ b/solution.py
@@ -14,7 +14,7 @@
 ID_ROWS = 16
 
 epsilon = 1e-06
-W1, W2, W3 = 8.0, 8.0, 8.0
+W1, W2, W3, PREP, QUERY, MIXED, BACK, PROJECT, SPLIT = 8.0, 8.0, 8.0, 20.0, 0.1, 0.1, 2.0, 2.0, 20.0
 
 f32 = jnp.float32
 bf16 = jnp.bfloat16
@@ -69,81 +69,69 @@
     return (down == seg_row[i]) & order
 
 
-def split_body(w, kv_mine, kv_other, sem):
-    c = lax.axis_index("dp") % 2
-    copies = []
-    for target, which in ((kv_mine, c), (kv_other, 1 - c)):
-        for n in range(4):
-            at = columns(4 + 4 * (n // 2) + 2 * (n % 2) + which, HEAD_DIM)
-            copies.append(pltpu.make_async_copy(w.at[:, at], target.at[:, head(n)], sem.at[len(copies)]))
+def run_all(copies, sem):
+    copies = [pltpu.make_async_copy(source, target, sem.at[n]) for n, (source, target) in enumerate(copies)]
     for copy in copies:
         copy.start()
     for copy in copies:
         copy.wait()
 
 
-def pack_body(w, w_out, seg, kv_other, pair, far, q_other, sem):
+def kv_columns(n, which):
+    return columns(4 + 4 * (n // 2) + 2 * (n % 2) + which, HEAD_DIM)
+
+
+def split_half_body(w, half, sem):
+    c, rows = lax.axis_index("dp") % 2, half.shape[0]
+    part = pl.ds(pl.multiple_of(lax.axis_index("groups") * rows, rows), rows)
+    run_all([(w.at[part, kv_columns(n, 1 - c)], half.at[:, head(n)]) for n in range(4)], sem)
+
+
+def split_kv_body(w, seg, _, mine, other, sem):
+    c = lax.axis_index("dp") % 2
+    rows, length = w.shape[0], seg.shape[1]
+    other[rows:, :length] = jnp.broadcast_to(seg[...].astype(f32), (ID_ROWS, length)).astype(bf16)
+    copies = []
+    for target, which in ((mine, c), (other, 1 - c)):
+        copies += [(w.at[:, kv_columns(n, which)], target.at[:rows, head(n)]) for n in range(4)]
+    run_all(copies, sem)
+
+
+def split_q_body(w, w_out, far, other, sem):
     c = lax.axis_index("dp") % 2
     rows, half = w_out.shape[0], w_out.shape[1] // 2
-    full = w.shape[0]
     copies = [
         (w_out.at[:, :half], far.at[:rows, 2 * HEAD_DIM :]),
         (w_out.at[:, half:], far.at[rows:, 2 * HEAD_DIM :]),
     ]
-    for g in range(2):
-        mine, other = columns(2 * g + c, HEAD_DIM), columns(2 * g + 1 - c, HEAD_DIM)
-        copies.append((w.at[:, mine], far.at[:, head(g)]))
-        copies.append((w.at[:, other], q_other.at[:, head(g)]))
-        copies.append((w.at[:, other], pair.at[:full, head(4 + g)]))
-    copies = [pltpu.make_async_copy(source, target, sem.at[n]) for n, (source, target) in enumerate(copies)]
-    for copy in copies:
-        copy.start()
-    pair[:full, KV_COLUMNS] = kv_other[...]
-    pair[full:, : seg.shape[1]] = jnp.broadcast_to(seg[...].astype(f32), (ID_ROWS, seg.shape[1])).astype(bf16)
-    for copy in copies:
-        copy.wait()
-
-
-def split(w):
-    out = jax.ShapeDtypeStruct((w.shape[0], 4 * HEAD_DIM), bf16)
+    for target, which in ((far, c), (other, 1 - c)):
+        copies += [(w.at[:, columns(2 * g + which, HEAD_DIM)], target.at[:, head(g)]) for g in range(2)]
+    run_all(copies, sem)
+
+
+def split(body, shapes, copies, us, w, *rest, specs=()):
     return pl.pallas_call(
-        split_body,
-        out_shape=[out, out],
-        in_specs=[ANY],
-        out_specs=[VMEM, VMEM],
-        scratch_shapes=[pltpu.SemaphoreType.DMA((8,))],
-        cost_estimate=pl.CostEstimate(flops=10**9, transcendentals=0, bytes_accessed=10**6),
-    )(w)
-
-
-def pack(w, w_out, seg, kv_other):
-    rows = w.shape[0]
-    return pl.pallas_call(
-        pack_body,
-        out_shape=[
-            jax.ShapeDtypeStruct((rows + ID_ROWS, 6 * HEAD_DIM), bf16),
-            jax.ShapeDtypeStruct((rows, 6 * HEAD_DIM), bf16),
-            jax.ShapeDtypeStruct((rows, 2 * HEAD_DIM), bf16),
-        ],
-        in_specs=[ANY, ANY, VMEM, VMEM],
-        out_specs=[VMEM] * 3,
-        scratch_shapes=[pltpu.SemaphoreType.DMA((8,))],
-        cost_estimate=pl.CostEstimate(flops=10**9, transcendentals=0, bytes_accessed=10**6),
-    )(w, w_out, seg, kv_other)
-
-
-KV_COLUMNS = slice(0, 4 * HEAD_DIM)
-PAIR_Q_COLUMNS = slice(4 * HEAD_DIM, 6 * HEAD_DIM)
-FAR_Q_COLUMNS = slice(0, 2 * HEAD_DIM)
+        body,
+        out_shape=[jax.ShapeDtypeStruct(shape, bf16) for shape in shapes],
+        in_specs=[ANY, *specs],
+        out_specs=[VMEM] * len(shapes),
+        scratch_shapes=[pltpu.SemaphoreType.DMA((copies,))],
+        compiler_params=pltpu.CompilerParams(vmem_limit_bytes=8 * 1024 * 1024),
+        cost_estimate=pl.CostEstimate(flops=int(us * 1e9), transcendentals=0, bytes_accessed=10**6),
+    )(w, *rest)
+
+
+FAR_Q = slice(0, 2 * HEAD_DIM)
 
 
 def out_rows(far):
     rows = far.shape[0] // 2
-    return jnp.concatenate([far[:rows, 2 * HEAD_DIM :], far[rows:, 2 * HEAD_DIM :]], axis=1)
-
-
-def pair_ids(pair, length):
-    return pair[pair.shape[0] - ID_ROWS : pair.shape[0] - ID_ROWS + 1, :length].astype(f32)
+    return far[:rows, 2 * HEAD_DIM :], far[rows:, 2 * HEAD_DIM :]
+
+
+def halves():
+    at = lax.axis_index("groups")
+    return at, 1 - at
 
 
 def sources(step):
@@ -153,9 +141,9 @@
     return (at % 2 == 1, at >= 2) if step > 0 else (at % 2 == 0, at < 2)
 
 
-def prep_body(tokens, partner, seg, gain, w0, pair, normed, inv_rms, seg_col, seg_row, raw):
+def prep_body(tokens, partner, seg, gain, w0, w1, normed, inv_rms, seg_col, seg_row, raw):
     length = seg.shape[1]
-    for i, (part, ids) in enumerate(((tokens, seg[...].astype(f32)), (partner, pair_ids(pair, length)))):
+    for i, (part, ids) in enumerate(((tokens, seg[...].astype(f32)), (partner, w1[w0.shape[0] : w0.shape[0] + 1, :length].astype(f32)))):
         x = part[...].astype(f32)
         inv = lax.rsqrt(jnp.mean(x * x, axis=1, keepdims=True) + epsilon)
         if i == 0:
@@ -166,11 +154,24 @@
         seg_row[i] = ids
         seg_col[i] = jnp.broadcast_to(ids, (HEAD_DIM, length)).T
     rows = w0.shape[0]
-    raw[...] = dot_nn(normed[0], w0[...]) + dot_nn(normed[1], pair[:rows, KV_COLUMNS])
-
-
-def kv_body(near, normed, w2, w3, seg_col, feat_k, values, state):
-    raw = near[...] + dot_nn(normed[2], w2[...]) + dot_nn(normed[3], w3[...])
+    raw[...] = dot_nn(normed[0], w0[...]) + dot_nn(normed[1], w1[:rows])
+
+
+def store_state(state, state_far, i, g, value):
+    for target in (state, state_far):
+        target[i, head(g), :] = value.astype(bf16)
+
+
+def store_ids(state, state_far, i, ids):
+    for target in (state, state_far):
+        rows = target.shape[1] - 2 * HEAD_DIM
+        target[i, 2 * HEAD_DIM :, :] = jnp.broadcast_to(ids, (rows, HEAD_DIM)).astype(bf16)
+
+
+def kv_body(near, normed, w2, w3, w3_other, seg_col, feat_k, values, state, state_far):
+    raw = near[...] + dot_nn(normed[2], w2[...])
+    for at, w in zip(halves(), (w3, w3_other)):
+        raw += dot_nn(normed[3, :, columns(at, w.shape[0])], w[...])
     raw = raw.astype(bf16)
     length = seg_col.shape[1]
     for i in range(2):
@@ -182,20 +183,15 @@
             v = raw[rows, head(2 + g)]
             feat_k[i, g] = k.astype(bf16)
             values[i, g] = v
-            state[i, head(g), :] = dot_tn(jnp.where(tail, k, 0.0).astype(bf16), v).astype(bf16)
-        state[i, 2 * HEAD_DIM :, :] = jnp.broadcast_to(last, (ID_ROWS, HEAD_DIM)).astype(bf16)
-
-
-def query_body(
-    normed, own, pair, other, w3, feat_k, values, seg_col, seg_row, cot, cot_partner, gain,
-    feat_q, intra, upstream,
-):
-    rows, length = own.shape[0], seg_row.shape[2]
-    raw = dot_nn(normed[0], own[:, FAR_Q_COLUMNS])
-    raw += dot_nn(normed[1], pair[:rows, PAIR_Q_COLUMNS])
-    raw += dot_nn(normed[2], other[:, FAR_Q_COLUMNS])
-    raw += dot_nn(normed[3], w3[...])
+            store_state(state, state_far, i, g, dot_tn(jnp.where(tail, k, 0.0).astype(bf16), v))
+        store_ids(state, state_far, i, last)
+
+
+def query_body(normed, w0, w1, w2, w3, feat_k, values, seg_col, seg_row, feat_q, intra):
+    raw = dot_nn(normed[0], w0[:, FAR_Q]) + dot_nn(normed[1], w1[...])
+    raw += dot_nn(normed[2], w2[:, FAR_Q]) + dot_nn(normed[3], w3[...])
     raw = raw.astype(bf16)
+    length = seg_row.shape[2]
     for i in range(2):
         mask = causal(seg_col, seg_row, i)
         for g in range(2):
@@ -203,10 +199,14 @@
             feat_q[i, g] = q
             s = jnp.where(mask, dot_nt(q, feat_k[i, g]), 0.0).astype(bf16)
             intra[i, g] = dot_nn(s, values[i, g])
-    for j, o in enumerate((out_rows(own), out_rows(other))):
+
+
+def mixed_grad_body(cot, cot_partner, own, other, gain, upstream):
+    for j, o in enumerate((own, other)):
         full = lax.axis_index("dp") ^ (2 * j)
         for i, part in enumerate((cot, cot_partner)):
-            upstream[i, full // 2] = dot_nt(part[...], o) * gain[:, columns(full, HEAD_DIM)]
+            value = sum(dot_nt(part[:, n * 512 : (n + 1) * 512], half) for n, half in enumerate(out_rows(o)))
+            upstream[i, full // 2] = value * gain[:, columns(full, HEAD_DIM)]
 
 
 def received(step, pair, middle, further, i):
@@ -221,7 +221,7 @@
 
 def attn_body(
     pair, middle, further, seg_col, feat_q, intra, upstream, gain, cot, cot_partner,
-    mixed, d_attn, state, before, rest, a_send, b_send,
+    mixed, d_attn, state, state_far, before, rest, a_send, b_send,
 ):
     for i in range(2):
         first = seg_col[i, 0:1, :]
@@ -238,8 +238,8 @@
             inner = jnp.mean(attention * up, axis=1, keepdims=True)
             da = (ratio * up - ratio**3 * attention * inner).astype(bf16)
             d_attn[i, g] = da
-            state[i, head(g), :] = dot_tn(jnp.where(begin, q.astype(f32), 0.0).astype(bf16), da).astype(bf16)
-        state[i, 2 * HEAD_DIM :, :] = jnp.broadcast_to(first, (ID_ROWS, HEAD_DIM)).astype(bf16)
+            store_state(state, state_far, i, g, dot_tn(jnp.where(begin, q.astype(f32), 0.0).astype(bf16), da))
+        store_ids(state, state_far, i, first)
     half = HEAD_DIM // 2
     quarter = half // 2
     second = lax.axis_index("seq") % 2 == 1
@@ -289,11 +289,9 @@
 
 
 def back_body(
-    pair, before, middle, seg_col, seg_row, d_attn, values, feat_k, feat_q, mixed, own, other,
-    d_query, dk_intra, dv_intra, out_partner,
+    pair, before, middle, seg_col, seg_row, d_attn, values, feat_k, feat_q,
+    d_query, dk_intra, dv_intra,
 ):
-    x = lax.axis_index("dp") // 2
-    out_partner[...] = (dot_nn(mixed[1, x], out_rows(own)) + dot_nn(mixed[1, 1 - x], out_rows(other))).astype(bf16)
     for i in range(2):
         mask = causal(seg_col, seg_row, i)
         use_pair, _ = sources(1)
@@ -312,21 +310,22 @@
 
 def output_body(tokens, partner, mixed, own, other, output):
     x = lax.axis_index("dp") // 2
-    total = dot_nn(mixed[0, x], out_rows(own)) + dot_nn(mixed[0, 1 - x], out_rows(other))
-    output[...] = (tokens[...].astype(f32) + (total + partner[...].astype(f32))).astype(bf16)
+    for n, (a, b) in enumerate(zip(out_rows(own), out_rows(other))):
+        at = slice(n * 512, (n + 1) * 512)
+        total = dot_nn(mixed[0, x], a) + dot_nn(mixed[0, 1 - x], b)
+        output[:, at] = (tokens[:, at].astype(f32) + (total + partner[:, at].astype(f32))).astype(bf16)
 
 
 def project_back_body(
     pair, middle, further, seg_col, feat_k, values, dk_intra, dv_intra, d_query,
-    own_far, pair_in, other_far, q3, w0, w2, w3, own, partner,
+    q0, q1, q2, q3, w0, w1, w2, w3, w3_other, mixed, own, partner, out_partner, work,
 ):
+    x = lax.axis_index("dp") // 2
+    for n, (a, b) in enumerate(zip(out_rows(q0), out_rows(q2))):
+        out_partner[:, n * 512 : (n + 1) * 512] = (dot_nn(mixed[1, x], a) + dot_nn(mixed[1, 1 - x], b)).astype(bf16)
     rows = w0.shape[0]
-    weights = (
-        (own_far[:, FAR_Q_COLUMNS], w0[...]),
-        (pair_in[:rows, PAIR_Q_COLUMNS], pair_in[:rows, KV_COLUMNS]),
-        (other_far[:, FAR_Q_COLUMNS], w2[...]),
-        (q3[...], w3[...]),
-    )
+    q = (q0[:, FAR_Q], q1[...], q2[:, FAR_Q], q3[...])
+    w = (w0[...], w1[:rows], w2[...])
     for i in (1, 0):
         ids, total = received(-1, pair, middle, further, i)
         take = seg_col[i] == ids
@@ -339,12 +338,21 @@
             d_key.append((dk * jnp.minimum(k.astype(f32), 1.0)).astype(bf16))
             d_value.append(dv.astype(bf16))
         d_proj = jnp.concatenate(d_key + d_value, axis=1)
-        for j, (q, w) in enumerate(weights):
-            value = dot_nt(d_query[i], q) + dot_nt(d_proj, w)
+        pieces = [(j, slice(None), dot_nt(d_proj, w[j])) for j in range(3)]
+        pieces += [
+            (3, columns(at, part.shape[0]), dot_nt(d_proj, part[...])) for at, part in zip(halves(), (w3, w3_other))
+        ]
+        for j in range(4):
+            from_q = dot_nt(d_query[i], q[j])
             if i == 1:
-                partner[j ^ 1] = value.astype(bf16)
+                work[j ^ 1] = from_q
             else:
-                own[j] = value
+                own[j] = from_q
+        for j, at, value in pieces:
+            if i == 1:
+                partner[j ^ 1, :, at] = (work[j ^ 1, :, at] + value).astype(bf16)
+            else:
+                own[j, :, at] += value
 
 
 def final_body(own, partner, tokens, cot, inv_rms, gain, grad, work):
@@ -373,11 +381,11 @@
     return lax.ppermute(array, axis, [(i, i + step) for i in range(n) if 0 <= i + step < n])
 
 
-def carry(message, ends, step):
+def carry(message, longer, ends, step, late=None):
     n = lax.axis_size("seq")
     if n == 4:
         middle = lax.ppermute(message, "seq", [(1, 2), (2, 1)])
-        return flip(message, "seq", 1), middle, flip(message, "seq", 2)
+        return flip(message if late is None else late, "seq", 1), middle, flip(longer, "seq", 2)
     position = lax.axis_index("seq")
     begin, end = (ends[0], ends[1]) if step > 0 else (ends[1], ends[0])
     total = message[:, : 2 * HEAD_DIM].astype(f32)
@@ -396,7 +404,7 @@
     return near, near, near
 
 
-def reduce_weight(rest, a_send, b_send):
+def reduce_weight(rest, a_send, b_send, back, ends, d_attn):
     n = lax.axis_size("seq")
     half, width = a_send.shape
     quarter = half // 2
@@ -405,13 +413,15 @@
         [((half, width), f32), ((quarter, width), bf16), ((quarter, width), bf16)],
         rest, flip(a_send, "dp", 2), flip(b_send, "seq", 1), us=W1,
     )
+    a_send, back_late = lax.optimization_barrier((a_send, back[0]))
+    back_near = carry(back[0], back[1], ends, -1, back_late)
     outs = [((half, width), f32), ((half, width), bf16)]
     kept, send = call(weight_two_body, outs, kept, flip(a_send, "seq", 1), flip(b_send, "dp", 2), us=W2)
     reach = 2
     while reach < n:
         kept, send = call(weight_three_body, outs, kept, flip(send, "seq", reach), us=W3)
         reach *= 2
-    return kept, flip(send, "seq", 1)
+    return kept, flip(send, "seq", 1), back_near, d_attn
 
 
 def shards(tokens, segment_ids, norm_gain, w_qkv, head_gain, w_out, cotangent):
@@ -424,13 +434,17 @@
     gain_h = head_gain.reshape(1, width)
     wide = (2, 2, length, HEAD_DIM)
 
-    kv_mine, kv_other = split(w_qkv)
-    kv_x, kv_diagonal = flip(kv_mine, "dp", 2), flip(kv_other, "dp", 3)
-    partner = flip(flat, "dp", 1)
-    partner, w_late, out_late = lax.optimization_barrier((partner, w_qkv, w_out))
-    for_pair, far_own, q_other = pack(w_late, out_late, segment_ids, kv_other)
-    pair = flip(for_pair, "dp", 1)
-
+    shard_rows = w_qkv.shape[0]
+    (kv_half,) = split(split_half_body, [(shard_rows // 2, 4 * HEAD_DIM)], 4, 1.0, w_qkv)
+    kv_diagonal = flip(kv_half, "dp", 3)
+    kv_mine, kv_other = split(
+        split_kv_body,
+        [(shard_rows, 4 * HEAD_DIM), (shard_rows + ID_ROWS, 4 * HEAD_DIM)],
+        8, SPLIT, w_qkv, segment_ids, kv_half, specs=(VMEM, ANY),
+    )
+    kv_x, kv_pair = flip(kv_mine, "dp", 2), flip(kv_other, "dp", 1)
+    partner, cot_partner = flip(flat, "dp", 1), flip(cot, "dp", 1)
+    partner, kv_pair, cot_partner, w_late = lax.optimization_barrier((partner, kv_pair, cot_partner, w_qkv))
     normed, inv_rms, seg_col, seg_row, raw_near = call(
         prep_body,
         [
@@ -440,30 +454,41 @@
             ((2, 1, length), f32),
             ((2 * length, 4 * HEAD_DIM), f32),
         ],
-        flat, partner, segment_ids, gain, kv_mine, pair, us=20.0,
-    )
-    kv_x, far_own, q_other = lax.optimization_barrier((kv_x, far_own, q_other))
-    kv_diagonal, cot_partner = lax.optimization_barrier((kv_diagonal, flip(cot, "dp", 1)))
-    far_x, q_diagonal = flip(far_own, "dp", 2), flip(q_other, "dp", 3)
+        flat, partner, segment_ids, gain, kv_mine, kv_pair, us=PREP,
+    )
+    far_own, q_other = split(
+        split_q_body, [(shard_rows, 6 * HEAD_DIM), (shard_rows, 2 * HEAD_DIM)], 6, 1.0, w_late, w_out, specs=(ANY,)
+    )
+    kv_diagonal, inv_rms, far_own, q_other = lax.optimization_barrier((kv_diagonal, inv_rms, far_own, q_other))
+    kv_diagonal_other = flip(kv_diagonal, "groups", 1)
+    far_x = flip(far_own, "dp", 2)
+    kv_x, q_pair = lax.optimization_barrier((kv_x, flip(q_other, "dp", 1)))
+    wq = [far_own, q_pair, far_x, flip(q_other, "dp", 3)]
+    kv = [kv_mine, kv_pair, kv_x, kv_diagonal, kv_diagonal_other]
+    out = [far_own, far_x]
 
     message = ((2, 2 * HEAD_DIM + ID_ROWS, HEAD_DIM), bf16)
-    feat_k, values, state = call(
-        kv_body, [(wide, bf16), (wide, bf16), message], raw_near, normed, kv_x, kv_diagonal, seg_col
+    longer = ((2, 2 * HEAD_DIM + 2 * ID_ROWS, HEAD_DIM), bf16)
+    feat_k, values, state, state_far = call(
+        kv_body, [(wide, bf16), (wide, bf16), message, longer], raw_near, normed, *kv[2:], seg_col
     )
     ends = jnp.stack([seg_col[:, 0, 0], seg_col[:, -1, 0]])
-    near = carry(state, ends, 1)
-    feat_q, intra, upstream = call(
-        query_body,
-        [(wide, bf16), (wide, f32), (wide, f32)],
-        normed, far_own, pair, far_x, q_diagonal, feat_k, values, seg_col, seg_row, cot, cot_partner, gain_h, us=0.1,
+    near = carry(state, state_far, ends, 1)
+    (upstream,) = call(
+        mixed_grad_body, [(wide, f32)], cot, cot_partner, *out, gain_h, us=MIXED
+    )
+    upstream, feat_k, feat_k_late = lax.optimization_barrier((upstream, feat_k, feat_k))
+    feat_q, intra = call(
+        query_body, [(wide, bf16), (wide, f32)], normed, *wq, feat_k_late, values, seg_col, seg_row, us=QUERY
     )
     rows = HEAD_DIM // 2
-    mixed, d_attn, back, before, rest, a_send, b_send = call(
+    mixed, d_attn, back, back_far, before, rest, a_send, b_send = call(
         attn_body,
         [
             (wide, bf16),
             (wide, bf16),
             message,
+            longer,
             ((2, 2 * HEAD_DIM, HEAD_DIM), bf16),
             ((2 * rows, D), f32),
             ((rows, D), bf16),
@@ -471,24 +496,23 @@
         ],
         *near, seg_col, feat_q, intra, upstream, gain_h, cot, cot_partner,
     )
-    back_near = carry(back, ends, -1)
     scale = 1.0 / math.sqrt(length * lax.axis_size("dp") * n)
-    kept, arrived = reduce_weight(rest, a_send, b_send)
-    d_query, dk_intra, dv_intra, out_partner = call(
+    kept, arrived, back_near, d_attn = reduce_weight(rest, a_send, b_send, (back, back_far), ends, d_attn)
+    d_query, dk_intra, dv_intra = call(
         back_body,
-        [((2, length, 2 * HEAD_DIM), bf16), (wide, f32), (wide, f32), ((length, D), bf16)],
-        near[0], before, near[1], seg_col, seg_row, d_attn, values, feat_k, feat_q, mixed, far_own, far_x,
+        [((2, length, 2 * HEAD_DIM), bf16), (wide, f32), (wide, f32)],
+        near[0], before, near[1], seg_col, seg_row, d_attn, values, feat_k, feat_q, us=BACK,
+    )
+    own, theirs, out_partner = call(
+        project_back_body,
+        [((4, length, D // 4), f32), ((4, length, D // 4), bf16), ((length, D), bf16)],
+        *back_near, seg_col, feat_k, values, dk_intra, dv_intra, d_query,
+        *wq, *kv, mixed, us=PROJECT, scratch=[((4, length, D // 4), f32)],
     )
     (output,) = call(
         output_body,
         [((length, D), bf16)],
-        flat, flip(out_partner, "dp", 1), mixed, far_own, far_x,
-    )
-    own, theirs = call(
-        project_back_body,
-        [((4, length, D // 4), f32), ((4, length, D // 4), bf16)],
-        *back_near, seg_col, feat_k, values, dk_intra, dv_intra, d_query,
-        far_own, pair, far_x, q_diagonal, kv_mine, kv_x, kv_diagonal,
+        flat, flip(out_partner, "dp", 1), mixed, *out,
     )
     (grad,) = call(
         final_body,

time: 69.2 us -> 62.5 us (0.903)
  waiting for transfers between devices: 21.3 us -> 14.6 us
  Pallas kernels: 20.1 us -> 16.1 us
  starting transfers between devices: 26.7 us -> 28.9 us
  local copies, waits for them, and re-layouts: 0.04 us -> 1.95 us
    ppermute x19 -> x21, waiting for transfers between devices: 21.3 us -> 14.6 us  [flip(): return lax.ppermute(array, axis, [(i, i ^ bit) for i in range(n)])]
    pallas_call x2 -> x3, Pallas kernels: 5.11 us -> 0.41 us  [split(): pl.pallas_call(body, out_shape=[jax.ShapeDtypeStruct(shape, bf16) for sha...]
    ppermute x19 -> x21, starting transfers between devices: 25.2 us -> 27.4 us  [flip(): return lax.ppermute(array, axis, [(i, i ^ bit) for i in range(n)])]
    unnamed x16, local copies, waits for them, and re-layouts: 0.04 us -> 1.95 us
    pallas_call x12 -> x13, Pallas kernels: 15 us -> 15.7 us  [call(): pl.pallas_call(body, out_shape=[jax.ShapeDtypeStruct(shape, dtype) for sh...]
  transfers between devices with their start and end apart: 21 -> 23, of which waited for: 8 -> 9; matrix products, arithmetic and copies ran while one was open for 0% -> 0% of each run, Pallas kernels for 26% -> 22%
where the time goes in v5:
time: 62.5 us; the launch traced here: 62.3 us
  starting transfers between devices  28.9 us (46%)
  Pallas kernels  16.1 us (26%)
  waiting for transfers between devices  14.6 us (23%)
  local copies, waits for them, and re-layouts  1.95 us (3%)
  between operations  0.82 us (1%)
    ppermute x21, starting transfers between devices, flip(): return lax.ppermute(array, axis, [(i, i ^ bit) for i in range(n)])  27.4 us
    pallas_call x13, Pallas kernels, call(): pl.pallas_call(body, out_shape=[jax.ShapeDtypeStruct(shape, dtype) for sh...  15.7 us
    ppermute x21, waiting for transfers between devices, flip(): return lax.ppermute(array, axis, [(i, i ^ bit) for i in range(n)])  14.6 us
    unnamed x16, local copies, waits for them, and re-layouts  1.95 us
    ppermute x2, starting transfers between devices, carry(): middle = lax.ppermute(message, 'seq', [(1, 2), (2, 1)])  1.5 us
  transfers between devices with their start and end apart: 23, of which 9 were waited for; matrix products, arithmetic and copies ran while one was open for 0% of the time, Pallas kernels for 22%

profile of v5, /device:TPU:0, one launch (start us, length us, event | category | flops | bytes accessed | tf_op | source)
XLA Modules:
  0.0 62.3 jit_solution(10555396977750108708)
XLA Ops:
  1.2 1.1 %copy-done.2 = bf16[256,1536]{1,0:T(8,128)(2,1)S(1)} copy-done((bf16[256,1536]{1,0:T(8,128)(2,1)S(1)}, bf16[256,1536]{1,0:T(8,128)(2,1)}, u32[]{:S(2)}) %copy-start.2) | copy-done | bytes 786456
  3.7 2.6 %collective-permute-start.4 = (bf16[128,512]{1,0:T(8,128)(2,1)S(1)}, bf16[128,512]{1,0:T(8,128)(2,1)S(1)}, u32[]{:S(2)}, u32[]{:S(2)}) collective-permute-start(bf16[128,512]{1,0:T(8,128)(2,1)S(1)} %shard_map.94._), channel_id=1, source_target_pairs={{0,3},{1,2},{2,1},{3,0},{4,7},{5,6},{6,5},{7,4},{8,11},{9,10},{10,... | collective-permute-start | bytes 393224 | tf_op jit(solution)/shard_map/ppermute | solution.py:376
  6.5 1.0 %shard_map.96 = (bf16[4,768,256]{2,1,0:T(8,128)(2,1)S(1)}, f32[384,1]{1,0:T(8,128)S(1)}, f32[2,384,128]{2,1,0:T(8,128)S(1)}, f32[2,1,384]{2,1,0:T(1,128)S(1)}, f32[768,512]{1,0:T(8,128)S(1)}) custom-call(bf16[384,1024]{1,0:T(8,128)(2,1)S(1)} %bitcast.13, bf16[384,1024]{1,0:T(8,128)(2,1)S(1)} %collective-permute-done.partner, s32[1,384]{1,0:T(1,128)S(1)} %copy-done.7, ...), custom_call_target="tpu_custom_call" | custom-call | flops 20000000000 | bytes 60000000 | tf_op jit(solution)/shard_map/pallas_call | solution.py:48
  7.8 2.4 %collective-permute-done.4.w3 = bf16[128,512]{1,0:T(8,128)(2,1)S(1)} collective-permute-done((bf16[128,512]{1,0:T(8,128)(2,1)S(1)}, bf16[128,512]{1,0:T(8,128)(2,1)S(1)}, u32[]{:S(2)}, u32[]{:S(2)}) %collective-permute-start.4) | collective-permute-done | bytes 131104 | tf_op jit(solution)/shard_map/ppermute | solution.py:376
  10.5 2.0 %collective-permute-start.6 = (bf16[128,512]{1,0:T(8,128)(2,1)S(1)}, bf16[128,512]{1,0:T(8,128)(2,1)S(1)}, u32[]{:S(2)}, u32[]{:S(2)}) collective-permute-start(bf16[128,512]{1,0:T(8,128)(2,1)S(1)} %collective-permute-done.4.w3), channel_id=1, source_target_pairs={{0,16},{16,0},{1,17},{17,1},{2,18},{18,2},{3,19},{19,3},{4,20},{20... | collective-permute-start | bytes 393224 | tf_op jit(solution)/shard_map/ppermute | solution.py:376
  12.5 1.5 %collective-permute-start.10 = (bf16[256,768]{1,0:T(8,128)(2,1)S(1)}, bf16[256,768]{1,0:T(8,128)(2,1)S(1)}, u32[]{:S(2)}, u32[]{:S(2)}) collective-permute-start(bf16[256,768]{1,0:T(8,128)(2,1)S(1)} %get-tuple-element.73.own.w0.q0), channel_id=1, source_target_pairs={{0,2},{1,3},{2,0},{3,1},{4,6},{5,7},{6,4},{7,5},{8,10},{9,11},{10,... | collective-permute-start | bytes 1179656 | tf_op jit(solution)/shard_map/ppermute | solution.py:376
  14.0 2.3 %collective-permute-done.3.w2 = bf16[256,512]{1,0:T(8,128)(2,1)S(1)} collective-permute-done((bf16[256,512]{1,0:T(8,128)(2,1)S(1)}, bf16[256,512]{1,0:T(8,128)(2,1)S(1)}, u32[]{:S(2)}, u32[]{:S(2)}) %collective-permute-start.3) | collective-permute-done | bytes 262176 | tf_op jit(solution)/shard_map/ppermute | solution.py:376
  16.3 1.1 %shard_map.98 = (bf16[2,2,384,128]{3,2,1,0:T(8,128)(2,1)S(1)}, bf16[2,2,384,128]{3,2,1,0:T(8,128)(2,1)S(1)}, bf16[2,272,128]{2,1,0:T(8,128)(2,1)S(1)}, bf16[2,288,128]{2,1,0:T(8,128)(2,1)S(1)}) custom-call(f32[768,512]{1,0:T(8,128)S(1)} %get-tuple-element.61.near, bf16[4,768,256]{2,1,0:T(8,128)(2,1)S(1)} %get-tuple-element.62.normed, ...), custom_call_target="tpu_custom_call" | custom-call | flops 2000000000 | bytes 6000000 | tf_op jit(solution)/shard_map/pallas_call | solution.py:48
  17.4 3.2 %collective-permute-start.9 = (bf16[2,288,128]{2,1,0:T(8,128)(2,1)S(1)}, bf16[2,288,128]{2,1,0:T(8,128)(2,1)S(1)}, u32[]{:S(2)}, u32[]{:S(2)}) collective-permute-start(bf16[2,288,128]{2,1,0:T(8,128)(2,1)S(1)} %get-tuple-element.72), channel_id=1, source_target_pairs={{0,8},{4,12},{8,0},{12,4},{1,9},{5,13},{9,1},{13,5},{2,10},{6,14},... | collective-permute-start | bytes 442376 | tf_op jit(solution)/shard_map/ppermute | solution.py:376
  21.3 2.9 %collective-permute-start.7 = (bf16[2,272,128]{2,1,0:T(8,128)(2,1)S(1)}, bf16[2,272,128]{2,1,0:T(8,128)(2,1)S(1)}, u32[]{:S(2)}, u32[]{:S(2)}) collective-permute-start(bf16[2,272,128]{2,1,0:T(8,128)(2,1)S(1)} %get-tuple-element.71), channel_id=1, source_target_pairs={{0,4},{4,0},{8,12},{12,8},{1,5},{5,1},{9,13},{13,9},{2,6},{6,2},{1... | collective-permute-start | bytes 417800 | tf_op jit(solution)/shard_map/ppermute | solution.py:376
  24.7 1.0 %shard_map.99.upstream = f32[2,2,384,128]{3,2,1,0:T(8,128)S(1)} custom-call(bf16[384,1024]{1,0:T(8,128)(2,1)S(1)} %bitcast.7, bf16[384,1024]{1,0:T(8,128)(2,1)S(1)} %collective-permute-done.2.cot_partner, bf16[256,768]{1,0:T(8,128)(2,1)S(1)} %get-tuple-element.73.own.w0.q0, bf16[256,768]{1,0:T(8,128)(2,1)S(1)} %collective-permute-done.10.other.w2.q2, ...), custom_call_target="tpu_custom_call" | custom-call | flops 100000000 | bytes 300000 | tf_op jit(solution)/shard_map/pallas_call | solution.py:48
  25.7 1.3 %collective-permute-done.11.w3.q3 = bf16[256,256]{1,0:T(8,128)(2,1)S(1)} collective-permute-done((bf16[256,256]{1,0:T(8,128)(2,1)S(1)}, bf16[256,256]{1,0:T(8,128)(2,1)S(1)}, u32[]{:S(2)}, u32[]{:S(2)}) %collective-permute-start.11) | collective-permute-done | bytes 131104 | tf_op jit(solution)/shard_map/ppermute | solution.py:376
  27.0 2.0 %shard_map.100 = (bf16[2,2,384,128]{3,2,1,0:T(8,128)(2,1)S(1)}, f32[2,2,384,128]{3,2,1,0:T(8,128)S(1)}) custom-call(bf16[4,768,256]{2,1,0:T(8,128)(2,1)S(1)} %get-tuple-element.62.normed, bf16[256,768]{1,0:T(8,128)(2,1)S(1)} %get-tuple-element.73.own.w0.q0, bf16[256,256]{1,0:T(8,128)(2,1)S(1)} %collective-permute-done.5.w1.q1, ...), custom_call_target="tpu_custom_call" | custom-call | flops 100000000 | bytes 300000 | tf_op jit(solution)/shard_map/pallas_call | solution.py:48
  29.8 1.6 %shard_map.101 = (bf16[2,2,384,128]{3,2,1,0:T(8,128)(2,1)S(1)}, bf16[2,2,384,128]{3,2,1,0:T(8,128)(2,1)S(1)}, bf16[2,272,128]{2,1,0:T(8,128)(2,1)S(1)}, bf16[2,2...) custom-call(bf16[2,272,128]{2,1,0:T(8,128)(2,1)S(1)} %collective-per, ...), custom_call_target="tpu_custom_call" | custom-call | flops 2000000000 | bytes 6000000 | tf_op jit(solution)/shard_map/pallas_call | solution.py:48
  31.4 1.6 %collective-permute-start.12 = (bf16[64,1024]{1,0:T(8,128)(2,1)S(1)}, bf16[64,1024]{1,0:T(8,128)(2,1)S(1)}, u32[]{:S(2)}, u32[]{:S(2)}) collective-permute-start(bf16[64,1024]{1,0:T(8,128)(2,1)S(1)} %get-tuple-element.84), channel_id=1, source_target_pairs={{0,2},{1,3},{2,0},{3,1},{4,6},{5,7},{6,4},{7,5},{8,10},{9,11},{10,... | collective-permute-start | bytes 393224 | tf_op jit(solution)/shard_map/ppermute | solution.py:376
  34.5 4.6 %collective-permute-start.16 = (bf16[2,288,128]{2,1,0:T(8,128)(2,1)S(1)}, bf16[2,288,128]{2,1,0:T(8,128)(2,1)S(1)}, u32[]{:S(2)}, u32[]{:S(2)}) collective-permute-start(bf16[2,288,128]{2,1,0:T(8,128)(2,1)S(1)} %get-tuple-element.89), channel_id=1, source_target_pairs={{0,8},{4,12},{8,0},{12,4},{1,9},{5,13},{9,1},{13,5},{2,10},{6,14},... | collective-permute-start | bytes 442376 | tf_op jit(solution)/shard_map/ppermute | solution.py:376
  40.4 2.1 %shard_map.103 = (bf16[2,384,256]{2,1,0:T(8,128)(2,1)S(1)}, f32[2,2,384,128]{3,2,1,0:T(8,128)S(1)}, f32[2,2,384,128]{3,2,1,0:T(8,128)S(1)}) custom-call(bf16[2,272,128]{2,1,0:T(8,128)(2,1)S(1)} %collective-permute-done.7.pair, bf16[2,256,128]{2,1,0:T(8,128)(2,1)S(1)} %get-tuple-element.91.before, bf16[2,272,128]{2,1,0:T(8,128)(2,1)S(1)} %collective-permute-done.8.middle, ...), custom_call_target="tpu_custom_call" | custom-call | flops 2000000000 | bytes 6000000 | tf_op jit(solution)/shard_map/pallas_call | solution.py:48
  42.4 1.5 %collective-permute-start.14 = (bf16[2,272,128]{2,1,0:T(8,128)(2,1)S(1)}, bf16[2,272,128]{2,1,0:T(8,128)(2,1)S(1)}, u32[]{:S(2)}, u32[]{:S(2)}) collective-permute-start(bf16[2,272,128]{2,1,0:T(8,128)(2,1)S(1)} %get-tuple-element.88), channel_id=1, source_target_pairs={{0,4},{4,0},{8,12},{12,8},{1,5},{5,1},{9,13},{13,9},{2,6},{6,2},{1... | collective-permute-start | bytes 417800 | tf_op jit(solution)/shard_map/ppermute | solution.py:376
  44.2 3.5 %collective-permute-start.21 = (bf16[64,1024]{1,0:T(8,128)(2,1)S(1)}, bf16[64,1024]{1,0:T(8,128)(2,1)S(1)}, u32[]{:S(2)}, u32[]{:S(2)}) collective-permute-start(bf16[64,1024]{1,0:T(8,128)(2,1)S(1)} %get-tuple-element.105), channel_id=1, source_target_pairs={{0,8},{4,12},{8,0},{12,4},{1,9},{5,13},{9,1},{13,5},{2,10},{6,14},... | collective-permute-start | bytes 393224 | tf_op jit(solution)/shard_map/ppermute | solution.py:376
  47.7 4.9 %collective-permute-done.16.further = bf16[2,288,128]{2,1,0:T(8,128)(2,1)S(1)} collective-permute-done((bf16[2,288,128]{2,1,0:T(8,128)(2,1)S(1)}, bf16[2,288,128]{2,1,0:T(8,128)(2,1)S(1)}, u32[]{:S(2)}, u32[]{:S(2)}) %collective-permute-start.16) | collective-permute-done | bytes 147488 | tf_op jit(solution)/shard_map/ppermute | solution.py:376
  52.6 2.7 %shard_map.104 = (f32[4,384,256]{2,1,0:T(8,128)S(1)}, bf16[4,384,256]{2,1,0:T(8,128)(2,1)S(1)}, bf16[384,1024]{1,0:T(8,128)(2,1)S(1)}) custom-call(bf16[2,272,128]{2,1,0:T(8,128)(2,1)S(1)} %collective-permute-done.14.pair, bf16[2,272,128]{2,1,0:T(8,128)(2,1)S(1)} %collective-permute-done.15.middle, bf16[2,288,128]{2,1,0:T(8,128)(2,1)S(1)} %collective-permute-done.16.further, ...), custom_call_target="tpu_custom_call" | custom-call | flops 2000000000 | bytes 6000000 | tf_op jit(solution)/shard_map/pallas_call | solution.py:48
  56.0 1.6 %collective-permute-done.17.partner = bf16[384,1024]{1,0:T(8,128)(2,1)S(1)} collective-permute-done((bf16[384,1024]{1,0:T(8,128)(2,1)S(1)}, bf16[384,1024]{1,0:T(8,128)(2,1)S(1)}, u32[]{:S(2)}, u32[]{:S(2)}) %collective-permute-start.17) | collective-permute-done | bytes 786464 | tf_op jit(solution)/shard_map/ppermute | solution.py:376
  57.6 1.5 %shard_map.105 = bf16[384,1024]{1,0:T(8,128)(2,1)} custom-call(bf16[384,1024]{1,0:T(8,128)(2,1)S(1)} %bitcast.14, bf16[384,1024]{1,0:T(8,128)(2,1)S(1)} %collective-permute-done.17.partner, bf16[2,2,384,128]{3,2,1,0:T(8,128)(2,1)S(1)} %get-tuple-element.96.mixed, bf16[256,768]{1,0:T(8,128)(2,1)S(1)} %get-tuple-element.73.own.w0.q0, ...), custom_call_target="tpu_custom_call" | custom-call | flops 2000000000 | bytes 6000000 | tf_op jit(solution)/shard_map/pallas_call | solution.py:48
  59.1 1.8 %shard_map.106 = bf16[384,1024]{1,0:T(8,128)(2,1)} custom-call(f32[4,384,256]{2,1,0:T(8,128)S(1)} %get-tuple-element.98.own, bf16[4,384,256]{2,1,0:T(8,128)(2,1)S(1)} %collective-permute-done.18.partner, bf16[384,1024]{1,0:T(8,128)(2,1)S(1)} %bitcast.15, bf16[384,1024]{1,0:T(8,128)(2,1)S(1)} %bitcast.9, f32[384,1]{1,0:T(8,128)S(1)} %get-tuple-element.100.inv_rms, ...), custom_call_target="tpu_custom_call" | custom-call | flops 2000000000 | bytes 6000000 | tf_op jit(solution)/shard_map/pallas_call | solution.py:48
  (54 shorter events, 9.8 us)
Async XLA Ops:
  0.6 5.8 %collective-permute-start = (bf16[384,1024]{1,0:T(8,128)(2,1)}, bf16[384,1024]{1,0:T(8,128)(2,1)S(1)}, u32[]{:S(2)}, u32[]{:S(2)}) collective-permute-start(bf16[384,1024]{1,0:T(8,128)(2,1)} %bitcast.12), channel_id=1, source_target_pairs={{0,1},{1,0},{2,3},{3,2},{4,5},{5,4},{6,7},{7,6},{8,9},{9,8},{10,11... | collective-permute-start | bytes 2359304 | tf_op jit(solution)/shard_map/ppermute | solution.py:376
  1.1 5.3 %collective-permute-start.2 = (bf16[384,1024]{1,0:T(8,128)(2,1)}, bf16[384,1024]{1,0:T(8,128)(2,1)S(1)}, u32[]{:S(2)}, u32[]{:S(2)}) collective-permute-start(bf16[384,1024]{1,0:T(8,128)(2,1)} %bitcast.6), channel_id=1, source_target_pairs={{0,1},{1,0},{2,3},{3,2},{4,5},{5,4},{6,7},{7,6},{8,9},{9,8},{10,11... | collective-permute-start | bytes 2359304 | tf_op jit(solution)/shard_map/ppermute | solution.py:376
  3.2 3.2 %collective-permute-start.1 = (bf16[272,512]{1,0:T(8,128)(2,1)S(1)}, bf16[272,512]{1,0:T(8,128)(2,1)S(1)}, u32[]{:S(2)}, u32[]{:S(2)}) collective-permute-start(bf16[272,512]{1,0:T(8,128)(2,1)S(1)} %get-tuple-element.57), channel_id=1, source_target_pairs={{0,1},{1,0},{2,3},{3,2},{4,5},{5,4},{6,7},{7,6},{8,9},{9,8},{10,11... | collective-permute-start | bytes 835592 | tf_op jit(solution)/shard_map/ppermute | solution.py:376
  3.7 6.4 %collective-permute-start.4 = (bf16[128,512]{1,0:T(8,128)(2,1)S(1)}, bf16[128,512]{1,0:T(8,128)(2,1)S(1)}, u32[]{:S(2)}, u32[]{:S(2)}) collective-permute-start(bf16[128,512]{1,0:T(8,128)(2,1)S(1)} %shard_map.94._), channel_id=1, source_target_pairs={{0,3},{1,2},{2,1},{3,0},{4,7},{5,6},{6,5},{7,4},{8,11},{9,10},{10,... | collective-permute-start | bytes 393224 | tf_op jit(solution)/shard_map/ppermute | solution.py:376
  6.4 9.9 %collective-permute-start.3 = (bf16[256,512]{1,0:T(8,128)(2,1)S(1)}, bf16[256,512]{1,0:T(8,128)(2,1)S(1)}, u32[]{:S(2)}, u32[]{:S(2)}) collective-permute-start(bf16[256,512]{1,0:T(8,128)(2,1)S(1)} %get-tuple-element.59.w0), channel_id=1, source_target_pairs={{0,2},{1,3},{2,0},{3,1},{4,6},{5,7},{6,4},{7,5},{8,10},{9,11},{10,... | collective-permute-start | bytes 786440 | tf_op jit(solution)/shard_map/ppermute | solution.py:376
  10.2 6.1 %collective-permute-start.5 = (bf16[256,256]{1,0:T(8,128)(2,1)S(1)}, bf16[256,256]{1,0:T(8,128)(2,1)S(1)}, u32[]{:S(2)}, u32[]{:S(2)}) collective-permute-start(bf16[256,256]{1,0:T(8,128)(2,1)S(1)} %get-tuple-element.67), channel_id=1, source_target_pairs={{0,1},{1,0},{2,3},{3,2},{4,5},{5,4},{6,7},{7,6},{8,9},{9,8},{10,11... | collective-permute-start | bytes 393224 | tf_op jit(solution)/shard_map/ppermute | solution.py:376
  10.5 5.8 %collective-permute-start.6 = (bf16[128,512]{1,0:T(8,128)(2,1)S(1)}, bf16[128,512]{1,0:T(8,128)(2,1)S(1)}, u32[]{:S(2)}, u32[]{:S(2)}) collective-permute-start(bf16[128,512]{1,0:T(8,128)(2,1)S(1)} %collective-permute-done.4.w3), channel_id=1, source_target_pairs={{0,16},{16,0},{1,17},{17,1},{2,18},{18,2},{3,19},{19,3},{4,20},{20... | collective-permute-start | bytes 393224 | tf_op jit(solution)/shard_map/ppermute | solution.py:376
  12.5 12.2 %collective-permute-start.10 = (bf16[256,768]{1,0:T(8,128)(2,1)S(1)}, bf16[256,768]{1,0:T(8,128)(2,1)S(1)}, u32[]{:S(2)}, u32[]{:S(2)}) collective-permute-start(bf16[256,768]{1,0:T(8,128)(2,1)S(1)} %get-tuple-element.73.own.w0.q0), channel_id=1, source_target_pairs={{0,2},{1,3},{2,0},{3,1},{4,6},{5,7},{6,4},{7,5},{8,10},{9,11},{10,... | collective-permute-start | bytes 1179656 | tf_op jit(solution)/shard_map/ppermute | solution.py:376
  16.3 8.4 %copy-start = (bf16[1,384,1024]{2,1,0:T(8,128)(2,1)S(1)}, bf16[1,384,1024]{2,1,0:T(8,128)(2,1)}, u32[]{:S(2)}) copy-start(bf16[1,384,1024]{2,1,0:T(8,128)(2,1)} %param.13) | copy-start | bytes 2359300
  17.4 12.4 %collective-permute-start.9 = (bf16[2,288,128]{2,1,0:T(8,128)(2,1)S(1)}, bf16[2,288,128]{2,1,0:T(8,128)(2,1)S(1)}, u32[]{:S(2)}, u32[]{:S(2)}) collective-permute-start(bf16[2,288,128]{2,1,0:T(8,128)(2,1)S(1)} %get-tuple-element.72), channel_id=1, source_target_pairs={{0,8},{4,12},{8,0},{12,4},{1,9},{5,13},{9,1},{13,5},{2,10},{6,14},... | collective-permute-start | bytes 442376 | tf_op jit(solution)/shard_map/ppermute | solution.py:376
  20.6 6.4 %collective-permute-start.11 = (bf16[256,256]{1,0:T(8,128)(2,1)S(1)}, bf16[256,256]{1,0:T(8,128)(2,1)S(1)}, u32[]{:S(2)}, u32[]{:S(2)}) collective-permute-start(bf16[256,256]{1,0:T(8,128)(2,1)S(1)} %get-tuple-element.67), channel_id=1, source_target_pairs={{0,3},{1,2},{2,1},{3,0},{4,7},{5,6},{6,5},{7,4},{8,11},{9,10},{10,... | collective-permute-start | bytes 393224 | tf_op jit(solution)/shard_map/ppermute | solution.py:376
  20.6 8.4 %collective-permute-start.8 = (bf16[2,272,128]{2,1,0:T(8,128)(2,1)S(1)}, bf16[2,272,128]{2,1,0:T(8,128)(2,1)S(1)}, u32[]{:S(2)}, u32[]{:S(2)}) collective-permute-start(bf16[2,272,128]{2,1,0:T(8,128)(2,1)S(1)} %get-tuple-element.71), channel_id=1, source_target_pairs={{4,8},{8,4},{5,9},{9,5},{6,10},{10,6},{7,11},{11,7},{20,24},{24,20... | collective-permute-start | bytes 417800 | tf_op jit(solution)/shard_map/ppermute | solution.py:387
  21.3 8.5 %collective-permute-start.7 = (bf16[2,272,128]{2,1,0:T(8,128)(2,1)S(1)}, bf16[2,272,128]{2,1,0:T(8,128)(2,1)S(1)}, u32[]{:S(2)}, u32[]{:S(2)}) collective-permute-start(bf16[2,272,128]{2,1,0:T(8,128)(2,1)S(1)} %get-tuple-element.71), channel_id=1, source_target_pairs={{0,4},{4,0},{8,12},{12,8},{1,5},{5,1},{9,13},{13,9},{2,6},{6,2},{1... | collective-permute-start | bytes 417800 | tf_op jit(solution)/shard_map/ppermute | solution.py:376
  31.4 7.8 %collective-permute-start.12 = (bf16[64,1024]{1,0:T(8,128)(2,1)S(1)}, bf16[64,1024]{1,0:T(8,128)(2,1)S(1)}, u32[]{:S(2)}, u32[]{:S(2)}) collective-permute-start(bf16[64,1024]{1,0:T(8,128)(2,1)S(1)} %get-tuple-element.84), channel_id=1, source_target_pairs={{0,2},{1,3},{2,0},{3,1},{4,6},{5,7},{6,4},{7,5},{8,10},{9,11},{10,... | collective-permute-start | bytes 393224 | tf_op jit(solution)/shard_map/ppermute | solution.py:376
  32.9 6.2 %collective-permute-start.13 = (bf16[2,32,1024]{2,1,0:T(8,128)(2,1)S(1)}, bf16[2,32,1024]{2,1,0:T(8,128)(2,1)S(1)}, u32[]{:S(2)}, u32[]{:S(2)}) collective-permute-start(bf16[2,32,1024]{2,1,0:T(8,128)(2,1)S(1)} %get-tuple-element.85), channel_id=1, source_target_pairs={{0,4},{4,0},{8,12},{12,8},{1,5},{5,1},{9,13},{13,9},{2,6},{6,2},{1... | collective-permute-start | bytes 393224 | tf_op jit(solution)/shard_map/ppermute | solution.py:376
  33.7 14.1 %collective-permute-start.15 = (bf16[2,272,128]{2,1,0:T(8,128)(2,1)S(1)}, bf16[2,272,128]{2,1,0:T(8,128)(2,1)S(1)}, u32[]{:S(2)}, u32[]{:S(2)}) collective-permute-start(bf16[2,272,128]{2,1,0:T(8,128)(2,1)S(1)} %get-tuple-element.88), channel_id=1, source_target_pairs={{4,8},{8,4},{5,9},{9,5},{6,10},{10,6},{7,11},{11,7},{20,24},{24,20... | collective-permute-start | bytes 417800 | tf_op jit(solution)/shard_map/ppermute | solution.py:387
  34.5 18.1 %collective-permute-start.16 = (bf16[2,288,128]{2,1,0:T(8,128)(2,1)S(1)}, bf16[2,288,128]{2,1,0:T(8,128)(2,1)S(1)}, u32[]{:S(2)}, u32[]{:S(2)}) collective-permute-start(bf16[2,288,128]{2,1,0:T(8,128)(2,1)S(1)} %get-tuple-element.89), channel_id=1, source_target_pairs={{0,8},{4,12},{8,0},{12,4},{1,9},{5,13},{9,1},{13,5},{2,10},{6,14},... | collective-permute-start | bytes 442376 | tf_op jit(solution)/shard_map/ppermute | solution.py:376
  39.2 4.7 %collective-permute-start.19 = (bf16[32,1024]{1,0:T(8,128)(2,1)S(1)}, bf16[32,1024]{1,0:T(8,128)(2,1)S(1)}, u32[]{:S(2)}, u32[]{:S(2)}) collective-permute-start(bf16[32,1024]{1,0:T(8,128)(2,1)S(1)} %get-tuple-element.102), channel_id=1, source_target_pairs={{0,4},{4,0},{8,12},{12,8},{1,5},{5,1},{9,13},{13,9},{2,6},{6,2},{1... | collective-permute-start | bytes 196616 | tf_op jit(solution)/shard_map/ppermute | solution.py:376
  39.9 4.3 %collective-permute-start.20 = (bf16[32,1024]{1,0:T(8,128)(2,1)S(1)}, bf16[32,1024]{1,0:T(8,128)(2,1)S(1)}, u32[]{:S(2)}, u32[]{:S(2)}) collective-permute-start(bf16[32,1024]{1,0:T(8,128)(2,1)S(1)} %get-tuple-element.103), channel_id=1, source_target_pairs={{0,2},{1,3},{2,0},{3,1},{4,6},{5,7},{6,4},{7,5},{8,10},{9,11},{10,... | collective-permute-start | bytes 196616 | tf_op jit(solution)/shard_map/ppermute | solution.py:376
  42.4 10.2 %collective-permute-start.14 = (bf16[2,272,128]{2,1,0:T(8,128)(2,1)S(1)}, bf16[2,272,128]{2,1,0:T(8,128)(2,1)S(1)}, u32[]{:S(2)}, u32[]{:S(2)}) collective-permute-start(bf16[2,272,128]{2,1,0:T(8,128)(2,1)S(1)} %get-tuple-element.88), channel_id=1, source_target_pairs={{0,4},{4,0},{8,12},{12,8},{1,5},{5,1},{9,13},{13,9},{2,6},{6,2},{1... | collective-permute-start | bytes 417800 | tf_op jit(solution)/shard_map/ppermute | solution.py:376
  44.2 11.7 %collective-permute-start.21 = (bf16[64,1024]{1,0:T(8,128)(2,1)S(1)}, bf16[64,1024]{1,0:T(8,128)(2,1)S(1)}, u32[]{:S(2)}, u32[]{:S(2)}) collective-permute-start(bf16[64,1024]{1,0:T(8,128)(2,1)S(1)} %get-tuple-element.105), channel_id=1, source_target_pairs={{0,8},{4,12},{8,0},{12,4},{1,9},{5,13},{9,1},{13,5},{2,10},{6,14},... | collective-permute-start | bytes 393224 | tf_op jit(solution)/shard_map/ppermute | solution.py:376
  55.3 2.4 %collective-permute-start.17 = (bf16[384,1024]{1,0:T(8,128)(2,1)S(1)}, bf16[384,1024]{1,0:T(8,128)(2,1)S(1)}, u32[]{:S(2)}, u32[]{:S(2)}) collective-permute-start(bf16[384,1024]{1,0:T(8,128)(2,1)S(1)} %get-tuple-element.97), channel_id=1, source_target_pairs={{0,1},{1,0},{2,3},{3,2},{4,5},{5,4},{6,7},{7,6},{8,9},{9,8},{10,11... | collective-permute-start | bytes 2359304 | tf_op jit(solution)/shard_map/ppermute | solution.py:376
  55.4 3.8 %collective-permute-start.18 = (bf16[4,384,256]{2,1,0:T(8,128)(2,1)S(1)}, bf16[4,384,256]{2,1,0:T(8,128)(2,1)S(1)}, u32[]{:S(2)}, u32[]{:S(2)}) collective-permute-start(bf16[4,384,256]{2,1,0:T(8,128)(2,1)S(1)} %get-tuple-element.99), channel_id=1, source_target_pairs={{0,1},{1,0},{2,3},{3,2},{4,5},{5,4},{6,7},{7,6},{8,9},{9,8},{10,11... | collective-permute-start | bytes 2359304 | tf_op jit(solution)/shard_map/ppermute | solution.py:376
  55.9 5.5 %collective-permute-start.22 = (bf16[64,1024]{1,0:T(8,128)(2,1)S(1)}, bf16[64,1024]{1,0:T(8,128)(2,1)S(1)}, u32[]{:S(2)}, u32[]{:S(2)}) collective-permute-start(bf16[64,1024]{1,0:T(8,128)(2,1)S(1)} %get-tuple-element.110), channel_id=1, source_target_pairs={{0,4},{4,0},{8,12},{12,8},{1,5},{5,1},{9,13},{13,9},{2,6},{6,2},{1... | collective-permute-start | bytes 393224 | tf_op jit(solution)/shard_map/ppermute | solution.py:376
  (7 other events, 19.3 us)

commit v6 on v5

--- a/solution.py
+++ b/solution.py
@@ -14,7 +14,7 @@
 ID_ROWS = 16
 
 epsilon = 1e-06
-W1, W2, W3, PREP, QUERY, MIXED, BACK, PROJECT, SPLIT = 8.0, 8.0, 8.0, 20.0, 0.1, 0.1, 2.0, 2.0, 20.0
+W1, W2, W3, PREP, QUERY, MIXED, BACK, PROJECT, SPLIT, FILL = 8.0, 8.0, 8.0, 20.0, 0.5, 0.1, 0.1, 2.0, 20.0, 2.0
 
 f32 = jnp.float32
 bf16 = jnp.bfloat16
@@ -94,17 +94,14 @@
     copies = []
     for target, which in ((mine, c), (other, 1 - c)):
         copies += [(w.at[:, kv_columns(n, which)], target.at[:rows, head(n)]) for n in range(4)]
+    copies += [(w.at[:, columns(2 * g + 1 - c, HEAD_DIM)], other.at[:rows, head(4 + g)]) for g in range(2)]
     run_all(copies, sem)
 
 
-def split_q_body(w, w_out, far, other, sem):
+def split_q_body(w, mine, other, sem):
     c = lax.axis_index("dp") % 2
-    rows, half = w_out.shape[0], w_out.shape[1] // 2
-    copies = [
-        (w_out.at[:, :half], far.at[:rows, 2 * HEAD_DIM :]),
-        (w_out.at[:, half:], far.at[rows:, 2 * HEAD_DIM :]),
-    ]
-    for target, which in ((far, c), (other, 1 - c)):
+    copies = []
+    for target, which in ((mine, c), (other, 1 - c)):
         copies += [(w.at[:, columns(2 * g + which, HEAD_DIM)], target.at[:, head(g)]) for g in range(2)]
     run_all(copies, sem)
 
@@ -121,12 +118,8 @@
     )(w, *rest)
 
 
-FAR_Q = slice(0, 2 * HEAD_DIM)
-
-
-def out_rows(far):
-    rows = far.shape[0] // 2
-    return far[:rows, 2 * HEAD_DIM :], far[rows:, 2 * HEAD_DIM :]
+KV_COLUMNS = slice(0, 4 * HEAD_DIM)
+PAIR_Q = slice(4 * HEAD_DIM, 6 * HEAD_DIM)
 
 
 def halves():
@@ -141,9 +134,9 @@
     return (at % 2 == 1, at >= 2) if step > 0 else (at % 2 == 0, at < 2)
 
 
-def prep_body(tokens, partner, seg, gain, w0, w1, normed, inv_rms, seg_col, seg_row, raw):
-    length = seg.shape[1]
-    for i, (part, ids) in enumerate(((tokens, seg[...].astype(f32)), (partner, w1[w0.shape[0] : w0.shape[0] + 1, :length].astype(f32)))):
+def prep_body(tokens, partner, gain, w0, normed, inv_rms, raw):
+    length = tokens.shape[0]
+    for i, part in enumerate((tokens, partner)):
         x = part[...].astype(f32)
         inv = lax.rsqrt(jnp.mean(x * x, axis=1, keepdims=True) + epsilon)
         if i == 0:
@@ -151,29 +144,29 @@
         for j in range(4):
             at = columns(lax.axis_index("dp") ^ j, 256)
             normed[j, i * length : (i + 1) * length] = (part[:, at].astype(f32) * inv * gain[:, at]).astype(bf16)
+    raw[...] = dot_nn(normed[0], w0[...])
+
+
+def store_state(targets, i, g, value):
+    for target in targets:
+        target[i, head(g), :] = value.astype(bf16)
+
+
+def store_ids(targets, i, ids):
+    for target in targets:
+        rows = target.shape[1] - 2 * HEAD_DIM
+        target[i, 2 * HEAD_DIM :, :] = jnp.broadcast_to(ids, (rows, HEAD_DIM)).astype(bf16)
+
+
+def kv_body(near, normed, seg, w1, w2, w3, w3_other, feat_k, values, state, state_mid, state_far, seg_col, seg_row):
+    shard_rows, length = w2.shape[0], seg.shape[1]
+    for i, ids in enumerate((seg[...].astype(f32), w1[shard_rows : shard_rows + 1, :length].astype(f32))):
         seg_row[i] = ids
         seg_col[i] = jnp.broadcast_to(ids, (HEAD_DIM, length)).T
-    rows = w0.shape[0]
-    raw[...] = dot_nn(normed[0], w0[...]) + dot_nn(normed[1], w1[:rows])
-
-
-def store_state(state, state_far, i, g, value):
-    for target in (state, state_far):
-        target[i, head(g), :] = value.astype(bf16)
-
-
-def store_ids(state, state_far, i, ids):
-    for target in (state, state_far):
-        rows = target.shape[1] - 2 * HEAD_DIM
-        target[i, 2 * HEAD_DIM :, :] = jnp.broadcast_to(ids, (rows, HEAD_DIM)).astype(bf16)
-
-
-def kv_body(near, normed, w2, w3, w3_other, seg_col, feat_k, values, state, state_far):
-    raw = near[...] + dot_nn(normed[2], w2[...])
+    raw = near[...] + dot_nn(normed[1], w1[:shard_rows, KV_COLUMNS]) + dot_nn(normed[2], w2[...])
     for at, w in zip(halves(), (w3, w3_other)):
         raw += dot_nn(normed[3, :, columns(at, w.shape[0])], w[...])
     raw = raw.astype(bf16)
-    length = seg_col.shape[1]
     for i in range(2):
         last = seg_col[i, length - 1 : length, :]
         tail = seg_col[i] == last
@@ -183,13 +176,13 @@
             v = raw[rows, head(2 + g)]
             feat_k[i, g] = k.astype(bf16)
             values[i, g] = v
-            store_state(state, state_far, i, g, dot_tn(jnp.where(tail, k, 0.0).astype(bf16), v))
-        store_ids(state, state_far, i, last)
+            store_state((state, state_mid, state_far), i, g, dot_tn(jnp.where(tail, k, 0.0).astype(bf16), v))
+        store_ids((state, state_mid, state_far), i, last)
 
 
 def query_body(normed, w0, w1, w2, w3, feat_k, values, seg_col, seg_row, feat_q, intra):
-    raw = dot_nn(normed[0], w0[:, FAR_Q]) + dot_nn(normed[1], w1[...])
-    raw += dot_nn(normed[2], w2[:, FAR_Q]) + dot_nn(normed[3], w3[...])
+    raw = dot_nn(normed[0], w0[...]) + dot_nn(normed[1], w1[: w0.shape[0], PAIR_Q])
+    raw += dot_nn(normed[2], w2[...]) + dot_nn(normed[3], w3[...])
     raw = raw.astype(bf16)
     length = seg_row.shape[2]
     for i in range(2):
@@ -205,15 +198,15 @@
     for j, o in enumerate((own, other)):
         full = lax.axis_index("dp") ^ (2 * j)
         for i, part in enumerate((cot, cot_partner)):
-            value = sum(dot_nt(part[:, n * 512 : (n + 1) * 512], half) for n, half in enumerate(out_rows(o)))
-            upstream[i, full // 2] = value * gain[:, columns(full, HEAD_DIM)]
+            upstream[i, full // 2] = dot_nt(part[...], o[...]) * gain[:, columns(full, HEAD_DIM)]
 
 
 def received(step, pair, middle, further, i):
     use_pair, use_further = sources(step)
-    near = jnp.where(use_pair, pair[i].astype(f32), middle[i].astype(f32))
+    used = 2 * HEAD_DIM + ID_ROWS
+    near = jnp.where(use_pair, pair[i, :used].astype(f32), middle[i, :used].astype(f32))
     ids = near[2 * HEAD_DIM : 2 * HEAD_DIM + 1, :]
-    far = further[i].astype(f32)
+    far = further[i, :used].astype(f32)
     same = (far[2 * HEAD_DIM : 2 * HEAD_DIM + 1, :] == ids) & use_further
     total = near[: 2 * HEAD_DIM] + jnp.where(same, far[: 2 * HEAD_DIM], 0.0)
     return ids, total.astype(bf16)
@@ -221,7 +214,7 @@
 
 def attn_body(
     pair, middle, further, seg_col, feat_q, intra, upstream, gain, cot, cot_partner,
-    mixed, d_attn, state, state_far, before, rest, a_send, b_send,
+    mixed, d_attn, state, state_mid, state_far, before, rest, a_send, b_send,
 ):
     for i in range(2):
         first = seg_col[i, 0:1, :]
@@ -238,8 +231,8 @@
             inner = jnp.mean(attention * up, axis=1, keepdims=True)
             da = (ratio * up - ratio**3 * attention * inner).astype(bf16)
             d_attn[i, g] = da
-            store_state(state, state_far, i, g, dot_tn(jnp.where(begin, q.astype(f32), 0.0).astype(bf16), da))
-        store_ids(state, state_far, i, first)
+            store_state((state, state_mid, state_far), i, g, dot_tn(jnp.where(begin, q.astype(f32), 0.0).astype(bf16), da))
+        store_ids((state, state_mid, state_far), i, first)
     half = HEAD_DIM // 2
     quarter = half // 2
     second = lax.axis_index("seq") % 2 == 1
@@ -308,24 +301,17 @@
             dv_intra[i, g] = dot_tn(s, da)
 
 
-def output_body(tokens, partner, mixed, own, other, output):
+def partner_output_body(mixed, own, other, out_partner):
     x = lax.axis_index("dp") // 2
-    for n, (a, b) in enumerate(zip(out_rows(own), out_rows(other))):
-        at = slice(n * 512, (n + 1) * 512)
-        total = dot_nn(mixed[0, x], a) + dot_nn(mixed[0, 1 - x], b)
-        output[:, at] = (tokens[:, at].astype(f32) + (total + partner[:, at].astype(f32))).astype(bf16)
+    out_partner[...] = (dot_nn(mixed[1, x], own[...]) + dot_nn(mixed[1, 1 - x], other[...])).astype(bf16)
 
 
 def project_back_body(
     pair, middle, further, seg_col, feat_k, values, dk_intra, dv_intra, d_query,
-    q0, q1, q2, q3, w0, w1, w2, w3, w3_other, mixed, own, partner, out_partner, work,
+    q0, q1, q2, q3, w0, w1, w2, w3, w3_other, own, partner, work,
 ):
-    x = lax.axis_index("dp") // 2
-    for n, (a, b) in enumerate(zip(out_rows(q0), out_rows(q2))):
-        out_partner[:, n * 512 : (n + 1) * 512] = (dot_nn(mixed[1, x], a) + dot_nn(mixed[1, 1 - x], b)).astype(bf16)
-    rows = w0.shape[0]
-    q = (q0[:, FAR_Q], q1[...], q2[:, FAR_Q], q3[...])
-    w = (w0[...], w1[:rows], w2[...])
+    q = (q0[...], q1[: w0.shape[0], PAIR_Q], q2[...], q3[...])
+    w = (w0[...], w1[: w0.shape[0], KV_COLUMNS], w2[...])
     for i in (1, 0):
         ids, total = received(-1, pair, middle, further, i)
         take = seg_col[i] == ids
@@ -355,7 +341,12 @@
                 own[j, :, at] += value
 
 
-def final_body(own, partner, tokens, cot, inv_rms, gain, grad, work):
+def final_body(
+    own, partner, out_partner, tokens, cot, inv_rms, gain, mixed, w_own, w_other, output, grad, work
+):
+    x = lax.axis_index("dp") // 2
+    total = dot_nn(mixed[0, x], w_own[...]) + dot_nn(mixed[0, 1 - x], w_other[...])
+    output[...] = (tokens[...].astype(f32) + (total + out_partner[...].astype(f32))).astype(bf16)
     inner = None
     for j in range(4):
         at = columns(lax.axis_index("dp") ^ j, 256)
@@ -381,11 +372,11 @@
     return lax.ppermute(array, axis, [(i, i + step) for i in range(n) if 0 <= i + step < n])
 
 
-def carry(message, longer, ends, step, late=None):
+def carry(message, middle, further, ends, step, late=None):
     n = lax.axis_size("seq")
     if n == 4:
-        middle = lax.ppermute(message, "seq", [(1, 2), (2, 1)])
-        return flip(message if late is None else late, "seq", 1), middle, flip(longer, "seq", 2)
+        middle = lax.ppermute(middle, "seq", [(1, 2), (2, 1)])
+        return flip(message if late is None else late, "seq", 1), middle, flip(further, "seq", 2)
     position = lax.axis_index("seq")
     begin, end = (ends[0], ends[1]) if step > 0 else (ends[1], ends[0])
     total = message[:, : 2 * HEAD_DIM].astype(f32)
@@ -414,14 +405,15 @@
         rest, flip(a_send, "dp", 2), flip(b_send, "seq", 1), us=W1,
     )
     a_send, back_late = lax.optimization_barrier((a_send, back[0]))
-    back_near = carry(back[0], back[1], ends, -1, back_late)
+    back_near = carry(*back, ends, -1, back_late)
     outs = [((half, width), f32), ((half, width), bf16)]
     kept, send = call(weight_two_body, outs, kept, flip(a_send, "seq", 1), flip(b_send, "dp", 2), us=W2)
+    send, d_attn = lax.optimization_barrier((send, d_attn))
     reach = 2
     while reach < n:
         kept, send = call(weight_three_body, outs, kept, flip(send, "seq", reach), us=W3)
         reach *= 2
-    return kept, flip(send, "seq", 1), back_near, d_attn
+    return kept, send, back_near, d_attn
 
 
 def shards(tokens, segment_ids, norm_gain, w_qkv, head_gain, w_out, cotangent):
@@ -439,56 +431,47 @@
     kv_diagonal = flip(kv_half, "dp", 3)
     kv_mine, kv_other = split(
         split_kv_body,
-        [(shard_rows, 4 * HEAD_DIM), (shard_rows + ID_ROWS, 4 * HEAD_DIM)],
-        8, SPLIT, w_qkv, segment_ids, kv_half, specs=(VMEM, ANY),
-    )
+        [(shard_rows, 4 * HEAD_DIM), (shard_rows + ID_ROWS, 6 * HEAD_DIM)],
+        10, SPLIT, w_qkv, segment_ids, kv_half, specs=(VMEM, ANY),
+    )
+    kv_half, flat, cot = lax.optimization_barrier((kv_half, flat, cot))
     kv_x, kv_pair = flip(kv_mine, "dp", 2), flip(kv_other, "dp", 1)
     partner, cot_partner = flip(flat, "dp", 1), flip(cot, "dp", 1)
-    partner, kv_pair, cot_partner, w_late = lax.optimization_barrier((partner, kv_pair, cot_partner, w_qkv))
-    normed, inv_rms, seg_col, seg_row, raw_near = call(
+    kv_diagonal_other = flip(kv_diagonal, "groups", 1)
+    kv_diagonal, partner, cot_partner, w_late = lax.optimization_barrier((kv_diagonal, partner, cot_partner, w_qkv))
+    normed, inv_rms, raw_near = call(
         prep_body,
-        [
-            ((4, 2 * length, D // 4), bf16),
-            ((length, 1), f32),
-            ((2, length, HEAD_DIM), f32),
-            ((2, 1, length), f32),
-            ((2 * length, 4 * HEAD_DIM), f32),
-        ],
-        flat, partner, segment_ids, gain, kv_mine, kv_pair, us=PREP,
-    )
-    far_own, q_other = split(
-        split_q_body, [(shard_rows, 6 * HEAD_DIM), (shard_rows, 2 * HEAD_DIM)], 6, 1.0, w_late, w_out, specs=(ANY,)
-    )
-    kv_diagonal, inv_rms, far_own, q_other = lax.optimization_barrier((kv_diagonal, inv_rms, far_own, q_other))
-    kv_diagonal_other = flip(kv_diagonal, "groups", 1)
-    far_x = flip(far_own, "dp", 2)
-    kv_x, q_pair = lax.optimization_barrier((kv_x, flip(q_other, "dp", 1)))
-    wq = [far_own, q_pair, far_x, flip(q_other, "dp", 3)]
+        [((4, 2 * length, D // 4), bf16), ((length, 1), f32), ((2 * length, 4 * HEAD_DIM), f32)],
+        flat, partner, gain, kv_mine, us=PREP,
+    )
+    q_mine, q_other = split(split_q_body, [(shard_rows, 2 * HEAD_DIM)] * 2, 4, 1.0, w_late)
+    inv_rms, q_mine, q_other, out_own, kv_pair = lax.optimization_barrier((inv_rms, q_mine, q_other, w_out, kv_pair))
+    wq = [q_mine, kv_pair, flip(q_mine, "dp", 2), flip(q_other, "dp", 3)]
     kv = [kv_mine, kv_pair, kv_x, kv_diagonal, kv_diagonal_other]
-    out = [far_own, far_x]
-
-    message = ((2, 2 * HEAD_DIM + ID_ROWS, HEAD_DIM), bf16)
-    longer = ((2, 2 * HEAD_DIM + 2 * ID_ROWS, HEAD_DIM), bf16)
-    feat_k, values, state, state_far = call(
-        kv_body, [(wide, bf16), (wide, bf16), message, longer], raw_near, normed, *kv[2:], seg_col
+    out = [out_own, flip(out_own, "dp", 2)]
+
+    messages = [((2, 2 * HEAD_DIM + m * ID_ROWS, HEAD_DIM), bf16) for m in (1, 1, 2)]
+    feat_k, values, state, state_mid, state_far, seg_col, seg_row = call(
+        kv_body,
+        [(wide, bf16), (wide, bf16), *messages, ((2, length, HEAD_DIM), f32), ((2, 1, length), f32)],
+        raw_near, normed, segment_ids, *kv[1:],
     )
     ends = jnp.stack([seg_col[:, 0, 0], seg_col[:, -1, 0]])
-    near = carry(state, state_far, ends, 1)
+    near = carry(state, state_mid, state_far, ends, 1)
+    feat_q, intra = call(
+        query_body, [(wide, bf16), (wide, f32)], normed, *wq, feat_k, values, seg_col, seg_row, us=QUERY
+    )
+    feat_q, cot_late = lax.optimization_barrier((feat_q, cot_partner))
     (upstream,) = call(
-        mixed_grad_body, [(wide, f32)], cot, cot_partner, *out, gain_h, us=MIXED
-    )
-    upstream, feat_k, feat_k_late = lax.optimization_barrier((upstream, feat_k, feat_k))
-    feat_q, intra = call(
-        query_body, [(wide, bf16), (wide, f32)], normed, *wq, feat_k_late, values, seg_col, seg_row, us=QUERY
+        mixed_grad_body, [(wide, f32)], cot, cot_late, *out, gain_h, us=MIXED
     )
     rows = HEAD_DIM // 2
-    mixed, d_attn, back, back_far, before, rest, a_send, b_send = call(
+    mixed, d_attn, back, back_mid, back_far, before, rest, a_send, b_send = call(
         attn_body,
         [
             (wide, bf16),
             (wide, bf16),
-            message,
-            longer,
+            *messages,
             ((2, 2 * HEAD_DIM, HEAD_DIM), bf16),
             ((2 * rows, D), f32),
             ((rows, D), bf16),
@@ -497,29 +480,27 @@
         *near, seg_col, feat_q, intra, upstream, gain_h, cot, cot_partner,
     )
     scale = 1.0 / math.sqrt(length * lax.axis_size("dp") * n)
-    kept, arrived, back_near, d_attn = reduce_weight(rest, a_send, b_send, (back, back_far), ends, d_attn)
+    kept, sent, back_near, d_attn = reduce_weight(rest, a_send, b_send, (back, back_mid, back_far), ends, d_attn)
+    (out_partner,) = call(partner_output_body, [((length, D), bf16)], mixed, *out, us=FILL)
     d_query, dk_intra, dv_intra = call(
         back_body,
         [((2, length, 2 * HEAD_DIM), bf16), (wide, f32), (wide, f32)],
         near[0], before, near[1], seg_col, seg_row, d_attn, values, feat_k, feat_q, us=BACK,
     )
-    own, theirs, out_partner = call(
+    own, theirs = call(
         project_back_body,
-        [((4, length, D // 4), f32), ((4, length, D // 4), bf16), ((length, D), bf16)],
+        [((4, length, D // 4), f32), ((4, length, D // 4), bf16)],
         *back_near, seg_col, feat_k, values, dk_intra, dv_intra, d_query,
-        *wq, *kv, mixed, us=PROJECT, scratch=[((4, length, D // 4), f32)],
-    )
-    (output,) = call(
-        output_body,
-        [((length, D), bf16)],
-        flat, flip(out_partner, "dp", 1), mixed, *out,
-    )
-    (grad,) = call(
+        *wq, *kv, us=PROJECT, scratch=[((4, length, D // 4), f32)],
+    )
+    theirs, out_partner = lax.optimization_barrier((theirs, out_partner))
+    output, grad = call(
         final_body,
-        [((length, D), bf16)],
-        own, flip(theirs, "dp", 1), flat, cot, inv_rms, gain,
+        [((length, D), bf16), ((length, D), bf16)],
+        own, flip(theirs, "dp", 1), flip(out_partner, "dp", 1), flat, cot, inv_rms, gain, mixed, *out,
         scratch=[((4, length, D // 4), f32)],
     )
+    arrived = flip(sent, "seq", 1)
     output, grad, kept = lax.optimization_barrier((output, grad, kept))
     (grad_out_weight,) = call(
         functools.partial(weight_last_body, scale), [((HEAD_DIM, D), f32)], kept, arrived

time: 62.5 us -> 58.7 us (0.939)
  waiting for transfers between devices: 14.6 us -> 9.94 us
  starting transfers between devices: 28.9 us -> 30.8 us
  Pallas kernels: 16.1 us -> 15.3 us
    ppermute x21, waiting for transfers between devices: 14.6 us -> 9.93 us  [flip(): return lax.ppermute(array, axis, [(i, i ^ bit) for i in range(n)])]
    ppermute x21, starting transfers between devices: 27.4 us -> 29.3 us  [flip(): return lax.ppermute(array, axis, [(i, i ^ bit) for i in range(n)])]
    pallas_call x13, Pallas kernels: 15.7 us -> 14.9 us  [call(): pl.pallas_call(body, out_shape=[jax.ShapeDtypeStruct(shape, dtype) for sh...]
  transfers between devices with their start and end apart: 23 -> 23, of which waited for: 9 -> 8; matrix products, arithmetic and copies ran while one was open for 0% -> 0% of each run, Pallas kernels for 22% -> 22%
where the time goes in v6:
time: 58.7 us; the launch traced here: 58.4 us
  starting transfers between devices  30.8 us (52%)
  Pallas kernels  15.3 us (26%)
  waiting for transfers between devices  9.94 us (17%)
  local copies, waits for them, and re-layouts  1.52 us (3%)
  between operations  0.85 us (1%)
    ppermute x21, starting transfers between devices, flip(): return lax.ppermute(array, axis, [(i, i ^ bit) for i in range(n)])  29.3 us
    pallas_call x13, Pallas kernels, call(): pl.pallas_call(body, out_shape=[jax.ShapeDtypeStruct(shape, dtype) for sh...  14.9 us
    ppermute x21, waiting for transfers between devices, flip(): return lax.ppermute(array, axis, [(i, i ^ bit) for i in range(n)])  9.93 us
    unnamed x16, local copies, waits for them, and re-layouts  1.52 us
    ppermute x2, starting transfers between devices, carry(): middle = lax.ppermute(middle, 'seq', [(1, 2), (2, 1)])  1.5 us
  transfers between devices with their start and end apart: 23, of which 8 were waited for; matrix products, arithmetic and copies ran while one was open for 0% of the time, Pallas kernels for 22%

profile of v6, /device:TPU:0, one launch (start us, length us, event | category | flops | bytes accessed | tf_op | source)
XLA Modules:
  0.0 58.4 jit_solution(5156842288542968156)
XLA Ops:
  0.7 1.2 %copy-done.3 = bf16[256,1536]{1,0:T(8,128)(2,1)S(1)} copy-done((bf16[256,1536]{1,0:T(8,128)(2,1)S(1)}, bf16[256,1536]{1,0:T(8,128)(2,1)}, u32[]{:S(2)}) %copy-start.3) | copy-done | bytes 786456
  1.9 2.4 %collective-permute-start = (bf16[128,512]{1,0:T(8,128)(2,1)S(1)}, bf16[128,512]{1,0:T(8,128)(2,1)S(1)}, u32[]{:S(2)}, u32[]{:S(2)}) collective-permute-start(bf16[128,512]{1,0:T(8,128)(2,1)S(1)} %shard_map.94._), channel_id=1, source_target_pairs={{0,3},{1,2},{2,1},{3,0},{4,7},{5,6},{6,5},{7,4},{8,11},{9,10},{10,... | collective-permute-start | bytes 393224 | tf_op jit(solution)/shard_map/ppermute | solution.py:367
  5.4 1.4 %collective-permute-start.4 = (bf16[256,512]{1,0:T(8,128)(2,1)S(1)}, bf16[256,512]{1,0:T(8,128)(2,1)S(1)}, u32[]{:S(2)}, u32[]{:S(2)}) collective-permute-start(bf16[256,512]{1,0:T(8,128)(2,1)S(1)} %get-tuple-element.67.w0), channel_id=1, source_target_pairs={{0,2},{1,3},{2,0},{3,1},{4,6},{5,7},{6,4},{7,5},{8,10},{9,11},{10,... | collective-permute-start | bytes 786440 | tf_op jit(solution)/shard_map/ppermute | solution.py:367
  6.8 1.5 %collective-permute-done.w3 = bf16[128,512]{1,0:T(8,128)(2,1)S(1)} collective-permute-done((bf16[128,512]{1,0:T(8,128)(2,1)S(1)}, bf16[128,512]{1,0:T(8,128)(2,1)S(1)}, u32[]{:S(2)}, u32[]{:S(2)}) %collective-permute-start) | collective-permute-done | bytes 131104 | tf_op jit(solution)/shard_map/ppermute | solution.py:367
  8.3 2.4 %collective-permute-start.5 = (bf16[128,512]{1,0:T(8,128)(2,1)S(1)}, bf16[128,512]{1,0:T(8,128)(2,1)S(1)}, u32[]{:S(2)}, u32[]{:S(2)}) collective-permute-start(bf16[128,512]{1,0:T(8,128)(2,1)S(1)} %collective-permute-done.w3), channel_id=1, source_target_pairs={{0,16},{16,0},{1,17},{17,1},{2,18},{18,2},{3,19},{19,3},{4,20},{20... | collective-permute-start | bytes 393224 | tf_op jit(solution)/shard_map/ppermute | solution.py:367
  12.0 1.0 %collective-permute-start.10 = (bf16[256,256]{1,0:T(8,128)(2,1)S(1)}, bf16[256,256]{1,0:T(8,128)(2,1)S(1)}, u32[]{:S(2)}, u32[]{:S(2)}) collective-permute-start(bf16[256,256]{1,0:T(8,128)(2,1)S(1)} %get-tuple-element.82), channel_id=1, source_target_pairs={{0,3},{1,2},{2,1},{3,0},{4,7},{5,6},{6,5},{7,4},{8,11},{9,10},{10,... | collective-permute-start | bytes 393224 | tf_op jit(solution)/shard_map/ppermute | solution.py:367
  13.6 1.4 %collective-permute-start.11 = (bf16[128,1024]{1,0:T(8,128)(2,1)S(1)}, bf16[128,1024]{1,0:T(8,128)(2,1)S(1)}, u32[]{:S(2)}, u32[]{:S(2)}) collective-permute-start(bf16[128,1024]{1,0:T(8,128)(2,1)S(1)} %copy-done.1), channel_id=1, source_target_pairs={{0,2},{1,3},{2,0},{3,1},{4,6},{5,7},{6,4},{7,5},{8,10},{9,11},{10,... | collective-permute-start | bytes 786440 | tf_op jit(solution)/shard_map/ppermute | solution.py:367
  15.0 1.4 %shard_map.98 = (bf16[2,2,384,128]{3,2,1,0:T(8,128)(2,1)S(1)}, bf16[2,2,384,128]{3,2,1,0:T(8,128)(2,1)S(1)}, bf16[2,272,128]{2,1,0:T(8,128)(2,1)S(1)}, bf16[2,27...) custom-call(f32[768,512]{1,0:T(8,128)S(1)} %get-tuple-element.68.nea, ...), custom_call_target="tpu_custom_call" | custom-call | flops 2000000000 | bytes 6000000 | tf_op jit(solution)/shard_map/pallas_call | solution.py:48
  16.4 2.7 %collective-permute-start.8 = (bf16[2,288,128]{2,1,0:T(8,128)(2,1)S(1)}, bf16[2,288,128]{2,1,0:T(8,128)(2,1)S(1)}, u32[]{:S(2)}, u32[]{:S(2)}) collective-permute-start(bf16[2,288,128]{2,1,0:T(8,128)(2,1)S(1)} %get-tuple-element.79), channel_id=1, source_target_pairs={{0,8},{4,12},{8,0},{12,4},{1,9},{5,13},{9,1},{13,5},{2,10},{6,14},... | collective-permute-start | bytes 442376 | tf_op jit(solution)/shard_map/ppermute | solution.py:367
  19.1 1.6 %collective-permute-start.6 = (bf16[2,272,128]{2,1,0:T(8,128)(2,1)S(1)}, bf16[2,272,128]{2,1,0:T(8,128)(2,1)S(1)}, u32[]{:S(2)}, u32[]{:S(2)}) collective-permute-start(bf16[2,272,128]{2,1,0:T(8,128)(2,1)S(1)} %get-tuple-element.77), channel_id=1, source_target_pairs={{0,4},{4,0},{8,12},{12,8},{1,5},{5,1},{9,13},{13,9},{2,6},{6,2},{1... | collective-permute-start | bytes 417800 | tf_op jit(solution)/shard_map/ppermute | solution.py:367
  21.3 2.0 %shard_map.99 = (bf16[2,2,384,128]{3,2,1,0:T(8,128)(2,1)S(1)}, f32[2,2,384,128]{3,2,1,0:T(8,128)S(1)}) custom-call(bf16[4,768,256]{2,1,0:T(8,128)(2,1)S(1)} %get-tuple-element.69.normed, bf16[256,256]{1,0:T(8,128)(2,1)S(1)} %get-tuple-element.81.w0.q0, bf16[272,768]{1,0:T(8,128)(2,1)S(1)} %collective-permute-done.3.w1.q1, ...), custom_call_target="tpu_custom_call" | custom-call | flops 500000000 | bytes 1500000 | tf_op jit(solution)/shard_map/pallas_call | solution.py:48
  23.4 2.9 %collective-permute-done.11.other.w_other = bf16[128,1024]{1,0:T(8,128)(2,1)S(1)} collective-permute-done((bf16[128,1024]{1,0:T(8,128)(2,1)S(1)}, bf16[128,1024]{1,0:T(8,128)(2,1)S(1)}, u32[]{:S(2)}, u32[]{:S(2)}) %collective-permute-start.11) | collective-permute-done | bytes 262176 | tf_op jit(solution)/shard_map/ppermute | solution.py:367
  27.3 1.6 %shard_map.101 = (bf16[2,2,384,128]{3,2,1,0:T(8,128)(2,1)S(1)}, bf16[2,2,384,128]{3,2,1,0:T(8,128)(2,1)S(1)}, bf16[2,272,128]{2,1,0:T(8,128)(2,1)S(1)}, bf16[2,2...) custom-call(bf16[2,272,128]{2,1,0:T(8,128)(2,1)S(1)} %collective-per, ...), custom_call_target="tpu_custom_call" | custom-call | flops 2000000000 | bytes 6000000 | tf_op jit(solution)/shard_map/pallas_call | solution.py:48
  28.9 1.6 %collective-permute-start.12 = (bf16[64,1024]{1,0:T(8,128)(2,1)S(1)}, bf16[64,1024]{1,0:T(8,128)(2,1)S(1)}, u32[]{:S(2)}, u32[]{:S(2)}) collective-permute-start(bf16[64,1024]{1,0:T(8,128)(2,1)S(1)} %get-tuple-element.93), channel_id=1, source_target_pairs={{0,2},{1,3},{2,0},{3,1},{4,6},{5,7},{6,4},{7,5},{8,10},{9,11},{10,... | collective-permute-start | bytes 393224 | tf_op jit(solution)/shard_map/ppermute | solution.py:367
  30.5 2.6 %collective-permute-start.13 = (bf16[2,32,1024]{2,1,0:T(8,128)(2,1)S(1)}, bf16[2,32,1024]{2,1,0:T(8,128)(2,1)S(1)}, u32[]{:S(2)}, u32[]{:S(2)}) collective-permute-start(bf16[2,32,1024]{2,1,0:T(8,128)(2,1)S(1)} %get-tuple-element.94), channel_id=1, source_target_pairs={{0,4},{4,0},{8,12},{12,8},{1,5},{5,1},{9,13},{13,9},{2,6},{6,2},{1... | collective-permute-start | bytes 393224 | tf_op jit(solution)/shard_map/ppermute | solution.py:367
  33.9 3.2 %collective-permute-start.16 = (bf16[2,288,128]{2,1,0:T(8,128)(2,1)S(1)}, bf16[2,288,128]{2,1,0:T(8,128)(2,1)S(1)}, u32[]{:S(2)}, u32[]{:S(2)}) collective-permute-start(bf16[2,288,128]{2,1,0:T(8,128)(2,1)S(1)} %get-tuple-element.99), channel_id=1, source_target_pairs={{0,8},{4,12},{8,0},{12,4},{1,9},{5,13},{9,1},{13,5},{2,10},{6,14},... | collective-permute-start | bytes 442376 | tf_op jit(solution)/shard_map/ppermute | solution.py:367
  37.2 1.1 %collective-permute-start.17 = (bf16[32,1024]{1,0:T(8,128)(2,1)S(1)}, bf16[32,1024]{1,0:T(8,128)(2,1)S(1)}, u32[]{:S(2)}, u32[]{:S(2)}) collective-permute-start(bf16[32,1024]{1,0:T(8,128)(2,1)S(1)} %get-tuple-element.102), channel_id=1, source_target_pairs={{0,4},{4,0},{8,12},{12,8},{1,5},{5,1},{9,13},{13,9},{2,6},{6,2},{1... | collective-permute-start | bytes 196616 | tf_op jit(solution)/shard_map/ppermute | solution.py:367
  40.7 2.1 %collective-permute-done.17.a_in = bf16[32,1024]{1,0:T(8,128)(2,1)S(1)} collective-permute-done((bf16[32,1024]{1,0:T(8,128)(2,1)S(1)}, bf16[32,1024]{1,0:T(8,128)(2,1)S(1)}, u32[]{:S(2)}, u32[]{:S(2)}) %collective-permute-start.17) | collective-permute-done | bytes 65568 | tf_op jit(solution)/shard_map/ppermute | solution.py:367
  42.8 4.0 %collective-permute-start.21 = (bf16[64,1024]{1,0:T(8,128)(2,1)S(1)}, bf16[64,1024]{1,0:T(8,128)(2,1)S(1)}, u32[]{:S(2)}, u32[]{:S(2)}) collective-permute-start(bf16[64,1024]{1,0:T(8,128)(2,1)S(1)} %get-tuple-element.119), channel_id=1, source_target_pairs={{0,8},{4,12},{8,0},{12,4},{1,9},{5,13},{9,1},{13,5},{2,10},{6,14},... | collective-permute-start | bytes 393224 | tf_op jit(solution)/shard_map/ppermute | solution.py:367
  46.9 2.1 %shard_map.104 = (bf16[2,384,256]{2,1,0:T(8,128)(2,1)S(1)}, f32[2,2,384,128]{3,2,1,0:T(8,128)S(1)}, f32[2,2,384,128]{3,2,1,0:T(8,128)S(1)}) custom-call(bf16[2,272,128]{2,1,0:T(8,128)(2,1)S(1)} %collective-permute-done.6.pair, bf16[2,256,128]{2,1,0:T(8,128)(2,1)S(1)} %get-tuple-element.100.before, bf16[2,272,128]{2,1,0:T(8,128)(2,1)S(1)} %collective-permute-done.7.middle, ...), custom_call_target="tpu_custom_call" | custom-call | flops 100000000 | bytes 300000 | tf_op jit(solution)/shard_map/pallas_call | solution.py:48
  49.1 2.3 %shard_map.105 = (f32[4,384,256]{2,1,0:T(8,128)S(1)}, bf16[4,384,256]{2,1,0:T(8,128)(2,1)S(1)}) custom-call(bf16[2,272,128]{2,1,0:T(8,128)(2,1)S(1)} %collective-permute-done.14.pair, bf16[2,272,128]{2,1,0:T(8,128)(2,1)S(1)} %collective-permute-done.15.middle, bf16[2,288,128]{2,1,0:T(8,128)(2,1)S(1)} %collective-permute-done.16.further, ...), custom_call_target="tpu_custom_call" | custom-call | flops 2000000000 | bytes 6000000 | tf_op jit(solution)/shard_map/pallas_call | solution.py:48
  52.5 1.2 %collective-permute-done.19.partner = bf16[4,384,256]{2,1,0:T(8,128)(2,1)S(1)} collective-permute-done((bf16[4,384,256]{2,1,0:T(8,128)(2,1)S(1)}, bf16[4,384,256]{2,1,0:T(8,128)(2,1)S(1)}, u32[]{:S(2)}, u32[]{:S(2)}) %collective-permute-start.19) | collective-permute-done | bytes 786464 | tf_op jit(solution)/shard_map/ppermute | solution.py:367
  53.8 1.1 %collective-permute-done.20.out_partner = bf16[384,1024]{1,0:T(8,128)(2,1)S(1)} collective-permute-done((bf16[384,1024]{1,0:T(8,128)(2,1)S(1)}, bf16[384,1024]{1,0:T(8,128)(2,1)S(1)}, u32[]{:S(2)}, u32[]{:S(2)}) %collective-permute-start.20) | collective-permute-done | bytes 786464 | tf_op jit(solution)/shard_map/ppermute | solution.py:367
  54.9 2.2 %shard_map.107 = (bf16[384,1024]{1,0:T(8,128)(2,1)}, bf16[384,1024]{1,0:T(8,128)(2,1)}) custom-call(f32[4,384,256]{2,1,0:T(8,128)S(1)} %get-tuple-element.110.own, bf16[4,384,256]{2,1,0:T(8,128)(2,1)S(1)} %collective-permute-done.19.partner, bf16[384,1024]{1,0:T(8,128)(2,1)S(1)} %collective-permute-done.20.out_partner, bf16[384,1024]{1,0:T(8,128)(2,1)S(1)} %bitcast.14, ...), custom_call_target="tpu_custom_call" | custom-call | flops 2000000000 | bytes 6000000 | tf_op jit(solution)/shard_map/pallas_call | solution.py:48
  (54 shorter events, 10.5 us)
Async XLA Ops:
  1.9 6.3 %collective-permute-start = (bf16[128,512]{1,0:T(8,128)(2,1)S(1)}, bf16[128,512]{1,0:T(8,128)(2,1)S(1)}, u32[]{:S(2)}, u32[]{:S(2)}) collective-permute-start(bf16[128,512]{1,0:T(8,128)(2,1)S(1)} %shard_map.94._), channel_id=1, source_target_pairs={{0,3},{1,2},{2,1},{3,0},{4,7},{5,6},{6,5},{7,4},{8,11},{9,10},{10,... | collective-permute-start | bytes 393224 | tf_op jit(solution)/shard_map/ppermute | solution.py:367
  4.4 6.3 %copy-start.6 = (f32[1024]{0:T(1024)S(1)}, f32[1024]{0:T(1024)}, u32[]{:S(2)}) copy-start(f32[1024]{0:T(1024)} %param.9) | copy-start | bytes 12292
  4.4 6.3 %collective-permute-start.1 = (bf16[384,1024]{1,0:T(8,128)(2,1)S(1)}, bf16[384,1024]{1,0:T(8,128)(2,1)S(1)}, u32[]{:S(2)}, u32[]{:S(2)}) collective-permute-start(bf16[384,1024]{1,0:T(8,128)(2,1)S(1)} %bitcast.12), channel_id=1, source_target_pairs={{0,1},{1,0},{2,3},{3,2},{4,5},{5,4},{6,7},{7,6},{8,9},{9,8},{10,11... | collective-permute-start | bytes 2359304 | tf_op jit(solution)/shard_map/ppermute | solution.py:367
  5.1 5.7 %collective-permute-start.2 = (bf16[384,1024]{1,0:T(8,128)(2,1)S(1)}, bf16[384,1024]{1,0:T(8,128)(2,1)S(1)}, u32[]{:S(2)}, u32[]{:S(2)}) collective-permute-start(bf16[384,1024]{1,0:T(8,128)(2,1)S(1)} %bitcast.6), channel_id=1, source_target_pairs={{0,1},{1,0},{2,3},{3,2},{4,5},{5,4},{6,7},{7,6},{8,9},{9,8},{10,11... | collective-permute-start | bytes 2359304 | tf_op jit(solution)/shard_map/ppermute | solution.py:367
  5.4 9.7 %collective-permute-start.4 = (bf16[256,512]{1,0:T(8,128)(2,1)S(1)}, bf16[256,512]{1,0:T(8,128)(2,1)S(1)}, u32[]{:S(2)}, u32[]{:S(2)}) collective-permute-start(bf16[256,512]{1,0:T(8,128)(2,1)S(1)} %get-tuple-element.67.w0), channel_id=1, source_target_pairs={{0,2},{1,3},{2,0},{3,1},{4,6},{5,7},{6,4},{7,5},{8,10},{9,11},{10,... | collective-permute-start | bytes 786440 | tf_op jit(solution)/shard_map/ppermute | solution.py:367
  6.7 5.2 %collective-permute-start.3 = (bf16[272,768]{1,0:T(8,128)(2,1)S(1)}, bf16[272,768]{1,0:T(8,128)(2,1)S(1)}, u32[]{:S(2)}, u32[]{:S(2)}) collective-permute-start(bf16[272,768]{1,0:T(8,128)(2,1)S(1)} %get-tuple-element.74), channel_id=1, source_target_pairs={{0,1},{1,0},{2,3},{3,2},{4,5},{5,4},{6,7},{7,6},{8,9},{9,8},{10,11... | collective-permute-start | bytes 1253384 | tf_op jit(solution)/shard_map/ppermute | solution.py:367
  8.3 6.8 %collective-permute-start.5 = (bf16[128,512]{1,0:T(8,128)(2,1)S(1)}, bf16[128,512]{1,0:T(8,128)(2,1)S(1)}, u32[]{:S(2)}, u32[]{:S(2)}) collective-permute-start(bf16[128,512]{1,0:T(8,128)(2,1)S(1)} %collective-permute-done.w3), channel_id=1, source_target_pairs={{0,16},{16,0},{1,17},{17,1},{2,18},{18,2},{3,19},{19,3},{4,20},{20... | collective-permute-start | bytes 393224 | tf_op jit(solution)/shard_map/ppermute | solution.py:367
  12.0 8.7 %collective-permute-start.10 = (bf16[256,256]{1,0:T(8,128)(2,1)S(1)}, bf16[256,256]{1,0:T(8,128)(2,1)S(1)}, u32[]{:S(2)}, u32[]{:S(2)}) collective-permute-start(bf16[256,256]{1,0:T(8,128)(2,1)S(1)} %get-tuple-element.82), channel_id=1, source_target_pairs={{0,3},{1,2},{2,1},{3,0},{4,7},{5,6},{6,5},{7,4},{8,11},{9,10},{10,... | collective-permute-start | bytes 393224 | tf_op jit(solution)/shard_map/ppermute | solution.py:367
  13.0 8.3 %collective-permute-start.9 = (bf16[256,256]{1,0:T(8,128)(2,1)S(1)}, bf16[256,256]{1,0:T(8,128)(2,1)S(1)}, u32[]{:S(2)}, u32[]{:S(2)}) collective-permute-start(bf16[256,256]{1,0:T(8,128)(2,1)S(1)} %get-tuple-element.81.w0.q0), channel_id=1, source_target_pairs={{0,2},{1,3},{2,0},{3,1},{4,6},{5,7},{6,4},{7,5},{8,10},{9,11},{10,... | collective-permute-start | bytes 393224 | tf_op jit(solution)/shard_map/ppermute | solution.py:367
  13.6 12.6 %collective-permute-start.11 = (bf16[128,1024]{1,0:T(8,128)(2,1)S(1)}, bf16[128,1024]{1,0:T(8,128)(2,1)S(1)}, u32[]{:S(2)}, u32[]{:S(2)}) collective-permute-start(bf16[128,1024]{1,0:T(8,128)(2,1)S(1)} %copy-done.1), channel_id=1, source_target_pairs={{0,2},{1,3},{2,0},{3,1},{4,6},{5,7},{6,4},{7,5},{8,10},{9,11},{10,... | collective-permute-start | bytes 786440 | tf_op jit(solution)/shard_map/ppermute | solution.py:367
  16.4 10.9 %collective-permute-start.8 = (bf16[2,288,128]{2,1,0:T(8,128)(2,1)S(1)}, bf16[2,288,128]{2,1,0:T(8,128)(2,1)S(1)}, u32[]{:S(2)}, u32[]{:S(2)}) collective-permute-start(bf16[2,288,128]{2,1,0:T(8,128)(2,1)S(1)} %get-tuple-element.79), channel_id=1, source_target_pairs={{0,8},{4,12},{8,0},{12,4},{1,9},{5,13},{9,1},{13,5},{2,10},{6,14},... | collective-permute-start | bytes 442376 | tf_op jit(solution)/shard_map/ppermute | solution.py:367
  19.1 8.2 %collective-permute-start.6 = (bf16[2,272,128]{2,1,0:T(8,128)(2,1)S(1)}, bf16[2,272,128]{2,1,0:T(8,128)(2,1)S(1)}, u32[]{:S(2)}, u32[]{:S(2)}) collective-permute-start(bf16[2,272,128]{2,1,0:T(8,128)(2,1)S(1)} %get-tuple-element.77), channel_id=1, source_target_pairs={{0,4},{4,0},{8,12},{12,8},{1,5},{5,1},{9,13},{13,9},{2,6},{6,2},{1... | collective-permute-start | bytes 417800 | tf_op jit(solution)/shard_map/ppermute | solution.py:367
  20.6 6.6 %collective-permute-start.7 = (bf16[2,272,128]{2,1,0:T(8,128)(2,1)S(1)}, bf16[2,272,128]{2,1,0:T(8,128)(2,1)S(1)}, u32[]{:S(2)}, u32[]{:S(2)}) collective-permute-start(bf16[2,272,128]{2,1,0:T(8,128)(2,1)S(1)} %get-tuple-element.78), channel_id=1, source_target_pairs={{4,8},{8,4},{5,9},{9,5},{6,10},{10,6},{7,11},{11,7},{20,24},{24,20... | collective-permute-start | bytes 417800 | tf_op jit(solution)/shard_map/ppermute | solution.py:378
  28.9 8.2 %collective-permute-start.12 = (bf16[64,1024]{1,0:T(8,128)(2,1)S(1)}, bf16[64,1024]{1,0:T(8,128)(2,1)S(1)}, u32[]{:S(2)}, u32[]{:S(2)}) collective-permute-start(bf16[64,1024]{1,0:T(8,128)(2,1)S(1)} %get-tuple-element.93), channel_id=1, source_target_pairs={{0,2},{1,3},{2,0},{3,1},{4,6},{5,7},{6,4},{7,5},{8,10},{9,11},{10,... | collective-permute-start | bytes 393224 | tf_op jit(solution)/shard_map/ppermute | solution.py:367
  30.5 6.7 %collective-permute-start.13 = (bf16[2,32,1024]{2,1,0:T(8,128)(2,1)S(1)}, bf16[2,32,1024]{2,1,0:T(8,128)(2,1)S(1)}, u32[]{:S(2)}, u32[]{:S(2)}) collective-permute-start(bf16[2,32,1024]{2,1,0:T(8,128)(2,1)S(1)} %get-tuple-element.94), channel_id=1, source_target_pairs={{0,4},{4,0},{8,12},{12,8},{1,5},{5,1},{9,13},{13,9},{2,6},{6,2},{1... | collective-permute-start | bytes 393224 | tf_op jit(solution)/shard_map/ppermute | solution.py:367
  33.0 15.9 %collective-permute-start.15 = (bf16[2,272,128]{2,1,0:T(8,128)(2,1)S(1)}, bf16[2,272,128]{2,1,0:T(8,128)(2,1)S(1)}, u32[]{:S(2)}, u32[]{:S(2)}) collective-permute-start(bf16[2,272,128]{2,1,0:T(8,128)(2,1)S(1)} %get-tuple-element.98), channel_id=1, source_target_pairs={{4,8},{8,4},{5,9},{9,5},{6,10},{10,6},{7,11},{11,7},{20,24},{24,20... | collective-permute-start | bytes 417800 | tf_op jit(solution)/shard_map/ppermute | solution.py:378
  33.9 15.2 %collective-permute-start.16 = (bf16[2,288,128]{2,1,0:T(8,128)(2,1)S(1)}, bf16[2,288,128]{2,1,0:T(8,128)(2,1)S(1)}, u32[]{:S(2)}, u32[]{:S(2)}) collective-permute-start(bf16[2,288,128]{2,1,0:T(8,128)(2,1)S(1)} %get-tuple-element.99), channel_id=1, source_target_pairs={{0,8},{4,12},{8,0},{12,4},{1,9},{5,13},{9,1},{13,5},{2,10},{6,14},... | collective-permute-start | bytes 442376 | tf_op jit(solution)/shard_map/ppermute | solution.py:367
  37.2 5.6 %collective-permute-start.17 = (bf16[32,1024]{1,0:T(8,128)(2,1)S(1)}, bf16[32,1024]{1,0:T(8,128)(2,1)S(1)}, u32[]{:S(2)}, u32[]{:S(2)}) collective-permute-start(bf16[32,1024]{1,0:T(8,128)(2,1)S(1)} %get-tuple-element.102), channel_id=1, source_target_pairs={{0,4},{4,0},{8,12},{12,8},{1,5},{5,1},{9,13},{13,9},{2,6},{6,2},{1... | collective-permute-start | bytes 196616 | tf_op jit(solution)/shard_map/ppermute | solution.py:367
  38.3 4.5 %collective-permute-start.18 = (bf16[32,1024]{1,0:T(8,128)(2,1)S(1)}, bf16[32,1024]{1,0:T(8,128)(2,1)S(1)}, u32[]{:S(2)}, u32[]{:S(2)}) collective-permute-start(bf16[32,1024]{1,0:T(8,128)(2,1)S(1)} %get-tuple-element.103), channel_id=1, source_target_pairs={{0,2},{1,3},{2,0},{3,1},{4,6},{5,7},{6,4},{7,5},{8,10},{9,11},{10,... | collective-permute-start | bytes 196616 | tf_op jit(solution)/shard_map/ppermute | solution.py:367
  39.6 9.5 %collective-permute-start.14 = (bf16[2,272,128]{2,1,0:T(8,128)(2,1)S(1)}, bf16[2,272,128]{2,1,0:T(8,128)(2,1)S(1)}, u32[]{:S(2)}, u32[]{:S(2)}) collective-permute-start(bf16[2,272,128]{2,1,0:T(8,128)(2,1)S(1)} %get-tuple-element.97), channel_id=1, source_target_pairs={{0,4},{4,0},{8,12},{12,8},{1,5},{5,1},{9,13},{13,9},{2,6},{6,2},{1... | collective-permute-start | bytes 417800 | tf_op jit(solution)/shard_map/ppermute | solution.py:367
  42.8 9.6 %collective-permute-start.21 = (bf16[64,1024]{1,0:T(8,128)(2,1)S(1)}, bf16[64,1024]{1,0:T(8,128)(2,1)S(1)}, u32[]{:S(2)}, u32[]{:S(2)}) collective-permute-start(bf16[64,1024]{1,0:T(8,128)(2,1)S(1)} %get-tuple-element.119), channel_id=1, source_target_pairs={{0,8},{4,12},{8,0},{12,4},{1,9},{5,13},{9,1},{13,5},{2,10},{6,14},... | collective-permute-start | bytes 393224 | tf_op jit(solution)/shard_map/ppermute | solution.py:367
  51.4 2.4 %collective-permute-start.19 = (bf16[4,384,256]{2,1,0:T(8,128)(2,1)S(1)}, bf16[4,384,256]{2,1,0:T(8,128)(2,1)S(1)}, u32[]{:S(2)}, u32[]{:S(2)}) collective-permute-start(bf16[4,384,256]{2,1,0:T(8,128)(2,1)S(1)} %get-tuple-element.113), channel_id=1, source_target_pairs={{0,1},{1,0},{2,3},{3,2},{4,5},{5,4},{6,7},{7,6},{8,9},{9,8},{10,11... | collective-permute-start | bytes 2359304 | tf_op jit(solution)/shard_map/ppermute | solution.py:367
  51.5 3.4 %collective-permute-start.20 = (bf16[384,1024]{1,0:T(8,128)(2,1)S(1)}, bf16[384,1024]{1,0:T(8,128)(2,1)S(1)}, u32[]{:S(2)}, u32[]{:S(2)}) collective-permute-start(bf16[384,1024]{1,0:T(8,128)(2,1)S(1)} %shard_map.106), channel_id=1, source_target_pairs={{0,1},{1,0},{2,3},{3,2},{4,5},{5,4},{6,7},{7,6},{8,9},{9,8},{10,11... | collective-permute-start | bytes 2359304 | tf_op jit(solution)/shard_map/ppermute | solution.py:367
  52.4 5.1 %collective-permute-start.22 = (bf16[64,1024]{1,0:T(8,128)(2,1)S(1)}, bf16[64,1024]{1,0:T(8,128)(2,1)S(1)}, u32[]{:S(2)}, u32[]{:S(2)}) collective-permute-start(bf16[64,1024]{1,0:T(8,128)(2,1)S(1)} %get-tuple-element.124), channel_id=1, source_target_pairs={{0,4},{4,0},{8,12},{12,8},{1,5},{5,1},{9,13},{13,9},{2,6},{6,2},{1... | collective-permute-start | bytes 393224 | tf_op jit(solution)/shard_map/ppermute | solution.py:367
  (7 other events, 19.3 us)

commit v7 on v6

--- a/solution.py
+++ b/solution.py
@@ -132,6 +132,14 @@
     if n != 4:
         return at < 0, at < 0
     return (at % 2 == 1, at >= 2) if step > 0 else (at % 2 == 0, at < 2)
+
+
+def pair_body(near, normed, seg, w1, raw, seg_col, seg_row):
+    rows, length = w1.shape[0] - ID_ROWS, seg.shape[1]
+    for i, ids in enumerate((seg[...].astype(f32), w1[rows : rows + 1, :length].astype(f32))):
+        seg_row[i] = ids
+        seg_col[i] = jnp.broadcast_to(ids, (HEAD_DIM, length)).T
+    raw[...] = near[...] + dot_nn(normed[1], w1[:rows, KV_COLUMNS])
 
 
 def prep_body(tokens, partner, gain, w0, normed, inv_rms, raw):
@@ -158,12 +166,9 @@
         target[i, 2 * HEAD_DIM :, :] = jnp.broadcast_to(ids, (rows, HEAD_DIM)).astype(bf16)
 
 
-def kv_body(near, normed, seg, w1, w2, w3, w3_other, feat_k, values, state, state_mid, state_far, seg_col, seg_row):
-    shard_rows, length = w2.shape[0], seg.shape[1]
-    for i, ids in enumerate((seg[...].astype(f32), w1[shard_rows : shard_rows + 1, :length].astype(f32))):
-        seg_row[i] = ids
-        seg_col[i] = jnp.broadcast_to(ids, (HEAD_DIM, length)).T
-    raw = near[...] + dot_nn(normed[1], w1[:shard_rows, KV_COLUMNS]) + dot_nn(normed[2], w2[...])
+def kv_body(near, normed, w2, w3, w3_other, seg_col, feat_k, values, state, state_mid, state_far):
+    length = seg_col.shape[1]
+    raw = near[...] + dot_nn(normed[2], w2[...])
     for at, w in zip(halves(), (w3, w3_other)):
         raw += dot_nn(normed[3, :, columns(at, w.shape[0])], w[...])
     raw = raw.astype(bf16)
@@ -427,7 +432,8 @@
     wide = (2, 2, length, HEAD_DIM)
 
     shard_rows = w_qkv.shape[0]
-    (kv_half,) = split(split_half_body, [(shard_rows // 2, 4 * HEAD_DIM)], 4, 1.0, w_qkv)
+    w_first = pltpu.with_memory_space_constraint(w_qkv, pltpu.HBM)
+    (kv_half,) = split(split_half_body, [(shard_rows // 2, 4 * HEAD_DIM)], 4, 1.0, w_first)
     kv_diagonal = flip(kv_half, "dp", 3)
     kv_mine, kv_other = split(
         split_kv_body,
@@ -444,17 +450,20 @@
         [((4, 2 * length, D // 4), bf16), ((length, 1), f32), ((2 * length, 4 * HEAD_DIM), f32)],
         flat, partner, gain, kv_mine, us=PREP,
     )
+    raw_near, seg_col, seg_row = call(
+        pair_body,
+        [((2 * length, 4 * HEAD_DIM), f32), ((2, length, HEAD_DIM), f32), ((2, 1, length), f32)],
+        raw_near, normed, segment_ids, kv_pair,
+    )
     q_mine, q_other = split(split_q_body, [(shard_rows, 2 * HEAD_DIM)] * 2, 4, 1.0, w_late)
-    inv_rms, q_mine, q_other, out_own, kv_pair = lax.optimization_barrier((inv_rms, q_mine, q_other, w_out, kv_pair))
+    raw_near, q_mine, q_other, out_own = lax.optimization_barrier((raw_near, q_mine, q_other, w_out))
     wq = [q_mine, kv_pair, flip(q_mine, "dp", 2), flip(q_other, "dp", 3)]
     kv = [kv_mine, kv_pair, kv_x, kv_diagonal, kv_diagonal_other]
     out = [out_own, flip(out_own, "dp", 2)]
 
     messages = [((2, 2 * HEAD_DIM + m * ID_ROWS, HEAD_DIM), bf16) for m in (1, 1, 2)]
-    feat_k, values, state, state_mid, state_far, seg_col, seg_row = call(
-        kv_body,
-        [(wide, bf16), (wide, bf16), *messages, ((2, length, HEAD_DIM), f32), ((2, 1, length), f32)],
-        raw_near, normed, segment_ids, *kv[1:],
+    feat_k, values, state, state_mid, state_far = call(
+        kv_body, [(wide, bf16), (wide, bf16), *messages], raw_near, normed, *kv[2:], seg_col
     )
     ends = jnp.stack([seg_col[:, 0, 0], seg_col[:, -1, 0]])
     near = carry(state, state_mid, state_far, ends, 1)

time: 58.7 us -> 58.2 us (level)
  local copies, waits for them, and re-layouts: 1.52 us -> 0.03 us
  Pallas kernels: 15.3 us -> 16.5 us
  starting transfers between devices: 30.8 us -> 29.8 us
  waiting for transfers between devices: 9.94 us -> 10.9 us
    unnamed x16 -> x14, local copies, waits for them, and re-layouts: 1.52 us -> 0.03 us
    ppermute x21, starting transfers between devices: 29.3 us -> 28.3 us  [flip(): return lax.ppermute(array, axis, [(i, i ^ bit) for i in range(n)])]
    pallas_call x3, Pallas kernels: 0.4 us -> 1.36 us  [split(): pl.pallas_call(body, out_shape=[jax.ShapeDtypeStruct(shape, bf16) for sha...]
    ppermute x21, waiting for transfers between devices: 9.93 us -> 10.9 us  [flip(): return lax.ppermute(array, axis, [(i, i ^ bit) for i in range(n)])]
    pallas_call x13 -> x14, Pallas kernels: 14.9 us -> 15.1 us  [call(): pl.pallas_call(body, out_shape=[jax.ShapeDtypeStruct(shape, dtype) for sh...]
where the time goes in v7:
time: 58.2 us; the launch traced here: 58 us
  starting transfers between devices  29.8 us (51%)
  Pallas kernels  16.5 us (28%)
  waiting for transfers between devices  10.9 us (19%)
  between operations  0.87 us (1%)
    ppermute x21, starting transfers between devices, flip(): return lax.ppermute(array, axis, [(i, i ^ bit) for i in range(n)])  28.3 us
    pallas_call x14, Pallas kernels, call(): pl.pallas_call(body, out_shape=[jax.ShapeDtypeStruct(shape, dtype) for sh...  15.1 us
    ppermute x21, waiting for transfers between devices, flip(): return lax.ppermute(array, axis, [(i, i ^ bit) for i in range(n)])  10.9 us
    ppermute x2, starting transfers between devices, carry(): middle = lax.ppermute(middle, 'seq', [(1, 2), (2, 1)])  1.5 us
    pallas_call x3, Pallas kernels, split(): pl.pallas_call(body, out_shape=[jax.ShapeDtypeStruct(shape, bf16) for sha...  1.36 us
  transfers between devices with their start and end apart: 23, of which 8 were waited for; matrix products, arithmetic and copies ran while one was open for 0% of the time, Pallas kernels for 22%

profile of v7, /device:TPU:0, one launch (start us, length us, event | category | flops | bytes accessed | tf_op | source)
XLA Modules:
  0.0 58.0 jit_solution(10594558562707320360)
XLA Ops:
  0.7 1.0 %shard_map.94._ = bf16[128,512]{1,0:T(8,128)(2,1)S(1)} custom-call(bf16[256,1536]{1,0:T(8,128)(2,1)} %w.4), custom_call_target="tpu_custom_call" | custom-call | flops 1000000000 | bytes 1000000 | tf_op jit(solution)/shard_map/pallas_call | solution.py:110
  1.7 2.4 %collective-permute-start = (bf16[128,512]{1,0:T(8,128)(2,1)S(1)}, bf16[128,512]{1,0:T(8,128)(2,1)S(1)}, u32[]{:S(2)}, u32[]{:S(2)}) collective-permute-start(bf16[128,512]{1,0:T(8,128)(2,1)S(1)} %shard_map.94._), channel_id=1, source_target_pairs={{0,3},{1,2},{2,1},{3,0},{4,7},{5,6},{6,5},{7,4},{8,11},{9,10},{10,... | collective-permute-start | bytes 393224 | tf_op jit(solution)/shard_map/ppermute | solution.py:372
  5.7 2.3 %collective-permute-done.w3 = bf16[128,512]{1,0:T(8,128)(2,1)S(1)} collective-permute-done((bf16[128,512]{1,0:T(8,128)(2,1)S(1)}, bf16[128,512]{1,0:T(8,128)(2,1)S(1)}, u32[]{:S(2)}, u32[]{:S(2)}) %collective-permute-start) | collective-permute-done | bytes 131104 | tf_op jit(solution)/shard_map/ppermute | solution.py:372
  8.0 2.4 %collective-permute-start.5 = (bf16[128,512]{1,0:T(8,128)(2,1)S(1)}, bf16[128,512]{1,0:T(8,128)(2,1)S(1)}, u32[]{:S(2)}, u32[]{:S(2)}) collective-permute-start(bf16[128,512]{1,0:T(8,128)(2,1)S(1)} %collective-permute-done.w3), channel_id=1, source_target_pairs={{0,16},{16,0},{1,17},{17,1},{2,18},{18,2},{3,19},{19,3},{4,20},{20... | collective-permute-start | bytes 393224 | tf_op jit(solution)/shard_map/ppermute | solution.py:372
  11.8 1.0 %collective-permute-start.10 = (bf16[256,256]{1,0:T(8,128)(2,1)S(1)}, bf16[256,256]{1,0:T(8,128)(2,1)S(1)}, u32[]{:S(2)}, u32[]{:S(2)}) collective-permute-start(bf16[256,256]{1,0:T(8,128)(2,1)S(1)} %get-tuple-element.82), channel_id=1, source_target_pairs={{0,3},{1,2},{2,1},{3,0},{4,7},{5,6},{6,5},{7,4},{8,11},{9,10},{10,... | collective-permute-start | bytes 393224 | tf_op jit(solution)/shard_map/ppermute | solution.py:372
  13.5 1.4 %collective-permute-start.11 = (bf16[128,1024]{1,0:T(8,128)(2,1)S(1)}, bf16[128,1024]{1,0:T(8,128)(2,1)S(1)}, u32[]{:S(2)}, u32[]{:S(2)}) collective-permute-start(bf16[128,1024]{1,0:T(8,128)(2,1)S(1)} %copy-done.1), channel_id=1, source_target_pairs={{0,2},{1,3},{2,0},{3,1},{4,6},{5,7},{6,4},{7,5},{8,10},{9,11},{10,... | collective-permute-start | bytes 786440 | tf_op jit(solution)/shard_map/ppermute | solution.py:372
  14.9 1.1 %shard_map.99 = (bf16[2,2,384,128]{3,2,1,0:T(8,128)(2,1)S(1)}, bf16[2,2,384,128]{3,2,1,0:T(8,128)(2,1)S(1)}, bf16[2,272,128]{2,1,0:T(8,128)(2,1)S(1)}, bf16[2,27...) custom-call(f32[768,512]{1,0:T(8,128)S(1)} %get-tuple-element.75.near, bf16[4,768,256]{2,1,0:T(8,128)(2,1)S(1)} %get-tuple-element.69.normed, ...), custom_call_target="tpu_custom_call" | custom-call | flops 2000000000 | bytes 6000000 | tf_op jit(solution)/shard_map/pallas_call | solution.py:48
  16.0 2.7 %collective-permute-start.8 = (bf16[2,288,128]{2,1,0:T(8,128)(2,1)S(1)}, bf16[2,288,128]{2,1,0:T(8,128)(2,1)S(1)}, u32[]{:S(2)}, u32[]{:S(2)}) collective-permute-start(bf16[2,288,128]{2,1,0:T(8,128)(2,1)S(1)} %get-tuple-element.80), channel_id=1, source_target_pairs={{0,8},{4,12},{8,0},{12,4},{1,9},{5,13},{9,1},{13,5},{2,10},{6,14},... | collective-permute-start | bytes 442376 | tf_op jit(solution)/shard_map/ppermute | solution.py:372
  18.7 1.6 %collective-permute-start.6 = (bf16[2,272,128]{2,1,0:T(8,128)(2,1)S(1)}, bf16[2,272,128]{2,1,0:T(8,128)(2,1)S(1)}, u32[]{:S(2)}, u32[]{:S(2)}) collective-permute-start(bf16[2,272,128]{2,1,0:T(8,128)(2,1)S(1)} %get-tuple-element.78), channel_id=1, source_target_pairs={{0,4},{4,0},{8,12},{12,8},{1,5},{5,1},{9,13},{13,9},{2,6},{6,2},{1... | collective-permute-start | bytes 417800 | tf_op jit(solution)/shard_map/ppermute | solution.py:372
  21.0 2.0 %shard_map.100 = (bf16[2,2,384,128]{3,2,1,0:T(8,128)(2,1)S(1)}, f32[2,2,384,128]{3,2,1,0:T(8,128)S(1)}) custom-call(bf16[4,768,256]{2,1,0:T(8,128)(2,1)S(1)} %get-tuple-element.69.normed, bf16[256,256]{1,0:T(8,128)(2,1)S(1)} %get-tuple-element.81.w0.q0, bf16[272,768]{1,0:T(8,128)(2,1)S(1)} %collective-permute-done.3.w1.q1, ...), custom_call_target="tpu_custom_call" | custom-call | flops 500000000 | bytes 1500000 | tf_op jit(solution)/shard_map/pallas_call | solution.py:48
  23.0 3.1 %collective-permute-done.11.other.w_other = bf16[128,1024]{1,0:T(8,128)(2,1)S(1)} collective-permute-done((bf16[128,1024]{1,0:T(8,128)(2,1)S(1)}, bf16[128,1024]{1,0:T(8,128)(2,1)S(1)}, u32[]{:S(2)}, u32[]{:S(2)}) %collective-permute-start.11) | collective-permute-done | bytes 262176 | tf_op jit(solution)/shard_map/ppermute | solution.py:372
  27.1 1.6 %shard_map.102 = (bf16[2,2,384,128]{3,2,1,0:T(8,128)(2,1)S(1)}, bf16[2,2,384,128]{3,2,1,0:T(8,128)(2,1)S(1)}, bf16[2,272,128]{2,1,0:T(8,128)(2,1)S(1)}, bf16[2,2...) custom-call(bf16[2,272,128]{2,1,0:T(8,128)(2,1)S(1)} %collective-per, ...), custom_call_target="tpu_custom_call" | custom-call | flops 2000000000 | bytes 6000000 | tf_op jit(solution)/shard_map/pallas_call | solution.py:48
  28.7 1.6 %collective-permute-start.12 = (bf16[64,1024]{1,0:T(8,128)(2,1)S(1)}, bf16[64,1024]{1,0:T(8,128)(2,1)S(1)}, u32[]{:S(2)}, u32[]{:S(2)}) collective-permute-start(bf16[64,1024]{1,0:T(8,128)(2,1)S(1)} %get-tuple-element.93), channel_id=1, source_target_pairs={{0,2},{1,3},{2,0},{3,1},{4,6},{5,7},{6,4},{7,5},{8,10},{9,11},{10,... | collective-permute-start | bytes 393224 | tf_op jit(solution)/shard_map/ppermute | solution.py:372
  30.3 2.2 %collective-permute-start.13 = (bf16[2,32,1024]{2,1,0:T(8,128)(2,1)S(1)}, bf16[2,32,1024]{2,1,0:T(8,128)(2,1)S(1)}, u32[]{:S(2)}, u32[]{:S(2)}) collective-permute-start(bf16[2,32,1024]{2,1,0:T(8,128)(2,1)S(1)} %get-tuple-element.94), channel_id=1, source_target_pairs={{0,4},{4,0},{8,12},{12,8},{1,5},{5,1},{9,13},{13,9},{2,6},{6,2},{1... | collective-permute-start | bytes 393224 | tf_op jit(solution)/shard_map/ppermute | solution.py:372
  33.4 3.3 %collective-permute-start.16 = (bf16[2,288,128]{2,1,0:T(8,128)(2,1)S(1)}, bf16[2,288,128]{2,1,0:T(8,128)(2,1)S(1)}, u32[]{:S(2)}, u32[]{:S(2)}) collective-permute-start(bf16[2,288,128]{2,1,0:T(8,128)(2,1)S(1)} %get-tuple-element.99), channel_id=1, source_target_pairs={{0,8},{4,12},{8,0},{12,4},{1,9},{5,13},{9,1},{13,5},{2,10},{6,14},... | collective-permute-start | bytes 442376 | tf_op jit(solution)/shard_map/ppermute | solution.py:372
  36.7 1.1 %collective-permute-start.17 = (bf16[32,1024]{1,0:T(8,128)(2,1)S(1)}, bf16[32,1024]{1,0:T(8,128)(2,1)S(1)}, u32[]{:S(2)}, u32[]{:S(2)}) collective-permute-start(bf16[32,1024]{1,0:T(8,128)(2,1)S(1)} %get-tuple-element.102), channel_id=1, source_target_pairs={{0,4},{4,0},{8,12},{12,8},{1,5},{5,1},{9,13},{13,9},{2,6},{6,2},{1... | collective-permute-start | bytes 196616 | tf_op jit(solution)/shard_map/ppermute | solution.py:372
  39.3 1.0 %collective-permute-start.14 = (bf16[2,272,128]{2,1,0:T(8,128)(2,1)S(1)}, bf16[2,272,128]{2,1,0:T(8,128)(2,1)S(1)}, u32[]{:S(2)}, u32[]{:S(2)}) collective-permute-start(bf16[2,272,128]{2,1,0:T(8,128)(2,1)S(1)} %get-tuple-element.97), channel_id=1, source_target_pairs={{0,4},{4,0},{8,12},{12,8},{1,5},{5,1},{9,13},{13,9},{2,6},{6,2},{1... | collective-permute-start | bytes 417800 | tf_op jit(solution)/shard_map/ppermute | solution.py:372
  40.3 2.0 %collective-permute-done.17.a_in = bf16[32,1024]{1,0:T(8,128)(2,1)S(1)} collective-permute-done((bf16[32,1024]{1,0:T(8,128)(2,1)S(1)}, bf16[32,1024]{1,0:T(8,128)(2,1)S(1)}, u32[]{:S(2)}, u32[]{:S(2)}) %collective-permute-start.17) | collective-permute-done | bytes 65568 | tf_op jit(solution)/shard_map/ppermute | solution.py:372
  42.4 4.0 %collective-permute-start.21 = (bf16[64,1024]{1,0:T(8,128)(2,1)S(1)}, bf16[64,1024]{1,0:T(8,128)(2,1)S(1)}, u32[]{:S(2)}, u32[]{:S(2)}) collective-permute-start(bf16[64,1024]{1,0:T(8,128)(2,1)S(1)} %get-tuple-element.119), channel_id=1, source_target_pairs={{0,8},{4,12},{8,0},{12,4},{1,9},{5,13},{9,1},{13,5},{2,10},{6,14},... | collective-permute-start | bytes 393224 | tf_op jit(solution)/shard_map/ppermute | solution.py:372
  46.4 2.1 %shard_map.105 = (bf16[2,384,256]{2,1,0:T(8,128)(2,1)S(1)}, f32[2,2,384,128]{3,2,1,0:T(8,128)S(1)}, f32[2,2,384,128]{3,2,1,0:T(8,128)S(1)}) custom-call(bf16[2,272,128]{2,1,0:T(8,128)(2,1)S(1)} %collective-permute-done.6.pair, bf16[2,256,128]{2,1,0:T(8,128)(2,1)S(1)} %get-tuple-element.100.before, bf16[2,272,128]{2,1,0:T(8,128)(2,1)S(1)} %collective-permute-done.7.middle, ...), custom_call_target="tpu_custom_call" | custom-call | flops 100000000 | bytes 300000 | tf_op jit(solution)/shard_map/pallas_call | solution.py:48
  48.7 2.3 %shard_map.106 = (f32[4,384,256]{2,1,0:T(8,128)S(1)}, bf16[4,384,256]{2,1,0:T(8,128)(2,1)S(1)}) custom-call(bf16[2,272,128]{2,1,0:T(8,128)(2,1)S(1)} %collective-permute-done.14.pair, bf16[2,272,128]{2,1,0:T(8,128)(2,1)S(1)} %collective-permute-done.15.middle, bf16[2,288,128]{2,1,0:T(8,128)(2,1)S(1)} %collective-permute-done.16.further, ...), custom_call_target="tpu_custom_call" | custom-call | flops 2000000000 | bytes 6000000 | tf_op jit(solution)/shard_map/pallas_call | solution.py:48
  52.0 1.3 %collective-permute-done.19.partner = bf16[4,384,256]{2,1,0:T(8,128)(2,1)S(1)} collective-permute-done((bf16[4,384,256]{2,1,0:T(8,128)(2,1)S(1)}, bf16[4,384,256]{2,1,0:T(8,128)(2,1)S(1)}, u32[]{:S(2)}, u32[]{:S(2)}) %collective-permute-start.19) | collective-permute-done | bytes 786464 | tf_op jit(solution)/shard_map/ppermute | solution.py:372
  53.3 1.1 %collective-permute-done.20.out_partner = bf16[384,1024]{1,0:T(8,128)(2,1)S(1)} collective-permute-done((bf16[384,1024]{1,0:T(8,128)(2,1)S(1)}, bf16[384,1024]{1,0:T(8,128)(2,1)S(1)}, u32[]{:S(2)}, u32[]{:S(2)}) %collective-permute-start.20) | collective-permute-done | bytes 786464 | tf_op jit(solution)/shard_map/ppermute | solution.py:372
  54.5 2.2 %shard_map.108 = (bf16[384,1024]{1,0:T(8,128)(2,1)}, bf16[384,1024]{1,0:T(8,128)(2,1)}) custom-call(f32[4,384,256]{2,1,0:T(8,128)S(1)} %get-tuple-element.110.own, bf16[4,384,256]{2,1,0:T(8,128)(2,1)S(1)} %collective-permute-done.19.partner, bf16[384,1024]{1,0:T(8,128)(2,1)S(1)} %collective-permute-done.20.out_partner, bf16[384,1024]{1,0:T(8,128)(2,1)S(1)} %bitcast.14, ...), custom_call_target="tpu_custom_call" | custom-call | flops 2000000000 | bytes 6000000 | tf_op jit(solution)/shard_map/pallas_call | solution.py:48
  (53 shorter events, 10.2 us)
Async XLA Ops:
  1.7 6.3 %collective-permute-start = (bf16[128,512]{1,0:T(8,128)(2,1)S(1)}, bf16[128,512]{1,0:T(8,128)(2,1)S(1)}, u32[]{:S(2)}, u32[]{:S(2)}) collective-permute-start(bf16[128,512]{1,0:T(8,128)(2,1)S(1)} %shard_map.94._), channel_id=1, source_target_pairs={{0,3},{1,2},{2,1},{3,0},{4,7},{5,6},{6,5},{7,4},{8,11},{9,10},{10,... | collective-permute-start | bytes 393224 | tf_op jit(solution)/shard_map/ppermute | solution.py:372
  4.1 6.3 %copy-start.5 = (f32[1024]{0:T(1024)S(1)}, f32[1024]{0:T(1024)}, u32[]{:S(2)}) copy-start(f32[1024]{0:T(1024)} %param.9) | copy-start | bytes 12292
  4.1 6.3 %collective-permute-start.1 = (bf16[384,1024]{1,0:T(8,128)(2,1)S(1)}, bf16[384,1024]{1,0:T(8,128)(2,1)S(1)}, u32[]{:S(2)}, u32[]{:S(2)}) collective-permute-start(bf16[384,1024]{1,0:T(8,128)(2,1)S(1)} %bitcast.12), channel_id=1, source_target_pairs={{0,1},{1,0},{2,3},{3,2},{4,5},{5,4},{6,7},{7,6},{8,9},{9,8},{10,11... | collective-permute-start | bytes 2359304 | tf_op jit(solution)/shard_map/ppermute | solution.py:372
  4.8 5.7 %collective-permute-start.2 = (bf16[384,1024]{1,0:T(8,128)(2,1)S(1)}, bf16[384,1024]{1,0:T(8,128)(2,1)S(1)}, u32[]{:S(2)}, u32[]{:S(2)}) collective-permute-start(bf16[384,1024]{1,0:T(8,128)(2,1)S(1)} %bitcast.6), channel_id=1, source_target_pairs={{0,1},{1,0},{2,3},{3,2},{4,5},{5,4},{6,7},{7,6},{8,9},{9,8},{10,11... | collective-permute-start | bytes 2359304 | tf_op jit(solution)/shard_map/ppermute | solution.py:372
  5.1 9.8 %collective-permute-start.4 = (bf16[256,512]{1,0:T(8,128)(2,1)S(1)}, bf16[256,512]{1,0:T(8,128)(2,1)S(1)}, u32[]{:S(2)}, u32[]{:S(2)}) collective-permute-start(bf16[256,512]{1,0:T(8,128)(2,1)S(1)} %get-tuple-element.67.w0), channel_id=1, source_target_pairs={{0,2},{1,3},{2,0},{3,1},{4,6},{5,7},{6,4},{7,5},{8,10},{9,11},{10,... | collective-permute-start | bytes 786440 | tf_op jit(solution)/shard_map/ppermute | solution.py:372
  5.7 5.6 %collective-permute-start.3 = (bf16[272,768]{1,0:T(8,128)(2,1)S(1)}, bf16[272,768]{1,0:T(8,128)(2,1)S(1)}, u32[]{:S(2)}, u32[]{:S(2)}) collective-permute-start(bf16[272,768]{1,0:T(8,128)(2,1)S(1)} %get-tuple-element.70), channel_id=1, source_target_pairs={{0,1},{1,0},{2,3},{3,2},{4,5},{5,4},{6,7},{7,6},{8,9},{9,8},{10,11... | collective-permute-start | bytes 1253384 | tf_op jit(solution)/shard_map/ppermute | solution.py:372
  8.0 6.9 %collective-permute-start.5 = (bf16[128,512]{1,0:T(8,128)(2,1)S(1)}, bf16[128,512]{1,0:T(8,128)(2,1)S(1)}, u32[]{:S(2)}, u32[]{:S(2)}) collective-permute-start(bf16[128,512]{1,0:T(8,128)(2,1)S(1)} %collective-permute-done.w3), channel_id=1, source_target_pairs={{0,16},{16,0},{1,17},{17,1},{2,18},{18,2},{3,19},{19,3},{4,20},{20... | collective-permute-start | bytes 393224 | tf_op jit(solution)/shard_map/ppermute | solution.py:372
  11.8 8.4 %collective-permute-start.10 = (bf16[256,256]{1,0:T(8,128)(2,1)S(1)}, bf16[256,256]{1,0:T(8,128)(2,1)S(1)}, u32[]{:S(2)}, u32[]{:S(2)}) collective-permute-start(bf16[256,256]{1,0:T(8,128)(2,1)S(1)} %get-tuple-element.82), channel_id=1, source_target_pairs={{0,3},{1,2},{2,1},{3,0},{4,7},{5,6},{6,5},{7,4},{8,11},{9,10},{10,... | collective-permute-start | bytes 393224 | tf_op jit(solution)/shard_map/ppermute | solution.py:372
  12.9 8.1 %collective-permute-start.9 = (bf16[256,256]{1,0:T(8,128)(2,1)S(1)}, bf16[256,256]{1,0:T(8,128)(2,1)S(1)}, u32[]{:S(2)}, u32[]{:S(2)}) collective-permute-start(bf16[256,256]{1,0:T(8,128)(2,1)S(1)} %get-tuple-element.81.w0.q0), channel_id=1, source_target_pairs={{0,2},{1,3},{2,0},{3,1},{4,6},{5,7},{6,4},{7,5},{8,10},{9,11},{10,... | collective-permute-start | bytes 393224 | tf_op jit(solution)/shard_map/ppermute | solution.py:372
  13.5 12.6 %collective-permute-start.11 = (bf16[128,1024]{1,0:T(8,128)(2,1)S(1)}, bf16[128,1024]{1,0:T(8,128)(2,1)S(1)}, u32[]{:S(2)}, u32[]{:S(2)}) collective-permute-start(bf16[128,1024]{1,0:T(8,128)(2,1)S(1)} %copy-done.1), channel_id=1, source_target_pairs={{0,2},{1,3},{2,0},{3,1},{4,6},{5,7},{6,4},{7,5},{8,10},{9,11},{10,... | collective-permute-start | bytes 786440 | tf_op jit(solution)/shard_map/ppermute | solution.py:372
  16.0 11.1 %collective-permute-start.8 = (bf16[2,288,128]{2,1,0:T(8,128)(2,1)S(1)}, bf16[2,288,128]{2,1,0:T(8,128)(2,1)S(1)}, u32[]{:S(2)}, u32[]{:S(2)}) collective-permute-start(bf16[2,288,128]{2,1,0:T(8,128)(2,1)S(1)} %get-tuple-element.80), channel_id=1, source_target_pairs={{0,8},{4,12},{8,0},{12,4},{1,9},{5,13},{9,1},{13,5},{2,10},{6,14},... | collective-permute-start | bytes 442376 | tf_op jit(solution)/shard_map/ppermute | solution.py:372
  18.7 8.4 %collective-permute-start.6 = (bf16[2,272,128]{2,1,0:T(8,128)(2,1)S(1)}, bf16[2,272,128]{2,1,0:T(8,128)(2,1)S(1)}, u32[]{:S(2)}, u32[]{:S(2)}) collective-permute-start(bf16[2,272,128]{2,1,0:T(8,128)(2,1)S(1)} %get-tuple-element.78), channel_id=1, source_target_pairs={{0,4},{4,0},{8,12},{12,8},{1,5},{5,1},{9,13},{13,9},{2,6},{6,2},{1... | collective-permute-start | bytes 417800 | tf_op jit(solution)/shard_map/ppermute | solution.py:372
  20.3 6.8 %collective-permute-start.7 = (bf16[2,272,128]{2,1,0:T(8,128)(2,1)S(1)}, bf16[2,272,128]{2,1,0:T(8,128)(2,1)S(1)}, u32[]{:S(2)}, u32[]{:S(2)}) collective-permute-start(bf16[2,272,128]{2,1,0:T(8,128)(2,1)S(1)} %get-tuple-element.79), channel_id=1, source_target_pairs={{4,8},{8,4},{5,9},{9,5},{6,10},{10,6},{7,11},{11,7},{20,24},{24,20... | collective-permute-start | bytes 417800 | tf_op jit(solution)/shard_map/ppermute | solution.py:383
  28.7 7.9 %collective-permute-start.12 = (bf16[64,1024]{1,0:T(8,128)(2,1)S(1)}, bf16[64,1024]{1,0:T(8,128)(2,1)S(1)}, u32[]{:S(2)}, u32[]{:S(2)}) collective-permute-start(bf16[64,1024]{1,0:T(8,128)(2,1)S(1)} %get-tuple-element.93), channel_id=1, source_target_pairs={{0,2},{1,3},{2,0},{3,1},{4,6},{5,7},{6,4},{7,5},{8,10},{9,11},{10,... | collective-permute-start | bytes 393224 | tf_op jit(solution)/shard_map/ppermute | solution.py:372
  30.3 6.3 %collective-permute-start.13 = (bf16[2,32,1024]{2,1,0:T(8,128)(2,1)S(1)}, bf16[2,32,1024]{2,1,0:T(8,128)(2,1)S(1)}, u32[]{:S(2)}, u32[]{:S(2)}) collective-permute-start(bf16[2,32,1024]{2,1,0:T(8,128)(2,1)S(1)} %get-tuple-element.94), channel_id=1, source_target_pairs={{0,4},{4,0},{8,12},{12,8},{1,5},{5,1},{9,13},{13,9},{2,6},{6,2},{1... | collective-permute-start | bytes 393224 | tf_op jit(solution)/shard_map/ppermute | solution.py:372
  32.5 16.0 %collective-permute-start.15 = (bf16[2,272,128]{2,1,0:T(8,128)(2,1)S(1)}, bf16[2,272,128]{2,1,0:T(8,128)(2,1)S(1)}, u32[]{:S(2)}, u32[]{:S(2)}) collective-permute-start(bf16[2,272,128]{2,1,0:T(8,128)(2,1)S(1)} %get-tuple-element.98), channel_id=1, source_target_pairs={{4,8},{8,4},{5,9},{9,5},{6,10},{10,6},{7,11},{11,7},{20,24},{24,20... | collective-permute-start | bytes 417800 | tf_op jit(solution)/shard_map/ppermute | solution.py:383
  33.4 15.3 %collective-permute-start.16 = (bf16[2,288,128]{2,1,0:T(8,128)(2,1)S(1)}, bf16[2,288,128]{2,1,0:T(8,128)(2,1)S(1)}, u32[]{:S(2)}, u32[]{:S(2)}) collective-permute-start(bf16[2,288,128]{2,1,0:T(8,128)(2,1)S(1)} %get-tuple-element.99), channel_id=1, source_target_pairs={{0,8},{4,12},{8,0},{12,4},{1,9},{5,13},{9,1},{13,5},{2,10},{6,14},... | collective-permute-start | bytes 442376 | tf_op jit(solution)/shard_map/ppermute | solution.py:372
  36.7 5.6 %collective-permute-start.17 = (bf16[32,1024]{1,0:T(8,128)(2,1)S(1)}, bf16[32,1024]{1,0:T(8,128)(2,1)S(1)}, u32[]{:S(2)}, u32[]{:S(2)}) collective-permute-start(bf16[32,1024]{1,0:T(8,128)(2,1)S(1)} %get-tuple-element.102), channel_id=1, source_target_pairs={{0,4},{4,0},{8,12},{12,8},{1,5},{5,1},{9,13},{13,9},{2,6},{6,2},{1... | collective-permute-start | bytes 196616 | tf_op jit(solution)/shard_map/ppermute | solution.py:372
  37.8 4.5 %collective-permute-start.18 = (bf16[32,1024]{1,0:T(8,128)(2,1)S(1)}, bf16[32,1024]{1,0:T(8,128)(2,1)S(1)}, u32[]{:S(2)}, u32[]{:S(2)}) collective-permute-start(bf16[32,1024]{1,0:T(8,128)(2,1)S(1)} %get-tuple-element.103), channel_id=1, source_target_pairs={{0,2},{1,3},{2,0},{3,1},{4,6},{5,7},{6,4},{7,5},{8,10},{9,11},{10,... | collective-permute-start | bytes 196616 | tf_op jit(solution)/shard_map/ppermute | solution.py:372
  39.3 9.4 %collective-permute-start.14 = (bf16[2,272,128]{2,1,0:T(8,128)(2,1)S(1)}, bf16[2,272,128]{2,1,0:T(8,128)(2,1)S(1)}, u32[]{:S(2)}, u32[]{:S(2)}) collective-permute-start(bf16[2,272,128]{2,1,0:T(8,128)(2,1)S(1)} %get-tuple-element.97), channel_id=1, source_target_pairs={{0,4},{4,0},{8,12},{12,8},{1,5},{5,1},{9,13},{13,9},{2,6},{6,2},{1... | collective-permute-start | bytes 417800 | tf_op jit(solution)/shard_map/ppermute | solution.py:372
  42.4 9.5 %collective-permute-start.21 = (bf16[64,1024]{1,0:T(8,128)(2,1)S(1)}, bf16[64,1024]{1,0:T(8,128)(2,1)S(1)}, u32[]{:S(2)}, u32[]{:S(2)}) collective-permute-start(bf16[64,1024]{1,0:T(8,128)(2,1)S(1)} %get-tuple-element.119), channel_id=1, source_target_pairs={{0,8},{4,12},{8,0},{12,4},{1,9},{5,13},{9,1},{13,5},{2,10},{6,14},... | collective-permute-start | bytes 393224 | tf_op jit(solution)/shard_map/ppermute | solution.py:372
  51.0 2.4 %collective-permute-start.19 = (bf16[4,384,256]{2,1,0:T(8,128)(2,1)S(1)}, bf16[4,384,256]{2,1,0:T(8,128)(2,1)S(1)}, u32[]{:S(2)}, u32[]{:S(2)}) collective-permute-start(bf16[4,384,256]{2,1,0:T(8,128)(2,1)S(1)} %get-tuple-element.113), channel_id=1, source_target_pairs={{0,1},{1,0},{2,3},{3,2},{4,5},{5,4},{6,7},{7,6},{8,9},{9,8},{10,11... | collective-permute-start | bytes 2359304 | tf_op jit(solution)/shard_map/ppermute | solution.py:372
  51.1 3.4 %collective-permute-start.20 = (bf16[384,1024]{1,0:T(8,128)(2,1)S(1)}, bf16[384,1024]{1,0:T(8,128)(2,1)S(1)}, u32[]{:S(2)}, u32[]{:S(2)}) collective-permute-start(bf16[384,1024]{1,0:T(8,128)(2,1)S(1)} %shard_map.107), channel_id=1, source_target_pairs={{0,1},{1,0},{2,3},{3,2},{4,5},{5,4},{6,7},{7,6},{8,9},{9,8},{10,11... | collective-permute-start | bytes 2359304 | tf_op jit(solution)/shard_map/ppermute | solution.py:372
  52.0 5.2 %collective-permute-start.22 = (bf16[64,1024]{1,0:T(8,128)(2,1)S(1)}, bf16[64,1024]{1,0:T(8,128)(2,1)S(1)}, u32[]{:S(2)}, u32[]{:S(2)}) collective-permute-start(bf16[64,1024]{1,0:T(8,128)(2,1)S(1)} %get-tuple-element.124), channel_id=1, source_target_pairs={{0,4},{4,0},{8,12},{12,8},{1,5},{5,1},{9,13},{13,9},{2,6},{6,2},{1... | collective-permute-start | bytes 393224 | tf_op jit(solution)/shard_map/ppermute | solution.py:372
  (6 other events, 23.1 us)

commit v8 on v7

--- a/solution.py
+++ b/solution.py
@@ -443,13 +443,14 @@
     kv_half, flat, cot = lax.optimization_barrier((kv_half, flat, cot))
     kv_x, kv_pair = flip(kv_mine, "dp", 2), flip(kv_other, "dp", 1)
     partner, cot_partner = flip(flat, "dp", 1), flip(cot, "dp", 1)
-    kv_diagonal_other = flip(kv_diagonal, "groups", 1)
-    kv_diagonal, partner, cot_partner, w_late = lax.optimization_barrier((kv_diagonal, partner, cot_partner, w_qkv))
+    partner, cot_partner, w_late = lax.optimization_barrier((partner, cot_partner, w_qkv))
     normed, inv_rms, raw_near = call(
         prep_body,
         [((4, 2 * length, D // 4), bf16), ((length, 1), f32), ((2 * length, 4 * HEAD_DIM), f32)],
         flat, partner, gain, kv_mine, us=PREP,
     )
+    kv_diagonal, inv_rms = lax.optimization_barrier((kv_diagonal, inv_rms))
+    kv_diagonal_other = flip(kv_diagonal, "groups", 1)
     raw_near, seg_col, seg_row = call(
         pair_body,
         [((2 * length, 4 * HEAD_DIM), f32), ((2, length, HEAD_DIM), f32), ((2, 1, length), f32)],

time: 58.2 us -> 58.2 us (level)
  transfers between devices with their start and end apart: 23 -> 23, of which waited for: 8 -> 11; matrix products, arithmetic and copies ran while one was open for 0% -> 0% of each run, Pallas kernels for 22% -> 22%
where the time goes in v8:
time: 58.2 us; the launch traced here: 58 us
  starting transfers between devices  29.5 us (51%)
  Pallas kernels  16.5 us (28%)
  waiting for transfers between devices  11.1 us (19%)
  between operations  0.86 us (1%)
    ppermute x21, starting transfers between devices, flip(): return lax.ppermute(array, axis, [(i, i ^ bit) for i in range(n)])  28 us
    pallas_call x14, Pallas kernels, call(): pl.pallas_call(body, out_shape=[jax.ShapeDtypeStruct(shape, dtype) for sh...  15.1 us
    ppermute x21, waiting for transfers between devices, flip(): return lax.ppermute(array, axis, [(i, i ^ bit) for i in range(n)])  11.1 us
    ppermute x2, starting transfers between devices, carry(): middle = lax.ppermute(middle, 'seq', [(1, 2), (2, 1)])  1.5 us
    pallas_call x3, Pallas kernels, split(): pl.pallas_call(body, out_shape=[jax.ShapeDtypeStruct(shape, bf16) for sha...  1.36 us
  transfers between devices with their start and end apart: 23, of which 11 were waited for; matrix products, arithmetic and copies ran while one was open for 0% of the time, Pallas kernels for 22%

profile of v8, /device:TPU:0, one launch (start us, length us, event | category | flops | bytes accessed | tf_op | source)
XLA Modules:
  0.0 58.0 jit_solution(17719013449621079016)
XLA Ops:
  0.7 1.0 %shard_map.94._ = bf16[128,512]{1,0:T(8,128)(2,1)S(1)} custom-call(bf16[256,1536]{1,0:T(8,128)(2,1)} %w.4), custom_call_target="tpu_custom_call" | custom-call | flops 1000000000 | bytes 1000000 | tf_op jit(solution)/shard_map/pallas_call | solution.py:110
  1.7 2.4 %collective-permute-start.4 = (bf16[128,512]{1,0:T(8,128)(2,1)S(1)}, bf16[128,512]{1,0:T(8,128)(2,1)S(1)}, u32[]{:S(2)}, u32[]{:S(2)}) collective-permute-start(bf16[128,512]{1,0:T(8,128)(2,1)S(1)} %shard_map.94._), channel_id=1, source_target_pairs={{0,3},{1,2},{2,1},{3,0},{4,7},{5,6},{6,5},{7,4},{8,11},{9,10},{10,... | collective-permute-start | bytes 393224 | tf_op jit(solution)/shard_map/ppermute | solution.py:372
  6.7 1.1 %collective-permute-done.1.cot_partner = bf16[384,1024]{1,0:T(8,128)(2,1)S(1)} collective-permute-done((bf16[384,1024]{1,0:T(8,128)(2,1)S(1)}, bf16[384,1024]{1,0:T(8,128)(2,1)S(1)}, u32[]{:S(2)}, u32[]{:S(2)}) %collective-permute-start.1) | collective-permute-done | bytes 786464 | tf_op jit(solution)/shard_map/ppermute | solution.py:372
  8.7 1.8 %collective-permute-start.5 = (bf16[128,512]{1,0:T(8,128)(2,1)S(1)}, bf16[128,512]{1,0:T(8,128)(2,1)S(1)}, u32[]{:S(2)}, u32[]{:S(2)}) collective-permute-start(bf16[128,512]{1,0:T(8,128)(2,1)S(1)} %collective-permute-done.4.w3), channel_id=1, source_target_pairs={{0,16},{16,0},{1,17},{17,1},{2,18},{18,2},{3,19},{19,3},{4,20},{20... | collective-permute-start | bytes 393224 | tf_op jit(solution)/shard_map/ppermute | solution.py:372
  11.0 1.0 %collective-permute-start.10 = (bf16[256,256]{1,0:T(8,128)(2,1)S(1)}, bf16[256,256]{1,0:T(8,128)(2,1)S(1)}, u32[]{:S(2)}, u32[]{:S(2)}) collective-permute-start(bf16[256,256]{1,0:T(8,128)(2,1)S(1)} %get-tuple-element.84), channel_id=1, source_target_pairs={{0,3},{1,2},{2,1},{3,0},{4,7},{5,6},{6,5},{7,4},{8,11},{9,10},{10,... | collective-permute-start | bytes 393224 | tf_op jit(solution)/shard_map/ppermute | solution.py:372
  12.7 1.4 %collective-permute-start.11 = (bf16[128,1024]{1,0:T(8,128)(2,1)S(1)}, bf16[128,1024]{1,0:T(8,128)(2,1)S(1)}, u32[]{:S(2)}, u32[]{:S(2)}) collective-permute-start(bf16[128,1024]{1,0:T(8,128)(2,1)S(1)} %copy-done.1), channel_id=1, source_target_pairs={{0,2},{1,3},{2,0},{3,1},{4,6},{5,7},{6,4},{7,5},{8,10},{9,11},{10,... | collective-permute-start | bytes 786440 | tf_op jit(solution)/shard_map/ppermute | solution.py:372
  14.5 1.1 %shard_map.99 = (bf16[2,2,384,128]{3,2,1,0:T(8,128)(2,1)S(1)}, bf16[2,2,384,128]{3,2,1,0:T(8,128)(2,1)S(1)}, bf16[2,272,128]{2,1,0:T(8,128)(2,1)S(1)}, bf16[2,27...) custom-call(f32[768,512]{1,0:T(8,128)S(1)} %get-tuple-element.76.near, bf16[4,768,256]{2,1,0:T(8,128)(2,1)S(1)} %get-tuple-element.70.normed, ...), custom_call_target="tpu_custom_call" | custom-call | flops 2000000000 | bytes 6000000 | tf_op jit(solution)/shard_map/pallas_call | solution.py:48
  15.7 2.8 %collective-permute-start.8 = (bf16[2,288,128]{2,1,0:T(8,128)(2,1)S(1)}, bf16[2,288,128]{2,1,0:T(8,128)(2,1)S(1)}, u32[]{:S(2)}, u32[]{:S(2)}) collective-permute-start(bf16[2,288,128]{2,1,0:T(8,128)(2,1)S(1)} %get-tuple-element.82), channel_id=1, source_target_pairs={{0,8},{4,12},{8,0},{12,4},{1,9},{5,13},{9,1},{13,5},{2,10},{6,14},... | collective-permute-start | bytes 442376 | tf_op jit(solution)/shard_map/ppermute | solution.py:372
  18.5 1.6 %collective-permute-start.6 = (bf16[2,272,128]{2,1,0:T(8,128)(2,1)S(1)}, bf16[2,272,128]{2,1,0:T(8,128)(2,1)S(1)}, u32[]{:S(2)}, u32[]{:S(2)}) collective-permute-start(bf16[2,272,128]{2,1,0:T(8,128)(2,1)S(1)} %get-tuple-element.80), channel_id=1, source_target_pairs={{0,4},{4,0},{8,12},{12,8},{1,5},{5,1},{9,13},{13,9},{2,6},{6,2},{1... | collective-permute-start | bytes 417800 | tf_op jit(solution)/shard_map/ppermute | solution.py:372
  20.7 2.0 %shard_map.100 = (bf16[2,2,384,128]{3,2,1,0:T(8,128)(2,1)S(1)}, f32[2,2,384,128]{3,2,1,0:T(8,128)S(1)}) custom-call(bf16[4,768,256]{2,1,0:T(8,128)(2,1)S(1)} %get-tuple-element.70.normed, bf16[256,256]{1,0:T(8,128)(2,1)S(1)} %get-tuple-element.83.w0.q0, bf16[272,768]{1,0:T(8,128)(2,1)S(1)} %collective-permute-done.2.w1.q1, ...), custom_call_target="tpu_custom_call" | custom-call | flops 500000000 | bytes 1500000 | tf_op jit(solution)/shard_map/pallas_call | solution.py:48
  22.8 2.5 %collective-permute-done.11.other.w_other = bf16[128,1024]{1,0:T(8,128)(2,1)S(1)} collective-permute-done((bf16[128,1024]{1,0:T(8,128)(2,1)S(1)}, bf16[128,1024]{1,0:T(8,128)(2,1)S(1)}, u32[]{:S(2)}, u32[]{:S(2)}) %collective-permute-start.11) | collective-permute-done | bytes 262176 | tf_op jit(solution)/shard_map/ppermute | solution.py:372
  26.5 1.6 %shard_map.102 = (bf16[2,2,384,128]{3,2,1,0:T(8,128)(2,1)S(1)}, bf16[2,2,384,128]{3,2,1,0:T(8,128)(2,1)S(1)}, bf16[2,272,128]{2,1,0:T(8,128)(2,1)S(1)}, bf16[2,2...) custom-call(bf16[2,272,128]{2,1,0:T(8,128)(2,1)S(1)} %collective-per, ...), custom_call_target="tpu_custom_call" | custom-call | flops 2000000000 | bytes 6000000 | tf_op jit(solution)/shard_map/pallas_call | solution.py:48
  28.1 1.9 %collective-permute-start.12 = (bf16[64,1024]{1,0:T(8,128)(2,1)S(1)}, bf16[64,1024]{1,0:T(8,128)(2,1)S(1)}, u32[]{:S(2)}, u32[]{:S(2)}) collective-permute-start(bf16[64,1024]{1,0:T(8,128)(2,1)S(1)} %get-tuple-element.95), channel_id=1, source_target_pairs={{0,2},{1,3},{2,0},{3,1},{4,6},{5,7},{6,4},{7,5},{8,10},{9,11},{10,... | collective-permute-start | bytes 393224 | tf_op jit(solution)/shard_map/ppermute | solution.py:372
  30.0 2.5 %collective-permute-start.13 = (bf16[2,32,1024]{2,1,0:T(8,128)(2,1)S(1)}, bf16[2,32,1024]{2,1,0:T(8,128)(2,1)S(1)}, u32[]{:S(2)}, u32[]{:S(2)}) collective-permute-start(bf16[2,32,1024]{2,1,0:T(8,128)(2,1)S(1)} %get-tuple-element.96), channel_id=1, source_target_pairs={{0,4},{4,0},{8,12},{12,8},{1,5},{5,1},{9,13},{13,9},{2,6},{6,2},{1... | collective-permute-start | bytes 393224 | tf_op jit(solution)/shard_map/ppermute | solution.py:372
  33.4 3.2 %collective-permute-start.16 = (bf16[2,288,128]{2,1,0:T(8,128)(2,1)S(1)}, bf16[2,288,128]{2,1,0:T(8,128)(2,1)S(1)}, u32[]{:S(2)}, u32[]{:S(2)}) collective-permute-start(bf16[2,288,128]{2,1,0:T(8,128)(2,1)S(1)} %get-tuple-element.101), channel_id=1, source_target_pairs={{0,8},{4,12},{8,0},{12,4},{1,9},{5,13},{9,1},{13,5},{2,10},{6,14},... | collective-permute-start | bytes 442376 | tf_op jit(solution)/shard_map/ppermute | solution.py:372
  36.7 1.1 %collective-permute-start.17 = (bf16[32,1024]{1,0:T(8,128)(2,1)S(1)}, bf16[32,1024]{1,0:T(8,128)(2,1)S(1)}, u32[]{:S(2)}, u32[]{:S(2)}) collective-permute-start(bf16[32,1024]{1,0:T(8,128)(2,1)S(1)} %get-tuple-element.104), channel_id=1, source_target_pairs={{0,4},{4,0},{8,12},{12,8},{1,5},{5,1},{9,13},{13,9},{2,6},{6,2},{1... | collective-permute-start | bytes 196616 | tf_op jit(solution)/shard_map/ppermute | solution.py:372
  38.9 1.0 %collective-permute-start.14 = (bf16[2,272,128]{2,1,0:T(8,128)(2,1)S(1)}, bf16[2,272,128]{2,1,0:T(8,128)(2,1)S(1)}, u32[]{:S(2)}, u32[]{:S(2)}) collective-permute-start(bf16[2,272,128]{2,1,0:T(8,128)(2,1)S(1)} %get-tuple-element.99), channel_id=1, source_target_pairs={{0,4},{4,0},{8,12},{12,8},{1,5},{5,1},{9,13},{13,9},{2,6},{6,2},{1... | collective-permute-start | bytes 417800 | tf_op jit(solution)/shard_map/ppermute | solution.py:372
  39.9 2.4 %collective-permute-done.17.a_in = bf16[32,1024]{1,0:T(8,128)(2,1)S(1)} collective-permute-done((bf16[32,1024]{1,0:T(8,128)(2,1)S(1)}, bf16[32,1024]{1,0:T(8,128)(2,1)S(1)}, u32[]{:S(2)}, u32[]{:S(2)}) %collective-permute-start.17) | collective-permute-done | bytes 65568 | tf_op jit(solution)/shard_map/ppermute | solution.py:372
  42.3 4.0 %collective-permute-start.21 = (bf16[64,1024]{1,0:T(8,128)(2,1)S(1)}, bf16[64,1024]{1,0:T(8,128)(2,1)S(1)}, u32[]{:S(2)}, u32[]{:S(2)}) collective-permute-start(bf16[64,1024]{1,0:T(8,128)(2,1)S(1)} %get-tuple-element.121), channel_id=1, source_target_pairs={{0,8},{4,12},{8,0},{12,4},{1,9},{5,13},{9,1},{13,5},{2,10},{6,14},... | collective-permute-start | bytes 393224 | tf_op jit(solution)/shard_map/ppermute | solution.py:372
  46.4 2.1 %shard_map.105 = (bf16[2,384,256]{2,1,0:T(8,128)(2,1)S(1)}, f32[2,2,384,128]{3,2,1,0:T(8,128)S(1)}, f32[2,2,384,128]{3,2,1,0:T(8,128)S(1)}) custom-call(bf16[2,272,128]{2,1,0:T(8,128)(2,1)S(1)} %collective-permute-done.6.pair, bf16[2,256,128]{2,1,0:T(8,128)(2,1)S(1)} %get-tuple-element.102.before, bf16[2,272,128]{2,1,0:T(8,128)(2,1)S(1)} %collective-permute-done.7.middle, ...), custom_call_target="tpu_custom_call" | custom-call | flops 100000000 | bytes 300000 | tf_op jit(solution)/shard_map/pallas_call | solution.py:48
  48.6 2.3 %shard_map.106 = (f32[4,384,256]{2,1,0:T(8,128)S(1)}, bf16[4,384,256]{2,1,0:T(8,128)(2,1)S(1)}) custom-call(bf16[2,272,128]{2,1,0:T(8,128)(2,1)S(1)} %collective-permute-done.14.pair, bf16[2,272,128]{2,1,0:T(8,128)(2,1)S(1)} %collective-permute-done.15.middle, bf16[2,288,128]{2,1,0:T(8,128)(2,1)S(1)} %collective-permute-done.16.further, ...), custom_call_target="tpu_custom_call" | custom-call | flops 2000000000 | bytes 6000000 | tf_op jit(solution)/shard_map/pallas_call | solution.py:48
  52.0 1.3 %collective-permute-done.19.partner = bf16[4,384,256]{2,1,0:T(8,128)(2,1)S(1)} collective-permute-done((bf16[4,384,256]{2,1,0:T(8,128)(2,1)S(1)}, bf16[4,384,256]{2,1,0:T(8,128)(2,1)S(1)}, u32[]{:S(2)}, u32[]{:S(2)}) %collective-permute-start.19) | collective-permute-done | bytes 786464 | tf_op jit(solution)/shard_map/ppermute | solution.py:372
  53.3 1.1 %collective-permute-done.20.out_partner = bf16[384,1024]{1,0:T(8,128)(2,1)S(1)} collective-permute-done((bf16[384,1024]{1,0:T(8,128)(2,1)S(1)}, bf16[384,1024]{1,0:T(8,128)(2,1)S(1)}, u32[]{:S(2)}, u32[]{:S(2)}) %collective-permute-start.20) | collective-permute-done | bytes 786464 | tf_op jit(solution)/shard_map/ppermute | solution.py:372
  54.4 2.2 %shard_map.108 = (bf16[384,1024]{1,0:T(8,128)(2,1)}, bf16[384,1024]{1,0:T(8,128)(2,1)}) custom-call(f32[4,384,256]{2,1,0:T(8,128)S(1)} %get-tuple-element.112.own, bf16[4,384,256]{2,1,0:T(8,128)(2,1)S(1)} %collective-permute-done.19.partner, bf16[384,1024]{1,0:T(8,128)(2,1)S(1)} %collective-permute-done.20.out_partner, bf16[384,1024]{1,0:T(8,128)(2,1)S(1)} %bitcast.14, ...), custom_call_target="tpu_custom_call" | custom-call | flops 2000000000 | bytes 6000000 | tf_op jit(solution)/shard_map/pallas_call | solution.py:48
  (53 shorter events, 11.5 us)
Async XLA Ops:
  1.7 7.0 %collective-permute-start.4 = (bf16[128,512]{1,0:T(8,128)(2,1)S(1)}, bf16[128,512]{1,0:T(8,128)(2,1)S(1)}, u32[]{:S(2)}, u32[]{:S(2)}) collective-permute-start(bf16[128,512]{1,0:T(8,128)(2,1)S(1)} %shard_map.94._), channel_id=1, source_target_pairs={{0,3},{1,2},{2,1},{3,0},{4,7},{5,6},{6,5},{7,4},{8,11},{9,10},{10,... | collective-permute-start | bytes 393224 | tf_op jit(solution)/shard_map/ppermute | solution.py:372
  4.1 2.6 %collective-permute-start = (bf16[384,1024]{1,0:T(8,128)(2,1)S(1)}, bf16[384,1024]{1,0:T(8,128)(2,1)S(1)}, u32[]{:S(2)}, u32[]{:S(2)}) collective-permute-start(bf16[384,1024]{1,0:T(8,128)(2,1)S(1)} %bitcast.12), channel_id=1, source_target_pairs={{0,1},{1,0},{2,3},{3,2},{4,5},{5,4},{6,7},{7,6},{8,9},{9,8},{10,11... | collective-permute-start | bytes 2359304 | tf_op jit(solution)/shard_map/ppermute | solution.py:372
  4.8 3.0 %collective-permute-start.1 = (bf16[384,1024]{1,0:T(8,128)(2,1)S(1)}, bf16[384,1024]{1,0:T(8,128)(2,1)S(1)}, u32[]{:S(2)}, u32[]{:S(2)}) collective-permute-start(bf16[384,1024]{1,0:T(8,128)(2,1)S(1)} %bitcast.6), channel_id=1, source_target_pairs={{0,1},{1,0},{2,3},{3,2},{4,5},{5,4},{6,7},{7,6},{8,9},{9,8},{10,11... | collective-permute-start | bytes 2359304 | tf_op jit(solution)/shard_map/ppermute | solution.py:372
  5.1 8.9 %collective-permute-start.3 = (bf16[256,512]{1,0:T(8,128)(2,1)S(1)}, bf16[256,512]{1,0:T(8,128)(2,1)S(1)}, u32[]{:S(2)}, u32[]{:S(2)}) collective-permute-start(bf16[256,512]{1,0:T(8,128)(2,1)S(1)} %get-tuple-element.68.w0), channel_id=1, source_target_pairs={{0,2},{1,3},{2,0},{3,1},{4,6},{5,7},{6,4},{7,5},{8,10},{9,11},{10,... | collective-permute-start | bytes 786440 | tf_op jit(solution)/shard_map/ppermute | solution.py:372
  5.7 4.7 %collective-permute-start.2 = (bf16[272,768]{1,0:T(8,128)(2,1)S(1)}, bf16[272,768]{1,0:T(8,128)(2,1)S(1)}, u32[]{:S(2)}, u32[]{:S(2)}) collective-permute-start(bf16[272,768]{1,0:T(8,128)(2,1)S(1)} %get-tuple-element.71), channel_id=1, source_target_pairs={{0,1},{1,0},{2,3},{3,2},{4,5},{5,4},{6,7},{7,6},{8,9},{9,8},{10,11... | collective-permute-start | bytes 1253384 | tf_op jit(solution)/shard_map/ppermute | solution.py:372
  8.7 5.8 %collective-permute-start.5 = (bf16[128,512]{1,0:T(8,128)(2,1)S(1)}, bf16[128,512]{1,0:T(8,128)(2,1)S(1)}, u32[]{:S(2)}, u32[]{:S(2)}) collective-permute-start(bf16[128,512]{1,0:T(8,128)(2,1)S(1)} %collective-permute-done.4.w3), channel_id=1, source_target_pairs={{0,16},{16,0},{1,17},{17,1},{2,18},{18,2},{3,19},{19,3},{4,20},{20... | collective-permute-start | bytes 393224 | tf_op jit(solution)/shard_map/ppermute | solution.py:372
  11.0 9.1 %collective-permute-start.10 = (bf16[256,256]{1,0:T(8,128)(2,1)S(1)}, bf16[256,256]{1,0:T(8,128)(2,1)S(1)}, u32[]{:S(2)}, u32[]{:S(2)}) collective-permute-start(bf16[256,256]{1,0:T(8,128)(2,1)S(1)} %get-tuple-element.84), channel_id=1, source_target_pairs={{0,3},{1,2},{2,1},{3,0},{4,7},{5,6},{6,5},{7,4},{8,11},{9,10},{10,... | collective-permute-start | bytes 393224 | tf_op jit(solution)/shard_map/ppermute | solution.py:372
  12.0 8.7 %collective-permute-start.9 = (bf16[256,256]{1,0:T(8,128)(2,1)S(1)}, bf16[256,256]{1,0:T(8,128)(2,1)S(1)}, u32[]{:S(2)}, u32[]{:S(2)}) collective-permute-start(bf16[256,256]{1,0:T(8,128)(2,1)S(1)} %get-tuple-element.83.w0.q0), channel_id=1, source_target_pairs={{0,2},{1,3},{2,0},{3,1},{4,6},{5,7},{6,4},{7,5},{8,10},{9,11},{10,... | collective-permute-start | bytes 393224 | tf_op jit(solution)/shard_map/ppermute | solution.py:372
  12.7 12.6 %collective-permute-start.11 = (bf16[128,1024]{1,0:T(8,128)(2,1)S(1)}, bf16[128,1024]{1,0:T(8,128)(2,1)S(1)}, u32[]{:S(2)}, u32[]{:S(2)}) collective-permute-start(bf16[128,1024]{1,0:T(8,128)(2,1)S(1)} %copy-done.1), channel_id=1, source_target_pairs={{0,2},{1,3},{2,0},{3,1},{4,6},{5,7},{6,4},{7,5},{8,10},{9,11},{10,... | collective-permute-start | bytes 786440 | tf_op jit(solution)/shard_map/ppermute | solution.py:372
  15.7 10.8 %collective-permute-start.8 = (bf16[2,288,128]{2,1,0:T(8,128)(2,1)S(1)}, bf16[2,288,128]{2,1,0:T(8,128)(2,1)S(1)}, u32[]{:S(2)}, u32[]{:S(2)}) collective-permute-start(bf16[2,288,128]{2,1,0:T(8,128)(2,1)S(1)} %get-tuple-element.82), channel_id=1, source_target_pairs={{0,8},{4,12},{8,0},{12,4},{1,9},{5,13},{9,1},{13,5},{2,10},{6,14},... | collective-permute-start | bytes 442376 | tf_op jit(solution)/shard_map/ppermute | solution.py:372
  18.5 7.8 %collective-permute-start.6 = (bf16[2,272,128]{2,1,0:T(8,128)(2,1)S(1)}, bf16[2,272,128]{2,1,0:T(8,128)(2,1)S(1)}, u32[]{:S(2)}, u32[]{:S(2)}) collective-permute-start(bf16[2,272,128]{2,1,0:T(8,128)(2,1)S(1)} %get-tuple-element.80), channel_id=1, source_target_pairs={{0,4},{4,0},{8,12},{12,8},{1,5},{5,1},{9,13},{13,9},{2,6},{6,2},{1... | collective-permute-start | bytes 417800 | tf_op jit(solution)/shard_map/ppermute | solution.py:372
  20.0 6.2 %collective-permute-start.7 = (bf16[2,272,128]{2,1,0:T(8,128)(2,1)S(1)}, bf16[2,272,128]{2,1,0:T(8,128)(2,1)S(1)}, u32[]{:S(2)}, u32[]{:S(2)}) collective-permute-start(bf16[2,272,128]{2,1,0:T(8,128)(2,1)S(1)} %get-tuple-element.81), channel_id=1, source_target_pairs={{4,8},{8,4},{5,9},{9,5},{6,10},{10,6},{7,11},{11,7},{20,24},{24,20... | collective-permute-start | bytes 417800 | tf_op jit(solution)/shard_map/ppermute | solution.py:383
  20.7 4.6 %copy-start.2 = (f32[512]{0:T(512)S(1)}, f32[512]{0:T(512)}, u32[]{:S(2)}) copy-start(f32[512]{0:T(512)} %param.11) | copy-start | bytes 6148
  28.1 8.5 %collective-permute-start.12 = (bf16[64,1024]{1,0:T(8,128)(2,1)S(1)}, bf16[64,1024]{1,0:T(8,128)(2,1)S(1)}, u32[]{:S(2)}, u32[]{:S(2)}) collective-permute-start(bf16[64,1024]{1,0:T(8,128)(2,1)S(1)} %get-tuple-element.95), channel_id=1, source_target_pairs={{0,2},{1,3},{2,0},{3,1},{4,6},{5,7},{6,4},{7,5},{8,10},{9,11},{10,... | collective-permute-start | bytes 393224 | tf_op jit(solution)/shard_map/ppermute | solution.py:372
  30.0 6.6 %collective-permute-start.13 = (bf16[2,32,1024]{2,1,0:T(8,128)(2,1)S(1)}, bf16[2,32,1024]{2,1,0:T(8,128)(2,1)S(1)}, u32[]{:S(2)}, u32[]{:S(2)}) collective-permute-start(bf16[2,32,1024]{2,1,0:T(8,128)(2,1)S(1)} %get-tuple-element.96), channel_id=1, source_target_pairs={{0,4},{4,0},{8,12},{12,8},{1,5},{5,1},{9,13},{13,9},{2,6},{6,2},{1... | collective-permute-start | bytes 393224 | tf_op jit(solution)/shard_map/ppermute | solution.py:372
  32.5 15.9 %collective-permute-start.15 = (bf16[2,272,128]{2,1,0:T(8,128)(2,1)S(1)}, bf16[2,272,128]{2,1,0:T(8,128)(2,1)S(1)}, u32[]{:S(2)}, u32[]{:S(2)}) collective-permute-start(bf16[2,272,128]{2,1,0:T(8,128)(2,1)S(1)} %get-tuple-element.100), channel_id=1, source_target_pairs={{4,8},{8,4},{5,9},{9,5},{6,10},{10,6},{7,11},{11,7},{20,24},{24,20... | collective-permute-start | bytes 417800 | tf_op jit(solution)/shard_map/ppermute | solution.py:383
  33.4 15.2 %collective-permute-start.16 = (bf16[2,288,128]{2,1,0:T(8,128)(2,1)S(1)}, bf16[2,288,128]{2,1,0:T(8,128)(2,1)S(1)}, u32[]{:S(2)}, u32[]{:S(2)}) collective-permute-start(bf16[2,288,128]{2,1,0:T(8,128)(2,1)S(1)} %get-tuple-element.101), channel_id=1, source_target_pairs={{0,8},{4,12},{8,0},{12,4},{1,9},{5,13},{9,1},{13,5},{2,10},{6,14},... | collective-permute-start | bytes 442376 | tf_op jit(solution)/shard_map/ppermute | solution.py:372
  36.7 5.6 %collective-permute-start.17 = (bf16[32,1024]{1,0:T(8,128)(2,1)S(1)}, bf16[32,1024]{1,0:T(8,128)(2,1)S(1)}, u32[]{:S(2)}, u32[]{:S(2)}) collective-permute-start(bf16[32,1024]{1,0:T(8,128)(2,1)S(1)} %get-tuple-element.104), channel_id=1, source_target_pairs={{0,4},{4,0},{8,12},{12,8},{1,5},{5,1},{9,13},{13,9},{2,6},{6,2},{1... | collective-permute-start | bytes 196616 | tf_op jit(solution)/shard_map/ppermute | solution.py:372
  37.8 4.5 %collective-permute-start.18 = (bf16[32,1024]{1,0:T(8,128)(2,1)S(1)}, bf16[32,1024]{1,0:T(8,128)(2,1)S(1)}, u32[]{:S(2)}, u32[]{:S(2)}) collective-permute-start(bf16[32,1024]{1,0:T(8,128)(2,1)S(1)} %get-tuple-element.105), channel_id=1, source_target_pairs={{0,2},{1,3},{2,0},{3,1},{4,6},{5,7},{6,4},{7,5},{8,10},{9,11},{10,... | collective-permute-start | bytes 196616 | tf_op jit(solution)/shard_map/ppermute | solution.py:372
  38.9 9.7 %collective-permute-start.14 = (bf16[2,272,128]{2,1,0:T(8,128)(2,1)S(1)}, bf16[2,272,128]{2,1,0:T(8,128)(2,1)S(1)}, u32[]{:S(2)}, u32[]{:S(2)}) collective-permute-start(bf16[2,272,128]{2,1,0:T(8,128)(2,1)S(1)} %get-tuple-element.99), channel_id=1, source_target_pairs={{0,4},{4,0},{8,12},{12,8},{1,5},{5,1},{9,13},{13,9},{2,6},{6,2},{1... | collective-permute-start | bytes 417800 | tf_op jit(solution)/shard_map/ppermute | solution.py:372
  42.3 9.6 %collective-permute-start.21 = (bf16[64,1024]{1,0:T(8,128)(2,1)S(1)}, bf16[64,1024]{1,0:T(8,128)(2,1)S(1)}, u32[]{:S(2)}, u32[]{:S(2)}) collective-permute-start(bf16[64,1024]{1,0:T(8,128)(2,1)S(1)} %get-tuple-element.121), channel_id=1, source_target_pairs={{0,8},{4,12},{8,0},{12,4},{1,9},{5,13},{9,1},{13,5},{2,10},{6,14},... | collective-permute-start | bytes 393224 | tf_op jit(solution)/shard_map/ppermute | solution.py:372
  51.0 2.4 %collective-permute-start.19 = (bf16[4,384,256]{2,1,0:T(8,128)(2,1)S(1)}, bf16[4,384,256]{2,1,0:T(8,128)(2,1)S(1)}, u32[]{:S(2)}, u32[]{:S(2)}) collective-permute-start(bf16[4,384,256]{2,1,0:T(8,128)(2,1)S(1)} %get-tuple-element.115), channel_id=1, source_target_pairs={{0,1},{1,0},{2,3},{3,2},{4,5},{5,4},{6,7},{7,6},{8,9},{9,8},{10,11... | collective-permute-start | bytes 2359304 | tf_op jit(solution)/shard_map/ppermute | solution.py:372
  51.0 3.4 %collective-permute-start.20 = (bf16[384,1024]{1,0:T(8,128)(2,1)S(1)}, bf16[384,1024]{1,0:T(8,128)(2,1)S(1)}, u32[]{:S(2)}, u32[]{:S(2)}) collective-permute-start(bf16[384,1024]{1,0:T(8,128)(2,1)S(1)} %shard_map.107), channel_id=1, source_target_pairs={{0,1},{1,0},{2,3},{3,2},{4,5},{5,4},{6,7},{7,6},{8,9},{9,8},{10,11... | collective-permute-start | bytes 2359304 | tf_op jit(solution)/shard_map/ppermute | solution.py:372
  52.0 5.2 %collective-permute-start.22 = (bf16[64,1024]{1,0:T(8,128)(2,1)S(1)}, bf16[64,1024]{1,0:T(8,128)(2,1)S(1)}, u32[]{:S(2)}, u32[]{:S(2)}) collective-permute-start(bf16[64,1024]{1,0:T(8,128)(2,1)S(1)} %get-tuple-element.126), channel_id=1, source_target_pairs={{0,4},{4,0},{8,12},{12,8},{1,5},{5,1},{9,13},{13,9},{2,6},{6,2},{1... | collective-permute-start | bytes 393224 | tf_op jit(solution)/shard_map/ppermute | solution.py:372
  (6 other events, 21.7 us)
